TPU v7x, 32 devices: a whole 2x2x4 slice. The times are simulated.
32 devices in a mesh: lon: 4 (over y, x), sec: 8 (over z, core).
Axes of the slice: x: 2, y: 2, z: 4, core: 2. Of those that a mesh axis runs over, the one named last changes fastest.
Arguments:
- moisture: float32 [16, 128, 1024], P(None, 'sec', 'lon'), may hold values from 0 to 2
- heat: float32 [16, 128, 1024], P(None, 'sec', 'lon'), may hold values from -6 to 6
- moist_cond: float32 [16, 128, 1024], P(None, 'sec', 'lon'), may hold values from 0.05 to 2
- heat_cond: float32 [16, 128, 1024], P(None, 'sec', 'lon'), may hold values from 0.1 to 3
- rain: float32 [128, 1024], P('sec', 'lon'), may hold values from 0.01 to 1
- surface_flux: float32 [128, 1024], P('sec', 'lon'), may hold values from -6 to 6
- cell_reach: int32 [128, 1024], P('sec', 'lon'), may hold values from 0 to 16383
- records: bfloat16 [4, 16384, 256], P('lon', 'sec'), may hold values from 0 to 2
- unit_hydro: bfloat16 [4, 16384, 256], P('lon', 'sec'), may hold values from 0.049804688 to 1
- down_basin: int32 [4, 16384], P('lon', 'sec'), may hold values from 0 to 4095
- basin_home: int32 [4, 4096], P('lon'), may hold values from 0 to 4095, as said below
- send_index: int32 [4, 8, 8, 512], P('lon', 'sec'), may hold values from 0 to 2047, as said below
- send_count: int32 [4, 8, 8], P('lon', 'sec'), may hold values from 0 to 512, as said below
Outputs:
- moist_out: float32 [16, 128, 1024], P(None, 'sec', 'lon')
- heat_out: float32 [16, 128, 1024], P(None, 'sec', 'lon')
- record_out: bfloat16 [4, 16384, 256], P('lon', 'sec')
- basin_inflow: float32 [4, 4096, 256], P('lon', 'sec')
Inputs may be any that keep to these rules, and one draw needn't show every extreme that they name: `send_index`: within a longitude group, device s lists each of its 2048 reaches in exactly one used slot; a reach listed in block d drains into a basin whose basin_home lies in d * 512 to (d+1) * 512 - 1. Unused slots hold 0. `send_count`: in every group one owner receives 512 reaches from every device of sec; counts of owners 2 m and 2 m + 1 from one device add up to 512. `basin_home`: each group's row is a permutation.
All inputs are finite; a program needn't handle non-finite values.
Results may differ from a plain program's by a relative error of at most 0.009.
Values may be sent and summed in bfloat16 or wider, within the bound.
No kernel may reach another device: no remote copies, remote signals or barrier semaphores. Data moves between devices by JAX's collectives and lax.ppermute only.
A program may use at most 64 MiB of HBM per device.

v0:
```python
import jax
import jax.numpy as jnp
from jax import lax
from jax.experimental import pallas as pl
from jax.experimental.pallas import tpu as pltpu
from jax.sharding import PartitionSpec as P

LATERAL = 0.2
LANES = 128
PACK_ROWS = 16
F32 = jnp.float32
BF16 = jnp.bfloat16
I32 = jnp.int32
VMEM = pl.BlockSpec(memory_space=pltpu.VMEM)
HBM = pl.BlockSpec(memory_space=pltpu.HBM)


def call(body, outs, *args, ins=None, out_specs=None, scratch=(), mib=8, flops=0, moved=0):
    ins = list(ins) if ins else [VMEM] * len(args)
    args = [
        pltpu.with_memory_space_constraint(arg, pltpu.HBM) if spec is HBM else arg
        for arg, spec in zip(args, ins)
    ]
    return pl.pallas_call(
        body,
        out_shape=list(outs),
        in_specs=ins,
        out_specs=list(out_specs) if out_specs else [VMEM] * len(outs),
        scratch_shapes=list(scratch),
        compiler_params=pltpu.CompilerParams(vmem_limit_bytes=mib * 1024 * 1024),
        cost_estimate=pl.CostEstimate(flops=flops, bytes_accessed=moved, transcendentals=0),
    )(*args)


def fetch(sources, targets, sems):
    copies = [
        pltpu.make_async_copy(src, dst, sems.at[i])
        for i, (src, dst) in enumerate(zip(sources, targets))
    ]
    for copy in copies:
        copy.start()
    return copies


def parity(axis):
    return lax.rem(lax.axis_index(axis), 2)


def edges_body(
    moist_in, heat_in, home_in, down_in, listed_in,
    moist, heat, home, down, listed, sec_near, sec_far, lon_near, lon_far, sems,
):
    copies = fetch(
        (moist_in, heat_in, home_in, down_in, listed_in), (moist, heat, home, down, listed), sems
    )
    layers, rows, cols = moist.shape
    lane = lax.broadcasted_iota(I32, (rows, LANES), 1)
    west = jnp.zeros((rows, LANES), F32)
    east = jnp.zeros((rows, LANES), F32)
    sec_even = parity("sec") == 0
    for f, ref in enumerate((moist, heat)):
        copies[f].wait()
        north = ref[:, 0, :]
        south = ref[:, rows - 1, :]
        sec_near[f * layers : (f + 1) * layers, :] = jnp.where(sec_even, south, north).astype(BF16)
        sec_far[f * layers : (f + 1) * layers, :] = jnp.where(sec_even, north, south).astype(BF16)
        for layer in range(layers):
            k = f * layers + layer
            west = jnp.where(lane == k, ref[layer, :, 0:1], west)
            east = jnp.where(lane == k, ref[layer, :, cols - 1 : cols], east)
    lon_even = parity("lon") == 0
    lon_near[...] = jnp.where(lon_even, east, west).astype(BF16)
    lon_far[...] = jnp.where(lon_even, west, east).astype(BF16)
    for copy in copies[2:]:
        copy.wait()


def lookup(table, hi, lo):
    out = jnp.zeros(hi.shape, table.dtype)
    for row in range(table.shape[0]):
        line = jnp.broadcast_to(table[row : row + 1, :], hi.shape)
        got = jnp.take_along_axis(line, lo, axis=1)
        out = jnp.where(hi == row, got, out)
    return out


def index_body(
    listed, home, down, count_in, moist_k_in, heat_k_in, rain_in, flux_in, cell_in, records_in, hydro_in,
    order, ids, moist_k, heat_k, rain, flux, cell, records, hydro, count, sems,
):
    copies = fetch(
        (count_in, moist_k_in, heat_k_in, rain_in, flux_in, cell_in, records_in, hydro_in),
        (count, moist_k, heat_k, rain, flux, cell, records, hydro),
        sems,
    )
    slot = lookup(home[...], down[...] >> 7, down[...] & (LANES - 1))
    copies[0].wait()
    pairs, width = listed.shape[0] // 2, listed.shape[1]
    tiles = width // LANES
    chip = lax.axis_index("sec") // 2
    chip_basins = home.shape[0] * LANES // pairs
    pos = lax.broadcasted_iota(I32, (1, width), 1)
    for m in range(pairs):
        c = count[0, 0, 2 * m]
        second = pltpu.roll(listed[2 * m + 1 : 2 * m + 2, :], lax.rem(c, width), 1)
        line = jnp.where(pos < c, listed[2 * m : 2 * m + 1, :], second)
        away = lax.rem(m - chip + pairs, pairs)
        for t in range(tiles):
            order[pl.ds(away * tiles + t, 1), :] = line[:, t * LANES : (t + 1) * LANES]
    at = order[...]
    place = lookup(slot, at >> 7, at & (LANES - 1))
    pad = jnp.zeros((PACK_ROWS - 2 * tiles, LANES), F32)
    for away in range(pairs):
        m = lax.rem(away + chip, pairs)
        mine = place[away * tiles : (away + 1) * tiles, :] - m * chip_basins
        ids[m] = jnp.concatenate(
            [(mine >> 8).astype(F32), (mine & 255).astype(F32), pad], axis=0
        ).astype(BF16)
    for copy in copies[1:]:
        copy.wait()


def shift_time(x):
    steps = x.shape[1]
    lane = lax.broadcasted_iota(I32, x.shape, 1)
    return jnp.where(lane == steps - 1, 0.0, pltpu.roll(x, steps - 1, 1))


def picked(order, away, tiles, reaches):
    turned = order[...].astype(F32).T
    lane = lax.broadcasted_iota(I32, (LANES, reaches), 1).astype(F32)
    parts = [
        jnp.where(lane == turned[:, t : t + 1], 1.0, 0.0).astype(BF16)
        for t in range(away * tiles, (away + 1) * tiles)
    ]
    return parts[0] if len(parts) == 1 else jnp.concatenate(parts, axis=0)


def first_body(away, order, records, hydro, rec_packed, hyd_packed):
    hot = picked(order, away, rec_packed.shape[0] // LANES, records.shape[0])
    rec = jnp.dot(hot, records[...], preferred_element_type=F32)
    rec_packed[...] = shift_time(rec).astype(BF16)
    hyd_packed[...] = jnp.dot(hot, hydro[...], preferred_element_type=F32).astype(BF16)


def land_body(
    moist, heat, moist_k, heat_k, rain, flux, cell, sec_near, sec_far, lon_near, lon_far, ids,
    moist_out, heat_out, terms,
):
    layers, rows, cols = moist.shape
    row = lax.broadcasted_iota(I32, (rows, cols), 0)
    col = lax.broadcasted_iota(I32, (rows, cols), 1)
    sec_even = parity("sec") == 0
    lon_even = parity("lon") == 0
    south_all = jnp.where(sec_even, sec_near[...].astype(F32), sec_far[...].astype(F32))
    north_all = jnp.where(sec_even, sec_far[...].astype(F32), sec_near[...].astype(F32))
    east_all = jnp.where(lon_even, lon_near[...].astype(F32), lon_far[...].astype(F32))
    west_all = jnp.where(lon_even, lon_far[...].astype(F32), lon_near[...].astype(F32))
    for f, (x_ref, k_ref, top, out) in enumerate(
        ((moist, moist_k, rain, moist_out), (heat, heat_k, flux, heat_out))
    ):
        ratio = jnp.zeros((rows, cols), F32)
        value = jnp.zeros((rows, cols), F32)
        below = jnp.zeros((rows, cols), F32)
        ratios, values = [], []
        for layer in range(layers):
            k = f * layers + layer
            x = x_ref[layer]
            up = jnp.where(row == 0, north_all[k : k + 1, :], pltpu.roll(x, 1, 0))
            dn = jnp.where(row == rows - 1, south_all[k : k + 1, :], pltpu.roll(x, rows - 1, 0))
            lf = jnp.where(col == 0, west_all[:, k : k + 1], pltpu.roll(x, 1, 1))
            rt = jnp.where(col == cols - 1, east_all[:, k : k + 1], pltpu.roll(x, cols - 1, 1))
            rhs = x + LATERAL * (up + dn + lf + rt - 4.0 * x)
            if layer == 0:
                rhs = rhs + top[...]
            if layer < layers - 1:
                above = 0.5 * (k_ref[layer] + k_ref[layer + 1])
            else:
                above = jnp.zeros((rows, cols), F32)
            inv = 1.0 / (1.0 + below + above + below * ratio)
            ratio = -above * inv
            value = (rhs + below * value) * inv
            ratios.append(ratio)
            values.append(value)
            below = above
        x = values[-1]
        out[layers - 1] = x
        for layer in range(layers - 2, -1, -1):
            x = values[layer] - ratios[layer] * x
            out[layer] = x
    s = moist_out[0] - 1.0
    soft = jnp.maximum(s, 0.0) + jnp.log1p(jnp.exp(-jnp.abs(s)))
    gate = 1.0 / (1.0 + jnp.exp(-heat_out[0]))
    runoff = soft * gate + 0.5 * moist_k[layers - 1] * moist_out[layers - 1]
    cells = cell[...]
    hi = cells >> 7
    lo = cells & (LANES - 1)
    sections, blocks = terms.shape[0], terms.shape[1] - PACK_ROWS
    his = sections * blocks
    hi_iota = lax.broadcasted_iota(I32, (his, cols), 0)
    lo_iota = lax.broadcasted_iota(I32, (LANES, cols), 0)
    acc = jnp.zeros((his, LANES), F32)
    for i in range(rows):
        a = jnp.where(hi_iota == hi[i : i + 1, :], runoff[i : i + 1, :], 0.0).astype(BF16)
        b = jnp.where(lo_iota == lo[i : i + 1, :], 1.0, 0.0).astype(BF16)
        acc = acc + lax.dot_general(a, b, (((1,), (1,)), ((), ())), preferred_element_type=F32)
    terms[:, :blocks, :] = acc.reshape(sections, blocks, LANES).astype(BF16)
    for owner in range(sections):
        terms[owner, blocks:, :] = ids[owner // 2]


def send_body(away, got, order, rec_packed, hyd_packed, runoff, ready):
    blocks = runoff.shape[0]
    tiles = ready.shape[0] // LANES
    total = jnp.sum(got[:, :blocks, :].astype(F32), axis=0)
    runoff[...] = total
    at = order[...]
    turned = lookup(total, at >> 7, at & (LANES - 1)).T
    for t in range(tiles):
        rows = pl.ds(t * LANES, LANES)
        col = away * tiles + t
        ready[rows, :] = (
            rec_packed[rows, :].astype(F32) + turned[:, col : col + 1] * hyd_packed[rows, :].astype(F32)
        ).astype(BF16)


def record_body(away, runoff, records, hydro, order, out, kept, ready):
    turned = runoff[...].T
    for t in range(runoff.shape[0]):
        rows = pl.ds(t * LANES, LANES)
        fresh = (
            shift_time(records[rows, :].astype(F32)) + turned[:, t : t + 1] * hydro[rows, :].astype(F32)
        ).astype(BF16)
        out[rows, :] = fresh
        kept[rows, :] = fresh
    hot = picked(order, away, ready.shape[0] // LANES, kept.shape[0])
    ready[...] = jnp.dot(hot, kept[...], preferred_element_type=F32).astype(BF16)


def rest_body(aways, order, kept, landed, *ready):
    for away, out in zip(aways, ready):
        hot = picked(order, away, out.shape[0] // LANES, kept.shape[0])
        out[...] = jnp.dot(hot, kept[...], preferred_element_type=F32).astype(BF16)


def hot_of(got, aways, tiles, basins, other):
    chip = lax.axis_index("sec") // 2
    core = parity("sec")
    base = ((1 - core) if other else core) * basins
    slot = lax.broadcasted_iota(I32, (basins, LANES), 0) + base
    slot = slot.astype(F32)
    blocks = got.shape[1] - PACK_ROWS
    parts = []
    pairs = got.shape[0] // 2
    for away in aways:
        digits = got[2 * lax.rem(chip - away + pairs, pairs) + core, blocks:, :].astype(F32)
        place = digits[:tiles] * 256.0 + digits[tiles : 2 * tiles]
        for t in range(tiles):
            parts.append(jnp.where(slot == place[t : t + 1, :], 1.0, 0.0).astype(BF16))
    return parts[0] if len(parts) == 1 else jnp.concatenate(parts, axis=1)


def summed(got, aways, blocks, basins, other):
    tiles = blocks[0].shape[0] // LANES
    total = None
    for away, block in zip(aways, blocks):
        hot = hot_of(got, [away], tiles, basins, other)
        part = jnp.dot(hot, block[...], preferred_element_type=F32)
        total = part if total is None else total + part
    return total


def early_body(aways, got, *refs):
    blocks, (theirs, mine) = refs[: len(aways)], refs[len(aways) :]
    basins = mine.shape[0]
    theirs[...] = summed(got, aways, blocks, basins, True)
    mine[...] = summed(got, aways, blocks, basins, False)


def late_body(aways, other, so_far, got, *refs):
    blocks, out = refs[: len(aways)], refs[len(aways)]
    out[...] = (so_far[...] + summed(got, aways, blocks, out.shape[0], other)).astype(out.dtype)


def final_body(mine, passed, out, held, sems):
    rows = mine.shape[0]
    parts = 2
    size = rows // parts
    copies = []
    for i in range(parts):
        at = pl.ds(i * size, size)
        held[at, :] = mine[at, :] + passed[at, :].astype(F32)
        copy = pltpu.make_async_copy(held.at[at, :], out.at[at, :], sems.at[i])
        copy.start()
        copies.append(copy)
    for copy in copies:
        copy.wait()


def per_device(
    moisture, heat, moist_cond, heat_cond, rain, surface_flux, cell_reach,
    records, unit_hydro, down_basin, basin_home, send_index, send_count,
):
    lons = lax.axis_size("lon")
    sections = lax.axis_size("sec")
    layers, lats, cols = moisture.shape
    reaches, steps = records.shape[1:]
    cap = send_index.shape[3]
    pairs = sections // 2
    basins = basin_home.shape[1] // sections
    blocks = reaches // LANES
    shape = jax.ShapeDtypeStruct
    dma = pltpu.SemaphoreType.DMA

    home = basin_home.reshape(-1, LANES)
    down = down_basin.reshape(-1, LANES)
    listed = send_index.reshape(sections, cap)
    moist_v, heat_v, home_v, down_v, listed_v, sec_near, sec_far, lon_near, lon_far = call(
        edges_body,
        [
            shape(moisture.shape, F32),
            shape(heat.shape, F32),
            shape(home.shape, I32),
            shape(down.shape, I32),
            shape(listed.shape, I32),
            shape((2 * layers, cols), BF16),
            shape((2 * layers, cols), BF16),
            shape((lats, LANES), BF16),
            shape((lats, LANES), BF16),
        ],
        moisture, heat, home, down, listed,
        ins=[HBM] * 5,
        scratch=[dma((5,))],
        moved=moisture.size * 8,
    )
    swap = lambda count: [(i, i ^ 1) for i in range(count)]
    between = lambda count: [(i, i + 1) for i in range(1, count - 1, 2)] + [
        (i + 1, i) for i in range(1, count - 1, 2)
    ]
    got_sec_far = lax.ppermute(sec_far, "sec", between(sections))
    got_sec_near = lax.ppermute(sec_near, "sec", swap(sections))
    got_lon_far = lax.ppermute(lon_far, "lon", between(lons))
    got_lon_near = lax.ppermute(lon_near, "lon", swap(lons))

    order, ids, moist_k, heat_k, rain_v, flux_v, cell_v, records_v, hydro_v = call(
        index_body,
        [
            shape((blocks, LANES), I32),
            shape((pairs, PACK_ROWS, LANES), BF16),
            shape(moist_cond.shape, F32),
            shape(heat_cond.shape, F32),
            shape(rain.shape, F32),
            shape(surface_flux.shape, F32),
            shape(cell_reach.shape, I32),
            shape((reaches, steps), BF16),
            shape((reaches, steps), BF16),
        ],
        listed_v, home_v, down_v, send_count,
        moist_cond, heat_cond, rain, surface_flux, cell_reach, records[0], unit_hydro[0],
        ins=[VMEM] * 3 + [HBM] * 8,
        scratch=[pltpu.SMEM(send_count.shape, I32), dma((8,))],
        mib=12,
        moved=moisture.size * 16,
    )

    aways = []
    for k in range(1, pairs // 2 + 1):
        aways += [k] if 2 * k == pairs else [k, pairs - k]
    rec_packed, hyd_packed = call(
        lambda *refs: first_body(aways[0], *refs),
        [shape((cap, steps), BF16), shape((cap, steps), BF16)],
        order, records_v, hydro_v,
        mib=12,
        flops=4 * cap * reaches * steps,
        moved=reaches * steps * 4,
    )

    moist_out, heat_out, terms = call(
        land_body,
        [
            shape(moisture.shape, F32),
            shape(heat.shape, F32),
            shape((sections, blocks + PACK_ROWS, LANES), BF16),
        ],
        moist_v, heat_v, moist_k, heat_k, rain_v, flux_v, cell_v,
        got_sec_near, got_sec_far, got_lon_near, got_lon_far, ids,
        moved=moisture.size * 24,
    )

    got = lax.all_to_all(terms, "sec", split_axis=0, concat_axis=0, tiled=True)
    runoff, ready = call(
        lambda *refs: send_body(aways[0], *refs),
        [shape((blocks, LANES), F32), shape((cap, steps), BF16)],
        got, order, rec_packed, hyd_packed,
        moved=cap * steps * 6,
    )
    forward = lambda block, away: lax.ppermute(
        block, "sec", [(i, (i + 2 * away) % sections) for i in range(sections)]
    )
    arrived = {aways[0]: forward(ready, aways[0])}
    record_new, kept, ready = call(
        lambda *refs: record_body(aways[1], *refs),
        [shape((reaches, steps), BF16), shape((reaches, steps), BF16), shape((cap, steps), BF16)],
        runoff, records_v, hydro_v, order,
        mib=16,
        flops=2 * cap * reaches * steps,
        moved=reaches * steps * 8,
    )
    arrived[aways[1]] = forward(ready, aways[1])
    rest = aways[2:] + [0]
    *ready, own = call(
        lambda *refs: rest_body(rest, *refs),
        [shape((cap, steps), BF16)] * len(rest),
        order, kept, arrived[aways[0]],
        mib=16,
        flops=2 * cap * reaches * steps * len(rest),
        moved=reaches * steps * 4,
    )
    for away, block in zip(aways[2:], ready):
        arrived[away] = forward(block, away)
    late = aways[-1:]
    early = [0] + aways[:-1]
    arrived[0] = own
    theirs, mine = call(
        lambda *refs: early_body(early, *refs),
        [shape((basins, steps), F32), shape((basins, steps), F32)],
        got, *[arrived[a] for a in early],
        mib=12,
        moved=basins * steps * 16,
    )
    (theirs,) = call(
        lambda *refs: late_body(late, True, *refs),
        [shape((basins, steps), BF16)],
        theirs, got, *[arrived[a] for a in late],
        moved=basins * steps * 8,
    )
    passed = lax.ppermute(theirs, "sec", swap(sections))
    (mine,) = call(
        lambda *refs: late_body(late, False, *refs),
        [shape((basins, steps), F32)],
        mine, got, *[arrived[a] for a in late],
        moved=basins * steps * 8,
    )
    (inflow,) = call(
        final_body,
        [shape((basins, steps), F32)],
        mine, passed,
        out_specs=[HBM],
        scratch=[pltpu.VMEM((basins, steps), F32), dma((2,))],
        moved=basins * steps * 10,
    )
    return (moist_out, heat_out, record_new[None], inflow[None])


def solution(mesh):
    placed = (
        P(None, "sec", "lon"),
        P(None, "sec", "lon"),
        P(None, "sec", "lon"),
        P(None, "sec", "lon"),
        P("sec", "lon"),
        P("sec", "lon"),
        P("sec", "lon"),
        P("lon", "sec", None),
        P("lon", "sec", None),
        P("lon", "sec"),
        P("lon", None),
        P("lon", "sec", None, None),
        P("lon", "sec", None),
    )
    return jax.shard_map(
        per_device,
        mesh=mesh,
        in_specs=placed,
        out_specs=(
            P(None, "sec", "lon"),
            P(None, "sec", "lon"),
            P("lon", "sec", None),
            P("lon", "sec", None),
        ),
        check_vma=False,
    )
```

profile of v0, /device:TPU:5, one launch (start us, length us, event | category | flops | bytes accessed | tf_op | source)
XLA Modules:
  0.0 55.0 jit_solution(17268554078285631428)
XLA Ops:
  0.6 1.3 %shard_map.156 = (f32[16,16,256]{2,1,0:T(8,128)S(1)}, f32[16,16,256]{2,1,0:T(8,128)S(1)}, s32[32,128]{1,0:T(8,128)S(1)}, s32[16,128]{1,0:T(8,128)S(1)}, s32[8,51...) custom-call(f32[16,16,256]{2,1,0:T(8,128)} %moist_in.1, ...), custom_call_target="tpu_custom_call" | custom-call | bytes 524288 | tf_op jit(solution)/shard_map/pallas_call | solution.py:24
  2.0 0.7 %collective-permute-start = (bf16[32,256]{1,0:T(8,128)(2,1)S(1)}, bf16[32,256]{1,0:T(8,128)(2,1)S(1)}, u32[]{:S(2)}, u32[]{:S(2)}) collective-permute-start(bf16[32,256]{1,0:T(8,128)(2,1)S(1)} %get-tuple-element.46), channel_id=1, source_target_pairs={{0,1},{1,0},{2,3},{3,2},{4,5},{5,4},{6,7},{7,6},{8,9},{9,8},{10,11... | collective-permute-start | bytes 49160 | tf_op jit(solution)/shard_map/ppermute | solution.py:341
  2.7 3.1 %collective-permute-start.1 = (bf16[32,256]{1,0:T(8,128)(2,1)S(1)}, bf16[32,256]{1,0:T(8,128)(2,1)S(1)}, u32[]{:S(2)}, u32[]{:S(2)}) collective-permute-start(bf16[32,256]{1,0:T(8,128)(2,1)S(1)} %get-tuple-element.47), channel_id=1, source_target_pairs={{1,2},{3,4},{5,6},{2,1},{4,3},{6,5},{9,10},{11,12},{13,14},{10,9},... | collective-permute-start | bytes 49160 | tf_op jit(solution)/shard_map/ppermute | solution.py:340
  5.8 1.3 %collective-permute-start.2 = (bf16[16,128]{1,0:T(8,128)(2,1)S(1)}, bf16[16,128]{1,0:T(8,128)(2,1)S(1)}, u32[]{:S(2)}, u32[]{:S(2)}) collective-permute-start(bf16[16,128]{1,0:T(8,128)(2,1)S(1)} %get-tuple-element.48), channel_id=1, source_target_pairs={{0,8},{8,0},{16,24},{24,16},{1,9},{9,1},{17,25},{25,17},{2,10},{10... | collective-permute-start | bytes 12296 | tf_op jit(solution)/shard_map/ppermute | solution.py:343
  7.1 2.1 %collective-permute-start.3 = (bf16[16,128]{1,0:T(8,128)(2,1)S(1)}, bf16[16,128]{1,0:T(8,128)(2,1)S(1)}, u32[]{:S(2)}, u32[]{:S(2)}) collective-permute-start(bf16[16,128]{1,0:T(8,128)(2,1)S(1)} %get-tuple-element.49), channel_id=1, source_target_pairs={{8,16},{16,8},{9,17},{17,9},{10,18},{18,10},{11,19},{19,11},{12,20... | collective-permute-start | bytes 12296 | tf_op jit(solution)/shard_map/ppermute | solution.py:342
  9.2 1.8 %shard_map.157 = (s32[16,128]{1,0:T(8,128)S(1)}, bf16[4,16,128]{2,1,0:T(8,128)(2,1)S(1)}, f32[16,16,256]{2,1,0:T(8,128)S(1)}, f32[16,16,256]{2,1,0:T(8,128)S(1)}...) custom-call(s32[8,512]{1,0:T(8,128)S(1)} %get-tuple-element.38.liste, ...), custom_call_target="tpu_custom_call" | custom-call | bytes 1048576 | tf_op jit(solution)/shard_map/pallas_call | solution.py:24
  11.1 1.3 %collective-permute-done.3.lon_far = bf16[16,128]{1,0:T(8,128)(2,1)S(1)} collective-permute-done((bf16[16,128]{1,0:T(8,128)(2,1)S(1)}, bf16[16,128]{1,0:T(8,128)(2,1)S(1)}, u32[]{:S(2)}, u32[]{:S(2)}) %collective-permute-start.3) | collective-permute-done | bytes 4128 | tf_op jit(solution)/shard_map/ppermute | solution.py:342
  12.3 1.7 %shard_map.158 = (f32[16,16,256]{2,1,0:T(8,128)}, f32[16,16,256]{2,1,0:T(8,128)}, bf16[8,32,128]{2,1,0:T(8,128)(2,1)}) custom-call(f32[16,16,256]{2,1,0:T(8,128)S(1)} %get-tuple-element.36.moist, f32[16,16,256]{2,1,0:T(8,128)S(1)} %get-tuple-element.37.heat, f32[16,16,256]{2,1,0:T(8,128)S(1)} %get-tuple-element.41.moist_k, ...), custom_call_target="tpu_custom_call" | custom-call | bytes 1572864 | tf_op jit(solution)/shard_map/pallas_call | solution.py:24
  14.1 5.7 %all-to-all-start = ((bf16[8,32,128]{2,1,0:T(8,128)(2,1)}), bf16[8,32,128]{2,1,0:T(8,128)(2,1)S(1)}, u32[]{:S(2)}, u32[]{:S(2)}) async-start(bf16[8,32,128]{2,1,0:T(8,128)(2,1)} %get-tuple-element.53), calls=%async_computation | async-start | bytes 131072 | tf_op jit(solution)/shard_map/all_to_all | solution.py:390
  19.8 1.4 %shard_map.159 = (bf16[512,256]{1,0:T(8,128)(2,1)S(1)}, bf16[512,256]{1,0:T(8,128)(2,1)S(1)}) custom-call(s32[16,128]{1,0:T(8,128)S(1)} %get-tuple-element.54.refs_0_.refs_1_.refs_3_, bf16[2048,256]{1,0:T(8,128)(2,1)S(1)} %get-tuple-element.55.refs_1_, bf16[2048,256]{1,0:T(8,128)(2,1)S(1)} %get-tuple-element.56.refs_2_), custom_call_target="tpu_custom_call" | custom-call | flops 1073741824 | bytes 2097152 | tf_op jit(solution)/shard_map/pallas_call | solution.py:24
  21.2 3.6 %all-to-all-done.refs_0_.refs_1_ = bf16[8,32,128]{2,1,0:T(8,128)(2,1)S(1)} async-done(((bf16[8,32,128]{2,1,0:T(8,128)(2,1)}), bf16[8,32,128]{2,1,0:T(8,128)(2,1)S(1)}, u32[]{:S(2)}, u32[]{:S(2)}) %all-to-all-start) | async-done | bytes 65568 | tf_op jit(solution)/shard_map/all_to_all | solution.py:390
  24.8 0.4 shard_map.160
  25.2 0.6 %collective-permute-start.4 = (bf16[512,256]{1,0:T(8,128)(2,1)S(1)}, bf16[512,256]{1,0:T(8,128)(2,1)S(1)}, u32[]{:S(2)}, u32[]{:S(2)}) collective-permute-start(bf16[512,256]{1,0:T(8,128)(2,1)S(1)} %get-tuple-element.62), channel_id=1, source_target_pairs={{0,2},{1,3},{2,4},{3,5},{4,6},{5,7},{6,0},{7,1},{8,10},{9,11},{10,... | collective-permute-start | bytes 786440 | tf_op jit(solution)/shard_map/ppermute | solution.py:397
  25.8 2.0 %shard_map.161 = (bf16[2048,256]{1,0:T(8,128)(2,1)}, bf16[2048,256]{1,0:T(8,128)(2,1)S(1)}, bf16[512,256]{1,0:T(8,128)(2,1)S(1)}) custom-call(f32[16,128]{1,0:T(8,128)S(1)} %get-tuple-element.59.refs_0_, bf16[2048,256]{1,0:T(8,128)(2,1)S(1)} %get-tuple-element.55.refs_1_, bf16[2048,256]{1,0:T(8,128)(2,1)S(1)} %get-tuple-element.56.refs_2_, ...), custom_call_target="tpu_custom_call" | custom-call | flops 536870912 | bytes 4194304 | tf_op jit(solution)/shard_map/pallas_call | solution.py:24
  27.8 2.7 %collective-permute-start.5 = (bf16[512,256]{1,0:T(8,128)(2,1)S(1)}, bf16[512,256]{1,0:T(8,128)(2,1)S(1)}, u32[]{:S(2)}, u32[]{:S(2)}) collective-permute-start(bf16[512,256]{1,0:T(8,128)(2,1)S(1)} %get-tuple-element.64), channel_id=1, source_target_pairs={{0,6},{1,7},{2,0},{3,1},{4,2},{5,3},{6,4},{7,5},{8,14},{9,15},{10,... | collective-permute-start | bytes 786440 | tf_op jit(solution)/shard_map/ppermute | solution.py:397
  30.5 3.5 %collective-permute-done.4.refs_2_ = bf16[512,256]{1,0:T(8,128)(2,1)S(1)} collective-permute-done((bf16[512,256]{1,0:T(8,128)(2,1)S(1)}, bf16[512,256]{1,0:T(8,128)(2,1)S(1)}, u32[]{:S(2)}, u32[]{:S(2)}) %collective-permute-start.4) | collective-permute-done | bytes 262176 | tf_op jit(solution)/shard_map/ppermute | solution.py:397
  34.1 1.4 %shard_map.162 = (bf16[512,256]{1,0:T(8,128)(2,1)S(1)}, bf16[512,256]{1,0:T(8,128)(2,1)S(1)}) custom-call(s32[16,128]{1,0:T(8,128)S(1)} %get-tuple-element.54.refs_0_.refs_1_.refs_3_, bf16[2048,256]{1,0:T(8,128)(2,1)S(1)} %get-tuple-element.61.refs_1_, bf16[512,256]{1,0:T(8,128)(2,1)S(1)} %collective-permute-done.4.refs_2_), custom_call_target="tpu_custom_call" | custom-call | flops 1073741824 | bytes 2097152 | tf_op jit(solution)/shard_map/pallas_call | solution.py:24
  35.6 5.3 %collective-permute-done.5.refs_3_ = bf16[512,256]{1,0:T(8,128)(2,1)S(1)} collective-permute-done((bf16[512,256]{1,0:T(8,128)(2,1)S(1)}, bf16[512,256]{1,0:T(8,128)(2,1)S(1)}, u32[]{:S(2)}, u32[]{:S(2)}) %collective-permute-start.5) | collective-permute-done | bytes 262176 | tf_op jit(solution)/shard_map/ppermute | solution.py:397
  40.9 1.0 %shard_map.163 = (f32[512,256]{1,0:T(8,128)S(1)}, f32[512,256]{1,0:T(8,128)S(1)}) custom-call(bf16[8,32,128]{2,1,0:T(8,128)(2,1)S(1)} %all-to-all-done.refs_0_.refs_1_, bf16[512,256]{1,0:T(8,128)(2,1)S(1)} %get-tuple-element.63.refs_1_, bf16[512,256]{1,0:T(8,128)(2,1)S(1)} %collective-permute-done.4.refs_2_, bf16[512,256]{1,0:T(8,128)(2,1)S(1)} %collective-permute-done.5.refs_3_), custom_call_target="tpu_custom_call" | custom-call | bytes 2097152 | tf_op jit(solution)/shard_map/pallas_call | solution.py:24
  41.9 10.2 %collective-permute-done.6.refs_2_ = bf16[512,256]{1,0:T(8,128)(2,1)S(1)} collective-permute-done((bf16[512,256]{1,0:T(8,128)(2,1)S(1)}, bf16[512,256]{1,0:T(8,128)(2,1)S(1)}, u32[]{:S(2)}, u32[]{:S(2)}) %collective-permute-start.6) | collective-permute-done | bytes 262176 | tf_op jit(solution)/shard_map/ppermute | solution.py:397
  52.0 0.3 shard_map.165
  52.3 0.7 %collective-permute-start.7 = (bf16[512,256]{1,0:T(8,128)(2,1)S(1)}, bf16[512,256]{1,0:T(8,128)(2,1)S(1)}, u32[]{:S(2)}, u32[]{:S(2)}) collective-permute-start(bf16[512,256]{1,0:T(8,128)(2,1)S(1)} %shard_map.165), channel_id=1, source_target_pairs={{0,1},{1,0},{2,3},{3,2},{4,5},{5,4},{6,7},{7,6},{8,9},{9,8},{10,11... | collective-permute-start | bytes 786440 | tf_op jit(solution)/shard_map/ppermute | solution.py:437
  53.3 0.9 %collective-permute-done.7.passed = bf16[512,256]{1,0:T(8,128)(2,1)S(1)} collective-permute-done((bf16[512,256]{1,0:T(8,128)(2,1)S(1)}, bf16[512,256]{1,0:T(8,128)(2,1)S(1)}, u32[]{:S(2)}, u32[]{:S(2)}) %collective-permute-start.7) | collective-permute-done | bytes 262176 | tf_op jit(solution)/shard_map/ppermute | solution.py:437
  54.2 0.8 %shard_map.166 = f32[512,256]{1,0:T(8,128)} custom-call(f32[512,256]{1,0:T(8,128)S(1)} %shard_map.164.mine, bf16[512,256]{1,0:T(8,128)(2,1)S(1)} %collective-permute-done.7.passed), custom_call_target="tpu_custom_call" | custom-call | bytes 1310720 | tf_op jit(solution)/shard_map/pallas_call | solution.py:24
  (5 shorter events, 0.4 us)
Async XLA Ops:
  2.0 10.4 %collective-permute-start = (bf16[32,256]{1,0:T(8,128)(2,1)S(1)}, bf16[32,256]{1,0:T(8,128)(2,1)S(1)}, u32[]{:S(2)}, u32[]{:S(2)}) collective-permute-start(bf16[32,256]{1,0:T(8,128)(2,1)S(1)} %get-tuple-element.46), channel_id=1, source_target_pairs={{0,1},{1,0},{2,3},{3,2},{4,5},{5,4},{6,7},{7,6},{8,9},{9,8},{10,11... | collective-permute-start | bytes 49160 | tf_op jit(solution)/shard_map/ppermute | solution.py:341
  2.7 9.6 %collective-permute-start.1 = (bf16[32,256]{1,0:T(8,128)(2,1)S(1)}, bf16[32,256]{1,0:T(8,128)(2,1)S(1)}, u32[]{:S(2)}, u32[]{:S(2)}) collective-permute-start(bf16[32,256]{1,0:T(8,128)(2,1)S(1)} %get-tuple-element.47), channel_id=1, source_target_pairs={{1,2},{3,4},{5,6},{2,1},{4,3},{6,5},{9,10},{11,12},{13,14},{10,9},... | collective-permute-start | bytes 49160 | tf_op jit(solution)/shard_map/ppermute | solution.py:340
  5.8 5.2 %collective-permute-start.2 = (bf16[16,128]{1,0:T(8,128)(2,1)S(1)}, bf16[16,128]{1,0:T(8,128)(2,1)S(1)}, u32[]{:S(2)}, u32[]{:S(2)}) collective-permute-start(bf16[16,128]{1,0:T(8,128)(2,1)S(1)} %get-tuple-element.48), channel_id=1, source_target_pairs={{0,8},{8,0},{16,24},{24,16},{1,9},{9,1},{17,25},{25,17},{2,10},{10... | collective-permute-start | bytes 12296 | tf_op jit(solution)/shard_map/ppermute | solution.py:343
  7.1 5.2 %collective-permute-start.3 = (bf16[16,128]{1,0:T(8,128)(2,1)S(1)}, bf16[16,128]{1,0:T(8,128)(2,1)S(1)}, u32[]{:S(2)}, u32[]{:S(2)}) collective-permute-start(bf16[16,128]{1,0:T(8,128)(2,1)S(1)} %get-tuple-element.49), channel_id=1, source_target_pairs={{8,16},{16,8},{9,17},{17,9},{10,18},{18,10},{11,19},{19,11},{12,20... | collective-permute-start | bytes 12296 | tf_op jit(solution)/shard_map/ppermute | solution.py:342
  14.1 10.7 %all-to-all-start = ((bf16[8,32,128]{2,1,0:T(8,128)(2,1)}), bf16[8,32,128]{2,1,0:T(8,128)(2,1)S(1)}, u32[]{:S(2)}, u32[]{:S(2)}) async-start(bf16[8,32,128]{2,1,0:T(8,128)(2,1)} %get-tuple-element.53), calls=%async_computation | async-start | bytes 131072 | tf_op jit(solution)/shard_map/all_to_all | solution.py:390
  25.2 8.9 %collective-permute-start.4 = (bf16[512,256]{1,0:T(8,128)(2,1)S(1)}, bf16[512,256]{1,0:T(8,128)(2,1)S(1)}, u32[]{:S(2)}, u32[]{:S(2)}) collective-permute-start(bf16[512,256]{1,0:T(8,128)(2,1)S(1)} %get-tuple-element.62), channel_id=1, source_target_pairs={{0,2},{1,3},{2,4},{3,5},{4,6},{5,7},{6,0},{7,1},{8,10},{9,11},{10,... | collective-permute-start | bytes 786440 | tf_op jit(solution)/shard_map/ppermute | solution.py:397
  27.8 13.1 %collective-permute-start.5 = (bf16[512,256]{1,0:T(8,128)(2,1)S(1)}, bf16[512,256]{1,0:T(8,128)(2,1)S(1)}, u32[]{:S(2)}, u32[]{:S(2)}) collective-permute-start(bf16[512,256]{1,0:T(8,128)(2,1)S(1)} %get-tuple-element.64), channel_id=1, source_target_pairs={{0,6},{1,7},{2,0},{3,1},{4,2},{5,3},{6,4},{7,5},{8,14},{9,15},{10,... | collective-permute-start | bytes 786440 | tf_op jit(solution)/shard_map/ppermute | solution.py:397
  35.5 16.5 %collective-permute-start.6 = (bf16[512,256]{1,0:T(8,128)(2,1)S(1)}, bf16[512,256]{1,0:T(8,128)(2,1)S(1)}, u32[]{:S(2)}, u32[]{:S(2)}) collective-permute-start(bf16[512,256]{1,0:T(8,128)(2,1)S(1)} %get-tuple-element.66), channel_id=1, source_target_pairs={{0,4},{1,5},{2,6},{3,7},{4,0},{5,1},{6,2},{7,3},{8,12},{9,13},{10,... | collective-permute-start | bytes 786440 | tf_op jit(solution)/shard_map/ppermute | solution.py:397
  52.3 1.8 %collective-permute-start.7 = (bf16[512,256]{1,0:T(8,128)(2,1)S(1)}, bf16[512,256]{1,0:T(8,128)(2,1)S(1)}, u32[]{:S(2)}, u32[]{:S(2)}) collective-permute-start(bf16[512,256]{1,0:T(8,128)(2,1)S(1)} %shard_map.165), channel_id=1, source_target_pairs={{0,1},{1,0},{2,3},{3,2},{4,5},{5,4},{6,7},{7,6},{8,9},{9,8},{10,11... | collective-permute-start | bytes 786440 | tf_op jit(solution)/shard_map/ppermute | solution.py:437
where the time goes:
time: 55.3 us; the launch traced here: 55 us
  waiting for transfers between devices  24.8 us (45%)
  starting transfers between devices  16.9 us (31%)
  Pallas kernels  12.5 us (23%)
  between operations  0.72 us (1%)
    ppermute x3, waiting for transfers between devices, per_device(): lax.ppermute(block, 'sec', [(i, (i + 2 * away) % sections) for i in range...  19 us
    pallas_call x11, Pallas kernels, call(): pl.pallas_call(body, out_shape=list(outs), in_specs=ins, out_specs=list(o...  12.5 us
    all_to_all x1, starting transfers between devices, per_device(): got = lax.all_to_all(terms, 'sec', split_axis=0, concat_axis=0, tiled=True)  5.66 us
    all_to_all x1, waiting for transfers between devices, per_device(): got = lax.all_to_all(terms, 'sec', split_axis=0, concat_axis=0, tiled=True)  3.64 us
    ppermute x3, starting transfers between devices, per_device(): lax.ppermute(block, 'sec', [(i, (i + 2 * away) % sections) for i in range...  3.39 us
    ppermute x1, starting transfers between devices, per_device(): got_sec_far = lax.ppermute(sec_far, 'sec', between(sections))  3.1 us
    ppermute x1, starting transfers between devices, per_device(): got_lon_far = lax.ppermute(lon_far, 'lon', between(lons))  2.09 us
    ppermute x1, starting transfers between devices, per_device(): got_lon_near = lax.ppermute(lon_near, 'lon', swap(lons))  1.28 us
  transfers between devices with their start and end apart: 9, of which 6 were waited for; matrix products, arithmetic and copies ran while one was open for 0% of the time, Pallas kernels for 14%

commit v1 on v0

--- a/solution.py
+++ b/solution.py
@@ -46,13 +46,12 @@
     return lax.rem(lax.axis_index(axis), 2)
 
 
-def edges_body(
-    moist_in, heat_in, home_in, down_in, listed_in,
-    moist, heat, home, down, listed, sec_near, sec_far, lon_near, lon_far, sems,
-):
-    copies = fetch(
-        (moist_in, heat_in, home_in, down_in, listed_in), (moist, heat, home, down, listed), sems
-    )
+def edges_body(*refs):
+    count = 10
+    targets = refs[count : 2 * count]
+    moist, heat = targets[:2]
+    sec_near, sec_far, lon_near, lon_far, sems = refs[2 * count :]
+    copies = fetch(refs[:count], targets, sems)
     layers, rows, cols = moist.shape
     lane = lax.broadcasted_iota(I32, (rows, LANES), 1)
     west = jnp.zeros((rows, LANES), F32)
@@ -84,22 +83,15 @@
     return out
 
 
-def index_body(
-    listed, home, down, count_in, moist_k_in, heat_k_in, rain_in, flux_in, cell_in, records_in, hydro_in,
-    order, ids, moist_k, heat_k, rain, flux, cell, records, hydro, count, sems,
-):
-    copies = fetch(
-        (count_in, moist_k_in, heat_k_in, rain_in, flux_in, cell_in, records_in, hydro_in),
-        (count, moist_k, heat_k, rain, flux, cell, records, hydro),
-        sems,
-    )
+def index_body(listed, home, down, count_in, order, ids, count, sems):
+    copies = fetch((count_in,), (count,), sems)
     slot = lookup(home[...], down[...] >> 7, down[...] & (LANES - 1))
-    copies[0].wait()
     pairs, width = listed.shape[0] // 2, listed.shape[1]
     tiles = width // LANES
     chip = lax.axis_index("sec") // 2
     chip_basins = home.shape[0] * LANES // pairs
     pos = lax.broadcasted_iota(I32, (1, width), 1)
+    copies[0].wait()
     for m in range(pairs):
         c = count[0, 0, 2 * m]
         second = pltpu.roll(listed[2 * m + 1 : 2 * m + 2, :], lax.rem(c, width), 1)
@@ -113,11 +105,9 @@
     for away in range(pairs):
         m = lax.rem(away + chip, pairs)
         mine = place[away * tiles : (away + 1) * tiles, :] - m * chip_basins
-        ids[m] = jnp.concatenate(
+        ids[away] = jnp.concatenate(
             [(mine >> 8).astype(F32), (mine & 255).astype(F32), pad], axis=0
         ).astype(BF16)
-    for copy in copies[1:]:
-        copy.wait()
 
 
 def shift_time(x):
@@ -136,16 +126,19 @@
     return parts[0] if len(parts) == 1 else jnp.concatenate(parts, axis=0)
 
 
-def first_body(away, order, records, hydro, rec_packed, hyd_packed):
+def first_body(away, order, records_in, hydro_in, rec_packed, hyd_packed, records, hydro, sems):
+    copies = fetch((records_in, hydro_in), (records, hydro), sems)
     hot = picked(order, away, rec_packed.shape[0] // LANES, records.shape[0])
+    copies[0].wait()
     rec = jnp.dot(hot, records[...], preferred_element_type=F32)
+    copies[1].wait()
     rec_packed[...] = shift_time(rec).astype(BF16)
     hyd_packed[...] = jnp.dot(hot, hydro[...], preferred_element_type=F32).astype(BF16)
 
 
 def land_body(
-    moist, heat, moist_k, heat_k, rain, flux, cell, sec_near, sec_far, lon_near, lon_far, ids,
-    moist_out, heat_out, terms,
+    moist, heat, moist_k, heat_k, rain, flux, cell, sec_near, sec_far, lon_near, lon_far,
+    moist_out, heat_out, keep, give,
 ):
     layers, rows, cols = moist.shape
     row = lax.broadcasted_iota(I32, (rows, cols), 0)
@@ -195,8 +188,8 @@
     cells = cell[...]
     hi = cells >> 7
     lo = cells & (LANES - 1)
-    sections, blocks = terms.shape[0], terms.shape[1] - PACK_ROWS
-    his = sections * blocks
+    pairs, blocks = keep.shape[:2]
+    his = 2 * pairs * blocks
     hi_iota = lax.broadcasted_iota(I32, (his, cols), 0)
     lo_iota = lax.broadcasted_iota(I32, (LANES, cols), 0)
     acc = jnp.zeros((his, LANES), F32)
@@ -204,15 +197,28 @@
         a = jnp.where(hi_iota == hi[i : i + 1, :], runoff[i : i + 1, :], 0.0).astype(BF16)
         b = jnp.where(lo_iota == lo[i : i + 1, :], 1.0, 0.0).astype(BF16)
         acc = acc + lax.dot_general(a, b, (((1,), (1,)), ((), ())), preferred_element_type=F32)
-    terms[:, :blocks, :] = acc.reshape(sections, blocks, LANES).astype(BF16)
-    for owner in range(sections):
-        terms[owner, blocks:, :] = ids[owner // 2]
-
-
-def send_body(away, got, order, rec_packed, hyd_packed, runoff, ready):
+    both = acc.reshape(pairs, 2, blocks, LANES)
+    keep[...] = jnp.where(sec_even, both[:, 0], both[:, 1])
+    give[...] = jnp.where(sec_even, both[:, 1], both[:, 0]).astype(BF16)
+
+
+def terms_body(aways, keep, got, ids, own, *outs):
+    pairs, blocks = keep.shape[:2]
+    chip = lax.axis_index("sec") // 2
+    own[...] = keep[chip] + got[chip].astype(F32)
+    for away, out in zip(aways, outs):
+        m = lax.rem(chip + away, pairs)
+        out[:blocks, :] = (keep[m] + got[m].astype(F32)).astype(BF16)
+        out[blocks:, :] = ids[away]
+
+
+def send_body(away, own, order, rec_packed, hyd_packed, *refs):
+    terms, (runoff, ready) = refs[:-2], refs[-2:]
     blocks = runoff.shape[0]
     tiles = ready.shape[0] // LANES
-    total = jnp.sum(got[:, :blocks, :].astype(F32), axis=0)
+    total = own[...]
+    for term in terms:
+        total = total + term[:blocks, :].astype(F32)
     runoff[...] = total
     at = order[...]
     turned = lookup(total, at >> 7, at & (LANES - 1)).T
@@ -243,43 +249,44 @@
         out[...] = jnp.dot(hot, kept[...], preferred_element_type=F32).astype(BF16)
 
 
-def hot_of(got, aways, tiles, basins, other):
-    chip = lax.axis_index("sec") // 2
+def hot_of(digits, tiles, basins, other):
     core = parity("sec")
     base = ((1 - core) if other else core) * basins
     slot = lax.broadcasted_iota(I32, (basins, LANES), 0) + base
     slot = slot.astype(F32)
-    blocks = got.shape[1] - PACK_ROWS
-    parts = []
-    pairs = got.shape[0] // 2
-    for away in aways:
-        digits = got[2 * lax.rem(chip - away + pairs, pairs) + core, blocks:, :].astype(F32)
-        place = digits[:tiles] * 256.0 + digits[tiles : 2 * tiles]
-        for t in range(tiles):
-            parts.append(jnp.where(slot == place[t : t + 1, :], 1.0, 0.0).astype(BF16))
+    place = digits[:tiles] * 256.0 + digits[tiles : 2 * tiles]
+    parts = [jnp.where(slot == place[t : t + 1, :], 1.0, 0.0).astype(BF16) for t in range(tiles)]
     return parts[0] if len(parts) == 1 else jnp.concatenate(parts, axis=1)
 
 
-def summed(got, aways, blocks, basins, other):
+def summed(digits, blocks, basins, other):
     tiles = blocks[0].shape[0] // LANES
     total = None
-    for away, block in zip(aways, blocks):
-        hot = hot_of(got, [away], tiles, basins, other)
+    for digit, block in zip(digits, blocks):
+        hot = hot_of(digit, tiles, basins, other)
         part = jnp.dot(hot, block[...], preferred_element_type=F32)
         total = part if total is None else total + part
     return total
 
 
-def early_body(aways, got, *refs):
-    blocks, (theirs, mine) = refs[: len(aways)], refs[len(aways) :]
+def digits_of(terms):
+    return [ref[ref.shape[0] - PACK_ROWS :, :].astype(F32) for ref in terms]
+
+
+def early_body(ids, *refs):
+    theirs, mine = refs[-2:]
+    n = (len(refs) - 3) // 2
+    terms, blocks = refs[:n], refs[n:-2]
+    digits = [ids[0].astype(F32)] + digits_of(terms)
     basins = mine.shape[0]
-    theirs[...] = summed(got, aways, blocks, basins, True)
-    mine[...] = summed(got, aways, blocks, basins, False)
-
-
-def late_body(aways, other, so_far, got, *refs):
-    blocks, out = refs[: len(aways)], refs[len(aways)]
-    out[...] = (so_far[...] + summed(got, aways, blocks, out.shape[0], other)).astype(out.dtype)
+    theirs[...] = summed(digits, blocks, basins, True)
+    mine[...] = summed(digits, blocks, basins, False)
+
+
+def late_body(other, so_far, *refs):
+    out = refs[-1]
+    terms, blocks = refs[: len(refs) // 2], refs[len(refs) // 2 : -1]
+    out[...] = (so_far[...] + summed(digits_of(terms), blocks, out.shape[0], other)).astype(out.dtype)
 
 
 def final_body(mine, passed, out, held, sems):
@@ -315,24 +322,24 @@
     home = basin_home.reshape(-1, LANES)
     down = down_basin.reshape(-1, LANES)
     listed = send_index.reshape(sections, cap)
-    moist_v, heat_v, home_v, down_v, listed_v, sec_near, sec_far, lon_near, lon_far = call(
+    fetched = [
+        moisture, heat, moist_cond, heat_cond, rain, surface_flux, cell_reach, home, down, listed
+    ]
+    *fetched, sec_near, sec_far, lon_near, lon_far = call(
         edges_body,
-        [
-            shape(moisture.shape, F32),
-            shape(heat.shape, F32),
-            shape(home.shape, I32),
-            shape(down.shape, I32),
-            shape(listed.shape, I32),
+        [shape(x.shape, x.dtype) for x in fetched]
+        + [
             shape((2 * layers, cols), BF16),
             shape((2 * layers, cols), BF16),
             shape((lats, LANES), BF16),
             shape((lats, LANES), BF16),
         ],
-        moisture, heat, home, down, listed,
-        ins=[HBM] * 5,
-        scratch=[dma((5,))],
+        *fetched,
+        ins=[HBM] * len(fetched),
+        scratch=[dma((len(fetched),))],
         moved=moisture.size * 8,
     )
+    *land, home_v, down_v, listed_v = fetched
     swap = lambda count: [(i, i ^ 1) for i in range(count)]
     between = lambda count: [(i, i + 1) for i in range(1, count - 1, 2)] + [
         (i + 1, i) for i in range(1, count - 1, 2)
@@ -342,60 +349,55 @@
     got_lon_far = lax.ppermute(lon_far, "lon", between(lons))
     got_lon_near = lax.ppermute(lon_near, "lon", swap(lons))
 
-    order, ids, moist_k, heat_k, rain_v, flux_v, cell_v, records_v, hydro_v = call(
-        index_body,
-        [
-            shape((blocks, LANES), I32),
-            shape((pairs, PACK_ROWS, LANES), BF16),
-            shape(moist_cond.shape, F32),
-            shape(heat_cond.shape, F32),
-            shape(rain.shape, F32),
-            shape(surface_flux.shape, F32),
-            shape(cell_reach.shape, I32),
-            shape((reaches, steps), BF16),
-            shape((reaches, steps), BF16),
-        ],
-        listed_v, home_v, down_v, send_count,
-        moist_cond, heat_cond, rain, surface_flux, cell_reach, records[0], unit_hydro[0],
-        ins=[VMEM] * 3 + [HBM] * 8,
-        scratch=[pltpu.SMEM(send_count.shape, I32), dma((8,))],
-        mib=12,
-        moved=moisture.size * 16,
-    )
-
-    aways = []
-    for k in range(1, pairs // 2 + 1):
-        aways += [k] if 2 * k == pairs else [k, pairs - k]
-    rec_packed, hyd_packed = call(
-        lambda *refs: first_body(aways[0], *refs),
-        [shape((cap, steps), BF16), shape((cap, steps), BF16)],
-        order, records_v, hydro_v,
-        mib=12,
-        flops=4 * cap * reaches * steps,
-        moved=reaches * steps * 4,
-    )
-
-    moist_out, heat_out, terms = call(
+    moist_out, heat_out, keep, give = call(
         land_body,
         [
             shape(moisture.shape, F32),
             shape(heat.shape, F32),
-            shape((sections, blocks + PACK_ROWS, LANES), BF16),
+            shape((pairs, blocks, LANES), F32),
+            shape((pairs, blocks, LANES), BF16),
         ],
-        moist_v, heat_v, moist_k, heat_k, rain_v, flux_v, cell_v,
-        got_sec_near, got_sec_far, got_lon_near, got_lon_far, ids,
+        *land,
+        got_sec_near, got_sec_far, got_lon_near, got_lon_far,
         moved=moisture.size * 24,
     )
-
-    got = lax.all_to_all(terms, "sec", split_axis=0, concat_axis=0, tiled=True)
+    got = lax.ppermute(give, "sec", swap(sections))
+    order, ids = call(
+        index_body,
+        [shape((blocks, LANES), I32), shape((pairs, PACK_ROWS, LANES), BF16)],
+        listed_v, home_v, down_v, send_count,
+        ins=[VMEM] * 3 + [HBM],
+        scratch=[pltpu.SMEM(send_count.shape, I32), dma((1,))],
+        moved=moisture.size * 8,
+    )
+    aways = []
+    for k in range(1, pairs // 2 + 1):
+        aways += [k] if 2 * k == pairs else [k, pairs - k]
+    own_terms, *terms = call(
+        lambda *refs: terms_body(aways, *refs),
+        [shape((blocks, LANES), F32)] + [shape((blocks + PACK_ROWS, LANES), BF16)] * len(aways),
+        keep, got, ids,
+        moved=reaches * 8,
+    )
+    forward = lambda block, away: lax.ppermute(
+        block, "sec", [(i, (i + 2 * away) % sections) for i in range(sections)]
+    )
+    terms = {away: forward(term, away) for away, term in zip(aways, terms)}
+    rec_packed, hyd_packed, records_v, hydro_v = call(
+        lambda *refs: first_body(aways[0], *refs),
+        [shape((cap, steps), BF16)] * 2 + [shape((reaches, steps), BF16)] * 2,
+        order, records[0], unit_hydro[0],
+        ins=[VMEM, HBM, HBM],
+        scratch=[dma((2,))],
+        mib=12,
+        flops=4 * cap * reaches * steps,
+        moved=reaches * steps * 4,
+    )
     runoff, ready = call(
         lambda *refs: send_body(aways[0], *refs),
         [shape((blocks, LANES), F32), shape((cap, steps), BF16)],
-        got, order, rec_packed, hyd_packed,
+        own_terms, order, rec_packed, hyd_packed, *terms.values(),
         moved=cap * steps * 6,
-    )
-    forward = lambda block, away: lax.ppermute(
-        block, "sec", [(i, (i + 2 * away) % sections) for i in range(sections)]
     )
     arrived = {aways[0]: forward(ready, aways[0])}
     record_new, kept, ready = call(
@@ -419,26 +421,25 @@
     for away, block in zip(aways[2:], ready):
         arrived[away] = forward(block, away)
     late = aways[-1:]
-    early = [0] + aways[:-1]
-    arrived[0] = own
+    early = aways[:-1]
     theirs, mine = call(
-        lambda *refs: early_body(early, *refs),
+        early_body,
         [shape((basins, steps), F32), shape((basins, steps), F32)],
-        got, *[arrived[a] for a in early],
+        ids, *[terms[a] for a in early], own, *[arrived[a] for a in early],
         mib=12,
         moved=basins * steps * 16,
     )
     (theirs,) = call(
-        lambda *refs: late_body(late, True, *refs),
+        lambda *refs: late_body(True, *refs),
         [shape((basins, steps), BF16)],
-        theirs, got, *[arrived[a] for a in late],
+        theirs, *[terms[a] for a in late], *[arrived[a] for a in late],
         moved=basins * steps * 8,
     )
     passed = lax.ppermute(theirs, "sec", swap(sections))
     (mine,) = call(
-        lambda *refs: late_body(late, False, *refs),
+        lambda *refs: late_body(False, *refs),
         [shape((basins, steps), F32)],
-        mine, got, *[arrived[a] for a in late],
+        mine, *[terms[a] for a in late], *[arrived[a] for a in late],
         moved=basins * steps * 8,
     )
     (inflow,) = call(

time: 55.3 us -> 53.5 us (0.967)
  waiting for transfers between devices: 24.8 us -> 22.7 us
  Pallas kernels: 12.5 us -> 13.6 us
  starting transfers between devices: 16.9 us -> 16.2 us
    all_to_all x1 -> x0, starting transfers between devices: 5.66 us -> none  [per_device(): got = lax.all_to_all(terms, 'sec', split_axis=0, concat_axis=0, tiled=True)]
    ppermute x3 -> x6, starting transfers between devices: 3.39 us -> 8.32 us  [per_device(): lax.ppermute(block, 'sec', [(i, (i + 2 * away) % sections) for i in range...]
    all_to_all x1 -> x0, waiting for transfers between devices: 3.64 us -> none  [per_device(): got = lax.all_to_all(terms, 'sec', split_axis=0, concat_axis=0, tiled=True)]
    ppermute x1, waiting for transfers between devices: 1.27 us -> 3.13 us  [per_device(): got_lon_far = lax.ppermute(lon_far, 'lon', between(lons))]
    pallas_call x11 -> x12, Pallas kernels: 12.5 us -> 13.6 us  [call(): pl.pallas_call(body, out_shape=list(outs), in_specs=ins, out_specs=list(o...]
    ppermute x3 -> x6, waiting for transfers between devices: 19 us -> 18.5 us  [per_device(): lax.ppermute(block, 'sec', [(i, (i + 2 * away) % sections) for i in range...]
  transfers between devices with their start and end apart: 9 -> 12, of which waited for: 6 -> 6; matrix products, arithmetic and copies ran while one was open for 0% -> 0% of each run, Pallas kernels for 14% -> 17%
where the time goes in v1:
time: 53.5 us; the launch traced here: 53.3 us
  waiting for transfers between devices  22.7 us (42%)
  starting transfers between devices  16.2 us (30%)
  Pallas kernels  13.6 us (25%)
  between operations  0.75 us (1%)
    ppermute x6, waiting for transfers between devices, per_device(): lax.ppermute(block, 'sec', [(i, (i + 2 * away) % sections) for i in range...  18.5 us
    pallas_call x12, Pallas kernels, call(): pl.pallas_call(body, out_shape=list(outs), in_specs=ins, out_specs=list(o...  13.6 us
    ppermute x6, starting transfers between devices, per_device(): lax.ppermute(block, 'sec', [(i, (i + 2 * away) % sections) for i in range...  8.32 us
    ppermute x1, waiting for transfers between devices, per_device(): got_lon_far = lax.ppermute(lon_far, 'lon', between(lons))  3.13 us
    ppermute x1, starting transfers between devices, per_device(): got_sec_far = lax.ppermute(sec_far, 'sec', between(sections))  3.1 us
    ppermute x1, starting transfers between devices, per_device(): got_lon_far = lax.ppermute(lon_far, 'lon', between(lons))  2.09 us
    ppermute x1, starting transfers between devices, per_device(): got_lon_near = lax.ppermute(lon_near, 'lon', swap(lons))  1.28 us
  transfers between devices with their start and end apart: 12, of which 6 were waited for; matrix products, arithmetic and copies ran while one was open for 0% of the time, Pallas kernels for 17%

profile of v1, /device:TPU:5, one launch (start us, length us, event | category | flops | bytes accessed | tf_op | source)
XLA Modules:
  0.0 53.3 jit_solution(13170009296967123974)
XLA Ops:
  0.6 1.4 %shard_map.156 = (f32[16,16,256]{2,1,0:T(8,128)S(1)}, f32[16,16,256]{2,1,0:T(8,128)S(1)}, f32[16,16,256]{2,1,0:T(8,128)S(1)}, f32[16,16,256]{2,1,0:T(8,128)S(1)}...) custom-call(f32[16,16,256]{2,1,0:T(8,128)} %refs_0_.1, ...), custom_call_target="tpu_custom_call" | custom-call | bytes 524288 | tf_op jit(solution)/shard_map/pallas_call | solution.py:24
  2.0 0.7 %collective-permute-start = (bf16[32,256]{1,0:T(8,128)(2,1)S(1)}, bf16[32,256]{1,0:T(8,128)(2,1)S(1)}, u32[]{:S(2)}, u32[]{:S(2)}) collective-permute-start(bf16[32,256]{1,0:T(8,128)(2,1)S(1)} %get-tuple-element.48), channel_id=1, source_target_pairs={{0,1},{1,0},{2,3},{3,2},{4,5},{5,4},{6,7},{7,6},{8,9},{9,8},{10,11... | collective-permute-start | bytes 49160 | tf_op jit(solution)/shard_map/ppermute | solution.py:348
  2.8 3.1 %collective-permute-start.1 = (bf16[32,256]{1,0:T(8,128)(2,1)S(1)}, bf16[32,256]{1,0:T(8,128)(2,1)S(1)}, u32[]{:S(2)}, u32[]{:S(2)}) collective-permute-start(bf16[32,256]{1,0:T(8,128)(2,1)S(1)} %get-tuple-element.49), channel_id=1, source_target_pairs={{1,2},{3,4},{5,6},{2,1},{4,3},{6,5},{9,10},{11,12},{13,14},{10,9},... | collective-permute-start | bytes 49160 | tf_op jit(solution)/shard_map/ppermute | solution.py:347
  5.9 1.3 %collective-permute-start.2 = (bf16[16,128]{1,0:T(8,128)(2,1)S(1)}, bf16[16,128]{1,0:T(8,128)(2,1)S(1)}, u32[]{:S(2)}, u32[]{:S(2)}) collective-permute-start(bf16[16,128]{1,0:T(8,128)(2,1)S(1)} %get-tuple-element.50), channel_id=1, source_target_pairs={{0,8},{8,0},{16,24},{24,16},{1,9},{9,1},{17,25},{25,17},{2,10},{10... | collective-permute-start | bytes 12296 | tf_op jit(solution)/shard_map/ppermute | solution.py:350
  7.2 2.1 %collective-permute-start.3 = (bf16[16,128]{1,0:T(8,128)(2,1)S(1)}, bf16[16,128]{1,0:T(8,128)(2,1)S(1)}, u32[]{:S(2)}, u32[]{:S(2)}) collective-permute-start(bf16[16,128]{1,0:T(8,128)(2,1)S(1)} %get-tuple-element.51), channel_id=1, source_target_pairs={{8,16},{16,8},{9,17},{17,9},{10,18},{18,10},{11,19},{19,11},{12,20... | collective-permute-start | bytes 12296 | tf_op jit(solution)/shard_map/ppermute | solution.py:349
  9.3 3.1 %collective-permute-done.3.lon_far = bf16[16,128]{1,0:T(8,128)(2,1)S(1)} collective-permute-done((bf16[16,128]{1,0:T(8,128)(2,1)S(1)}, bf16[16,128]{1,0:T(8,128)(2,1)S(1)}, u32[]{:S(2)}, u32[]{:S(2)}) %collective-permute-start.3) | collective-permute-done | bytes 4128 | tf_op jit(solution)/shard_map/ppermute | solution.py:349
  12.4 1.4 %shard_map.157 = (f32[16,16,256]{2,1,0:T(8,128)}, f32[16,16,256]{2,1,0:T(8,128)}, f32[4,16,128]{2,1,0:T(8,128)S(1)}, bf16[4,16,128]{2,1,0:T(8,128)(2,1)S(1)}) custom-call(f32[16,16,256]{2,1,0:T(8,128)S(1)} %get-tuple-element.41.moist, f32[16,16,256]{2,1,0:T(8,128)S(1)} %get-tuple-element.42.heat, f32[16,16,256]{2,1,0:T(8,128)S(1)} %get-tuple-element.43.moist_k, ...), custom_call_target="tpu_custom_call" | custom-call | bytes 1572864 | tf_op jit(solution)/shard_map/pallas_call | solution.py:24
  13.8 0.9 %shard_map.158 = (s32[16,128]{1,0:T(8,128)S(1)}, bf16[4,16,128]{2,1,0:T(8,128)(2,1)S(1)}) custom-call(s32[8,512]{1,0:T(8,128)S(1)} %get-tuple-element.56.listed, s32[32,128]{1,0:T(8,128)S(1)} %get-tuple-element.57.home, s32[16,128]{1,0:T(8,128)S(1)} %get-tuple-element.58.down, s32[1,1,8]{2,1,0:T(1,128)} %count_in.1), custom_call_target="tpu_custom_call" | custom-call | bytes 524288 | tf_op jit(solution)/shard_map/pallas_call | solution.py:24
  15.0 1.9 %collective-permute-start.5 = (bf16[32,128]{1,0:T(8,128)(2,1)S(1)}, bf16[32,128]{1,0:T(8,128)(2,1)S(1)}, u32[]{:S(2)}, u32[]{:S(2)}) collective-permute-start(bf16[32,128]{1,0:T(8,128)(2,1)S(1)} %get-tuple-element.64), channel_id=1, source_target_pairs={{0,2},{1,3},{2,4},{3,5},{4,6},{5,7},{6,0},{7,1},{8,10},{9,11},{10,... | collective-permute-start | bytes 24584 | tf_op jit(solution)/shard_map/ppermute | solution.py:382
  16.9 2.1 %collective-permute-start.6 = (bf16[32,128]{1,0:T(8,128)(2,1)S(1)}, bf16[32,128]{1,0:T(8,128)(2,1)S(1)}, u32[]{:S(2)}, u32[]{:S(2)}) collective-permute-start(bf16[32,128]{1,0:T(8,128)(2,1)S(1)} %get-tuple-element.65), channel_id=1, source_target_pairs={{0,6},{1,7},{2,0},{3,1},{4,2},{5,3},{6,4},{7,5},{8,14},{9,15},{10,... | collective-permute-start | bytes 24584 | tf_op jit(solution)/shard_map/ppermute | solution.py:382
  19.0 0.4 collective-permute-start.7
  19.4 3.7 %shard_map.160 = (bf16[512,256]{1,0:T(8,128)(2,1)S(1)}, bf16[512,256]{1,0:T(8,128)(2,1)S(1)}, bf16[2048,256]{1,0:T(8,128)(2,1)S(1)}, bf16[2048,256]{1,0:T(8,128)(2,1)S(1)}) custom-call(s32[16,128]{1,0:T(8,128)S(1)} %get-tuple-element.61.refs_0_.refs_1_.refs_3_, bf16[2048,256]{1,0:T(8,128)(2,1)} %bitcast.11, bf16[2048,256]{1,0:T(8,128)(2,1)} %bitcast.12), custom_call_target="tpu_custom_call" | custom-call | flops 1073741824 | bytes 2097152 | tf_op jit(solution)/shard_map/pallas_call | solution.py:24
  23.5 1.3 %collective-permute-start.8 = (bf16[512,256]{1,0:T(8,128)(2,1)S(1)}, bf16[512,256]{1,0:T(8,128)(2,1)S(1)}, u32[]{:S(2)}, u32[]{:S(2)}) collective-permute-start(bf16[512,256]{1,0:T(8,128)(2,1)S(1)} %get-tuple-element.72), channel_id=1, source_target_pairs={{0,2},{1,3},{2,4},{3,5},{4,6},{5,7},{6,0},{7,1},{8,10},{9,11},{10,... | collective-permute-start | bytes 786440 | tf_op jit(solution)/shard_map/ppermute | solution.py:382
  24.9 2.0 %shard_map.162 = (bf16[2048,256]{1,0:T(8,128)(2,1)}, bf16[2048,256]{1,0:T(8,128)(2,1)S(1)}, bf16[512,256]{1,0:T(8,128)(2,1)S(1)}) custom-call(f32[16,128]{1,0:T(8,128)S(1)} %get-tuple-element.67.refs_0_, bf16[2048,256]{1,0:T(8,128)(2,1)S(1)} %get-tuple-element.68.refs_1_, bf16[2048,256]{1,0:T(8,128)(2,1)S(1)} %get-tuple-element.69.refs_2_, ...), custom_call_target="tpu_custom_call" | custom-call | flops 536870912 | bytes 4194304 | tf_op jit(solution)/shard_map/pallas_call | solution.py:24
  26.9 2.0 %collective-permute-start.9 = (bf16[512,256]{1,0:T(8,128)(2,1)S(1)}, bf16[512,256]{1,0:T(8,128)(2,1)S(1)}, u32[]{:S(2)}, u32[]{:S(2)}) collective-permute-start(bf16[512,256]{1,0:T(8,128)(2,1)S(1)} %get-tuple-element.74), channel_id=1, source_target_pairs={{0,6},{1,7},{2,0},{3,1},{4,2},{5,3},{6,4},{7,5},{8,14},{9,15},{10,... | collective-permute-start | bytes 786440 | tf_op jit(solution)/shard_map/ppermute | solution.py:382
  28.9 3.3 %collective-permute-done.8.refs_2_.refs_3_ = bf16[512,256]{1,0:T(8,128)(2,1)S(1)} collective-permute-done((bf16[512,256]{1,0:T(8,128)(2,1)S(1)}, bf16[512,256]{1,0:T(8,128)(2,1)S(1)}, u32[]{:S(2)}, u32[]{:S(2)}) %collective-permute-start.8) | collective-permute-done | bytes 262176 | tf_op jit(solution)/shard_map/ppermute | solution.py:382
  32.2 1.4 %shard_map.163 = (bf16[512,256]{1,0:T(8,128)(2,1)S(1)}, bf16[512,256]{1,0:T(8,128)(2,1)S(1)}) custom-call(s32[16,128]{1,0:T(8,128)S(1)} %get-tuple-element.61.refs_0_.refs_1_.refs_3_, bf16[2048,256]{1,0:T(8,128)(2,1)S(1)} %get-tuple-element.71.refs_1_, bf16[512,256]{1,0:T(8,128)(2,1)S(1)} %collective-permute-done.8.refs_2_.refs_3_), custom_call_target="tpu_custom_call" | custom-call | flops 1073741824 | bytes 2097152 | tf_op jit(solution)/shard_map/pallas_call | solution.py:24
  33.6 0.6 %collective-permute-start.10 = (bf16[512,256]{1,0:T(8,128)(2,1)S(1)}, bf16[512,256]{1,0:T(8,128)(2,1)S(1)}, u32[]{:S(2)}, u32[]{:S(2)}) collective-permute-start(bf16[512,256]{1,0:T(8,128)(2,1)S(1)} %get-tuple-element.76), channel_id=1, source_target_pairs={{0,4},{1,5},{2,6},{3,7},{4,0},{5,1},{6,2},{7,3},{8,12},{9,13},{10,... | collective-permute-start | bytes 786440 | tf_op jit(solution)/shard_map/ppermute | solution.py:382
  34.2 5.0 %collective-permute-done.9.refs_4_ = bf16[512,256]{1,0:T(8,128)(2,1)S(1)} collective-permute-done((bf16[512,256]{1,0:T(8,128)(2,1)S(1)}, bf16[512,256]{1,0:T(8,128)(2,1)S(1)}, u32[]{:S(2)}, u32[]{:S(2)}) %collective-permute-start.9) | collective-permute-done | bytes 262176 | tf_op jit(solution)/shard_map/ppermute | solution.py:382
  39.2 1.0 %shard_map.164 = (f32[512,256]{1,0:T(8,128)S(1)}, f32[512,256]{1,0:T(8,128)S(1)}) custom-call(bf16[4,16,128]{2,1,0:T(8,128)(2,1)S(1)} %get-tuple-element.59.refs_2_.ids, bf16[32,128]{1,0:T(8,128)(2,1)S(1)} %collective-permute-done.5.refs_4_.refs_0_, bf16[32,128]{1,0:T(8,128)(2,1)S(1)} %collective-permute-done.6.refs_5_.refs_1_, ...), custom_call_target="tpu_custom_call" | custom-call | bytes 2097152 | tf_op jit(solution)/shard_map/pallas_call | solution.py:24
  40.2 10.2 %collective-permute-done.10.refs_2_ = bf16[512,256]{1,0:T(8,128)(2,1)S(1)} collective-permute-done((bf16[512,256]{1,0:T(8,128)(2,1)S(1)}, bf16[512,256]{1,0:T(8,128)(2,1)S(1)}, u32[]{:S(2)}, u32[]{:S(2)}) %collective-permute-start.10) | collective-permute-done | bytes 262176 | tf_op jit(solution)/shard_map/ppermute | solution.py:382
  50.7 0.7 %collective-permute-start.11 = (bf16[512,256]{1,0:T(8,128)(2,1)S(1)}, bf16[512,256]{1,0:T(8,128)(2,1)S(1)}, u32[]{:S(2)}, u32[]{:S(2)}) collective-permute-start(bf16[512,256]{1,0:T(8,128)(2,1)S(1)} %shard_map.166), channel_id=1, source_target_pairs={{0,1},{1,0},{2,3},{3,2},{4,5},{5,4},{6,7},{7,6},{8,9},{9,8},{10,11... | collective-permute-start | bytes 786440 | tf_op jit(solution)/shard_map/ppermute | solution.py:438
  51.6 0.9 %collective-permute-done.11.passed = bf16[512,256]{1,0:T(8,128)(2,1)S(1)} collective-permute-done((bf16[512,256]{1,0:T(8,128)(2,1)S(1)}, bf16[512,256]{1,0:T(8,128)(2,1)S(1)}, u32[]{:S(2)}, u32[]{:S(2)}) %collective-permute-start.11) | collective-permute-done | bytes 262176 | tf_op jit(solution)/shard_map/ppermute | solution.py:438
  52.5 0.8 %shard_map.167 = f32[512,256]{1,0:T(8,128)} custom-call(f32[512,256]{1,0:T(8,128)S(1)} %shard_map.165.mine, bf16[512,256]{1,0:T(8,128)(2,1)S(1)} %collective-permute-done.11.passed), custom_call_target="tpu_custom_call" | custom-call | bytes 1310720 | tf_op jit(solution)/shard_map/pallas_call | solution.py:24
  (12 shorter events, 1.2 us)
Async XLA Ops:
  2.0 10.4 %collective-permute-start = (bf16[32,256]{1,0:T(8,128)(2,1)S(1)}, bf16[32,256]{1,0:T(8,128)(2,1)S(1)}, u32[]{:S(2)}, u32[]{:S(2)}) collective-permute-start(bf16[32,256]{1,0:T(8,128)(2,1)S(1)} %get-tuple-element.48), channel_id=1, source_target_pairs={{0,1},{1,0},{2,3},{3,2},{4,5},{5,4},{6,7},{7,6},{8,9},{9,8},{10,11... | collective-permute-start | bytes 49160 | tf_op jit(solution)/shard_map/ppermute | solution.py:348
  2.8 9.6 %collective-permute-start.1 = (bf16[32,256]{1,0:T(8,128)(2,1)S(1)}, bf16[32,256]{1,0:T(8,128)(2,1)S(1)}, u32[]{:S(2)}, u32[]{:S(2)}) collective-permute-start(bf16[32,256]{1,0:T(8,128)(2,1)S(1)} %get-tuple-element.49), channel_id=1, source_target_pairs={{1,2},{3,4},{5,6},{2,1},{4,3},{6,5},{9,10},{11,12},{13,14},{10,9},... | collective-permute-start | bytes 49160 | tf_op jit(solution)/shard_map/ppermute | solution.py:347
  5.9 3.4 %collective-permute-start.2 = (bf16[16,128]{1,0:T(8,128)(2,1)S(1)}, bf16[16,128]{1,0:T(8,128)(2,1)S(1)}, u32[]{:S(2)}, u32[]{:S(2)}) collective-permute-start(bf16[16,128]{1,0:T(8,128)(2,1)S(1)} %get-tuple-element.50), channel_id=1, source_target_pairs={{0,8},{8,0},{16,24},{24,16},{1,9},{9,1},{17,25},{25,17},{2,10},{10... | collective-permute-start | bytes 12296 | tf_op jit(solution)/shard_map/ppermute | solution.py:350
  7.2 5.2 %collective-permute-start.3 = (bf16[16,128]{1,0:T(8,128)(2,1)S(1)}, bf16[16,128]{1,0:T(8,128)(2,1)S(1)}, u32[]{:S(2)}, u32[]{:S(2)}) collective-permute-start(bf16[16,128]{1,0:T(8,128)(2,1)S(1)} %get-tuple-element.51), channel_id=1, source_target_pairs={{8,16},{16,8},{9,17},{17,9},{10,18},{18,10},{11,19},{19,11},{12,20... | collective-permute-start | bytes 12296 | tf_op jit(solution)/shard_map/ppermute | solution.py:349
  13.8 1.2 %collective-permute-start.4 = (bf16[4,16,128]{2,1,0:T(8,128)(2,1)S(1)}, bf16[4,16,128]{2,1,0:T(8,128)(2,1)S(1)}, u32[]{:S(2)}, u32[]{:S(2)}) collective-permute-start(bf16[4,16,128]{2,1,0:T(8,128)(2,1)S(1)} %get-tuple-element.55), channel_id=1, source_target_pairs={{0,1},{1,0},{2,3},{3,2},{4,5},{5,4},{6,7},{7,6},{8,9},{9,8},{10,11... | collective-permute-start | bytes 49160 | tf_op jit(solution)/shard_map/ppermute | solution.py:364
  15.0 8.1 %collective-permute-start.5 = (bf16[32,128]{1,0:T(8,128)(2,1)S(1)}, bf16[32,128]{1,0:T(8,128)(2,1)S(1)}, u32[]{:S(2)}, u32[]{:S(2)}) collective-permute-start(bf16[32,128]{1,0:T(8,128)(2,1)S(1)} %get-tuple-element.64), channel_id=1, source_target_pairs={{0,2},{1,3},{2,4},{3,5},{4,6},{5,7},{6,0},{7,1},{8,10},{9,11},{10,... | collective-permute-start | bytes 24584 | tf_op jit(solution)/shard_map/ppermute | solution.py:382
  16.9 6.2 %collective-permute-start.6 = (bf16[32,128]{1,0:T(8,128)(2,1)S(1)}, bf16[32,128]{1,0:T(8,128)(2,1)S(1)}, u32[]{:S(2)}, u32[]{:S(2)}) collective-permute-start(bf16[32,128]{1,0:T(8,128)(2,1)S(1)} %get-tuple-element.65), channel_id=1, source_target_pairs={{0,6},{1,7},{2,0},{3,1},{4,2},{5,3},{6,4},{7,5},{8,14},{9,15},{10,... | collective-permute-start | bytes 24584 | tf_op jit(solution)/shard_map/ppermute | solution.py:382
  19.0 4.1 %collective-permute-start.7 = (bf16[32,128]{1,0:T(8,128)(2,1)S(1)}, bf16[32,128]{1,0:T(8,128)(2,1)S(1)}, u32[]{:S(2)}, u32[]{:S(2)}) collective-permute-start(bf16[32,128]{1,0:T(8,128)(2,1)S(1)} %get-tuple-element.66), channel_id=1, source_target_pairs={{0,4},{1,5},{2,6},{3,7},{4,0},{5,1},{6,2},{7,3},{8,12},{9,13},{10,... | collective-permute-start | bytes 24584 | tf_op jit(solution)/shard_map/ppermute | solution.py:382
  23.5 8.6 %collective-permute-start.8 = (bf16[512,256]{1,0:T(8,128)(2,1)S(1)}, bf16[512,256]{1,0:T(8,128)(2,1)S(1)}, u32[]{:S(2)}, u32[]{:S(2)}) collective-permute-start(bf16[512,256]{1,0:T(8,128)(2,1)S(1)} %get-tuple-element.72), channel_id=1, source_target_pairs={{0,2},{1,3},{2,4},{3,5},{4,6},{5,7},{6,0},{7,1},{8,10},{9,11},{10,... | collective-permute-start | bytes 786440 | tf_op jit(solution)/shard_map/ppermute | solution.py:382
  26.9 12.3 %collective-permute-start.9 = (bf16[512,256]{1,0:T(8,128)(2,1)S(1)}, bf16[512,256]{1,0:T(8,128)(2,1)S(1)}, u32[]{:S(2)}, u32[]{:S(2)}) collective-permute-start(bf16[512,256]{1,0:T(8,128)(2,1)S(1)} %get-tuple-element.74), channel_id=1, source_target_pairs={{0,6},{1,7},{2,0},{3,1},{4,2},{5,3},{6,4},{7,5},{8,14},{9,15},{10,... | collective-permute-start | bytes 786440 | tf_op jit(solution)/shard_map/ppermute | solution.py:382
  33.6 16.8 %collective-permute-start.10 = (bf16[512,256]{1,0:T(8,128)(2,1)S(1)}, bf16[512,256]{1,0:T(8,128)(2,1)S(1)}, u32[]{:S(2)}, u32[]{:S(2)}) collective-permute-start(bf16[512,256]{1,0:T(8,128)(2,1)S(1)} %get-tuple-element.76), channel_id=1, source_target_pairs={{0,4},{1,5},{2,6},{3,7},{4,0},{5,1},{6,2},{7,3},{8,12},{9,13},{10,... | collective-permute-start | bytes 786440 | tf_op jit(solution)/shard_map/ppermute | solution.py:382
  50.7 1.8 %collective-permute-start.11 = (bf16[512,256]{1,0:T(8,128)(2,1)S(1)}, bf16[512,256]{1,0:T(8,128)(2,1)S(1)}, u32[]{:S(2)}, u32[]{:S(2)}) collective-permute-start(bf16[512,256]{1,0:T(8,128)(2,1)S(1)} %shard_map.166), channel_id=1, source_target_pairs={{0,1},{1,0},{2,3},{3,2},{4,5},{5,4},{6,7},{7,6},{8,9},{9,8},{10,11... | collective-permute-start | bytes 786440 | tf_op jit(solution)/shard_map/ppermute | solution.py:438

commit v2 on v1

--- a/solution.py
+++ b/solution.py
@@ -126,20 +126,25 @@
     return parts[0] if len(parts) == 1 else jnp.concatenate(parts, axis=0)
 
 
-def first_body(away, order, records_in, hydro_in, rec_packed, hyd_packed, records, hydro, sems):
-    copies = fetch((records_in, hydro_in), (records, hydro), sems)
+def first_body(away, order, records, hydro, rec_packed, hyd_packed):
     hot = picked(order, away, rec_packed.shape[0] // LANES, records.shape[0])
-    copies[0].wait()
     rec = jnp.dot(hot, records[...], preferred_element_type=F32)
-    copies[1].wait()
     rec_packed[...] = shift_time(rec).astype(BF16)
     hyd_packed[...] = jnp.dot(hot, hydro[...], preferred_element_type=F32).astype(BF16)
 
 
 def land_body(
-    moist, heat, moist_k, heat_k, rain, flux, cell, sec_near, sec_far, lon_near, lon_far,
-    moist_out, heat_out, keep, give,
+    moist, heat, moist_k, heat_k, rain, flux, cell, sec_near, sec_far, lon_near, lon_far, records_in, hydro_in,
+    moist_out, heat_out, keep, give, records, hydro, sems,
 ):
+    pieces = sems.shape[0] // 2
+    size = records.shape[0] // pieces
+    cuts = [pl.ds(i * size, size) for i in range(pieces)]
+    copies = fetch(
+        [ref.at[cut, :] for ref in (records_in, hydro_in) for cut in cuts],
+        [ref.at[cut, :] for ref in (records, hydro) for cut in cuts],
+        sems,
+    )
     layers, rows, cols = moist.shape
     row = lax.broadcasted_iota(I32, (rows, cols), 0)
     col = lax.broadcasted_iota(I32, (rows, cols), 1)
@@ -200,20 +205,28 @@
     both = acc.reshape(pairs, 2, blocks, LANES)
     keep[...] = jnp.where(sec_even, both[:, 0], both[:, 1])
     give[...] = jnp.where(sec_even, both[:, 1], both[:, 0]).astype(BF16)
-
-
-def terms_body(aways, keep, got, ids, own, *outs):
+    for copy in copies:
+        copy.wait()
+
+
+def terms_body(keep, got, ids, own, *outs):
     pairs, blocks = keep.shape[:2]
     chip = lax.axis_index("sec") // 2
     own[...] = keep[chip] + got[chip].astype(F32)
-    for away, out in zip(aways, outs):
-        m = lax.rem(chip + away, pairs)
+    for flip, out in enumerate(outs, 1):
+        m = chip ^ flip
         out[:blocks, :] = (keep[m] + got[m].astype(F32)).astype(BF16)
-        out[blocks:, :] = ids[away]
-
-
-def send_body(away, own, order, rec_packed, hyd_packed, *refs):
-    terms, (runoff, ready) = refs[:-2], refs[-2:]
+        out[blocks:, :] = ids[lax.rem(m - chip + pairs, pairs)]
+
+
+def send_body(away, own, order, ids, rec_packed, hyd_packed, *refs):
+    terms, (runoff, ready, places) = refs[:-3], refs[-3:]
+    pairs = places.shape[0]
+    chip = lax.axis_index("sec") // 2
+    places[0] = ids[0]
+    for flip, term in enumerate(terms, 1):
+        back = lax.rem(chip - (chip ^ flip) + pairs, pairs)
+        places[back] = term[term.shape[0] - PACK_ROWS :, :]
     blocks = runoff.shape[0]
     tiles = ready.shape[0] // LANES
     total = own[...]
@@ -230,23 +243,24 @@
         ).astype(BF16)
 
 
-def record_body(away, runoff, records, hydro, order, out, kept, ready):
+def record_body(aways, runoff, records, hydro, order, kept, *ready):
     turned = runoff[...].T
     for t in range(runoff.shape[0]):
         rows = pl.ds(t * LANES, LANES)
-        fresh = (
+        kept[rows, :] = (
             shift_time(records[rows, :].astype(F32)) + turned[:, t : t + 1] * hydro[rows, :].astype(F32)
         ).astype(BF16)
-        out[rows, :] = fresh
-        kept[rows, :] = fresh
-    hot = picked(order, away, ready.shape[0] // LANES, kept.shape[0])
-    ready[...] = jnp.dot(hot, kept[...], preferred_element_type=F32).astype(BF16)
-
-
-def rest_body(aways, order, kept, landed, *ready):
     for away, out in zip(aways, ready):
         hot = picked(order, away, out.shape[0] // LANES, kept.shape[0])
         out[...] = jnp.dot(hot, kept[...], preferred_element_type=F32).astype(BF16)
+
+
+def rest_body(order, kept, landed, out, own, sem):
+    copy = pltpu.make_async_copy(kept, out, sem)
+    copy.start()
+    hot = picked(order, 0, own.shape[0] // LANES, kept.shape[0])
+    own[...] = jnp.dot(hot, kept[...], preferred_element_type=F32).astype(BF16)
+    copy.wait()
 
 
 def hot_of(digits, tiles, basins, other):
@@ -269,24 +283,18 @@
     return total
 
 
-def digits_of(terms):
-    return [ref[ref.shape[0] - PACK_ROWS :, :].astype(F32) for ref in terms]
-
-
-def early_body(ids, *refs):
-    theirs, mine = refs[-2:]
-    n = (len(refs) - 3) // 2
-    terms, blocks = refs[:n], refs[n:-2]
-    digits = [ids[0].astype(F32)] + digits_of(terms)
+def early_body(aways, places, *refs):
+    blocks, (theirs, mine) = refs[:-2], refs[-2:]
+    digits = [places[away].astype(F32) for away in aways]
     basins = mine.shape[0]
     theirs[...] = summed(digits, blocks, basins, True)
     mine[...] = summed(digits, blocks, basins, False)
 
 
-def late_body(other, so_far, *refs):
-    out = refs[-1]
-    terms, blocks = refs[: len(refs) // 2], refs[len(refs) // 2 : -1]
-    out[...] = (so_far[...] + summed(digits_of(terms), blocks, out.shape[0], other)).astype(out.dtype)
+def late_body(aways, other, so_far, places, *refs):
+    blocks, out = refs[:-1], refs[-1]
+    digits = [places[away].astype(F32) for away in aways]
+    out[...] = (so_far[...] + summed(digits, blocks, out.shape[0], other)).astype(out.dtype)
 
 
 def final_body(mine, passed, out, held, sems):
@@ -349,16 +357,21 @@
     got_lon_far = lax.ppermute(lon_far, "lon", between(lons))
     got_lon_near = lax.ppermute(lon_near, "lon", swap(lons))
 
-    moist_out, heat_out, keep, give = call(
+    moist_out, heat_out, keep, give, records_v, hydro_v = call(
         land_body,
         [
             shape(moisture.shape, F32),
             shape(heat.shape, F32),
             shape((pairs, blocks, LANES), F32),
             shape((pairs, blocks, LANES), BF16),
+            shape((reaches, steps), BF16),
+            shape((reaches, steps), BF16),
         ],
         *land,
-        got_sec_near, got_sec_far, got_lon_near, got_lon_far,
+        got_sec_near, got_sec_far, got_lon_near, got_lon_far, records[0], unit_hydro[0],
+        ins=[VMEM] * (len(land) + 4) + [HBM] * 2,
+        scratch=[dma((8,))],
+        mib=12,
         moved=moisture.size * 24,
     )
     got = lax.ppermute(give, "sec", swap(sections))
@@ -374,72 +387,74 @@
     for k in range(1, pairs // 2 + 1):
         aways += [k] if 2 * k == pairs else [k, pairs - k]
     own_terms, *terms = call(
-        lambda *refs: terms_body(aways, *refs),
-        [shape((blocks, LANES), F32)] + [shape((blocks + PACK_ROWS, LANES), BF16)] * len(aways),
+        terms_body,
+        [shape((blocks, LANES), F32)] + [shape((blocks + PACK_ROWS, LANES), BF16)] * (pairs - 1),
         keep, got, ids,
         moved=reaches * 8,
     )
     forward = lambda block, away: lax.ppermute(
         block, "sec", [(i, (i + 2 * away) % sections) for i in range(sections)]
     )
-    terms = {away: forward(term, away) for away, term in zip(aways, terms)}
-    rec_packed, hyd_packed, records_v, hydro_v = call(
+    terms = [
+        lax.ppermute(term, "sec", [(i, i ^ (2 * flip)) for i in range(sections)])
+        for flip, term in enumerate(terms, 1)
+    ]
+    rec_packed, hyd_packed = call(
         lambda *refs: first_body(aways[0], *refs),
-        [shape((cap, steps), BF16)] * 2 + [shape((reaches, steps), BF16)] * 2,
-        order, records[0], unit_hydro[0],
-        ins=[VMEM, HBM, HBM],
-        scratch=[dma((2,))],
+        [shape((cap, steps), BF16)] * 2,
+        order, records_v, hydro_v,
         mib=12,
         flops=4 * cap * reaches * steps,
         moved=reaches * steps * 4,
     )
-    runoff, ready = call(
+    runoff, ready, places = call(
         lambda *refs: send_body(aways[0], *refs),
-        [shape((blocks, LANES), F32), shape((cap, steps), BF16)],
-        own_terms, order, rec_packed, hyd_packed, *terms.values(),
+        [shape((blocks, LANES), F32), shape((cap, steps), BF16), shape(ids.shape, BF16)],
+        own_terms, order, ids, rec_packed, hyd_packed, *terms,
         moved=cap * steps * 6,
     )
     arrived = {aways[0]: forward(ready, aways[0])}
-    record_new, kept, ready = call(
-        lambda *refs: record_body(aways[1], *refs),
-        [shape((reaches, steps), BF16), shape((reaches, steps), BF16), shape((cap, steps), BF16)],
+    kept, *ready = call(
+        lambda *refs: record_body(aways[1:], *refs),
+        [shape((reaches, steps), BF16)] + [shape((cap, steps), BF16)] * (len(aways) - 1),
         runoff, records_v, hydro_v, order,
         mib=16,
         flops=2 * cap * reaches * steps,
         moved=reaches * steps * 8,
     )
-    arrived[aways[1]] = forward(ready, aways[1])
-    rest = aways[2:] + [0]
-    *ready, own = call(
-        lambda *refs: rest_body(rest, *refs),
-        [shape((cap, steps), BF16)] * len(rest),
+    for away, block in zip(aways[1:], ready):
+        arrived[away] = forward(block, away)
+    record_new, own = call(
+        rest_body,
+        [shape((reaches, steps), BF16), shape((cap, steps), BF16)],
         order, kept, arrived[aways[0]],
+        out_specs=[HBM, VMEM],
+        scratch=[dma(())],
         mib=16,
-        flops=2 * cap * reaches * steps * len(rest),
+        flops=2 * cap * reaches * steps,
         moved=reaches * steps * 4,
     )
-    for away, block in zip(aways[2:], ready):
-        arrived[away] = forward(block, away)
     late = aways[-1:]
-    early = aways[:-1]
+    early = [0] + aways[:-1]
+    arrived[0] = own
     theirs, mine = call(
-        early_body,
+        lambda *refs: early_body(early, *refs),
         [shape((basins, steps), F32), shape((basins, steps), F32)],
-        ids, *[terms[a] for a in early], own, *[arrived[a] for a in early],
+        places, *[arrived[a] for a in early],
         mib=12,
         moved=basins * steps * 16,
     )
     (theirs,) = call(
-        lambda *refs: late_body(True, *refs),
+        lambda *refs: late_body(late, True, *refs),
         [shape((basins, steps), BF16)],
-        theirs, *[terms[a] for a in late], *[arrived[a] for a in late],
+        theirs, places, *[arrived[a] for a in late],
         moved=basins * steps * 8,
     )
     passed = lax.ppermute(theirs, "sec", swap(sections))
     (mine,) = call(
-        lambda *refs: late_body(False, *refs),
+        lambda *refs: late_body(late, False, *refs),
         [shape((basins, steps), F32)],
-        mine, *[terms[a] for a in late], *[arrived[a] for a in late],
+        mine, places, *[arrived[a] for a in late],
         moved=basins * steps * 8,
     )
     (inflow,) = call(

time: 53.5 us -> 54.7 us (1.022)
  waiting for transfers between devices: 22.7 us -> 25.3 us
  Pallas kernels: 13.6 us -> 12.1 us
    ppermute x6 -> x3, starting transfers between devices: 8.32 us -> 3.36 us  [per_device(): lax.ppermute(block, 'sec', [(i, (i + 2 * away) % sections) for i in range...]
    ppermute x0 -> x3, starting transfers between devices: none -> 4.24 us  [per_device(): lax.ppermute(term, 'sec', [(i, i ^ 2 * flip) for i in range(sections)])]
    ppermute x0 -> x3, waiting for transfers between devices: none -> 2.84 us  [per_device(): lax.ppermute(term, 'sec', [(i, i ^ 2 * flip) for i in range(sections)])]
    pallas_call x12, Pallas kernels: 13.6 us -> 12.1 us  [call(): pl.pallas_call(body, out_shape=list(outs), in_specs=ins, out_specs=list(o...]
    ppermute x1, starting transfers between devices: 0.66 us -> 1.39 us  [per_device(): passed = lax.ppermute(theirs, 'sec', swap(sections))]
    ppermute x6 -> x3, waiting for transfers between devices: 18.5 us -> 18.3 us  [per_device(): lax.ppermute(block, 'sec', [(i, (i + 2 * away) % sections) for i in range...]
  transfers between devices with their start and end apart: 12 -> 12, of which waited for: 6 -> 7; matrix products, arithmetic and copies ran while one was open for 0% -> 0% of each run, Pallas kernels for 17% -> 12%
where the time goes in v2:
time: 54.7 us; the launch traced here: 54.5 us
  waiting for transfers between devices  25.3 us (46%)
  starting transfers between devices  16.3 us (30%)
  Pallas kernels  12.1 us (22%)
  between operations  0.77 us (1%)
    ppermute x3, waiting for transfers between devices, per_device(): lax.ppermute(block, 'sec', [(i, (i + 2 * away) % sections) for i in range...  18.3 us
    pallas_call x12, Pallas kernels, call(): pl.pallas_call(body, out_shape=list(outs), in_specs=ins, out_specs=list(o...  12.1 us
    ppermute x3, starting transfers between devices, per_device(): lax.ppermute(term, 'sec', [(i, i ^ 2 * flip) for i in range(sections)])  4.24 us
    ppermute x3, starting transfers between devices, per_device(): lax.ppermute(block, 'sec', [(i, (i + 2 * away) % sections) for i in range...  3.36 us
    ppermute x1, waiting for transfers between devices, per_device(): got_lon_far = lax.ppermute(lon_far, 'lon', between(lons))  3.13 us
    ppermute x1, starting transfers between devices, per_device(): got_sec_far = lax.ppermute(sec_far, 'sec', between(sections))  3.1 us
    ppermute x3, waiting for transfers between devices, per_device(): lax.ppermute(term, 'sec', [(i, i ^ 2 * flip) for i in range(sections)])  2.84 us
    ppermute x1, starting transfers between devices, per_device(): got_lon_far = lax.ppermute(lon_far, 'lon', between(lons))  2.09 us
  transfers between devices with their start and end apart: 12, of which 7 were waited for; matrix products, arithmetic and copies ran while one was open for 0% of the time, Pallas kernels for 12%

profile of v2, /device:TPU:5, one launch (start us, length us, event | category | flops | bytes accessed | tf_op | source)
XLA Modules:
  0.0 54.5 jit_solution(13887504905619902650)
XLA Ops:
  0.6 1.4 %shard_map.156 = (f32[16,16,256]{2,1,0:T(8,128)S(1)}, f32[16,16,256]{2,1,0:T(8,128)S(1)}, f32[16,16,256]{2,1,0:T(8,128)S(1)}, f32[16,16,256]{2,1,0:T(8,128)S(1)}...) custom-call(f32[16,16,256]{2,1,0:T(8,128)} %refs_0_.1, ...), custom_call_target="tpu_custom_call" | custom-call | bytes 524288 | tf_op jit(solution)/shard_map/pallas_call | solution.py:24
  2.0 0.7 %collective-permute-start = (bf16[32,256]{1,0:T(8,128)(2,1)S(1)}, bf16[32,256]{1,0:T(8,128)(2,1)S(1)}, u32[]{:S(2)}, u32[]{:S(2)}) collective-permute-start(bf16[32,256]{1,0:T(8,128)(2,1)S(1)} %get-tuple-element.49), channel_id=1, source_target_pairs={{0,1},{1,0},{2,3},{3,2},{4,5},{5,4},{6,7},{7,6},{8,9},{9,8},{10,11... | collective-permute-start | bytes 49160 | tf_op jit(solution)/shard_map/ppermute | solution.py:356
  2.8 3.1 %collective-permute-start.1 = (bf16[32,256]{1,0:T(8,128)(2,1)S(1)}, bf16[32,256]{1,0:T(8,128)(2,1)S(1)}, u32[]{:S(2)}, u32[]{:S(2)}) collective-permute-start(bf16[32,256]{1,0:T(8,128)(2,1)S(1)} %get-tuple-element.50), channel_id=1, source_target_pairs={{1,2},{3,4},{5,6},{2,1},{4,3},{6,5},{9,10},{11,12},{13,14},{10,9},... | collective-permute-start | bytes 49160 | tf_op jit(solution)/shard_map/ppermute | solution.py:355
  5.9 1.3 %collective-permute-start.2 = (bf16[16,128]{1,0:T(8,128)(2,1)S(1)}, bf16[16,128]{1,0:T(8,128)(2,1)S(1)}, u32[]{:S(2)}, u32[]{:S(2)}) collective-permute-start(bf16[16,128]{1,0:T(8,128)(2,1)S(1)} %get-tuple-element.51), channel_id=1, source_target_pairs={{0,8},{8,0},{16,24},{24,16},{1,9},{9,1},{17,25},{25,17},{2,10},{10... | collective-permute-start | bytes 12296 | tf_op jit(solution)/shard_map/ppermute | solution.py:358
  7.2 2.1 %collective-permute-start.3 = (bf16[16,128]{1,0:T(8,128)(2,1)S(1)}, bf16[16,128]{1,0:T(8,128)(2,1)S(1)}, u32[]{:S(2)}, u32[]{:S(2)}) collective-permute-start(bf16[16,128]{1,0:T(8,128)(2,1)S(1)} %get-tuple-element.52), channel_id=1, source_target_pairs={{8,16},{16,8},{9,17},{17,9},{10,18},{18,10},{11,19},{19,11},{12,20... | collective-permute-start | bytes 12296 | tf_op jit(solution)/shard_map/ppermute | solution.py:357
  9.3 3.1 %collective-permute-done.3.lon_far = bf16[16,128]{1,0:T(8,128)(2,1)S(1)} collective-permute-done((bf16[16,128]{1,0:T(8,128)(2,1)S(1)}, bf16[16,128]{1,0:T(8,128)(2,1)S(1)}, u32[]{:S(2)}, u32[]{:S(2)}) %collective-permute-start.3) | collective-permute-done | bytes 4128 | tf_op jit(solution)/shard_map/ppermute | solution.py:357
  12.4 2.9 %shard_map.157 = (f32[16,16,256]{2,1,0:T(8,128)}, f32[16,16,256]{2,1,0:T(8,128)}, f32[4,16,128]{2,1,0:T(8,128)S(1)}, bf16[4,16,128]{2,1,0:T(8,128)(2,1)S(1)}, bf...) custom-call(f32[16,16,256]{2,1,0:T(8,128)S(1)} %get-tuple-element.42.moist, ...), custom_call_target="tpu_custom_call" | custom-call | bytes 1572864 | tf_op jit(solution)/shard_map/pallas_call | solution.py:24
  15.4 0.9 %shard_map.158 = (s32[16,128]{1,0:T(8,128)S(1)}, bf16[4,16,128]{2,1,0:T(8,128)(2,1)S(1)}) custom-call(s32[8,512]{1,0:T(8,128)S(1)} %get-tuple-element.55.listed, s32[32,128]{1,0:T(8,128)S(1)} %get-tuple-element.56.home, s32[16,128]{1,0:T(8,128)S(1)} %get-tuple-element.57.down, s32[1,1,8]{2,1,0:T(1,128)} %count_in.1), custom_call_target="tpu_custom_call" | custom-call | bytes 524288 | tf_op jit(solution)/shard_map/pallas_call | solution.py:24
  16.5 1.9 %collective-permute-start.5 = (bf16[32,128]{1,0:T(8,128)(2,1)S(1)}, bf16[32,128]{1,0:T(8,128)(2,1)S(1)}, u32[]{:S(2)}, u32[]{:S(2)}) collective-permute-start(bf16[32,128]{1,0:T(8,128)(2,1)S(1)} %get-tuple-element.67), channel_id=1, source_target_pairs={{0,2},{1,3},{2,0},{3,1},{4,6},{5,7},{6,4},{7,5},{8,10},{9,11},{10,... | collective-permute-start | bytes 24584 | tf_op jit(solution)/shard_map/ppermute | solution.py:399
  18.5 2.3 %collective-permute-start.6 = (bf16[32,128]{1,0:T(8,128)(2,1)S(1)}, bf16[32,128]{1,0:T(8,128)(2,1)S(1)}, u32[]{:S(2)}, u32[]{:S(2)}) collective-permute-start(bf16[32,128]{1,0:T(8,128)(2,1)S(1)} %get-tuple-element.68), channel_id=1, source_target_pairs={{0,4},{1,5},{2,6},{3,7},{4,0},{5,1},{6,2},{7,3},{8,12},{9,13},{10,... | collective-permute-start | bytes 24584 | tf_op jit(solution)/shard_map/ppermute | solution.py:399
  20.8 1.4 %shard_map.160 = (bf16[512,256]{1,0:T(8,128)(2,1)S(1)}, bf16[512,256]{1,0:T(8,128)(2,1)S(1)}) custom-call(s32[16,128]{1,0:T(8,128)S(1)} %get-tuple-element.58.refs_0_.refs_1_.refs_3_.order, bf16[2048,256]{1,0:T(8,128)(2,1)S(1)} %get-tuple-element.63.refs_1_, bf16[2048,256]{1,0:T(8,128)(2,1)S(1)} %get-tuple-element.64.refs_2_), custom_call_target="tpu_custom_call" | custom-call | flops 1073741824 | bytes 2097152 | tf_op jit(solution)/shard_map/pallas_call | solution.py:24
  22.2 2.8 %collective-permute-done.7.refs_7_ = bf16[32,128]{1,0:T(8,128)(2,1)S(1)} collective-permute-done((bf16[32,128]{1,0:T(8,128)(2,1)S(1)}, bf16[32,128]{1,0:T(8,128)(2,1)S(1)}, u32[]{:S(2)}, u32[]{:S(2)}) %collective-permute-start.7) | collective-permute-done | bytes 8224 | tf_op jit(solution)/shard_map/ppermute | solution.py:399
  25.1 0.4 shard_map.161
  25.5 1.7 %shard_map.162 = (bf16[2048,256]{1,0:T(8,128)(2,1)S(1)}, bf16[512,256]{1,0:T(8,128)(2,1)S(1)}, bf16[512,256]{1,0:T(8,128)(2,1)S(1)}) custom-call(f32[16,128]{1,0:T(8,128)S(1)} %get-tuple-element.70.refs_0_, bf16[2048,256]{1,0:T(8,128)(2,1)S(1)} %get-tuple-element.63.refs_1_, bf16[2048,256]{1,0:T(8,128)(2,1)S(1)} %get-tuple-element.64.refs_2_, ...), custom_call_target="tpu_custom_call" | custom-call | flops 536870912 | bytes 4194304 | tf_op jit(solution)/shard_map/pallas_call | solution.py:24
  27.2 3.3 %collective-permute-start.9 = (bf16[512,256]{1,0:T(8,128)(2,1)S(1)}, bf16[512,256]{1,0:T(8,128)(2,1)S(1)}, u32[]{:S(2)}, u32[]{:S(2)}) collective-permute-start(bf16[512,256]{1,0:T(8,128)(2,1)S(1)} %get-tuple-element.76), channel_id=1, source_target_pairs={{0,6},{1,7},{2,0},{3,1},{4,2},{5,3},{6,4},{7,5},{8,14},{9,15},{10,... | collective-permute-start | bytes 786440 | tf_op jit(solution)/shard_map/ppermute | solution.py:395
  30.5 2.7 %collective-permute-done.8.landed.refs_2_ = bf16[512,256]{1,0:T(8,128)(2,1)S(1)} collective-permute-done((bf16[512,256]{1,0:T(8,128)(2,1)S(1)}, bf16[512,256]{1,0:T(8,128)(2,1)S(1)}, u32[]{:S(2)}, u32[]{:S(2)}) %collective-permute-start.8) | collective-permute-done | bytes 262176 | tf_op jit(solution)/shard_map/ppermute | solution.py:395
  33.3 1.0 %shard_map.163 = (bf16[2048,256]{1,0:T(8,128)(2,1)}, bf16[512,256]{1,0:T(8,128)(2,1)S(1)}) custom-call(s32[16,128]{1,0:T(8,128)S(1)} %get-tuple-element.58.refs_0_.refs_1_.refs_3_.order, bf16[2048,256]{1,0:T(8,128)(2,1)S(1)} %get-tuple-element.71.kept, bf16[512,256]{1,0:T(8,128)(2,1)S(1)} %collective-permute-done.8.landed.refs_2_), custom_call_target="tpu_custom_call" | custom-call | flops 536870912 | bytes 2097152 | tf_op jit(solution)/shard_map/pallas_call | solution.py:24
  34.3 7.1 %collective-permute-done.9.refs_3_ = bf16[512,256]{1,0:T(8,128)(2,1)S(1)} collective-permute-done((bf16[512,256]{1,0:T(8,128)(2,1)S(1)}, bf16[512,256]{1,0:T(8,128)(2,1)S(1)}, u32[]{:S(2)}, u32[]{:S(2)}) %collective-permute-start.9) | collective-permute-done | bytes 262176 | tf_op jit(solution)/shard_map/ppermute | solution.py:395
  41.4 1.0 %shard_map.164 = (f32[512,256]{1,0:T(8,128)S(1)}, f32[512,256]{1,0:T(8,128)S(1)}) custom-call(bf16[4,16,128]{2,1,0:T(8,128)(2,1)S(1)} %get-tuple-element.74.refs_0_.refs_1_, bf16[512,256]{1,0:T(8,128)(2,1)S(1)} %get-tuple-element.75.refs_1_, bf16[512,256]{1,0:T(8,128)(2,1)S(1)} %collective-permute-done.8.landed.refs_2_, ...), custom_call_target="tpu_custom_call" | custom-call | bytes 2097152 | tf_op jit(solution)/shard_map/pallas_call | solution.py:24
  42.3 8.4 %collective-permute-done.10.refs_2_ = bf16[512,256]{1,0:T(8,128)(2,1)S(1)} collective-permute-done((bf16[512,256]{1,0:T(8,128)(2,1)S(1)}, bf16[512,256]{1,0:T(8,128)(2,1)S(1)}, u32[]{:S(2)}, u32[]{:S(2)}) %collective-permute-start.10) | collective-permute-done | bytes 262176 | tf_op jit(solution)/shard_map/ppermute | solution.py:395
  50.8 0.3 shard_map.166
  51.1 1.4 %collective-permute-start.11 = (bf16[512,256]{1,0:T(8,128)(2,1)S(1)}, bf16[512,256]{1,0:T(8,128)(2,1)S(1)}, u32[]{:S(2)}, u32[]{:S(2)}) collective-permute-start(bf16[512,256]{1,0:T(8,128)(2,1)S(1)} %shard_map.166), channel_id=1, source_target_pairs={{0,1},{1,0},{2,3},{3,2},{4,5},{5,4},{6,7},{7,6},{8,9},{9,8},{10,11... | collective-permute-start | bytes 786440 | tf_op jit(solution)/shard_map/ppermute | solution.py:453
  52.8 0.9 %collective-permute-done.11.passed = bf16[512,256]{1,0:T(8,128)(2,1)S(1)} collective-permute-done((bf16[512,256]{1,0:T(8,128)(2,1)S(1)}, bf16[512,256]{1,0:T(8,128)(2,1)S(1)}, u32[]{:S(2)}, u32[]{:S(2)}) %collective-permute-start.11) | collective-permute-done | bytes 262176 | tf_op jit(solution)/shard_map/ppermute | solution.py:453
  53.7 0.8 %shard_map.167 = f32[512,256]{1,0:T(8,128)} custom-call(f32[512,256]{1,0:T(8,128)S(1)} %shard_map.165.mine, bf16[512,256]{1,0:T(8,128)(2,1)S(1)} %collective-permute-done.11.passed), custom_call_target="tpu_custom_call" | custom-call | bytes 1310720 | tf_op jit(solution)/shard_map/pallas_call | solution.py:24
  (12 shorter events, 0.7 us)
Async XLA Ops:
  2.0 10.4 %collective-permute-start = (bf16[32,256]{1,0:T(8,128)(2,1)S(1)}, bf16[32,256]{1,0:T(8,128)(2,1)S(1)}, u32[]{:S(2)}, u32[]{:S(2)}) collective-permute-start(bf16[32,256]{1,0:T(8,128)(2,1)S(1)} %get-tuple-element.49), channel_id=1, source_target_pairs={{0,1},{1,0},{2,3},{3,2},{4,5},{5,4},{6,7},{7,6},{8,9},{9,8},{10,11... | collective-permute-start | bytes 49160 | tf_op jit(solution)/shard_map/ppermute | solution.py:356
  2.8 9.6 %collective-permute-start.1 = (bf16[32,256]{1,0:T(8,128)(2,1)S(1)}, bf16[32,256]{1,0:T(8,128)(2,1)S(1)}, u32[]{:S(2)}, u32[]{:S(2)}) collective-permute-start(bf16[32,256]{1,0:T(8,128)(2,1)S(1)} %get-tuple-element.50), channel_id=1, source_target_pairs={{1,2},{3,4},{5,6},{2,1},{4,3},{6,5},{9,10},{11,12},{13,14},{10,9},... | collective-permute-start | bytes 49160 | tf_op jit(solution)/shard_map/ppermute | solution.py:355
  5.9 3.4 %collective-permute-start.2 = (bf16[16,128]{1,0:T(8,128)(2,1)S(1)}, bf16[16,128]{1,0:T(8,128)(2,1)S(1)}, u32[]{:S(2)}, u32[]{:S(2)}) collective-permute-start(bf16[16,128]{1,0:T(8,128)(2,1)S(1)} %get-tuple-element.51), channel_id=1, source_target_pairs={{0,8},{8,0},{16,24},{24,16},{1,9},{9,1},{17,25},{25,17},{2,10},{10... | collective-permute-start | bytes 12296 | tf_op jit(solution)/shard_map/ppermute | solution.py:358
  7.2 5.2 %collective-permute-start.3 = (bf16[16,128]{1,0:T(8,128)(2,1)S(1)}, bf16[16,128]{1,0:T(8,128)(2,1)S(1)}, u32[]{:S(2)}, u32[]{:S(2)}) collective-permute-start(bf16[16,128]{1,0:T(8,128)(2,1)S(1)} %get-tuple-element.52), channel_id=1, source_target_pairs={{8,16},{16,8},{9,17},{17,9},{10,18},{18,10},{11,19},{19,11},{12,20... | collective-permute-start | bytes 12296 | tf_op jit(solution)/shard_map/ppermute | solution.py:357
  15.3 1.2 %collective-permute-start.4 = (bf16[4,16,128]{2,1,0:T(8,128)(2,1)S(1)}, bf16[4,16,128]{2,1,0:T(8,128)(2,1)S(1)}, u32[]{:S(2)}, u32[]{:S(2)}) collective-permute-start(bf16[4,16,128]{2,1,0:T(8,128)(2,1)S(1)} %get-tuple-element.60), channel_id=1, source_target_pairs={{0,1},{1,0},{2,3},{3,2},{4,5},{5,4},{6,7},{7,6},{8,9},{9,8},{10,11... | collective-permute-start | bytes 49160 | tf_op jit(solution)/shard_map/ppermute | solution.py:377
  16.5 5.7 %collective-permute-start.5 = (bf16[32,128]{1,0:T(8,128)(2,1)S(1)}, bf16[32,128]{1,0:T(8,128)(2,1)S(1)}, u32[]{:S(2)}, u32[]{:S(2)}) collective-permute-start(bf16[32,128]{1,0:T(8,128)(2,1)S(1)} %get-tuple-element.67), channel_id=1, source_target_pairs={{0,2},{1,3},{2,0},{3,1},{4,6},{5,7},{6,4},{7,5},{8,10},{9,11},{10,... | collective-permute-start | bytes 24584 | tf_op jit(solution)/shard_map/ppermute | solution.py:399
  18.5 3.8 %collective-permute-start.6 = (bf16[32,128]{1,0:T(8,128)(2,1)S(1)}, bf16[32,128]{1,0:T(8,128)(2,1)S(1)}, u32[]{:S(2)}, u32[]{:S(2)}) collective-permute-start(bf16[32,128]{1,0:T(8,128)(2,1)S(1)} %get-tuple-element.68), channel_id=1, source_target_pairs={{0,4},{1,5},{2,6},{3,7},{4,0},{5,1},{6,2},{7,3},{8,12},{9,13},{10,... | collective-permute-start | bytes 24584 | tf_op jit(solution)/shard_map/ppermute | solution.py:399
  20.8 4.3 %collective-permute-start.7 = (bf16[32,128]{1,0:T(8,128)(2,1)S(1)}, bf16[32,128]{1,0:T(8,128)(2,1)S(1)}, u32[]{:S(2)}, u32[]{:S(2)}) collective-permute-start(bf16[32,128]{1,0:T(8,128)(2,1)S(1)} %get-tuple-element.69), channel_id=1, source_target_pairs={{0,6},{1,7},{2,4},{3,5},{4,2},{5,3},{6,0},{7,1},{8,14},{9,15},{10,... | collective-permute-start | bytes 24584 | tf_op jit(solution)/shard_map/ppermute | solution.py:399
  25.5 7.8 %collective-permute-start.8 = (bf16[512,256]{1,0:T(8,128)(2,1)S(1)}, bf16[512,256]{1,0:T(8,128)(2,1)S(1)}, u32[]{:S(2)}, u32[]{:S(2)}) collective-permute-start(bf16[512,256]{1,0:T(8,128)(2,1)S(1)} %get-tuple-element.72), channel_id=1, source_target_pairs={{0,2},{1,3},{2,4},{3,5},{4,6},{5,7},{6,0},{7,1},{8,10},{9,11},{10,... | collective-permute-start | bytes 786440 | tf_op jit(solution)/shard_map/ppermute | solution.py:395
  27.2 14.1 %collective-permute-start.9 = (bf16[512,256]{1,0:T(8,128)(2,1)S(1)}, bf16[512,256]{1,0:T(8,128)(2,1)S(1)}, u32[]{:S(2)}, u32[]{:S(2)}) collective-permute-start(bf16[512,256]{1,0:T(8,128)(2,1)S(1)} %get-tuple-element.76), channel_id=1, source_target_pairs={{0,6},{1,7},{2,0},{3,1},{4,2},{5,3},{6,4},{7,5},{8,14},{9,15},{10,... | collective-permute-start | bytes 786440 | tf_op jit(solution)/shard_map/ppermute | solution.py:395
  30.5 20.2 %collective-permute-start.10 = (bf16[512,256]{1,0:T(8,128)(2,1)S(1)}, bf16[512,256]{1,0:T(8,128)(2,1)S(1)}, u32[]{:S(2)}, u32[]{:S(2)}) collective-permute-start(bf16[512,256]{1,0:T(8,128)(2,1)S(1)} %get-tuple-element.78), channel_id=1, source_target_pairs={{0,4},{1,5},{2,6},{3,7},{4,0},{5,1},{6,2},{7,3},{8,12},{9,13},{10,... | collective-permute-start | bytes 786440 | tf_op jit(solution)/shard_map/ppermute | solution.py:395
  51.1 2.6 %collective-permute-start.11 = (bf16[512,256]{1,0:T(8,128)(2,1)S(1)}, bf16[512,256]{1,0:T(8,128)(2,1)S(1)}, u32[]{:S(2)}, u32[]{:S(2)}) collective-permute-start(bf16[512,256]{1,0:T(8,128)(2,1)S(1)} %shard_map.166), channel_id=1, source_target_pairs={{0,1},{1,0},{2,3},{3,2},{4,5},{5,4},{6,7},{7,6},{8,9},{9,8},{10,11... | collective-permute-start | bytes 786440 | tf_op jit(solution)/shard_map/ppermute | solution.py:453

commit v3 on v2

--- a/solution.py
+++ b/solution.py
@@ -96,14 +96,14 @@
         c = count[0, 0, 2 * m]
         second = pltpu.roll(listed[2 * m + 1 : 2 * m + 2, :], lax.rem(c, width), 1)
         line = jnp.where(pos < c, listed[2 * m : 2 * m + 1, :], second)
-        away = lax.rem(m - chip + pairs, pairs)
+        away = m ^ chip
         for t in range(tiles):
             order[pl.ds(away * tiles + t, 1), :] = line[:, t * LANES : (t + 1) * LANES]
     at = order[...]
     place = lookup(slot, at >> 7, at & (LANES - 1))
     pad = jnp.zeros((PACK_ROWS - 2 * tiles, LANES), F32)
     for away in range(pairs):
-        m = lax.rem(away + chip, pairs)
+        m = away ^ chip
         mine = place[away * tiles : (away + 1) * tiles, :] - m * chip_basins
         ids[away] = jnp.concatenate(
             [(mine >> 8).astype(F32), (mine & 255).astype(F32), pad], axis=0
@@ -134,17 +134,9 @@
 
 
 def land_body(
-    moist, heat, moist_k, heat_k, rain, flux, cell, sec_near, sec_far, lon_near, lon_far, records_in, hydro_in,
-    moist_out, heat_out, keep, give, records, hydro, sems,
+    moist, heat, moist_k, heat_k, rain, flux, cell, sec_near, sec_far, lon_near, lon_far,
+    moist_out, heat_out, keep, give,
 ):
-    pieces = sems.shape[0] // 2
-    size = records.shape[0] // pieces
-    cuts = [pl.ds(i * size, size) for i in range(pieces)]
-    copies = fetch(
-        [ref.at[cut, :] for ref in (records_in, hydro_in) for cut in cuts],
-        [ref.at[cut, :] for ref in (records, hydro) for cut in cuts],
-        sems,
-    )
     layers, rows, cols = moist.shape
     row = lax.broadcasted_iota(I32, (rows, cols), 0)
     col = lax.broadcasted_iota(I32, (rows, cols), 1)
@@ -205,8 +197,6 @@
     both = acc.reshape(pairs, 2, blocks, LANES)
     keep[...] = jnp.where(sec_even, both[:, 0], both[:, 1])
     give[...] = jnp.where(sec_even, both[:, 1], both[:, 0]).astype(BF16)
-    for copy in copies:
-        copy.wait()
 
 
 def terms_body(keep, got, ids, own, *outs):
@@ -216,17 +206,14 @@
     for flip, out in enumerate(outs, 1):
         m = chip ^ flip
         out[:blocks, :] = (keep[m] + got[m].astype(F32)).astype(BF16)
-        out[blocks:, :] = ids[lax.rem(m - chip + pairs, pairs)]
+        out[blocks:, :] = ids[flip]
 
 
 def send_body(away, own, order, ids, rec_packed, hyd_packed, *refs):
     terms, (runoff, ready, places) = refs[:-3], refs[-3:]
-    pairs = places.shape[0]
-    chip = lax.axis_index("sec") // 2
     places[0] = ids[0]
     for flip, term in enumerate(terms, 1):
-        back = lax.rem(chip - (chip ^ flip) + pairs, pairs)
-        places[back] = term[term.shape[0] - PACK_ROWS :, :]
+        places[flip] = term[term.shape[0] - PACK_ROWS :, :]
     blocks = runoff.shape[0]
     tiles = ready.shape[0] // LANES
     total = own[...]
@@ -357,21 +344,16 @@
     got_lon_far = lax.ppermute(lon_far, "lon", between(lons))
     got_lon_near = lax.ppermute(lon_near, "lon", swap(lons))
 
-    moist_out, heat_out, keep, give, records_v, hydro_v = call(
+    moist_out, heat_out, keep, give = call(
         land_body,
         [
             shape(moisture.shape, F32),
             shape(heat.shape, F32),
             shape((pairs, blocks, LANES), F32),
             shape((pairs, blocks, LANES), BF16),
-            shape((reaches, steps), BF16),
-            shape((reaches, steps), BF16),
         ],
         *land,
-        got_sec_near, got_sec_far, got_lon_near, got_lon_far, records[0], unit_hydro[0],
-        ins=[VMEM] * (len(land) + 4) + [HBM] * 2,
-        scratch=[dma((8,))],
-        mib=12,
+        got_sec_near, got_sec_far, got_lon_near, got_lon_far,
         moved=moisture.size * 24,
     )
     got = lax.ppermute(give, "sec", swap(sections))
@@ -385,7 +367,7 @@
     )
     aways = []
     for k in range(1, pairs // 2 + 1):
-        aways += [k] if 2 * k == pairs else [k, pairs - k]
+        aways += [k] if 2 * k == pairs else [pairs - k, k]
     own_terms, *terms = call(
         terms_body,
         [shape((blocks, LANES), F32)] + [shape((blocks + PACK_ROWS, LANES), BF16)] * (pairs - 1),
@@ -393,16 +375,13 @@
         moved=reaches * 8,
     )
     forward = lambda block, away: lax.ppermute(
-        block, "sec", [(i, (i + 2 * away) % sections) for i in range(sections)]
-    )
-    terms = [
-        lax.ppermute(term, "sec", [(i, i ^ (2 * flip)) for i in range(sections)])
-        for flip, term in enumerate(terms, 1)
-    ]
+        block, "sec", [(i, i ^ (2 * away)) for i in range(sections)]
+    )
+    terms = [forward(term, flip) for flip, term in enumerate(terms, 1)]
     rec_packed, hyd_packed = call(
         lambda *refs: first_body(aways[0], *refs),
         [shape((cap, steps), BF16)] * 2,
-        order, records_v, hydro_v,
+        order, records[0], unit_hydro[0],
         mib=12,
         flops=4 * cap * reaches * steps,
         moved=reaches * steps * 4,
@@ -417,7 +396,7 @@
     kept, *ready = call(
         lambda *refs: record_body(aways[1:], *refs),
         [shape((reaches, steps), BF16)] + [shape((cap, steps), BF16)] * (len(aways) - 1),
-        runoff, records_v, hydro_v, order,
+        runoff, records[0], unit_hydro[0], order,
         mib=16,
         flops=2 * cap * reaches * steps,
         moved=reaches * steps * 8,

time: 54.7 us -> 50.4 us (0.921)
  waiting for transfers between devices: 25.3 us -> 20.3 us
  starting transfers between devices: 16.3 us -> 18.4 us
  Pallas kernels: 12.1 us -> 10.8 us
    ppermute x6, waiting for transfers between devices: 21.1 us -> 16 us  [per_device(): lax.ppermute(block, 'sec', [(i, i ^ 2 * away) for i in range(sections)])]
    ppermute x1, starting transfers between devices: 1.39 us -> 3.28 us  [per_device(): passed = lax.ppermute(theirs, 'sec', swap(sections))]
    pallas_call x12, Pallas kernels: 12.1 us -> 10.8 us  [call(): pl.pallas_call(body, out_shape=list(outs), in_specs=ins, out_specs=list(o...]
  transfers between devices with their start and end apart: 12 -> 12, of which waited for: 7 -> 6; matrix products, arithmetic and copies ran while one was open for 0% -> 0% of each run, Pallas kernels for 12% -> 13%
where the time goes in v3:
time: 50.4 us; the launch traced here: 50.3 us
  waiting for transfers between devices  20.3 us (40%)
  starting transfers between devices  18.4 us (37%)
  Pallas kernels  10.8 us (21%)
  between operations  0.78 us (2%)
    ppermute x6, waiting for transfers between devices, per_device(): lax.ppermute(block, 'sec', [(i, i ^ 2 * away) for i in range(sections)])  16 us
    pallas_call x12, Pallas kernels, call(): pl.pallas_call(body, out_shape=list(outs), in_specs=ins, out_specs=list(o...  10.8 us
    ppermute x6, starting transfers between devices, per_device(): lax.ppermute(block, 'sec', [(i, i ^ 2 * away) for i in range(sections)])  7.9 us
    ppermute x1, starting transfers between devices, per_device(): passed = lax.ppermute(theirs, 'sec', swap(sections))  3.28 us
    ppermute x1, waiting for transfers between devices, per_device(): got_lon_far = lax.ppermute(lon_far, 'lon', between(lons))  3.13 us
    ppermute x1, starting transfers between devices, per_device(): got_sec_far = lax.ppermute(sec_far, 'sec', between(sections))  3.1 us
    ppermute x1, starting transfers between devices, per_device(): got_lon_far = lax.ppermute(lon_far, 'lon', between(lons))  2.09 us
    ppermute x1, starting transfers between devices, per_device(): got_lon_near = lax.ppermute(lon_near, 'lon', swap(lons))  1.28 us
  transfers between devices with their start and end apart: 12, of which 6 were waited for; matrix products, arithmetic and copies ran while one was open for 0% of the time, Pallas kernels for 13%

profile of v3, /device:TPU:5, one launch (start us, length us, event | category | flops | bytes accessed | tf_op | source)
XLA Modules:
  0.0 50.3 jit_solution(8018820074311385014)
XLA Ops:
  0.7 1.5 %shard_map.156 = (f32[16,16,256]{2,1,0:T(8,128)S(1)}, f32[16,16,256]{2,1,0:T(8,128)S(1)}, f32[16,16,256]{2,1,0:T(8,128)S(1)}, f32[16,16,256]{2,1,0:T(8,128)S(1)}...) custom-call(f32[16,16,256]{2,1,0:T(8,128)} %refs_0_.1, ...), custom_call_target="tpu_custom_call" | custom-call | bytes 524288 | tf_op jit(solution)/shard_map/pallas_call | solution.py:24
  2.2 0.7 %collective-permute-start = (bf16[32,256]{1,0:T(8,128)(2,1)S(1)}, bf16[32,256]{1,0:T(8,128)(2,1)S(1)}, u32[]{:S(2)}, u32[]{:S(2)}) collective-permute-start(bf16[32,256]{1,0:T(8,128)(2,1)S(1)} %get-tuple-element.47), channel_id=1, source_target_pairs={{0,1},{1,0},{2,3},{3,2},{4,5},{5,4},{6,7},{7,6},{8,9},{9,8},{10,11... | collective-permute-start | bytes 49160 | tf_op jit(solution)/shard_map/ppermute | solution.py:343
  2.9 3.1 %collective-permute-start.1 = (bf16[32,256]{1,0:T(8,128)(2,1)S(1)}, bf16[32,256]{1,0:T(8,128)(2,1)S(1)}, u32[]{:S(2)}, u32[]{:S(2)}) collective-permute-start(bf16[32,256]{1,0:T(8,128)(2,1)S(1)} %get-tuple-element.48), channel_id=1, source_target_pairs={{1,2},{3,4},{5,6},{2,1},{4,3},{6,5},{9,10},{11,12},{13,14},{10,9},... | collective-permute-start | bytes 49160 | tf_op jit(solution)/shard_map/ppermute | solution.py:342
  6.1 1.3 %collective-permute-start.2 = (bf16[16,128]{1,0:T(8,128)(2,1)S(1)}, bf16[16,128]{1,0:T(8,128)(2,1)S(1)}, u32[]{:S(2)}, u32[]{:S(2)}) collective-permute-start(bf16[16,128]{1,0:T(8,128)(2,1)S(1)} %get-tuple-element.49), channel_id=1, source_target_pairs={{0,8},{8,0},{16,24},{24,16},{1,9},{9,1},{17,25},{25,17},{2,10},{10... | collective-permute-start | bytes 12296 | tf_op jit(solution)/shard_map/ppermute | solution.py:345
  7.3 2.1 %collective-permute-start.3 = (bf16[16,128]{1,0:T(8,128)(2,1)S(1)}, bf16[16,128]{1,0:T(8,128)(2,1)S(1)}, u32[]{:S(2)}, u32[]{:S(2)}) collective-permute-start(bf16[16,128]{1,0:T(8,128)(2,1)S(1)} %get-tuple-element.50), channel_id=1, source_target_pairs={{8,16},{16,8},{9,17},{17,9},{10,18},{18,10},{11,19},{19,11},{12,20... | collective-permute-start | bytes 12296 | tf_op jit(solution)/shard_map/ppermute | solution.py:344
  9.4 3.1 %collective-permute-done.3.lon_far = bf16[16,128]{1,0:T(8,128)(2,1)S(1)} collective-permute-done((bf16[16,128]{1,0:T(8,128)(2,1)S(1)}, bf16[16,128]{1,0:T(8,128)(2,1)S(1)}, u32[]{:S(2)}, u32[]{:S(2)}) %collective-permute-start.3) | collective-permute-done | bytes 4128 | tf_op jit(solution)/shard_map/ppermute | solution.py:344
  12.6 1.4 %shard_map.157 = (f32[16,16,256]{2,1,0:T(8,128)}, f32[16,16,256]{2,1,0:T(8,128)}, f32[4,16,128]{2,1,0:T(8,128)S(1)}, bf16[4,16,128]{2,1,0:T(8,128)(2,1)S(1)}) custom-call(f32[16,16,256]{2,1,0:T(8,128)S(1)} %get-tuple-element.40.moist, f32[16,16,256]{2,1,0:T(8,128)S(1)} %get-tuple-element.41.heat, f32[16,16,256]{2,1,0:T(8,128)S(1)} %get-tuple-element.42.moist_k, ...), custom_call_target="tpu_custom_call" | custom-call | bytes 1572864 | tf_op jit(solution)/shard_map/pallas_call | solution.py:24
  14.0 0.9 %shard_map.158 = (s32[16,128]{1,0:T(8,128)S(1)}, bf16[4,16,128]{2,1,0:T(8,128)(2,1)S(1)}) custom-call(s32[8,512]{1,0:T(8,128)S(1)} %get-tuple-element.53.listed, s32[32,128]{1,0:T(8,128)S(1)} %get-tuple-element.54.home, s32[16,128]{1,0:T(8,128)S(1)} %get-tuple-element.55.down, s32[1,1,8]{2,1,0:T(1,128)} %count_in.1), custom_call_target="tpu_custom_call" | custom-call | bytes 524288 | tf_op jit(solution)/shard_map/pallas_call | solution.py:24
  15.2 1.9 %collective-permute-start.5 = (bf16[32,128]{1,0:T(8,128)(2,1)S(1)}, bf16[32,128]{1,0:T(8,128)(2,1)S(1)}, u32[]{:S(2)}, u32[]{:S(2)}) collective-permute-start(bf16[32,128]{1,0:T(8,128)(2,1)S(1)} %get-tuple-element.63), channel_id=1, source_target_pairs={{0,2},{1,3},{2,0},{3,1},{4,6},{5,7},{6,4},{7,5},{8,10},{9,11},{10,... | collective-permute-start | bytes 24584 | tf_op jit(solution)/shard_map/ppermute | solution.py:377
  17.1 2.3 %collective-permute-start.6 = (bf16[32,128]{1,0:T(8,128)(2,1)S(1)}, bf16[32,128]{1,0:T(8,128)(2,1)S(1)}, u32[]{:S(2)}, u32[]{:S(2)}) collective-permute-start(bf16[32,128]{1,0:T(8,128)(2,1)S(1)} %get-tuple-element.64), channel_id=1, source_target_pairs={{0,4},{1,5},{2,6},{3,7},{4,0},{5,1},{6,2},{7,3},{8,12},{9,13},{10,... | collective-permute-start | bytes 24584 | tf_op jit(solution)/shard_map/ppermute | solution.py:377
  19.4 1.4 %shard_map.160 = (bf16[512,256]{1,0:T(8,128)(2,1)S(1)}, bf16[512,256]{1,0:T(8,128)(2,1)S(1)}) custom-call(s32[16,128]{1,0:T(8,128)S(1)} %get-tuple-element.56.refs_0_.refs_1_.refs_3_.order, bf16[2048,256]{1,0:T(8,128)(2,1)S(1)} %bitcast.7, bf16[2048,256]{1,0:T(8,128)(2,1)S(1)} %bitcast.9), custom_call_target="tpu_custom_call" | custom-call | flops 1073741824 | bytes 2097152 | tf_op jit(solution)/shard_map/pallas_call | solution.py:24
  20.9 2.8 %collective-permute-done.7.refs_7_ = bf16[32,128]{1,0:T(8,128)(2,1)S(1)} collective-permute-done((bf16[32,128]{1,0:T(8,128)(2,1)S(1)}, bf16[32,128]{1,0:T(8,128)(2,1)S(1)}, u32[]{:S(2)}, u32[]{:S(2)}) %collective-permute-start.7) | collective-permute-done | bytes 8224 | tf_op jit(solution)/shard_map/ppermute | solution.py:377
  23.7 0.4 shard_map.161
  24.1 0.5 %collective-permute-start.8 = (bf16[512,256]{1,0:T(8,128)(2,1)S(1)}, bf16[512,256]{1,0:T(8,128)(2,1)S(1)}, u32[]{:S(2)}, u32[]{:S(2)}) collective-permute-start(bf16[512,256]{1,0:T(8,128)(2,1)S(1)} %get-tuple-element.68), channel_id=1, source_target_pairs={{0,6},{1,7},{2,4},{3,5},{4,2},{5,3},{6,0},{7,1},{8,14},{9,15},{10,... | collective-permute-start | bytes 786440 | tf_op jit(solution)/shard_map/ppermute | solution.py:377
  24.6 1.7 %shard_map.162 = (bf16[2048,256]{1,0:T(8,128)(2,1)S(1)}, bf16[512,256]{1,0:T(8,128)(2,1)S(1)}, bf16[512,256]{1,0:T(8,128)(2,1)S(1)}) custom-call(f32[16,128]{1,0:T(8,128)S(1)} %get-tuple-element.66.refs_0_, bf16[2048,256]{1,0:T(8,128)(2,1)S(1)} %bitcast.8, bf16[2048,256]{1,0:T(8,128)(2,1)S(1)} %bitcast.10, ...), custom_call_target="tpu_custom_call" | custom-call | flops 536870912 | bytes 4194304 | tf_op jit(solution)/shard_map/pallas_call | solution.py:24
  26.4 3.1 %collective-permute-start.10 = (bf16[512,256]{1,0:T(8,128)(2,1)S(1)}, bf16[512,256]{1,0:T(8,128)(2,1)S(1)}, u32[]{:S(2)}, u32[]{:S(2)}) collective-permute-start(bf16[512,256]{1,0:T(8,128)(2,1)S(1)} %get-tuple-element.74), channel_id=1, source_target_pairs={{0,4},{1,5},{2,6},{3,7},{4,0},{5,1},{6,2},{7,3},{8,12},{9,13},{10,... | collective-permute-start | bytes 786440 | tf_op jit(solution)/shard_map/ppermute | solution.py:377
  29.5 2.3 %collective-permute-done.8.landed.refs_2_ = bf16[512,256]{1,0:T(8,128)(2,1)S(1)} collective-permute-done((bf16[512,256]{1,0:T(8,128)(2,1)S(1)}, bf16[512,256]{1,0:T(8,128)(2,1)S(1)}, u32[]{:S(2)}, u32[]{:S(2)}) %collective-permute-start.8) | collective-permute-done | bytes 262176 | tf_op jit(solution)/shard_map/ppermute | solution.py:377
  31.8 1.0 %shard_map.163 = (bf16[2048,256]{1,0:T(8,128)(2,1)}, bf16[512,256]{1,0:T(8,128)(2,1)S(1)}) custom-call(s32[16,128]{1,0:T(8,128)S(1)} %get-tuple-element.56.refs_0_.refs_1_.refs_3_.order, bf16[2048,256]{1,0:T(8,128)(2,1)S(1)} %get-tuple-element.67.kept, bf16[512,256]{1,0:T(8,128)(2,1)S(1)} %collective-permute-done.8.landed.refs_2_), custom_call_target="tpu_custom_call" | custom-call | flops 536870912 | bytes 2097152 | tf_op jit(solution)/shard_map/pallas_call | solution.py:24
  32.8 10.9 %collective-permute-done.9.refs_3_ = bf16[512,256]{1,0:T(8,128)(2,1)S(1)} collective-permute-done((bf16[512,256]{1,0:T(8,128)(2,1)S(1)}, bf16[512,256]{1,0:T(8,128)(2,1)S(1)}, u32[]{:S(2)}, u32[]{:S(2)}) %collective-permute-start.9) | collective-permute-done | bytes 262176 | tf_op jit(solution)/shard_map/ppermute | solution.py:377
  43.7 1.0 %shard_map.164 = (f32[512,256]{1,0:T(8,128)S(1)}, f32[512,256]{1,0:T(8,128)S(1)}) custom-call(bf16[4,16,128]{2,1,0:T(8,128)(2,1)S(1)} %get-tuple-element.70.refs_0_.refs_1_, bf16[512,256]{1,0:T(8,128)(2,1)S(1)} %get-tuple-element.71.refs_1_, bf16[512,256]{1,0:T(8,128)(2,1)S(1)} %collective-permute-done.8.landed.refs_2_, ...), custom_call_target="tpu_custom_call" | custom-call | bytes 2097152 | tf_op jit(solution)/shard_map/pallas_call | solution.py:24
  44.7 0.3 shard_map.166
  45.0 3.3 %collective-permute-start.11 = (bf16[512,256]{1,0:T(8,128)(2,1)S(1)}, bf16[512,256]{1,0:T(8,128)(2,1)S(1)}, u32[]{:S(2)}, u32[]{:S(2)}) collective-permute-start(bf16[512,256]{1,0:T(8,128)(2,1)S(1)} %shard_map.166), channel_id=1, source_target_pairs={{0,1},{1,0},{2,3},{3,2},{4,5},{5,4},{6,7},{7,6},{8,9},{9,8},{10,11... | collective-permute-start | bytes 786440 | tf_op jit(solution)/shard_map/ppermute | solution.py:432
  48.6 0.9 %collective-permute-done.11.passed = bf16[512,256]{1,0:T(8,128)(2,1)S(1)} collective-permute-done((bf16[512,256]{1,0:T(8,128)(2,1)S(1)}, bf16[512,256]{1,0:T(8,128)(2,1)S(1)}, u32[]{:S(2)}, u32[]{:S(2)}) %collective-permute-start.11) | collective-permute-done | bytes 262176 | tf_op jit(solution)/shard_map/ppermute | solution.py:432
  49.4 0.8 %shard_map.167 = f32[512,256]{1,0:T(8,128)} custom-call(f32[512,256]{1,0:T(8,128)S(1)} %shard_map.165.mine, bf16[512,256]{1,0:T(8,128)(2,1)S(1)} %collective-permute-done.11.passed), custom_call_target="tpu_custom_call" | custom-call | bytes 1310720 | tf_op jit(solution)/shard_map/pallas_call | solution.py:24
  (16 shorter events, 0.7 us)
Async XLA Ops:
  0.6 18.8 %copy-start = (bf16[1,2048,256]{2,1,0:T(8,128)(2,1)S(1)}, bf16[1,2048,256]{2,1,0:T(8,128)(2,1)}, u32[]{:S(2)}) copy-start(bf16[1,2048,256]{2,1,0:T(8,128)(2,1)} %param.20) | copy-start | bytes 3145732
  0.6 18.8 %copy-start.1 = (bf16[1,2048,256]{2,1,0:T(8,128)(2,1)S(1)}, bf16[1,2048,256]{2,1,0:T(8,128)(2,1)}, u32[]{:S(2)}) copy-start(bf16[1,2048,256]{2,1,0:T(8,128)(2,1)} %param.21) | copy-start | bytes 3145732
  2.2 10.4 %collective-permute-start = (bf16[32,256]{1,0:T(8,128)(2,1)S(1)}, bf16[32,256]{1,0:T(8,128)(2,1)S(1)}, u32[]{:S(2)}, u32[]{:S(2)}) collective-permute-start(bf16[32,256]{1,0:T(8,128)(2,1)S(1)} %get-tuple-element.47), channel_id=1, source_target_pairs={{0,1},{1,0},{2,3},{3,2},{4,5},{5,4},{6,7},{7,6},{8,9},{9,8},{10,11... | collective-permute-start | bytes 49160 | tf_op jit(solution)/shard_map/ppermute | solution.py:343
  2.9 9.6 %collective-permute-start.1 = (bf16[32,256]{1,0:T(8,128)(2,1)S(1)}, bf16[32,256]{1,0:T(8,128)(2,1)S(1)}, u32[]{:S(2)}, u32[]{:S(2)}) collective-permute-start(bf16[32,256]{1,0:T(8,128)(2,1)S(1)} %get-tuple-element.48), channel_id=1, source_target_pairs={{1,2},{3,4},{5,6},{2,1},{4,3},{6,5},{9,10},{11,12},{13,14},{10,9},... | collective-permute-start | bytes 49160 | tf_op jit(solution)/shard_map/ppermute | solution.py:342
  6.1 3.4 %collective-permute-start.2 = (bf16[16,128]{1,0:T(8,128)(2,1)S(1)}, bf16[16,128]{1,0:T(8,128)(2,1)S(1)}, u32[]{:S(2)}, u32[]{:S(2)}) collective-permute-start(bf16[16,128]{1,0:T(8,128)(2,1)S(1)} %get-tuple-element.49), channel_id=1, source_target_pairs={{0,8},{8,0},{16,24},{24,16},{1,9},{9,1},{17,25},{25,17},{2,10},{10... | collective-permute-start | bytes 12296 | tf_op jit(solution)/shard_map/ppermute | solution.py:345
  7.3 5.2 %collective-permute-start.3 = (bf16[16,128]{1,0:T(8,128)(2,1)S(1)}, bf16[16,128]{1,0:T(8,128)(2,1)S(1)}, u32[]{:S(2)}, u32[]{:S(2)}) collective-permute-start(bf16[16,128]{1,0:T(8,128)(2,1)S(1)} %get-tuple-element.50), channel_id=1, source_target_pairs={{8,16},{16,8},{9,17},{17,9},{10,18},{18,10},{11,19},{19,11},{12,20... | collective-permute-start | bytes 12296 | tf_op jit(solution)/shard_map/ppermute | solution.py:344
  14.0 1.2 %collective-permute-start.4 = (bf16[4,16,128]{2,1,0:T(8,128)(2,1)S(1)}, bf16[4,16,128]{2,1,0:T(8,128)(2,1)S(1)}, u32[]{:S(2)}, u32[]{:S(2)}) collective-permute-start(bf16[4,16,128]{2,1,0:T(8,128)(2,1)S(1)} %get-tuple-element.58), channel_id=1, source_target_pairs={{0,1},{1,0},{2,3},{3,2},{4,5},{5,4},{6,7},{7,6},{8,9},{9,8},{10,11... | collective-permute-start | bytes 49160 | tf_op jit(solution)/shard_map/ppermute | solution.py:359
  15.2 5.7 %collective-permute-start.5 = (bf16[32,128]{1,0:T(8,128)(2,1)S(1)}, bf16[32,128]{1,0:T(8,128)(2,1)S(1)}, u32[]{:S(2)}, u32[]{:S(2)}) collective-permute-start(bf16[32,128]{1,0:T(8,128)(2,1)S(1)} %get-tuple-element.63), channel_id=1, source_target_pairs={{0,2},{1,3},{2,0},{3,1},{4,6},{5,7},{6,4},{7,5},{8,10},{9,11},{10,... | collective-permute-start | bytes 24584 | tf_op jit(solution)/shard_map/ppermute | solution.py:377
  17.1 3.8 %collective-permute-start.6 = (bf16[32,128]{1,0:T(8,128)(2,1)S(1)}, bf16[32,128]{1,0:T(8,128)(2,1)S(1)}, u32[]{:S(2)}, u32[]{:S(2)}) collective-permute-start(bf16[32,128]{1,0:T(8,128)(2,1)S(1)} %get-tuple-element.64), channel_id=1, source_target_pairs={{0,4},{1,5},{2,6},{3,7},{4,0},{5,1},{6,2},{7,3},{8,12},{9,13},{10,... | collective-permute-start | bytes 24584 | tf_op jit(solution)/shard_map/ppermute | solution.py:377
  19.4 4.3 %collective-permute-start.7 = (bf16[32,128]{1,0:T(8,128)(2,1)S(1)}, bf16[32,128]{1,0:T(8,128)(2,1)S(1)}, u32[]{:S(2)}, u32[]{:S(2)}) collective-permute-start(bf16[32,128]{1,0:T(8,128)(2,1)S(1)} %get-tuple-element.65), channel_id=1, source_target_pairs={{0,6},{1,7},{2,4},{3,5},{4,2},{5,3},{6,0},{7,1},{8,14},{9,15},{10,... | collective-permute-start | bytes 24584 | tf_op jit(solution)/shard_map/ppermute | solution.py:377
  24.1 7.7 %collective-permute-start.8 = (bf16[512,256]{1,0:T(8,128)(2,1)S(1)}, bf16[512,256]{1,0:T(8,128)(2,1)S(1)}, u32[]{:S(2)}, u32[]{:S(2)}) collective-permute-start(bf16[512,256]{1,0:T(8,128)(2,1)S(1)} %get-tuple-element.68), channel_id=1, source_target_pairs={{0,6},{1,7},{2,4},{3,5},{4,2},{5,3},{6,0},{7,1},{8,14},{9,15},{10,... | collective-permute-start | bytes 786440 | tf_op jit(solution)/shard_map/ppermute | solution.py:377
  26.4 17.4 %collective-permute-start.9 = (bf16[512,256]{1,0:T(8,128)(2,1)S(1)}, bf16[512,256]{1,0:T(8,128)(2,1)S(1)}, u32[]{:S(2)}, u32[]{:S(2)}) collective-permute-start(bf16[512,256]{1,0:T(8,128)(2,1)S(1)} %get-tuple-element.72), channel_id=1, source_target_pairs={{0,2},{1,3},{2,0},{3,1},{4,6},{5,7},{6,4},{7,5},{8,10},{9,11},{10,... | collective-permute-start | bytes 786440 | tf_op jit(solution)/shard_map/ppermute | solution.py:377
  26.4 18.3 %collective-permute-start.10 = (bf16[512,256]{1,0:T(8,128)(2,1)S(1)}, bf16[512,256]{1,0:T(8,128)(2,1)S(1)}, u32[]{:S(2)}, u32[]{:S(2)}) collective-permute-start(bf16[512,256]{1,0:T(8,128)(2,1)S(1)} %get-tuple-element.74), channel_id=1, source_target_pairs={{0,4},{1,5},{2,6},{3,7},{4,0},{5,1},{6,2},{7,3},{8,12},{9,13},{10,... | collective-permute-start | bytes 786440 | tf_op jit(solution)/shard_map/ppermute | solution.py:377
  45.0 4.4 %collective-permute-start.11 = (bf16[512,256]{1,0:T(8,128)(2,1)S(1)}, bf16[512,256]{1,0:T(8,128)(2,1)S(1)}, u32[]{:S(2)}, u32[]{:S(2)}) collective-permute-start(bf16[512,256]{1,0:T(8,128)(2,1)S(1)} %shard_map.166), channel_id=1, source_target_pairs={{0,1},{1,0},{2,3},{3,2},{4,5},{5,4},{6,7},{7,6},{8,9},{9,8},{10,11... | collective-permute-start | bytes 786440 | tf_op jit(solution)/shard_map/ppermute | solution.py:432

commit v4 on v3

--- a/solution.py
+++ b/solution.py
@@ -126,11 +126,10 @@
     return parts[0] if len(parts) == 1 else jnp.concatenate(parts, axis=0)
 
 
-def first_body(away, order, records, hydro, rec_packed, hyd_packed):
-    hot = picked(order, away, rec_packed.shape[0] // LANES, records.shape[0])
-    rec = jnp.dot(hot, records[...], preferred_element_type=F32)
-    rec_packed[...] = shift_time(rec).astype(BF16)
-    hyd_packed[...] = jnp.dot(hot, hydro[...], preferred_element_type=F32).astype(BF16)
+def first_body(away, shifted, order, rows, packed):
+    hot = picked(order, away, packed.shape[0] // LANES, rows.shape[0])
+    out = jnp.dot(hot, rows[...], preferred_element_type=F32)
+    packed[...] = (shift_time(out) if shifted else out).astype(BF16)
 
 
 def land_body(
@@ -199,26 +198,48 @@
     give[...] = jnp.where(sec_even, both[:, 1], both[:, 0]).astype(BF16)
 
 
-def terms_body(keep, got, ids, own, *outs):
-    pairs, blocks = keep.shape[:2]
-    chip = lax.axis_index("sec") // 2
-    own[...] = keep[chip] + got[chip].astype(F32)
-    for flip, out in enumerate(outs, 1):
-        m = chip ^ flip
-        out[:blocks, :] = (keep[m] + got[m].astype(F32)).astype(BF16)
-        out[blocks:, :] = ids[flip]
-
-
-def send_body(away, own, order, ids, rec_packed, hyd_packed, *refs):
-    terms, (runoff, ready, places) = refs[:-3], refs[-3:]
-    places[0] = ids[0]
-    for flip, term in enumerate(terms, 1):
-        places[flip] = term[term.shape[0] - PACK_ROWS :, :]
+def sources(bits):
+    found = [(0, None)]
+    for i, bit in enumerate(bits):
+        found += [(chip ^ bit, (i, slot)) for slot, (chip, _) in enumerate(found)]
+    return found
+
+
+def digits_at(ids, gots, where, dest, blocks):
+    if where is None:
+        return ids[dest]
+    exchange, slot = where
+    start = blocks + slot * PACK_ROWS
+    return gots[exchange][dest, start : start + PACK_ROWS, :]
+
+
+def terms_body(bits, *refs):
+    kept, give = refs[-2:]
+    ids, gots = refs[-3], refs[1 : len(bits)]
+    bit, blocks = bits[-1], kept.shape[1]
+    for dest in range(2 * bit):
+        if not gots:
+            keep, got = refs[0]
+            m = (lax.axis_index("sec") // 2) ^ dest
+            term = keep[m] + got[m].astype(F32)
+        else:
+            term = refs[0][dest] + gots[-1][dest, :blocks, :].astype(F32)
+        if dest < bit:
+            kept[dest] = term
+        else:
+            give[dest - bit, :blocks, :] = term.astype(BF16)
+            for slot, (_, where) in enumerate(sources(bits[:-1])):
+                start = blocks + slot * PACK_ROWS
+                give[dest - bit, start : start + PACK_ROWS, :] = digits_at(ids, gots, where, dest, blocks)
+
+
+def send_body(bits, away, own, order, ids, rec_packed, hyd_packed, *refs):
+    gots, (runoff, ready, places) = refs[:-3], refs[-3:]
     blocks = runoff.shape[0]
     tiles = ready.shape[0] // LANES
-    total = own[...]
-    for term in terms:
-        total = total + term[:blocks, :].astype(F32)
+    total = own[0] + gots[-1][0, :blocks, :].astype(F32)
+    for chip, where in sources(bits):
+        places[chip] = digits_at(ids, gots, where, 0, blocks)
     runoff[...] = total
     at = order[...]
     turned = lookup(total, at >> 7, at & (LANES - 1)).T
@@ -368,28 +389,40 @@
     aways = []
     for k in range(1, pairs // 2 + 1):
         aways += [k] if 2 * k == pairs else [pairs - k, k]
-    own_terms, *terms = call(
-        terms_body,
-        [shape((blocks, LANES), F32)] + [shape((blocks + PACK_ROWS, LANES), BF16)] * (pairs - 1),
-        keep, got, ids,
-        moved=reaches * 8,
-    )
     forward = lambda block, away: lax.ppermute(
         block, "sec", [(i, i ^ (2 * away)) for i in range(sections)]
     )
-    terms = [forward(term, flip) for flip, term in enumerate(terms, 1)]
-    rec_packed, hyd_packed = call(
-        lambda *refs: first_body(aways[0], *refs),
-        [shape((cap, steps), BF16)] * 2,
-        order, records[0], unit_hydro[0],
+    pack_first = lambda rows, shifted: call(
+        lambda *refs: first_body(aways[0], shifted, *refs),
+        [shape((cap, steps), BF16)],
+        order, rows,
         mib=12,
-        flops=4 * cap * reaches * steps,
-        moved=reaches * steps * 4,
-    )
+        flops=2 * cap * reaches * steps,
+        moved=reaches * steps * 2,
+    )[0]
+    rec_packed = pack_first(records[0], True)
+    bits = [pairs >> i for i in range(1, pairs.bit_length())]
+    gots, held = [], None
+    for i, bit in enumerate(bits):
+        first = [keep, got] if i == 0 else [held, rec_packed]
+        body = lambda *refs, i=i, part=bits[: i + 1]: terms_body(
+            part, refs[:2] if i == 0 else refs[0], *refs[2:]
+        )
+        held, give = call(
+            body,
+            [
+                shape((bit, blocks, LANES), F32),
+                shape((bit, blocks + 2**i * PACK_ROWS, LANES), BF16),
+            ],
+            *first, *gots, ids,
+            moved=reaches * 8,
+        )
+        gots.append(forward(give, bit))
+    hyd_packed = pack_first(unit_hydro[0], False)
     runoff, ready, places = call(
-        lambda *refs: send_body(aways[0], *refs),
+        lambda *refs: send_body(bits, aways[0], *refs),
         [shape((blocks, LANES), F32), shape((cap, steps), BF16), shape(ids.shape, BF16)],
-        own_terms, order, ids, rec_packed, hyd_packed, *terms,
+        held, order, ids, rec_packed, hyd_packed, *gots,
         moved=cap * steps * 6,
     )
     arrived = {aways[0]: forward(ready, aways[0])}

time: 50.4 us -> 51.3 us (1.018)
  waiting for transfers between devices: 20.3 us -> 22.5 us
  starting transfers between devices: 18.4 us -> 16.9 us
    ppermute x6 -> x5, waiting for transfers between devices: 16 us -> 18.2 us  [per_device(): lax.ppermute(block, 'sec', [(i, i ^ 2 * away) for i in range(sections)])]
    ppermute x1, starting transfers between devices: 3.28 us -> 1.54 us  [per_device(): passed = lax.ppermute(theirs, 'sec', swap(sections))]
    pallas_call x12 -> x14, Pallas kernels: 10.8 us -> 11.1 us  [call(): pl.pallas_call(body, out_shape=list(outs), in_specs=ins, out_specs=list(o...]
    ppermute x6 -> x5, starting transfers between devices: 7.9 us -> 8.14 us  [per_device(): lax.ppermute(block, 'sec', [(i, i ^ 2 * away) for i in range(sections)])]
  transfers between devices with their start and end apart: 12 -> 11, of which waited for: 6 -> 8; matrix products, arithmetic and copies ran while one was open for 0% -> 0% of each run, Pallas kernels for 13% -> 13%
where the time goes in v4:
time: 51.3 us; the launch traced here: 51.2 us
  waiting for transfers between devices  22.5 us (44%)
  starting transfers between devices  16.9 us (33%)
  Pallas kernels  11.1 us (22%)
  between operations  0.75 us (1%)
    ppermute x5, waiting for transfers between devices, per_device(): lax.ppermute(block, 'sec', [(i, i ^ 2 * away) for i in range(sections)])  18.2 us
    pallas_call x14, Pallas kernels, call(): pl.pallas_call(body, out_shape=list(outs), in_specs=ins, out_specs=list(o...  11.1 us
    ppermute x5, starting transfers between devices, per_device(): lax.ppermute(block, 'sec', [(i, i ^ 2 * away) for i in range(sections)])  8.14 us
    ppermute x1, waiting for transfers between devices, per_device(): got_lon_far = lax.ppermute(lon_far, 'lon', between(lons))  3.13 us
    ppermute x1, starting transfers between devices, per_device(): got_sec_far = lax.ppermute(sec_far, 'sec', between(sections))  3.1 us
    ppermute x1, starting transfers between devices, per_device(): got_lon_far = lax.ppermute(lon_far, 'lon', between(lons))  2.09 us
    ppermute x1, starting transfers between devices, per_device(): passed = lax.ppermute(theirs, 'sec', swap(sections))  1.54 us
    ppermute x1, starting transfers between devices, per_device(): got_lon_near = lax.ppermute(lon_near, 'lon', swap(lons))  1.28 us
  transfers between devices with their start and end apart: 11, of which 8 were waited for; matrix products, arithmetic and copies ran while one was open for 0% of the time, Pallas kernels for 13%

profile of v4, /device:TPU:5, one launch (start us, length us, event | category | flops | bytes accessed | tf_op | source)
XLA Modules:
  0.0 51.2 jit_solution(8586482893174309390)
XLA Ops:
  0.6 1.5 %shard_map.156 = (f32[16,16,256]{2,1,0:T(8,128)S(1)}, f32[16,16,256]{2,1,0:T(8,128)S(1)}, f32[16,16,256]{2,1,0:T(8,128)S(1)}, f32[16,16,256]{2,1,0:T(8,128)S(1)}...) custom-call(f32[16,16,256]{2,1,0:T(8,128)} %refs_0_.1, ...), custom_call_target="tpu_custom_call" | custom-call | bytes 524288 | tf_op jit(solution)/shard_map/pallas_call | solution.py:24
  2.1 0.7 %collective-permute-start = (bf16[32,256]{1,0:T(8,128)(2,1)S(1)}, bf16[32,256]{1,0:T(8,128)(2,1)S(1)}, u32[]{:S(2)}, u32[]{:S(2)}) collective-permute-start(bf16[32,256]{1,0:T(8,128)(2,1)S(1)} %get-tuple-element.45), channel_id=1, source_target_pairs={{0,1},{1,0},{2,3},{3,2},{4,5},{5,4},{6,7},{7,6},{8,9},{9,8},{10,11... | collective-permute-start | bytes 49160 | tf_op jit(solution)/shard_map/ppermute | solution.py:364
  2.9 3.1 %collective-permute-start.1 = (bf16[32,256]{1,0:T(8,128)(2,1)S(1)}, bf16[32,256]{1,0:T(8,128)(2,1)S(1)}, u32[]{:S(2)}, u32[]{:S(2)}) collective-permute-start(bf16[32,256]{1,0:T(8,128)(2,1)S(1)} %get-tuple-element.46), channel_id=1, source_target_pairs={{1,2},{3,4},{5,6},{2,1},{4,3},{6,5},{9,10},{11,12},{13,14},{10,9},... | collective-permute-start | bytes 49160 | tf_op jit(solution)/shard_map/ppermute | solution.py:363
  6.0 1.3 %collective-permute-start.2 = (bf16[16,128]{1,0:T(8,128)(2,1)S(1)}, bf16[16,128]{1,0:T(8,128)(2,1)S(1)}, u32[]{:S(2)}, u32[]{:S(2)}) collective-permute-start(bf16[16,128]{1,0:T(8,128)(2,1)S(1)} %get-tuple-element.47), channel_id=1, source_target_pairs={{0,8},{8,0},{16,24},{24,16},{1,9},{9,1},{17,25},{25,17},{2,10},{10... | collective-permute-start | bytes 12296 | tf_op jit(solution)/shard_map/ppermute | solution.py:366
  7.3 2.1 %collective-permute-start.3 = (bf16[16,128]{1,0:T(8,128)(2,1)S(1)}, bf16[16,128]{1,0:T(8,128)(2,1)S(1)}, u32[]{:S(2)}, u32[]{:S(2)}) collective-permute-start(bf16[16,128]{1,0:T(8,128)(2,1)S(1)} %get-tuple-element.48), channel_id=1, source_target_pairs={{8,16},{16,8},{9,17},{17,9},{10,18},{18,10},{11,19},{19,11},{12,20... | collective-permute-start | bytes 12296 | tf_op jit(solution)/shard_map/ppermute | solution.py:365
  9.4 3.1 %collective-permute-done.3.lon_far = bf16[16,128]{1,0:T(8,128)(2,1)S(1)} collective-permute-done((bf16[16,128]{1,0:T(8,128)(2,1)S(1)}, bf16[16,128]{1,0:T(8,128)(2,1)S(1)}, u32[]{:S(2)}, u32[]{:S(2)}) %collective-permute-start.3) | collective-permute-done | bytes 4128 | tf_op jit(solution)/shard_map/ppermute | solution.py:365
  12.5 1.4 %shard_map.157 = (f32[16,16,256]{2,1,0:T(8,128)}, f32[16,16,256]{2,1,0:T(8,128)}, f32[4,16,128]{2,1,0:T(8,128)S(1)}, bf16[4,16,128]{2,1,0:T(8,128)(2,1)S(1)}) custom-call(f32[16,16,256]{2,1,0:T(8,128)S(1)} %get-tuple-element.38.moist, f32[16,16,256]{2,1,0:T(8,128)S(1)} %get-tuple-element.39.heat, f32[16,16,256]{2,1,0:T(8,128)S(1)} %get-tuple-element.40.moist_k, ...), custom_call_target="tpu_custom_call" | custom-call | bytes 1572864 | tf_op jit(solution)/shard_map/pallas_call | solution.py:24
  13.9 0.9 %shard_map.158 = (s32[16,128]{1,0:T(8,128)S(1)}, bf16[4,16,128]{2,1,0:T(8,128)(2,1)S(1)}) custom-call(s32[8,512]{1,0:T(8,128)S(1)} %get-tuple-element.51.listed, s32[32,128]{1,0:T(8,128)S(1)} %get-tuple-element.52.home, s32[16,128]{1,0:T(8,128)S(1)} %get-tuple-element.53.down, s32[1,1,8]{2,1,0:T(1,128)} %count_in.1), custom_call_target="tpu_custom_call" | custom-call | bytes 524288 | tf_op jit(solution)/shard_map/pallas_call | solution.py:24
  15.1 2.9 %collective-permute-start.5 = (bf16[2,32,128]{2,1,0:T(8,128)(2,1)S(1)}, bf16[2,32,128]{2,1,0:T(8,128)(2,1)S(1)}, u32[]{:S(2)}, u32[]{:S(2)}) collective-permute-start(bf16[2,32,128]{2,1,0:T(8,128)(2,1)S(1)} %get-tuple-element.59), channel_id=1, source_target_pairs={{0,4},{1,5},{2,6},{3,7},{4,0},{5,1},{6,2},{7,3},{8,12},{9,13},{10,... | collective-permute-start | bytes 49160 | tf_op jit(solution)/shard_map/ppermute | solution.py:392
  18.1 0.9 %shard_map.160.refs_1_.refs_3_ = bf16[512,256]{1,0:T(8,128)(2,1)S(1)} custom-call(s32[16,128]{1,0:T(8,128)S(1)} %get-tuple-element.54.refs_0_.refs_1_.refs_3_.order, bf16[2048,256]{1,0:T(8,128)(2,1)S(1)} %bitcast.7), custom_call_target="tpu_custom_call" | custom-call | flops 536870912 | bytes 1048576 | tf_op jit(solution)/shard_map/pallas_call | solution.py:24
  19.2 1.3 %collective-permute-start.6 = (bf16[1,48,128]{2,1,0:T(8,128)(2,1)S(1)}, bf16[1,48,128]{2,1,0:T(8,128)(2,1)S(1)}, u32[]{:S(2)}, u32[]{:S(2)}) collective-permute-start(bf16[1,48,128]{2,1,0:T(8,128)(2,1)S(1)} %get-tuple-element.61), channel_id=1, source_target_pairs={{0,2},{1,3},{2,0},{3,1},{4,6},{5,7},{6,4},{7,5},{8,10},{9,11},{10,... | collective-permute-start | bytes 36872 | tf_op jit(solution)/shard_map/ppermute | solution.py:392
  20.5 0.8 %shard_map.162.refs_4_ = bf16[512,256]{1,0:T(8,128)(2,1)S(1)} custom-call(s32[16,128]{1,0:T(8,128)S(1)} %get-tuple-element.54.refs_0_.refs_1_.refs_3_.order, bf16[2048,256]{1,0:T(8,128)(2,1)S(1)} %bitcast.9), custom_call_target="tpu_custom_call" | custom-call | flops 536870912 | bytes 1048576 | tf_op jit(solution)/shard_map/pallas_call | solution.py:24
  21.4 0.4 collective-permute-done.6.refs_6_
  21.7 0.4 shard_map.163
  22.1 3.5 %collective-permute-start.7 = (bf16[512,256]{1,0:T(8,128)(2,1)S(1)}, bf16[512,256]{1,0:T(8,128)(2,1)S(1)}, u32[]{:S(2)}, u32[]{:S(2)}) collective-permute-start(bf16[512,256]{1,0:T(8,128)(2,1)S(1)} %get-tuple-element.64), channel_id=1, source_target_pairs={{0,6},{1,7},{2,4},{3,5},{4,2},{5,3},{6,0},{7,1},{8,14},{9,15},{10,... | collective-permute-start | bytes 786440 | tf_op jit(solution)/shard_map/ppermute | solution.py:392
  25.6 1.7 %shard_map.164 = (bf16[2048,256]{1,0:T(8,128)(2,1)S(1)}, bf16[512,256]{1,0:T(8,128)(2,1)S(1)}, bf16[512,256]{1,0:T(8,128)(2,1)S(1)}) custom-call(f32[16,128]{1,0:T(8,128)S(1)} %get-tuple-element.62.refs_0_, bf16[2048,256]{1,0:T(8,128)(2,1)S(1)} %bitcast.8, bf16[2048,256]{1,0:T(8,128)(2,1)S(1)} %bitcast.10, ...), custom_call_target="tpu_custom_call" | custom-call | flops 536870912 | bytes 4194304 | tf_op jit(solution)/shard_map/pallas_call | solution.py:24
  27.7 2.1 %collective-permute-done.7.landed.refs_2_ = bf16[512,256]{1,0:T(8,128)(2,1)S(1)} collective-permute-done((bf16[512,256]{1,0:T(8,128)(2,1)S(1)}, bf16[512,256]{1,0:T(8,128)(2,1)S(1)}, u32[]{:S(2)}, u32[]{:S(2)}) %collective-permute-start.7) | collective-permute-done | bytes 262176 | tf_op jit(solution)/shard_map/ppermute | solution.py:392
  29.8 1.0 %shard_map.165 = (bf16[2048,256]{1,0:T(8,128)(2,1)}, bf16[512,256]{1,0:T(8,128)(2,1)S(1)}) custom-call(s32[16,128]{1,0:T(8,128)S(1)} %get-tuple-element.54.refs_0_.refs_1_.refs_3_.order, bf16[2048,256]{1,0:T(8,128)(2,1)S(1)} %get-tuple-element.63.kept, bf16[512,256]{1,0:T(8,128)(2,1)S(1)} %collective-permute-done.7.landed.refs_2_), custom_call_target="tpu_custom_call" | custom-call | flops 536870912 | bytes 2097152 | tf_op jit(solution)/shard_map/pallas_call | solution.py:24
  30.8 5.8 %collective-permute-done.8.refs_3_ = bf16[512,256]{1,0:T(8,128)(2,1)S(1)} collective-permute-done((bf16[512,256]{1,0:T(8,128)(2,1)S(1)}, bf16[512,256]{1,0:T(8,128)(2,1)S(1)}, u32[]{:S(2)}, u32[]{:S(2)}) %collective-permute-start.8) | collective-permute-done | bytes 262176 | tf_op jit(solution)/shard_map/ppermute | solution.py:392
  36.6 1.0 %shard_map.166 = (f32[512,256]{1,0:T(8,128)S(1)}, f32[512,256]{1,0:T(8,128)S(1)}) custom-call(bf16[4,16,128]{2,1,0:T(8,128)(2,1)S(1)} %get-tuple-element.66.refs_0_.refs_1_, bf16[512,256]{1,0:T(8,128)(2,1)S(1)} %get-tuple-element.67.refs_1_, bf16[512,256]{1,0:T(8,128)(2,1)S(1)} %collective-permute-done.7.landed.refs_2_, ...), custom_call_target="tpu_custom_call" | custom-call | bytes 2097152 | tf_op jit(solution)/shard_map/pallas_call | solution.py:24
  37.6 9.7 %collective-permute-done.9.refs_2_ = bf16[512,256]{1,0:T(8,128)(2,1)S(1)} collective-permute-done((bf16[512,256]{1,0:T(8,128)(2,1)S(1)}, bf16[512,256]{1,0:T(8,128)(2,1)S(1)}, u32[]{:S(2)}, u32[]{:S(2)}) %collective-permute-start.9) | collective-permute-done | bytes 262176 | tf_op jit(solution)/shard_map/ppermute | solution.py:392
  47.6 1.5 %collective-permute-start.10 = (bf16[512,256]{1,0:T(8,128)(2,1)S(1)}, bf16[512,256]{1,0:T(8,128)(2,1)S(1)}, u32[]{:S(2)}, u32[]{:S(2)}) collective-permute-start(bf16[512,256]{1,0:T(8,128)(2,1)S(1)} %shard_map.168), channel_id=1, source_target_pairs={{0,1},{1,0},{2,3},{3,2},{4,5},{5,4},{6,7},{7,6},{8,9},{9,8},{10,11... | collective-permute-start | bytes 786440 | tf_op jit(solution)/shard_map/ppermute | solution.py:465
  49.5 0.9 %collective-permute-done.10.passed = bf16[512,256]{1,0:T(8,128)(2,1)S(1)} collective-permute-done((bf16[512,256]{1,0:T(8,128)(2,1)S(1)}, bf16[512,256]{1,0:T(8,128)(2,1)S(1)}, u32[]{:S(2)}, u32[]{:S(2)}) %collective-permute-start.10) | collective-permute-done | bytes 262176 | tf_op jit(solution)/shard_map/ppermute | solution.py:465
  50.3 0.8 %shard_map.169 = f32[512,256]{1,0:T(8,128)} custom-call(f32[512,256]{1,0:T(8,128)S(1)} %shard_map.167.mine, bf16[512,256]{1,0:T(8,128)(2,1)S(1)} %collective-permute-done.10.passed), custom_call_target="tpu_custom_call" | custom-call | bytes 1310720 | tf_op jit(solution)/shard_map/pallas_call | solution.py:24
  (16 shorter events, 1.5 us)
Async XLA Ops:
  0.6 17.4 %copy-start = (bf16[1,2048,256]{2,1,0:T(8,128)(2,1)S(1)}, bf16[1,2048,256]{2,1,0:T(8,128)(2,1)}, u32[]{:S(2)}) copy-start(bf16[1,2048,256]{2,1,0:T(8,128)(2,1)} %param.20) | copy-start | bytes 3145732
  2.1 10.4 %collective-permute-start = (bf16[32,256]{1,0:T(8,128)(2,1)S(1)}, bf16[32,256]{1,0:T(8,128)(2,1)S(1)}, u32[]{:S(2)}, u32[]{:S(2)}) collective-permute-start(bf16[32,256]{1,0:T(8,128)(2,1)S(1)} %get-tuple-element.45), channel_id=1, source_target_pairs={{0,1},{1,0},{2,3},{3,2},{4,5},{5,4},{6,7},{7,6},{8,9},{9,8},{10,11... | collective-permute-start | bytes 49160 | tf_op jit(solution)/shard_map/ppermute | solution.py:364
  2.9 9.6 %collective-permute-start.1 = (bf16[32,256]{1,0:T(8,128)(2,1)S(1)}, bf16[32,256]{1,0:T(8,128)(2,1)S(1)}, u32[]{:S(2)}, u32[]{:S(2)}) collective-permute-start(bf16[32,256]{1,0:T(8,128)(2,1)S(1)} %get-tuple-element.46), channel_id=1, source_target_pairs={{1,2},{3,4},{5,6},{2,1},{4,3},{6,5},{9,10},{11,12},{13,14},{10,9},... | collective-permute-start | bytes 49160 | tf_op jit(solution)/shard_map/ppermute | solution.py:363
  6.0 3.4 %collective-permute-start.2 = (bf16[16,128]{1,0:T(8,128)(2,1)S(1)}, bf16[16,128]{1,0:T(8,128)(2,1)S(1)}, u32[]{:S(2)}, u32[]{:S(2)}) collective-permute-start(bf16[16,128]{1,0:T(8,128)(2,1)S(1)} %get-tuple-element.47), channel_id=1, source_target_pairs={{0,8},{8,0},{16,24},{24,16},{1,9},{9,1},{17,25},{25,17},{2,10},{10... | collective-permute-start | bytes 12296 | tf_op jit(solution)/shard_map/ppermute | solution.py:366
  7.3 5.2 %collective-permute-start.3 = (bf16[16,128]{1,0:T(8,128)(2,1)S(1)}, bf16[16,128]{1,0:T(8,128)(2,1)S(1)}, u32[]{:S(2)}, u32[]{:S(2)}) collective-permute-start(bf16[16,128]{1,0:T(8,128)(2,1)S(1)} %get-tuple-element.48), channel_id=1, source_target_pairs={{8,16},{16,8},{9,17},{17,9},{10,18},{18,10},{11,19},{19,11},{12,20... | collective-permute-start | bytes 12296 | tf_op jit(solution)/shard_map/ppermute | solution.py:365
  13.9 1.2 %collective-permute-start.4 = (bf16[4,16,128]{2,1,0:T(8,128)(2,1)S(1)}, bf16[4,16,128]{2,1,0:T(8,128)(2,1)S(1)}, u32[]{:S(2)}, u32[]{:S(2)}) collective-permute-start(bf16[4,16,128]{2,1,0:T(8,128)(2,1)S(1)} %get-tuple-element.56), channel_id=1, source_target_pairs={{0,1},{1,0},{2,3},{3,2},{4,5},{5,4},{6,7},{7,6},{8,9},{9,8},{10,11... | collective-permute-start | bytes 49160 | tf_op jit(solution)/shard_map/ppermute | solution.py:380
  15.1 4.1 %collective-permute-start.5 = (bf16[2,32,128]{2,1,0:T(8,128)(2,1)S(1)}, bf16[2,32,128]{2,1,0:T(8,128)(2,1)S(1)}, u32[]{:S(2)}, u32[]{:S(2)}) collective-permute-start(bf16[2,32,128]{2,1,0:T(8,128)(2,1)S(1)} %get-tuple-element.59), channel_id=1, source_target_pairs={{0,4},{1,5},{2,6},{3,7},{4,0},{5,1},{6,2},{7,3},{8,12},{9,13},{10,... | collective-permute-start | bytes 49160 | tf_op jit(solution)/shard_map/ppermute | solution.py:392
  18.1 2.5 %copy-start.1 = (bf16[1,2048,256]{2,1,0:T(8,128)(2,1)S(1)}, bf16[1,2048,256]{2,1,0:T(8,128)(2,1)}, u32[]{:S(2)}) copy-start(bf16[1,2048,256]{2,1,0:T(8,128)(2,1)} %param.21) | copy-start | bytes 3145732
  19.2 2.5 %collective-permute-start.6 = (bf16[1,48,128]{2,1,0:T(8,128)(2,1)S(1)}, bf16[1,48,128]{2,1,0:T(8,128)(2,1)S(1)}, u32[]{:S(2)}, u32[]{:S(2)}) collective-permute-start(bf16[1,48,128]{2,1,0:T(8,128)(2,1)S(1)} %get-tuple-element.61), channel_id=1, source_target_pairs={{0,2},{1,3},{2,0},{3,1},{4,6},{5,7},{6,4},{7,5},{8,10},{9,11},{10,... | collective-permute-start | bytes 36872 | tf_op jit(solution)/shard_map/ppermute | solution.py:392
  22.1 7.7 %collective-permute-start.7 = (bf16[512,256]{1,0:T(8,128)(2,1)S(1)}, bf16[512,256]{1,0:T(8,128)(2,1)S(1)}, u32[]{:S(2)}, u32[]{:S(2)}) collective-permute-start(bf16[512,256]{1,0:T(8,128)(2,1)S(1)} %get-tuple-element.64), channel_id=1, source_target_pairs={{0,6},{1,7},{2,4},{3,5},{4,2},{5,3},{6,0},{7,1},{8,14},{9,15},{10,... | collective-permute-start | bytes 786440 | tf_op jit(solution)/shard_map/ppermute | solution.py:392
  27.4 9.3 %collective-permute-start.8 = (bf16[512,256]{1,0:T(8,128)(2,1)S(1)}, bf16[512,256]{1,0:T(8,128)(2,1)S(1)}, u32[]{:S(2)}, u32[]{:S(2)}) collective-permute-start(bf16[512,256]{1,0:T(8,128)(2,1)S(1)} %get-tuple-element.68), channel_id=1, source_target_pairs={{0,2},{1,3},{2,0},{3,1},{4,6},{5,7},{6,4},{7,5},{8,10},{9,11},{10,... | collective-permute-start | bytes 786440 | tf_op jit(solution)/shard_map/ppermute | solution.py:392
  27.4 19.9 %collective-permute-start.9 = (bf16[512,256]{1,0:T(8,128)(2,1)S(1)}, bf16[512,256]{1,0:T(8,128)(2,1)S(1)}, u32[]{:S(2)}, u32[]{:S(2)}) collective-permute-start(bf16[512,256]{1,0:T(8,128)(2,1)S(1)} %get-tuple-element.70), channel_id=1, source_target_pairs={{0,4},{1,5},{2,6},{3,7},{4,0},{5,1},{6,2},{7,3},{8,12},{9,13},{10,... | collective-permute-start | bytes 786440 | tf_op jit(solution)/shard_map/ppermute | solution.py:392
  47.6 2.7 %collective-permute-start.10 = (bf16[512,256]{1,0:T(8,128)(2,1)S(1)}, bf16[512,256]{1,0:T(8,128)(2,1)S(1)}, u32[]{:S(2)}, u32[]{:S(2)}) collective-permute-start(bf16[512,256]{1,0:T(8,128)(2,1)S(1)} %shard_map.168), channel_id=1, source_target_pairs={{0,1},{1,0},{2,3},{3,2},{4,5},{5,4},{6,7},{7,6},{8,9},{9,8},{10,11... | collective-permute-start | bytes 786440 | tf_op jit(solution)/shard_map/ppermute | solution.py:465

commit v5 on v3

--- a/solution.py
+++ b/solution.py
@@ -144,8 +144,11 @@
     lon_even = parity("lon") == 0
     south_all = jnp.where(sec_even, sec_near[...].astype(F32), sec_far[...].astype(F32))
     north_all = jnp.where(sec_even, sec_far[...].astype(F32), sec_near[...].astype(F32))
-    east_all = jnp.where(lon_even, lon_near[...].astype(F32), lon_far[...].astype(F32))
-    west_all = jnp.where(lon_even, lon_far[...].astype(F32), lon_near[...].astype(F32))
+    lon = lax.axis_index("lon")
+    outer = (lon == 0) | (lon == lax.axis_size("lon") - 1)
+    lon_beyond = jnp.where(outer, 0.0, lon_far[...].astype(F32))
+    east_all = jnp.where(lon_even, lon_near[...].astype(F32), lon_beyond)
+    west_all = jnp.where(lon_even, lon_beyond, lon_near[...].astype(F32))
     for f, (x_ref, k_ref, top, out) in enumerate(
         ((moist, moist_k, rain, moist_out), (heat, heat_k, flux, heat_out))
     ):
@@ -203,7 +206,7 @@
     pairs, blocks = keep.shape[:2]
     chip = lax.axis_index("sec") // 2
     own[...] = keep[chip] + got[chip].astype(F32)
-    for flip, out in enumerate(outs, 1):
+    for flip, out in zip(range(len(outs), 0, -1), outs):
         m = chip ^ flip
         out[:blocks, :] = (keep[m] + got[m].astype(F32)).astype(BF16)
         out[blocks:, :] = ids[flip]
@@ -212,7 +215,7 @@
 def send_body(away, own, order, ids, rec_packed, hyd_packed, *refs):
     terms, (runoff, ready, places) = refs[:-3], refs[-3:]
     places[0] = ids[0]
-    for flip, term in enumerate(terms, 1):
+    for flip, term in zip(range(len(terms), 0, -1), terms):
         places[flip] = term[term.shape[0] - PACK_ROWS :, :]
     blocks = runoff.shape[0]
     tiles = ready.shape[0] // LANES
@@ -242,14 +245,6 @@
         out[...] = jnp.dot(hot, kept[...], preferred_element_type=F32).astype(BF16)
 
 
-def rest_body(order, kept, landed, out, own, sem):
-    copy = pltpu.make_async_copy(kept, out, sem)
-    copy.start()
-    hot = picked(order, 0, own.shape[0] // LANES, kept.shape[0])
-    own[...] = jnp.dot(hot, kept[...], preferred_element_type=F32).astype(BF16)
-    copy.wait()
-
-
 def hot_of(digits, tiles, basins, other):
     core = parity("sec")
     base = ((1 - core) if other else core) * basins
@@ -270,12 +265,24 @@
     return total
 
 
-def early_body(aways, places, *refs):
+def rest_body(near, order, kept, places, landed, out, theirs, mine, own, sem):
+    copy = pltpu.make_async_copy(kept, out, sem)
+    copy.start()
+    hot = picked(order, 0, own.shape[0] // LANES, kept.shape[0])
+    own[...] = jnp.dot(hot, kept[...], preferred_element_type=F32).astype(BF16)
+    digits = [places[away].astype(F32) for away in (0, near)]
+    basins = mine.shape[0]
+    theirs[...] = summed(digits, [own, landed], basins, True)
+    mine[...] = summed(digits, [own, landed], basins, False)
+    copy.wait()
+
+
+def early_body(aways, theirs_so_far, mine_so_far, places, *refs):
     blocks, (theirs, mine) = refs[:-2], refs[-2:]
     digits = [places[away].astype(F32) for away in aways]
     basins = mine.shape[0]
-    theirs[...] = summed(digits, blocks, basins, True)
-    mine[...] = summed(digits, blocks, basins, False)
+    theirs[...] = theirs_so_far[...] + summed(digits, blocks, basins, True)
+    mine[...] = mine_so_far[...] + summed(digits, blocks, basins, False)
 
 
 def late_body(aways, other, so_far, places, *refs):
@@ -341,7 +348,9 @@
     ]
     got_sec_far = lax.ppermute(sec_far, "sec", between(sections))
     got_sec_near = lax.ppermute(sec_near, "sec", swap(sections))
-    got_lon_far = lax.ppermute(lon_far, "lon", between(lons))
+    got_lon_far = lax.ppermute(
+        lon_far, "lon", [(i, (i - 1 + 2 * (i % 2)) % lons) for i in range(lons)]
+    )
     got_lon_near = lax.ppermute(lon_near, "lon", swap(lons))
 
     moist_out, heat_out, keep, give = call(
@@ -377,7 +386,7 @@
     forward = lambda block, away: lax.ppermute(
         block, "sec", [(i, i ^ (2 * away)) for i in range(sections)]
     )
-    terms = [forward(term, flip) for flip, term in enumerate(terms, 1)]
+    terms = [forward(term, flip) for flip, term in zip(range(pairs - 1, 0, -1), terms)]
     rec_packed, hyd_packed = call(
         lambda *refs: first_body(aways[0], *refs),
         [shape((cap, steps), BF16)] * 2,
@@ -403,23 +412,22 @@
     )
     for away, block in zip(aways[1:], ready):
         arrived[away] = forward(block, away)
-    record_new, own = call(
-        rest_body,
-        [shape((reaches, steps), BF16), shape((cap, steps), BF16)],
-        order, kept, arrived[aways[0]],
-        out_specs=[HBM, VMEM],
-        scratch=[dma(())],
+    near, late = aways[0], aways[-1:]
+    record_new, theirs, mine = call(
+        lambda *refs: rest_body(near, *refs),
+        [shape((reaches, steps), BF16), shape((basins, steps), F32), shape((basins, steps), F32)],
+        order, kept, places, arrived[near],
+        out_specs=[HBM, VMEM, VMEM],
+        scratch=[pltpu.VMEM((cap, steps), BF16), dma(())],
         mib=16,
         flops=2 * cap * reaches * steps,
         moved=reaches * steps * 4,
     )
-    late = aways[-1:]
-    early = [0] + aways[:-1]
-    arrived[0] = own
+    early = [a for a in aways[:-1] if a != near]
     theirs, mine = call(
         lambda *refs: early_body(early, *refs),
         [shape((basins, steps), F32), shape((basins, steps), F32)],
-        places, *[arrived[a] for a in early],
+        theirs, mine, places, *[arrived[a] for a in early],
         mib=12,
         moved=basins * steps * 16,
     )

time: 50.4 us -> 50.4 us (level)
  the two profiles are of different devices: /device:TPU:5 before, /device:TPU:0 now
where the time goes in v5:
time: 50.4 us; the launch traced here: 50.2 us
  waiting for transfers between devices  21.7 us (43%)
  starting transfers between devices  16.1 us (32%)
  Pallas kernels  11.5 us (23%)
  between operations  0.76 us (2%)
    ppermute x6, waiting for transfers between devices, per_device(): lax.ppermute(block, 'sec', [(i, i ^ 2 * away) for i in range(sections)])  17.5 us
    pallas_call x12, Pallas kernels, call(): pl.pallas_call(body, out_shape=list(outs), in_specs=ins, out_specs=list(o...  11.5 us
    ppermute x6, starting transfers between devices, per_device(): lax.ppermute(block, 'sec', [(i, i ^ 2 * away) for i in range(sections)])  9.33 us
    ppermute x1, waiting for transfers between devices, per_device(): lax.ppermute(lon_far, 'lon', [(i, (i - 1 + 2 * (i % 2)) % lons) for i in...  2.92 us
    ppermute x1, starting transfers between devices, per_device(): got_lon_near = lax.ppermute(lon_near, 'lon', swap(lons))  2.58 us
    ppermute x1, starting transfers between devices, per_device(): got = lax.ppermute(give, 'sec', swap(sections))  1.51 us
    ppermute x1, starting transfers between devices, per_device(): lax.ppermute(lon_far, 'lon', [(i, (i - 1 + 2 * (i % 2)) % lons) for i in...  1.49 us
    ppermute x1, waiting for transfers between devices, per_device(): passed = lax.ppermute(theirs, 'sec', swap(sections))  1.21 us
  transfers between devices with their start and end apart: 12, of which 7 were waited for; matrix products, arithmetic and copies ran while one was open for 0% of the time, Pallas kernels for 14%

profile of v5, /device:TPU:0, one launch (start us, length us, event | category | flops | bytes accessed | tf_op | source)
XLA Modules:
  0.0 50.2 jit_solution(12459444787319608199)
XLA Ops:
  0.7 1.5 %shard_map.156 = (f32[16,16,256]{2,1,0:T(8,128)S(1)}, f32[16,16,256]{2,1,0:T(8,128)S(1)}, f32[16,16,256]{2,1,0:T(8,128)S(1)}, f32[16,16,256]{2,1,0:T(8,128)S(1)}...) custom-call(f32[16,16,256]{2,1,0:T(8,128)} %refs_0_.1, ...), custom_call_target="tpu_custom_call" | custom-call | bytes 524288 | tf_op jit(solution)/shard_map/pallas_call | solution.py:24
  2.2 0.5 %collective-permute-start = (bf16[32,256]{1,0:T(8,128)(2,1)S(1)}, bf16[32,256]{1,0:T(8,128)(2,1)S(1)}, u32[]{:S(2)}, u32[]{:S(2)}) collective-permute-start(bf16[32,256]{1,0:T(8,128)(2,1)S(1)} %get-tuple-element.48), channel_id=1, source_target_pairs={{0,1},{1,0},{2,3},{3,2},{4,5},{5,4},{6,7},{7,6},{8,9},{9,8},{10,11... | collective-permute-start | bytes 49160 | tf_op jit(solution)/shard_map/ppermute | solution.py:350
  2.7 0.7 %collective-permute-start.1 = (bf16[32,256]{1,0:T(8,128)(2,1)S(1)}, bf16[32,256]{1,0:T(8,128)(2,1)S(1)}, u32[]{:S(2)}, u32[]{:S(2)}) collective-permute-start(bf16[32,256]{1,0:T(8,128)(2,1)S(1)} %get-tuple-element.49), channel_id=1, source_target_pairs={{1,2},{3,4},{5,6},{2,1},{4,3},{6,5},{9,10},{11,12},{13,14},{10,9},... | collective-permute-start | bytes 49160 | tf_op jit(solution)/shard_map/ppermute | solution.py:349
  3.4 2.6 %collective-permute-start.2 = (bf16[16,128]{1,0:T(8,128)(2,1)S(1)}, bf16[16,128]{1,0:T(8,128)(2,1)S(1)}, u32[]{:S(2)}, u32[]{:S(2)}) collective-permute-start(bf16[16,128]{1,0:T(8,128)(2,1)S(1)} %get-tuple-element.50), channel_id=1, source_target_pairs={{0,8},{8,0},{16,24},{24,16},{1,9},{9,1},{17,25},{25,17},{2,10},{10... | collective-permute-start | bytes 12296 | tf_op jit(solution)/shard_map/ppermute | solution.py:354
  6.0 1.5 %collective-permute-start.3 = (bf16[16,128]{1,0:T(8,128)(2,1)S(1)}, bf16[16,128]{1,0:T(8,128)(2,1)S(1)}, u32[]{:S(2)}, u32[]{:S(2)}) collective-permute-start(bf16[16,128]{1,0:T(8,128)(2,1)S(1)} %get-tuple-element.51), channel_id=1, source_target_pairs={{0,24},{8,16},{16,8},{24,0},{1,25},{9,17},{17,9},{25,1},{2,26},{10... | collective-permute-start | bytes 12296 | tf_op jit(solution)/shard_map/ppermute | solution.py:351
  7.5 2.9 %collective-permute-done.3.lon_far = bf16[16,128]{1,0:T(8,128)(2,1)S(1)} collective-permute-done((bf16[16,128]{1,0:T(8,128)(2,1)S(1)}, bf16[16,128]{1,0:T(8,128)(2,1)S(1)}, u32[]{:S(2)}, u32[]{:S(2)}) %collective-permute-start.3) | collective-permute-done | bytes 4128 | tf_op jit(solution)/shard_map/ppermute | solution.py:351
  10.5 1.4 %shard_map.157 = (f32[16,16,256]{2,1,0:T(8,128)}, f32[16,16,256]{2,1,0:T(8,128)}, f32[4,16,128]{2,1,0:T(8,128)S(1)}, bf16[4,16,128]{2,1,0:T(8,128)(2,1)S(1)}) custom-call(f32[16,16,256]{2,1,0:T(8,128)S(1)} %get-tuple-element.41.moist, f32[16,16,256]{2,1,0:T(8,128)S(1)} %get-tuple-element.42.heat, f32[16,16,256]{2,1,0:T(8,128)S(1)} %get-tuple-element.43.moist_k, ...), custom_call_target="tpu_custom_call" | custom-call | bytes 1572864 | tf_op jit(solution)/shard_map/pallas_call | solution.py:24
  11.9 1.5 %collective-permute-start.4 = (bf16[4,16,128]{2,1,0:T(8,128)(2,1)S(1)}, bf16[4,16,128]{2,1,0:T(8,128)(2,1)S(1)}, u32[]{:S(2)}, u32[]{:S(2)}) collective-permute-start(bf16[4,16,128]{2,1,0:T(8,128)(2,1)S(1)} %get-tuple-element.59), channel_id=1, source_target_pairs={{0,1},{1,0},{2,3},{3,2},{4,5},{5,4},{6,7},{7,6},{8,9},{9,8},{10,11... | collective-permute-start | bytes 49160 | tf_op jit(solution)/shard_map/ppermute | solution.py:368
  13.4 0.9 %shard_map.158 = (s32[16,128]{1,0:T(8,128)S(1)}, bf16[4,16,128]{2,1,0:T(8,128)(2,1)S(1)}) custom-call(s32[8,512]{1,0:T(8,128)S(1)} %get-tuple-element.54.listed, s32[32,128]{1,0:T(8,128)S(1)} %get-tuple-element.55.home, s32[16,128]{1,0:T(8,128)S(1)} %get-tuple-element.56.down, s32[1,1,8]{2,1,0:T(1,128)} %count_in.1), custom_call_target="tpu_custom_call" | custom-call | bytes 524288 | tf_op jit(solution)/shard_map/pallas_call | solution.py:24
  14.4 4.2 %collective-permute-start.5 = (bf16[32,128]{1,0:T(8,128)(2,1)S(1)}, bf16[32,128]{1,0:T(8,128)(2,1)S(1)}, u32[]{:S(2)}, u32[]{:S(2)}) collective-permute-start(bf16[32,128]{1,0:T(8,128)(2,1)S(1)} %get-tuple-element.64), channel_id=1, source_target_pairs={{0,6},{1,7},{2,4},{3,5},{4,2},{5,3},{6,0},{7,1},{8,14},{9,15},{10,... | collective-permute-start | bytes 24584 | tf_op jit(solution)/shard_map/ppermute | solution.py:386
  18.5 0.6 %collective-permute-start.7 = (bf16[32,128]{1,0:T(8,128)(2,1)S(1)}, bf16[32,128]{1,0:T(8,128)(2,1)S(1)}, u32[]{:S(2)}, u32[]{:S(2)}) collective-permute-start(bf16[32,128]{1,0:T(8,128)(2,1)S(1)} %get-tuple-element.66), channel_id=1, source_target_pairs={{0,2},{1,3},{2,0},{3,1},{4,6},{5,7},{6,4},{7,5},{8,10},{9,11},{10,... | collective-permute-start | bytes 24584 | tf_op jit(solution)/shard_map/ppermute | solution.py:386
  19.2 1.4 %shard_map.160 = (bf16[512,256]{1,0:T(8,128)(2,1)S(1)}, bf16[512,256]{1,0:T(8,128)(2,1)S(1)}) custom-call(s32[16,128]{1,0:T(8,128)S(1)} %get-tuple-element.57.refs_0_.refs_1_.refs_3_, bf16[2048,256]{1,0:T(8,128)(2,1)S(1)} %bitcast.7, bf16[2048,256]{1,0:T(8,128)(2,1)S(1)} %bitcast.9), custom_call_target="tpu_custom_call" | custom-call | flops 1073741824 | bytes 2097152 | tf_op jit(solution)/shard_map/pallas_call | solution.py:24
  20.6 2.4 %collective-permute-done.6.refs_6_ = bf16[32,128]{1,0:T(8,128)(2,1)S(1)} collective-permute-done((bf16[32,128]{1,0:T(8,128)(2,1)S(1)}, bf16[32,128]{1,0:T(8,128)(2,1)S(1)}, u32[]{:S(2)}, u32[]{:S(2)}) %collective-permute-start.6) | collective-permute-done | bytes 8224 | tf_op jit(solution)/shard_map/ppermute | solution.py:386
  23.5 1.5 %collective-permute-start.8 = (bf16[512,256]{1,0:T(8,128)(2,1)S(1)}, bf16[512,256]{1,0:T(8,128)(2,1)S(1)}, u32[]{:S(2)}, u32[]{:S(2)}) collective-permute-start(bf16[512,256]{1,0:T(8,128)(2,1)S(1)} %get-tuple-element.70), channel_id=1, source_target_pairs={{0,6},{1,7},{2,4},{3,5},{4,2},{5,3},{6,0},{7,1},{8,14},{9,15},{10,... | collective-permute-start | bytes 786440 | tf_op jit(solution)/shard_map/ppermute | solution.py:386
  25.0 1.7 %shard_map.162 = (bf16[2048,256]{1,0:T(8,128)(2,1)S(1)}, bf16[512,256]{1,0:T(8,128)(2,1)S(1)}, bf16[512,256]{1,0:T(8,128)(2,1)S(1)}) custom-call(f32[16,128]{1,0:T(8,128)S(1)} %get-tuple-element.67.refs_0_, bf16[2048,256]{1,0:T(8,128)(2,1)S(1)} %bitcast.8, bf16[2048,256]{1,0:T(8,128)(2,1)S(1)} %bitcast.10, ...), custom_call_target="tpu_custom_call" | custom-call | flops 536870912 | bytes 4194304 | tf_op jit(solution)/shard_map/pallas_call | solution.py:24
  26.7 1.2 %collective-permute-start.9 = (bf16[512,256]{1,0:T(8,128)(2,1)S(1)}, bf16[512,256]{1,0:T(8,128)(2,1)S(1)}, u32[]{:S(2)}, u32[]{:S(2)}) collective-permute-start(bf16[512,256]{1,0:T(8,128)(2,1)S(1)} %get-tuple-element.74), channel_id=1, source_target_pairs={{0,2},{1,3},{2,0},{3,1},{4,6},{5,7},{6,4},{7,5},{8,10},{9,11},{10,... | collective-permute-start | bytes 786440 | tf_op jit(solution)/shard_map/ppermute | solution.py:386
  27.9 1.8 %collective-permute-start.10 = (bf16[512,256]{1,0:T(8,128)(2,1)S(1)}, bf16[512,256]{1,0:T(8,128)(2,1)S(1)}, u32[]{:S(2)}, u32[]{:S(2)}) collective-permute-start(bf16[512,256]{1,0:T(8,128)(2,1)S(1)} %get-tuple-element.76), channel_id=1, source_target_pairs={{0,4},{1,5},{2,6},{3,7},{4,0},{5,1},{6,2},{7,3},{8,12},{9,13},{10,... | collective-permute-start | bytes 786440 | tf_op jit(solution)/shard_map/ppermute | solution.py:386
  29.7 4.8 %collective-permute-done.8.refs_3_ = bf16[512,256]{1,0:T(8,128)(2,1)S(1)} collective-permute-done((bf16[512,256]{1,0:T(8,128)(2,1)S(1)}, bf16[512,256]{1,0:T(8,128)(2,1)S(1)}, u32[]{:S(2)}, u32[]{:S(2)}) %collective-permute-start.8) | collective-permute-done | bytes 262176 | tf_op jit(solution)/shard_map/ppermute | solution.py:386
  34.6 2.2 %shard_map.163 = (bf16[2048,256]{1,0:T(8,128)(2,1)}, f32[512,256]{1,0:T(8,128)S(1)}, f32[512,256]{1,0:T(8,128)S(1)}) custom-call(s32[16,128]{1,0:T(8,128)S(1)} %get-tuple-element.57.refs_0_.refs_1_.refs_3_, bf16[2048,256]{1,0:T(8,128)(2,1)S(1)} %get-tuple-element.68.refs_1_, bf16[4,16,128]{2,1,0:T(8,128)(2,1)S(1)} %get-tuple-element.69.refs_2_.refs_1_, ...), custom_call_target="tpu_custom_call" | custom-call | flops 536870912 | bytes 2097152 | tf_op jit(solution)/shard_map/pallas_call | solution.py:24
  36.8 3.3 %collective-permute-done.9.refs_3_ = bf16[512,256]{1,0:T(8,128)(2,1)S(1)} collective-permute-done((bf16[512,256]{1,0:T(8,128)(2,1)S(1)}, bf16[512,256]{1,0:T(8,128)(2,1)S(1)}, u32[]{:S(2)}, u32[]{:S(2)}) %collective-permute-start.9) | collective-permute-done | bytes 262176 | tf_op jit(solution)/shard_map/ppermute | solution.py:386
  40.1 0.4 shard_map.164
  40.5 6.9 %collective-permute-done.10.refs_2_ = bf16[512,256]{1,0:T(8,128)(2,1)S(1)} collective-permute-done((bf16[512,256]{1,0:T(8,128)(2,1)S(1)}, bf16[512,256]{1,0:T(8,128)(2,1)S(1)}, u32[]{:S(2)}, u32[]{:S(2)}) %collective-permute-start.10) | collective-permute-done | bytes 262176 | tf_op jit(solution)/shard_map/ppermute | solution.py:386
  48.1 1.2 %collective-permute-done.11.passed = bf16[512,256]{1,0:T(8,128)(2,1)S(1)} collective-permute-done((bf16[512,256]{1,0:T(8,128)(2,1)S(1)}, bf16[512,256]{1,0:T(8,128)(2,1)S(1)}, u32[]{:S(2)}, u32[]{:S(2)}) %collective-permute-start.11) | collective-permute-done | bytes 262176 | tf_op jit(solution)/shard_map/ppermute | solution.py:440
  49.4 0.8 %shard_map.167 = f32[512,256]{1,0:T(8,128)} custom-call(f32[512,256]{1,0:T(8,128)S(1)} %shard_map.165.mine, bf16[512,256]{1,0:T(8,128)(2,1)S(1)} %collective-permute-done.11.passed), custom_call_target="tpu_custom_call" | custom-call | bytes 1310720 | tf_op jit(solution)/shard_map/pallas_call | solution.py:24
  (16 shorter events, 1.2 us)
Async XLA Ops:
  0.6 18.5 %copy-start = (bf16[1,2048,256]{2,1,0:T(8,128)(2,1)S(1)}, bf16[1,2048,256]{2,1,0:T(8,128)(2,1)}, u32[]{:S(2)}) copy-start(bf16[1,2048,256]{2,1,0:T(8,128)(2,1)} %param.20) | copy-start | bytes 3145732
  0.6 18.5 %copy-start.1 = (bf16[1,2048,256]{2,1,0:T(8,128)(2,1)S(1)}, bf16[1,2048,256]{2,1,0:T(8,128)(2,1)}, u32[]{:S(2)}) copy-start(bf16[1,2048,256]{2,1,0:T(8,128)(2,1)} %param.21) | copy-start | bytes 3145732
  2.2 8.3 %collective-permute-start = (bf16[32,256]{1,0:T(8,128)(2,1)S(1)}, bf16[32,256]{1,0:T(8,128)(2,1)S(1)}, u32[]{:S(2)}, u32[]{:S(2)}) collective-permute-start(bf16[32,256]{1,0:T(8,128)(2,1)S(1)} %get-tuple-element.48), channel_id=1, source_target_pairs={{0,1},{1,0},{2,3},{3,2},{4,5},{5,4},{6,7},{7,6},{8,9},{9,8},{10,11... | collective-permute-start | bytes 49160 | tf_op jit(solution)/shard_map/ppermute | solution.py:350
  2.7 7.7 %collective-permute-start.1 = (bf16[32,256]{1,0:T(8,128)(2,1)S(1)}, bf16[32,256]{1,0:T(8,128)(2,1)S(1)}, u32[]{:S(2)}, u32[]{:S(2)}) collective-permute-start(bf16[32,256]{1,0:T(8,128)(2,1)S(1)} %get-tuple-element.49), channel_id=1, source_target_pairs={{1,2},{3,4},{5,6},{2,1},{4,3},{6,5},{9,10},{11,12},{13,14},{10,9},... | collective-permute-start | bytes 49160 | tf_op jit(solution)/shard_map/ppermute | solution.py:349
  3.4 4.2 %collective-permute-start.2 = (bf16[16,128]{1,0:T(8,128)(2,1)S(1)}, bf16[16,128]{1,0:T(8,128)(2,1)S(1)}, u32[]{:S(2)}, u32[]{:S(2)}) collective-permute-start(bf16[16,128]{1,0:T(8,128)(2,1)S(1)} %get-tuple-element.50), channel_id=1, source_target_pairs={{0,8},{8,0},{16,24},{24,16},{1,9},{9,1},{17,25},{25,17},{2,10},{10... | collective-permute-start | bytes 12296 | tf_op jit(solution)/shard_map/ppermute | solution.py:354
  6.0 4.5 %collective-permute-start.3 = (bf16[16,128]{1,0:T(8,128)(2,1)S(1)}, bf16[16,128]{1,0:T(8,128)(2,1)S(1)}, u32[]{:S(2)}, u32[]{:S(2)}) collective-permute-start(bf16[16,128]{1,0:T(8,128)(2,1)S(1)} %get-tuple-element.51), channel_id=1, source_target_pairs={{0,24},{8,16},{16,8},{24,0},{1,25},{9,17},{17,9},{25,1},{2,26},{10... | collective-permute-start | bytes 12296 | tf_op jit(solution)/shard_map/ppermute | solution.py:351
  11.9 2.4 %collective-permute-start.4 = (bf16[4,16,128]{2,1,0:T(8,128)(2,1)S(1)}, bf16[4,16,128]{2,1,0:T(8,128)(2,1)S(1)}, u32[]{:S(2)}, u32[]{:S(2)}) collective-permute-start(bf16[4,16,128]{2,1,0:T(8,128)(2,1)S(1)} %get-tuple-element.59), channel_id=1, source_target_pairs={{0,1},{1,0},{2,3},{3,2},{4,5},{5,4},{6,7},{7,6},{8,9},{9,8},{10,11... | collective-permute-start | bytes 49160 | tf_op jit(solution)/shard_map/ppermute | solution.py:368
  14.4 6.3 %collective-permute-start.5 = (bf16[32,128]{1,0:T(8,128)(2,1)S(1)}, bf16[32,128]{1,0:T(8,128)(2,1)S(1)}, u32[]{:S(2)}, u32[]{:S(2)}) collective-permute-start(bf16[32,128]{1,0:T(8,128)(2,1)S(1)} %get-tuple-element.64), channel_id=1, source_target_pairs={{0,6},{1,7},{2,4},{3,5},{4,2},{5,3},{6,0},{7,1},{8,14},{9,15},{10,... | collective-permute-start | bytes 24584 | tf_op jit(solution)/shard_map/ppermute | solution.py:386
  18.5 4.5 %collective-permute-start.6 = (bf16[32,128]{1,0:T(8,128)(2,1)S(1)}, bf16[32,128]{1,0:T(8,128)(2,1)S(1)}, u32[]{:S(2)}, u32[]{:S(2)}) collective-permute-start(bf16[32,128]{1,0:T(8,128)(2,1)S(1)} %get-tuple-element.65), channel_id=1, source_target_pairs={{0,4},{1,5},{2,6},{3,7},{4,0},{5,1},{6,2},{7,3},{8,12},{9,13},{10,... | collective-permute-start | bytes 24584 | tf_op jit(solution)/shard_map/ppermute | solution.py:386
  18.5 4.5 %collective-permute-start.7 = (bf16[32,128]{1,0:T(8,128)(2,1)S(1)}, bf16[32,128]{1,0:T(8,128)(2,1)S(1)}, u32[]{:S(2)}, u32[]{:S(2)}) collective-permute-start(bf16[32,128]{1,0:T(8,128)(2,1)S(1)} %get-tuple-element.66), channel_id=1, source_target_pairs={{0,2},{1,3},{2,0},{3,1},{4,6},{5,7},{6,4},{7,5},{8,10},{9,11},{10,... | collective-permute-start | bytes 24584 | tf_op jit(solution)/shard_map/ppermute | solution.py:386
  23.5 11.1 %collective-permute-start.8 = (bf16[512,256]{1,0:T(8,128)(2,1)S(1)}, bf16[512,256]{1,0:T(8,128)(2,1)S(1)}, u32[]{:S(2)}, u32[]{:S(2)}) collective-permute-start(bf16[512,256]{1,0:T(8,128)(2,1)S(1)} %get-tuple-element.70), channel_id=1, source_target_pairs={{0,6},{1,7},{2,4},{3,5},{4,2},{5,3},{6,0},{7,1},{8,14},{9,15},{10,... | collective-permute-start | bytes 786440 | tf_op jit(solution)/shard_map/ppermute | solution.py:386
  26.7 13.3 %collective-permute-start.9 = (bf16[512,256]{1,0:T(8,128)(2,1)S(1)}, bf16[512,256]{1,0:T(8,128)(2,1)S(1)}, u32[]{:S(2)}, u32[]{:S(2)}) collective-permute-start(bf16[512,256]{1,0:T(8,128)(2,1)S(1)} %get-tuple-element.74), channel_id=1, source_target_pairs={{0,2},{1,3},{2,0},{3,1},{4,6},{5,7},{6,4},{7,5},{8,10},{9,11},{10,... | collective-permute-start | bytes 786440 | tf_op jit(solution)/shard_map/ppermute | solution.py:386
  27.9 19.5 %collective-permute-start.10 = (bf16[512,256]{1,0:T(8,128)(2,1)S(1)}, bf16[512,256]{1,0:T(8,128)(2,1)S(1)}, u32[]{:S(2)}, u32[]{:S(2)}) collective-permute-start(bf16[512,256]{1,0:T(8,128)(2,1)S(1)} %get-tuple-element.76), channel_id=1, source_target_pairs={{0,4},{1,5},{2,6},{3,7},{4,0},{5,1},{6,2},{7,3},{8,12},{9,13},{10,... | collective-permute-start | bytes 786440 | tf_op jit(solution)/shard_map/ppermute | solution.py:386
  47.8 1.6 %collective-permute-start.11 = (bf16[512,256]{1,0:T(8,128)(2,1)S(1)}, bf16[512,256]{1,0:T(8,128)(2,1)S(1)}, u32[]{:S(2)}, u32[]{:S(2)}) collective-permute-start(bf16[512,256]{1,0:T(8,128)(2,1)S(1)} %shard_map.166), channel_id=1, source_target_pairs={{0,1},{1,0},{2,3},{3,2},{4,5},{5,4},{6,7},{7,6},{8,9},{9,8},{10,11... | collective-permute-start | bytes 786440 | tf_op jit(solution)/shard_map/ppermute | solution.py:440

commit v6 on v5

--- a/solution.py
+++ b/solution.py
@@ -142,11 +142,13 @@
     col = lax.broadcasted_iota(I32, (rows, cols), 1)
     sec_even = parity("sec") == 0
     lon_even = parity("lon") == 0
-    south_all = jnp.where(sec_even, sec_near[...].astype(F32), sec_far[...].astype(F32))
-    north_all = jnp.where(sec_even, sec_far[...].astype(F32), sec_near[...].astype(F32))
-    lon = lax.axis_index("lon")
-    outer = (lon == 0) | (lon == lax.axis_size("lon") - 1)
-    lon_beyond = jnp.where(outer, 0.0, lon_far[...].astype(F32))
+    outer = lambda axis: (lax.axis_index(axis) == 0) | (
+        lax.axis_index(axis) == lax.axis_size(axis) - 1
+    )
+    sec_beyond = jnp.where(outer("sec"), 0.0, sec_far[...].astype(F32))
+    lon_beyond = jnp.where(outer("lon"), 0.0, lon_far[...].astype(F32))
+    south_all = jnp.where(sec_even, sec_near[...].astype(F32), sec_beyond)
+    north_all = jnp.where(sec_even, sec_beyond, sec_near[...].astype(F32))
     east_all = jnp.where(lon_even, lon_near[...].astype(F32), lon_beyond)
     west_all = jnp.where(lon_even, lon_beyond, lon_near[...].astype(F32))
     for f, (x_ref, k_ref, top, out) in enumerate(
@@ -233,16 +235,23 @@
         ).astype(BF16)
 
 
-def record_body(aways, runoff, records, hydro, order, kept, *ready):
+def record_body(aways, runoff, records, hydro, order, places, out, theirs, mine, *refs):
+    ready, (kept, own, sem) = refs[:-3], refs[-3:]
     turned = runoff[...].T
     for t in range(runoff.shape[0]):
         rows = pl.ds(t * LANES, LANES)
         kept[rows, :] = (
             shift_time(records[rows, :].astype(F32)) + turned[:, t : t + 1] * hydro[rows, :].astype(F32)
         ).astype(BF16)
-    for away, out in zip(aways, ready):
-        hot = picked(order, away, out.shape[0] // LANES, kept.shape[0])
-        out[...] = jnp.dot(hot, kept[...], preferred_element_type=F32).astype(BF16)
+    copy = pltpu.make_async_copy(kept, out, sem)
+    copy.start()
+    for away, block in zip(aways + [0], list(ready) + [own]):
+        hot = picked(order, away, block.shape[0] // LANES, kept.shape[0])
+        block[...] = jnp.dot(hot, kept[...], preferred_element_type=F32).astype(BF16)
+    digits = [places[0].astype(F32)]
+    theirs[...] = summed(digits, [own], mine.shape[0], True)
+    mine[...] = summed(digits, [own], mine.shape[0], False)
+    copy.wait()
 
 
 def hot_of(digits, tiles, basins, other):
@@ -263,18 +272,6 @@
         part = jnp.dot(hot, block[...], preferred_element_type=F32)
         total = part if total is None else total + part
     return total
-
-
-def rest_body(near, order, kept, places, landed, out, theirs, mine, own, sem):
-    copy = pltpu.make_async_copy(kept, out, sem)
-    copy.start()
-    hot = picked(order, 0, own.shape[0] // LANES, kept.shape[0])
-    own[...] = jnp.dot(hot, kept[...], preferred_element_type=F32).astype(BF16)
-    digits = [places[away].astype(F32) for away in (0, near)]
-    basins = mine.shape[0]
-    theirs[...] = summed(digits, [own, landed], basins, True)
-    mine[...] = summed(digits, [own, landed], basins, False)
-    copy.wait()
 
 
 def early_body(aways, theirs_so_far, mine_so_far, places, *refs):
@@ -343,14 +340,12 @@
     )
     *land, home_v, down_v, listed_v = fetched
     swap = lambda count: [(i, i ^ 1) for i in range(count)]
-    between = lambda count: [(i, i + 1) for i in range(1, count - 1, 2)] + [
-        (i + 1, i) for i in range(1, count - 1, 2)
+    between = lambda count: [
+        (i, j if 0 <= j < count else i) for i, j in ((i, i - 1 + 2 * (i % 2)) for i in range(count))
     ]
     got_sec_far = lax.ppermute(sec_far, "sec", between(sections))
     got_sec_near = lax.ppermute(sec_near, "sec", swap(sections))
-    got_lon_far = lax.ppermute(
-        lon_far, "lon", [(i, (i - 1 + 2 * (i % 2)) % lons) for i in range(lons)]
-    )
+    got_lon_far = lax.ppermute(lon_far, "lon", between(lons))
     got_lon_near = lax.ppermute(lon_near, "lon", swap(lons))
 
     moist_out, heat_out, keep, give = call(
@@ -402,28 +397,20 @@
         moved=cap * steps * 6,
     )
     arrived = {aways[0]: forward(ready, aways[0])}
-    kept, *ready = call(
+    record_new, theirs, mine, *ready = call(
         lambda *refs: record_body(aways[1:], *refs),
-        [shape((reaches, steps), BF16)] + [shape((cap, steps), BF16)] * (len(aways) - 1),
-        runoff, records[0], unit_hydro[0], order,
+        [shape((reaches, steps), BF16), shape((basins, steps), F32), shape((basins, steps), F32)]
+        + [shape((cap, steps), BF16)] * (len(aways) - 1),
+        runoff, records[0], unit_hydro[0], order, places,
+        out_specs=[HBM] + [VMEM] * (len(aways) + 1),
+        scratch=[pltpu.VMEM((reaches, steps), BF16), pltpu.VMEM((cap, steps), BF16), dma(())],
         mib=16,
         flops=2 * cap * reaches * steps,
         moved=reaches * steps * 8,
     )
     for away, block in zip(aways[1:], ready):
         arrived[away] = forward(block, away)
-    near, late = aways[0], aways[-1:]
-    record_new, theirs, mine = call(
-        lambda *refs: rest_body(near, *refs),
-        [shape((reaches, steps), BF16), shape((basins, steps), F32), shape((basins, steps), F32)],
-        order, kept, places, arrived[near],
-        out_specs=[HBM, VMEM, VMEM],
-        scratch=[pltpu.VMEM((cap, steps), BF16), dma(())],
-        mib=16,
-        flops=2 * cap * reaches * steps,
-        moved=reaches * steps * 4,
-    )
-    early = [a for a in aways[:-1] if a != near]
+    early, late = aways[:1], aways[1:]
     theirs, mine = call(
         lambda *refs: early_body(early, *refs),
         [shape((basins, steps), F32), shape((basins, steps), F32)],

time: 50.4 us -> 51.2 us (1.016)
  the two profiles are of different devices: /device:TPU:0 before, /device:TPU:5 now
where the time goes in v6:
time: 51.2 us; the launch traced here: 51.1 us
  waiting for transfers between devices  21.7 us (42%)
  starting transfers between devices  17.7 us (35%)
  Pallas kernels  11 us (21%)
  between operations  0.75 us (1%)
    ppermute x6, waiting for transfers between devices, per_device(): lax.ppermute(block, 'sec', [(i, i ^ 2 * away) for i in range(sections)])  17.6 us
    pallas_call x11, Pallas kernels, call(): pl.pallas_call(body, out_shape=list(outs), in_specs=ins, out_specs=list(o...  11 us
    ppermute x6, starting transfers between devices, per_device(): lax.ppermute(block, 'sec', [(i, i ^ 2 * away) for i in range(sections)])  7.99 us
    ppermute x1, waiting for transfers between devices, per_device(): got_lon_far = lax.ppermute(lon_far, 'lon', between(lons))  3.13 us
    ppermute x1, starting transfers between devices, per_device(): got_sec_far = lax.ppermute(sec_far, 'sec', between(sections))  3.1 us
    ppermute x1, starting transfers between devices, per_device(): passed = lax.ppermute(theirs, 'sec', swap(sections))  2.46 us
    ppermute x1, starting transfers between devices, per_device(): got_lon_far = lax.ppermute(lon_far, 'lon', between(lons))  2.09 us
    ppermute x1, starting transfers between devices, per_device(): got_lon_near = lax.ppermute(lon_near, 'lon', swap(lons))  1.28 us
  transfers between devices with their start and end apart: 12, of which 7 were waited for; matrix products, arithmetic and copies ran while one was open for 0% of the time, Pallas kernels for 12%

profile of v6, /device:TPU:5, one launch (start us, length us, event | category | flops | bytes accessed | tf_op | source)
XLA Modules:
  0.0 51.1 jit_solution(10709936642617900289)
XLA Ops:
  0.7 1.5 %shard_map.156 = (f32[16,16,256]{2,1,0:T(8,128)S(1)}, f32[16,16,256]{2,1,0:T(8,128)S(1)}, f32[16,16,256]{2,1,0:T(8,128)S(1)}, f32[16,16,256]{2,1,0:T(8,128)S(1)}...) custom-call(f32[16,16,256]{2,1,0:T(8,128)} %refs_0_.1, ...), custom_call_target="tpu_custom_call" | custom-call | bytes 524288 | tf_op jit(solution)/shard_map/pallas_call | solution.py:24
  2.2 0.7 %collective-permute-start = (bf16[32,256]{1,0:T(8,128)(2,1)S(1)}, bf16[32,256]{1,0:T(8,128)(2,1)S(1)}, u32[]{:S(2)}, u32[]{:S(2)}) collective-permute-start(bf16[32,256]{1,0:T(8,128)(2,1)S(1)} %get-tuple-element.47), channel_id=1, source_target_pairs={{0,1},{1,0},{2,3},{3,2},{4,5},{5,4},{6,7},{7,6},{8,9},{9,8},{10,11... | collective-permute-start | bytes 49160 | tf_op jit(solution)/shard_map/ppermute | solution.py:347
  2.9 3.1 %collective-permute-start.1 = (bf16[32,256]{1,0:T(8,128)(2,1)S(1)}, bf16[32,256]{1,0:T(8,128)(2,1)S(1)}, u32[]{:S(2)}, u32[]{:S(2)}) collective-permute-start(bf16[32,256]{1,0:T(8,128)(2,1)S(1)} %get-tuple-element.48), channel_id=1, source_target_pairs={{0,0},{1,2},{2,1},{3,4},{4,3},{5,6},{6,5},{7,7},{8,8},{9,10},{10,9... | collective-permute-start | bytes 49160 | tf_op jit(solution)/shard_map/ppermute | solution.py:346
  6.1 1.3 %collective-permute-start.2 = (bf16[16,128]{1,0:T(8,128)(2,1)S(1)}, bf16[16,128]{1,0:T(8,128)(2,1)S(1)}, u32[]{:S(2)}, u32[]{:S(2)}) collective-permute-start(bf16[16,128]{1,0:T(8,128)(2,1)S(1)} %get-tuple-element.49), channel_id=1, source_target_pairs={{0,8},{8,0},{16,24},{24,16},{1,9},{9,1},{17,25},{25,17},{2,10},{10... | collective-permute-start | bytes 12296 | tf_op jit(solution)/shard_map/ppermute | solution.py:349
  7.3 2.1 %collective-permute-start.3 = (bf16[16,128]{1,0:T(8,128)(2,1)S(1)}, bf16[16,128]{1,0:T(8,128)(2,1)S(1)}, u32[]{:S(2)}, u32[]{:S(2)}) collective-permute-start(bf16[16,128]{1,0:T(8,128)(2,1)S(1)} %get-tuple-element.50), channel_id=1, source_target_pairs={{0,0},{8,16},{16,8},{24,24},{1,1},{9,17},{17,9},{25,25},{2,2},{10,... | collective-permute-start | bytes 12296 | tf_op jit(solution)/shard_map/ppermute | solution.py:348
  9.4 3.1 %collective-permute-done.3.lon_far = bf16[16,128]{1,0:T(8,128)(2,1)S(1)} collective-permute-done((bf16[16,128]{1,0:T(8,128)(2,1)S(1)}, bf16[16,128]{1,0:T(8,128)(2,1)S(1)}, u32[]{:S(2)}, u32[]{:S(2)}) %collective-permute-start.3) | collective-permute-done | bytes 4128 | tf_op jit(solution)/shard_map/ppermute | solution.py:348
  12.6 1.4 %shard_map.157 = (f32[16,16,256]{2,1,0:T(8,128)}, f32[16,16,256]{2,1,0:T(8,128)}, f32[4,16,128]{2,1,0:T(8,128)S(1)}, bf16[4,16,128]{2,1,0:T(8,128)(2,1)S(1)}) custom-call(f32[16,16,256]{2,1,0:T(8,128)S(1)} %get-tuple-element.40.moist, f32[16,16,256]{2,1,0:T(8,128)S(1)} %get-tuple-element.41.heat, f32[16,16,256]{2,1,0:T(8,128)S(1)} %get-tuple-element.42.moist_k, ...), custom_call_target="tpu_custom_call" | custom-call | bytes 1572864 | tf_op jit(solution)/shard_map/pallas_call | solution.py:24
  14.0 0.9 %shard_map.158 = (s32[16,128]{1,0:T(8,128)S(1)}, bf16[4,16,128]{2,1,0:T(8,128)(2,1)S(1)}) custom-call(s32[8,512]{1,0:T(8,128)S(1)} %get-tuple-element.55.listed, s32[32,128]{1,0:T(8,128)S(1)} %get-tuple-element.56.home, s32[16,128]{1,0:T(8,128)S(1)} %get-tuple-element.57.down, s32[1,1,8]{2,1,0:T(1,128)} %count_in.1), custom_call_target="tpu_custom_call" | custom-call | bytes 524288 | tf_op jit(solution)/shard_map/pallas_call | solution.py:24
  15.2 3.9 %collective-permute-start.5 = (bf16[32,128]{1,0:T(8,128)(2,1)S(1)}, bf16[32,128]{1,0:T(8,128)(2,1)S(1)}, u32[]{:S(2)}, u32[]{:S(2)}) collective-permute-start(bf16[32,128]{1,0:T(8,128)(2,1)S(1)} %get-tuple-element.63), channel_id=1, source_target_pairs={{0,6},{1,7},{2,4},{3,5},{4,2},{5,3},{6,0},{7,1},{8,14},{9,15},{10,... | collective-permute-start | bytes 24584 | tf_op jit(solution)/shard_map/ppermute | solution.py:381
  19.5 1.4 %shard_map.160 = (bf16[512,256]{1,0:T(8,128)(2,1)S(1)}, bf16[512,256]{1,0:T(8,128)(2,1)S(1)}) custom-call(s32[16,128]{1,0:T(8,128)S(1)} %get-tuple-element.60.refs_0_.refs_1_.refs_3_, bf16[2048,256]{1,0:T(8,128)(2,1)S(1)} %bitcast.7, bf16[2048,256]{1,0:T(8,128)(2,1)S(1)} %bitcast.9), custom_call_target="tpu_custom_call" | custom-call | flops 1073741824 | bytes 2097152 | tf_op jit(solution)/shard_map/pallas_call | solution.py:24
  21.0 1.6 %collective-permute-done.6.refs_6_ = bf16[32,128]{1,0:T(8,128)(2,1)S(1)} collective-permute-done((bf16[32,128]{1,0:T(8,128)(2,1)S(1)}, bf16[32,128]{1,0:T(8,128)(2,1)S(1)}, u32[]{:S(2)}, u32[]{:S(2)}) %collective-permute-start.6) | collective-permute-done | bytes 8224 | tf_op jit(solution)/shard_map/ppermute | solution.py:381
  22.6 0.4 shard_map.161
  23.0 1.7 %collective-permute-start.8 = (bf16[512,256]{1,0:T(8,128)(2,1)S(1)}, bf16[512,256]{1,0:T(8,128)(2,1)S(1)}, u32[]{:S(2)}, u32[]{:S(2)}) collective-permute-start(bf16[512,256]{1,0:T(8,128)(2,1)S(1)} %get-tuple-element.71), channel_id=1, source_target_pairs={{0,6},{1,7},{2,4},{3,5},{4,2},{5,3},{6,0},{7,1},{8,14},{9,15},{10,... | collective-permute-start | bytes 786440 | tf_op jit(solution)/shard_map/ppermute | solution.py:381
  24.6 3.1 %shard_map.162 = (bf16[2048,256]{1,0:T(8,128)(2,1)}, f32[512,256]{1,0:T(8,128)S(1)}, f32[512,256]{1,0:T(8,128)S(1)}, bf16[512,256]{1,0:T(8,128)(2,1)S(1)}, bf16[512,256]{1,0:T(8,128)(2,1)S(1)}) custom-call(f32[16,128]{1,0:T(8,128)S(1)} %get-tuple-element.66.refs_0_, bf16[2048,256]{1,0:T(8,128)(2,1)S(1)} %bitcast.8, bf16[2048,256]{1,0:T(8,128)(2,1)S(1)} %bitcast.10, ...), custom_call_target="tpu_custom_call" | custom-call | flops 536870912 | bytes 4194304 | tf_op jit(solution)/shard_map/pallas_call | solution.py:24
  27.9 1.8 %collective-permute-start.10 = (bf16[512,256]{1,0:T(8,128)(2,1)S(1)}, bf16[512,256]{1,0:T(8,128)(2,1)S(1)}, u32[]{:S(2)}, u32[]{:S(2)}) collective-permute-start(bf16[512,256]{1,0:T(8,128)(2,1)S(1)} %get-tuple-element.74), channel_id=1, source_target_pairs={{0,4},{1,5},{2,6},{3,7},{4,0},{5,1},{6,2},{7,3},{8,12},{9,13},{10,... | collective-permute-start | bytes 786440 | tf_op jit(solution)/shard_map/ppermute | solution.py:381
  29.8 1.3 %collective-permute-done.8.refs_3_ = bf16[512,256]{1,0:T(8,128)(2,1)S(1)} collective-permute-done((bf16[512,256]{1,0:T(8,128)(2,1)S(1)}, bf16[512,256]{1,0:T(8,128)(2,1)S(1)}, u32[]{:S(2)}, u32[]{:S(2)}) %collective-permute-start.8) | collective-permute-done | bytes 262176 | tf_op jit(solution)/shard_map/ppermute | solution.py:381
  31.1 0.4 shard_map.163
  31.5 8.3 %collective-permute-done.9.refs_2_ = bf16[512,256]{1,0:T(8,128)(2,1)S(1)} collective-permute-done((bf16[512,256]{1,0:T(8,128)(2,1)S(1)}, bf16[512,256]{1,0:T(8,128)(2,1)S(1)}, u32[]{:S(2)}, u32[]{:S(2)}) %collective-permute-start.9) | collective-permute-done | bytes 262176 | tf_op jit(solution)/shard_map/ppermute | solution.py:381
  39.9 6.3 %collective-permute-done.10.refs_3_ = bf16[512,256]{1,0:T(8,128)(2,1)S(1)} collective-permute-done((bf16[512,256]{1,0:T(8,128)(2,1)S(1)}, bf16[512,256]{1,0:T(8,128)(2,1)S(1)}, u32[]{:S(2)}, u32[]{:S(2)}) %collective-permute-start.10) | collective-permute-done | bytes 262176 | tf_op jit(solution)/shard_map/ppermute | solution.py:381
  46.2 0.4 shard_map.165
  46.6 2.5 %collective-permute-start.11 = (bf16[512,256]{1,0:T(8,128)(2,1)S(1)}, bf16[512,256]{1,0:T(8,128)(2,1)S(1)}, u32[]{:S(2)}, u32[]{:S(2)}) collective-permute-start(bf16[512,256]{1,0:T(8,128)(2,1)S(1)} %shard_map.165), channel_id=1, source_target_pairs={{0,1},{1,0},{2,3},{3,2},{4,5},{5,4},{6,7},{7,6},{8,9},{9,8},{10,11... | collective-permute-start | bytes 786440 | tf_op jit(solution)/shard_map/ppermute | solution.py:427
  49.1 0.4 shard_map.164.mine
  49.5 0.7 %collective-permute-done.11.passed = bf16[512,256]{1,0:T(8,128)(2,1)S(1)} collective-permute-done((bf16[512,256]{1,0:T(8,128)(2,1)S(1)}, bf16[512,256]{1,0:T(8,128)(2,1)S(1)}, u32[]{:S(2)}, u32[]{:S(2)}) %collective-permute-start.11) | collective-permute-done | bytes 262176 | tf_op jit(solution)/shard_map/ppermute | solution.py:427
  50.2 0.8 %shard_map.166 = f32[512,256]{1,0:T(8,128)} custom-call(f32[512,256]{1,0:T(8,128)S(1)} %shard_map.164.mine, bf16[512,256]{1,0:T(8,128)(2,1)S(1)} %collective-permute-done.11.passed), custom_call_target="tpu_custom_call" | custom-call | bytes 1310720 | tf_op jit(solution)/shard_map/pallas_call | solution.py:24
  (15 shorter events, 0.8 us)
Async XLA Ops:
  0.6 18.9 %copy-start = (bf16[1,2048,256]{2,1,0:T(8,128)(2,1)S(1)}, bf16[1,2048,256]{2,1,0:T(8,128)(2,1)}, u32[]{:S(2)}) copy-start(bf16[1,2048,256]{2,1,0:T(8,128)(2,1)} %param.20) | copy-start | bytes 3145732
  0.6 18.9 %copy-start.1 = (bf16[1,2048,256]{2,1,0:T(8,128)(2,1)S(1)}, bf16[1,2048,256]{2,1,0:T(8,128)(2,1)}, u32[]{:S(2)}) copy-start(bf16[1,2048,256]{2,1,0:T(8,128)(2,1)} %param.21) | copy-start | bytes 3145732
  2.2 10.4 %collective-permute-start = (bf16[32,256]{1,0:T(8,128)(2,1)S(1)}, bf16[32,256]{1,0:T(8,128)(2,1)S(1)}, u32[]{:S(2)}, u32[]{:S(2)}) collective-permute-start(bf16[32,256]{1,0:T(8,128)(2,1)S(1)} %get-tuple-element.47), channel_id=1, source_target_pairs={{0,1},{1,0},{2,3},{3,2},{4,5},{5,4},{6,7},{7,6},{8,9},{9,8},{10,11... | collective-permute-start | bytes 49160 | tf_op jit(solution)/shard_map/ppermute | solution.py:347
  2.9 9.6 %collective-permute-start.1 = (bf16[32,256]{1,0:T(8,128)(2,1)S(1)}, bf16[32,256]{1,0:T(8,128)(2,1)S(1)}, u32[]{:S(2)}, u32[]{:S(2)}) collective-permute-start(bf16[32,256]{1,0:T(8,128)(2,1)S(1)} %get-tuple-element.48), channel_id=1, source_target_pairs={{0,0},{1,2},{2,1},{3,4},{4,3},{5,6},{6,5},{7,7},{8,8},{9,10},{10,9... | collective-permute-start | bytes 49160 | tf_op jit(solution)/shard_map/ppermute | solution.py:346
  6.1 3.4 %collective-permute-start.2 = (bf16[16,128]{1,0:T(8,128)(2,1)S(1)}, bf16[16,128]{1,0:T(8,128)(2,1)S(1)}, u32[]{:S(2)}, u32[]{:S(2)}) collective-permute-start(bf16[16,128]{1,0:T(8,128)(2,1)S(1)} %get-tuple-element.49), channel_id=1, source_target_pairs={{0,8},{8,0},{16,24},{24,16},{1,9},{9,1},{17,25},{25,17},{2,10},{10... | collective-permute-start | bytes 12296 | tf_op jit(solution)/shard_map/ppermute | solution.py:349
  7.3 5.2 %collective-permute-start.3 = (bf16[16,128]{1,0:T(8,128)(2,1)S(1)}, bf16[16,128]{1,0:T(8,128)(2,1)S(1)}, u32[]{:S(2)}, u32[]{:S(2)}) collective-permute-start(bf16[16,128]{1,0:T(8,128)(2,1)S(1)} %get-tuple-element.50), channel_id=1, source_target_pairs={{0,0},{8,16},{16,8},{24,24},{1,1},{9,17},{17,9},{25,25},{2,2},{10,... | collective-permute-start | bytes 12296 | tf_op jit(solution)/shard_map/ppermute | solution.py:348
  14.0 1.2 %collective-permute-start.4 = (bf16[4,16,128]{2,1,0:T(8,128)(2,1)S(1)}, bf16[4,16,128]{2,1,0:T(8,128)(2,1)S(1)}, u32[]{:S(2)}, u32[]{:S(2)}) collective-permute-start(bf16[4,16,128]{2,1,0:T(8,128)(2,1)S(1)} %get-tuple-element.54), channel_id=1, source_target_pairs={{0,1},{1,0},{2,3},{3,2},{4,5},{5,4},{6,7},{7,6},{8,9},{9,8},{10,11... | collective-permute-start | bytes 49160 | tf_op jit(solution)/shard_map/ppermute | solution.py:363
  15.2 5.8 %collective-permute-start.5 = (bf16[32,128]{1,0:T(8,128)(2,1)S(1)}, bf16[32,128]{1,0:T(8,128)(2,1)S(1)}, u32[]{:S(2)}, u32[]{:S(2)}) collective-permute-start(bf16[32,128]{1,0:T(8,128)(2,1)S(1)} %get-tuple-element.63), channel_id=1, source_target_pairs={{0,6},{1,7},{2,4},{3,5},{4,2},{5,3},{6,0},{7,1},{8,14},{9,15},{10,... | collective-permute-start | bytes 24584 | tf_op jit(solution)/shard_map/ppermute | solution.py:381
  19.1 3.4 %collective-permute-start.6 = (bf16[32,128]{1,0:T(8,128)(2,1)S(1)}, bf16[32,128]{1,0:T(8,128)(2,1)S(1)}, u32[]{:S(2)}, u32[]{:S(2)}) collective-permute-start(bf16[32,128]{1,0:T(8,128)(2,1)S(1)} %get-tuple-element.64), channel_id=1, source_target_pairs={{0,4},{1,5},{2,6},{3,7},{4,0},{5,1},{6,2},{7,3},{8,12},{9,13},{10,... | collective-permute-start | bytes 24584 | tf_op jit(solution)/shard_map/ppermute | solution.py:381
  19.1 3.4 %collective-permute-start.7 = (bf16[32,128]{1,0:T(8,128)(2,1)S(1)}, bf16[32,128]{1,0:T(8,128)(2,1)S(1)}, u32[]{:S(2)}, u32[]{:S(2)}) collective-permute-start(bf16[32,128]{1,0:T(8,128)(2,1)S(1)} %get-tuple-element.65), channel_id=1, source_target_pairs={{0,2},{1,3},{2,0},{3,1},{4,6},{5,7},{6,4},{7,5},{8,10},{9,11},{10,... | collective-permute-start | bytes 24584 | tf_op jit(solution)/shard_map/ppermute | solution.py:381
  23.0 8.1 %collective-permute-start.8 = (bf16[512,256]{1,0:T(8,128)(2,1)S(1)}, bf16[512,256]{1,0:T(8,128)(2,1)S(1)}, u32[]{:S(2)}, u32[]{:S(2)}) collective-permute-start(bf16[512,256]{1,0:T(8,128)(2,1)S(1)} %get-tuple-element.71), channel_id=1, source_target_pairs={{0,6},{1,7},{2,4},{3,5},{4,2},{5,3},{6,0},{7,1},{8,14},{9,15},{10,... | collective-permute-start | bytes 786440 | tf_op jit(solution)/shard_map/ppermute | solution.py:381
  27.7 12.1 %collective-permute-start.9 = (bf16[512,256]{1,0:T(8,128)(2,1)S(1)}, bf16[512,256]{1,0:T(8,128)(2,1)S(1)}, u32[]{:S(2)}, u32[]{:S(2)}) collective-permute-start(bf16[512,256]{1,0:T(8,128)(2,1)S(1)} %get-tuple-element.73), channel_id=1, source_target_pairs={{0,2},{1,3},{2,0},{3,1},{4,6},{5,7},{6,4},{7,5},{8,10},{9,11},{10,... | collective-permute-start | bytes 786440 | tf_op jit(solution)/shard_map/ppermute | solution.py:381
  27.9 18.3 %collective-permute-start.10 = (bf16[512,256]{1,0:T(8,128)(2,1)S(1)}, bf16[512,256]{1,0:T(8,128)(2,1)S(1)}, u32[]{:S(2)}, u32[]{:S(2)}) collective-permute-start(bf16[512,256]{1,0:T(8,128)(2,1)S(1)} %get-tuple-element.74), channel_id=1, source_target_pairs={{0,4},{1,5},{2,6},{3,7},{4,0},{5,1},{6,2},{7,3},{8,12},{9,13},{10,... | collective-permute-start | bytes 786440 | tf_op jit(solution)/shard_map/ppermute | solution.py:381
  46.6 3.6 %collective-permute-start.11 = (bf16[512,256]{1,0:T(8,128)(2,1)S(1)}, bf16[512,256]{1,0:T(8,128)(2,1)S(1)}, u32[]{:S(2)}, u32[]{:S(2)}) collective-permute-start(bf16[512,256]{1,0:T(8,128)(2,1)S(1)} %shard_map.165), channel_id=1, source_target_pairs={{0,1},{1,0},{2,3},{3,2},{4,5},{5,4},{6,7},{7,6},{8,9},{9,8},{10,11... | collective-permute-start | bytes 786440 | tf_op jit(solution)/shard_map/ppermute | solution.py:427

commit v7 on v5

--- a/solution.py
+++ b/solution.py
@@ -44,6 +44,22 @@
 
 def parity(axis):
     return lax.rem(lax.axis_index(axis), 2)
+
+
+def gray(place):
+    return place ^ (place >> 1)
+
+
+def ring_place(chip, count):
+    shift = 1
+    while 2**shift <= count:
+        chip = chip ^ (chip >> shift)
+        shift *= 2
+    return chip
+
+
+def steps_on(chip, other, count):
+    return (ring_place(other, count) - ring_place(chip, count) + count) & (count - 1)
 
 
 def edges_body(*refs):
@@ -96,14 +112,14 @@
         c = count[0, 0, 2 * m]
         second = pltpu.roll(listed[2 * m + 1 : 2 * m + 2, :], lax.rem(c, width), 1)
         line = jnp.where(pos < c, listed[2 * m : 2 * m + 1, :], second)
-        away = m ^ chip
+        away = steps_on(chip, m, pairs)
         for t in range(tiles):
             order[pl.ds(away * tiles + t, 1), :] = line[:, t * LANES : (t + 1) * LANES]
     at = order[...]
     place = lookup(slot, at >> 7, at & (LANES - 1))
     pad = jnp.zeros((PACK_ROWS - 2 * tiles, LANES), F32)
     for away in range(pairs):
-        m = away ^ chip
+        m = gray((ring_place(chip, pairs) + away) & (pairs - 1))
         mine = place[away * tiles : (away + 1) * tiles, :] - m * chip_basins
         ids[away] = jnp.concatenate(
             [(mine >> 8).astype(F32), (mine & 255).astype(F32), pad], axis=0
@@ -209,14 +225,16 @@
     for flip, out in zip(range(len(outs), 0, -1), outs):
         m = chip ^ flip
         out[:blocks, :] = (keep[m] + got[m].astype(F32)).astype(BF16)
-        out[blocks:, :] = ids[flip]
+        out[blocks:, :] = ids[steps_on(chip, m, pairs)]
 
 
 def send_body(away, own, order, ids, rec_packed, hyd_packed, *refs):
     terms, (runoff, ready, places) = refs[:-3], refs[-3:]
+    pairs = places.shape[0]
+    chip = lax.axis_index("sec") // 2
     places[0] = ids[0]
     for flip, term in zip(range(len(terms), 0, -1), terms):
-        places[flip] = term[term.shape[0] - PACK_ROWS :, :]
+        places[steps_on(chip ^ flip, chip, pairs)] = term[term.shape[0] - PACK_ROWS :, :]
     blocks = runoff.shape[0]
     tiles = ready.shape[0] // LANES
     total = own[...]
@@ -374,9 +392,9 @@
         scratch=[pltpu.SMEM(send_count.shape, I32), dma((1,))],
         moved=moisture.size * 8,
     )
-    aways = []
-    for k in range(1, pairs // 2 + 1):
-        aways += [k] if 2 * k == pairs else [pairs - k, k]
+    aways = [pairs // 2]
+    for k in range(1, pairs // 2):
+        aways += [k, pairs - k]
     own_terms, *terms = call(
         terms_body,
         [shape((blocks, LANES), F32)] + [shape((blocks + PACK_ROWS, LANES), BF16)] * (pairs - 1),
@@ -384,9 +402,18 @@
         moved=reaches * 8,
     )
     forward = lambda block, away: lax.ppermute(
-        block, "sec", [(i, i ^ (2 * away)) for i in range(sections)]
-    )
-    terms = [forward(term, flip) for flip, term in zip(range(pairs - 1, 0, -1), terms)]
+        block,
+        "sec",
+        [
+            (2 * gray(i) + core, 2 * gray((i + away) % pairs) + core)
+            for i in range(pairs)
+            for core in range(2)
+        ],
+    )
+    terms = [
+        lax.ppermute(term, "sec", [(i, i ^ (2 * flip)) for i in range(sections)])
+        for flip, term in zip(range(pairs - 1, 0, -1), terms)
+    ]
     rec_packed, hyd_packed = call(
         lambda *refs: first_body(aways[0], *refs),
         [shape((cap, steps), BF16)] * 2,

time: 50.4 us -> 50.8 us (level)
  transfers between devices with their start and end apart: 12 -> 12, of which waited for: 7 -> 6; matrix products, arithmetic and copies ran while one was open for 0% -> 0% of each run, Pallas kernels for 14% -> 14%
where the time goes in v7:
time: 50.8 us; the launch traced here: 50.7 us
  waiting for transfers between devices  22.2 us (44%)
  starting transfers between devices  16.1 us (32%)
  Pallas kernels  11.5 us (23%)
  between operations  0.77 us (2%)
    ppermute x3, waiting for transfers between devices, per_device(): lax.ppermute(block, 'sec', [(2 * gray(i) + core, 2 * gray((i + away) % pa...  15.5 us
    pallas_call x12, Pallas kernels, call(): pl.pallas_call(body, out_shape=list(outs), in_specs=ins, out_specs=list(o...  11.5 us
    ppermute x3, starting transfers between devices, per_device(): lax.ppermute(term, 'sec', [(i, i ^ 2 * flip) for i in range(sections)])  4.81 us
    ppermute x3, starting transfers between devices, per_device(): lax.ppermute(block, 'sec', [(2 * gray(i) + core, 2 * gray((i + away) % pa...  4.5 us
    ppermute x1, waiting for transfers between devices, per_device(): lax.ppermute(lon_far, 'lon', [(i, (i - 1 + 2 * (i % 2)) % lons) for i in...  2.92 us
    ppermute x1, starting transfers between devices, per_device(): got_lon_near = lax.ppermute(lon_near, 'lon', swap(lons))  2.58 us
    ppermute x3, waiting for transfers between devices, per_device(): lax.ppermute(term, 'sec', [(i, i ^ 2 * flip) for i in range(sections)])  2.45 us
    ppermute x1, starting transfers between devices, per_device(): got = lax.ppermute(give, 'sec', swap(sections))  1.51 us
  transfers between devices with their start and end apart: 12, of which 6 were waited for; matrix products, arithmetic and copies ran while one was open for 0% of the time, Pallas kernels for 14%

profile of v7, /device:TPU:0, one launch (start us, length us, event | category | flops | bytes accessed | tf_op | source)
XLA Modules:
  0.0 50.7 jit_solution(17967116151794304709)
XLA Ops:
  0.7 1.5 %shard_map.156 = (f32[16,16,256]{2,1,0:T(8,128)S(1)}, f32[16,16,256]{2,1,0:T(8,128)S(1)}, f32[16,16,256]{2,1,0:T(8,128)S(1)}, f32[16,16,256]{2,1,0:T(8,128)S(1)}...) custom-call(f32[16,16,256]{2,1,0:T(8,128)} %refs_0_.1, ...), custom_call_target="tpu_custom_call" | custom-call | bytes 524288 | tf_op jit(solution)/shard_map/pallas_call | solution.py:24
  2.2 0.5 %collective-permute-start = (bf16[32,256]{1,0:T(8,128)(2,1)S(1)}, bf16[32,256]{1,0:T(8,128)(2,1)S(1)}, u32[]{:S(2)}, u32[]{:S(2)}) collective-permute-start(bf16[32,256]{1,0:T(8,128)(2,1)S(1)} %get-tuple-element.48), channel_id=1, source_target_pairs={{0,1},{1,0},{2,3},{3,2},{4,5},{5,4},{6,7},{7,6},{8,9},{9,8},{10,11... | collective-permute-start | bytes 49160 | tf_op jit(solution)/shard_map/ppermute | solution.py:368
  2.7 0.7 %collective-permute-start.1 = (bf16[32,256]{1,0:T(8,128)(2,1)S(1)}, bf16[32,256]{1,0:T(8,128)(2,1)S(1)}, u32[]{:S(2)}, u32[]{:S(2)}) collective-permute-start(bf16[32,256]{1,0:T(8,128)(2,1)S(1)} %get-tuple-element.49), channel_id=1, source_target_pairs={{1,2},{3,4},{5,6},{2,1},{4,3},{6,5},{9,10},{11,12},{13,14},{10,9},... | collective-permute-start | bytes 49160 | tf_op jit(solution)/shard_map/ppermute | solution.py:367
  3.4 2.6 %collective-permute-start.2 = (bf16[16,128]{1,0:T(8,128)(2,1)S(1)}, bf16[16,128]{1,0:T(8,128)(2,1)S(1)}, u32[]{:S(2)}, u32[]{:S(2)}) collective-permute-start(bf16[16,128]{1,0:T(8,128)(2,1)S(1)} %get-tuple-element.50), channel_id=1, source_target_pairs={{0,8},{8,0},{16,24},{24,16},{1,9},{9,1},{17,25},{25,17},{2,10},{10... | collective-permute-start | bytes 12296 | tf_op jit(solution)/shard_map/ppermute | solution.py:372
  6.0 1.5 %collective-permute-start.3 = (bf16[16,128]{1,0:T(8,128)(2,1)S(1)}, bf16[16,128]{1,0:T(8,128)(2,1)S(1)}, u32[]{:S(2)}, u32[]{:S(2)}) collective-permute-start(bf16[16,128]{1,0:T(8,128)(2,1)S(1)} %get-tuple-element.51), channel_id=1, source_target_pairs={{0,24},{8,16},{16,8},{24,0},{1,25},{9,17},{17,9},{25,1},{2,26},{10... | collective-permute-start | bytes 12296 | tf_op jit(solution)/shard_map/ppermute | solution.py:369
  7.5 2.9 %collective-permute-done.3.lon_far = bf16[16,128]{1,0:T(8,128)(2,1)S(1)} collective-permute-done((bf16[16,128]{1,0:T(8,128)(2,1)S(1)}, bf16[16,128]{1,0:T(8,128)(2,1)S(1)}, u32[]{:S(2)}, u32[]{:S(2)}) %collective-permute-start.3) | collective-permute-done | bytes 4128 | tf_op jit(solution)/shard_map/ppermute | solution.py:369
  10.5 1.4 %shard_map.157 = (f32[16,16,256]{2,1,0:T(8,128)}, f32[16,16,256]{2,1,0:T(8,128)}, f32[4,16,128]{2,1,0:T(8,128)S(1)}, bf16[4,16,128]{2,1,0:T(8,128)(2,1)S(1)}) custom-call(f32[16,16,256]{2,1,0:T(8,128)S(1)} %get-tuple-element.41.moist, f32[16,16,256]{2,1,0:T(8,128)S(1)} %get-tuple-element.42.heat, f32[16,16,256]{2,1,0:T(8,128)S(1)} %get-tuple-element.43.moist_k, ...), custom_call_target="tpu_custom_call" | custom-call | bytes 1572864 | tf_op jit(solution)/shard_map/pallas_call | solution.py:24
  11.9 1.5 %collective-permute-start.4 = (bf16[4,16,128]{2,1,0:T(8,128)(2,1)S(1)}, bf16[4,16,128]{2,1,0:T(8,128)(2,1)S(1)}, u32[]{:S(2)}, u32[]{:S(2)}) collective-permute-start(bf16[4,16,128]{2,1,0:T(8,128)(2,1)S(1)} %get-tuple-element.59), channel_id=1, source_target_pairs={{0,1},{1,0},{2,3},{3,2},{4,5},{5,4},{6,7},{7,6},{8,9},{9,8},{10,11... | collective-permute-start | bytes 49160 | tf_op jit(solution)/shard_map/ppermute | solution.py:386
  13.4 0.9 %shard_map.158 = (s32[16,128]{1,0:T(8,128)S(1)}, bf16[4,16,128]{2,1,0:T(8,128)(2,1)S(1)}) custom-call(s32[8,512]{1,0:T(8,128)S(1)} %get-tuple-element.54.listed, s32[32,128]{1,0:T(8,128)S(1)} %get-tuple-element.55.home, s32[16,128]{1,0:T(8,128)S(1)} %get-tuple-element.56.down, s32[1,1,8]{2,1,0:T(1,128)} %count_in.1), custom_call_target="tpu_custom_call" | custom-call | bytes 524288 | tf_op jit(solution)/shard_map/pallas_call | solution.py:24
  14.4 4.2 %collective-permute-start.5 = (bf16[32,128]{1,0:T(8,128)(2,1)S(1)}, bf16[32,128]{1,0:T(8,128)(2,1)S(1)}, u32[]{:S(2)}, u32[]{:S(2)}) collective-permute-start(bf16[32,128]{1,0:T(8,128)(2,1)S(1)} %get-tuple-element.64), channel_id=1, source_target_pairs={{0,6},{1,7},{2,4},{3,5},{4,2},{5,3},{6,0},{7,1},{8,14},{9,15},{10,... | collective-permute-start | bytes 24584 | tf_op jit(solution)/shard_map/ppermute | solution.py:414
  18.5 0.6 %collective-permute-start.7 = (bf16[32,128]{1,0:T(8,128)(2,1)S(1)}, bf16[32,128]{1,0:T(8,128)(2,1)S(1)}, u32[]{:S(2)}, u32[]{:S(2)}) collective-permute-start(bf16[32,128]{1,0:T(8,128)(2,1)S(1)} %get-tuple-element.66), channel_id=1, source_target_pairs={{0,2},{1,3},{2,0},{3,1},{4,6},{5,7},{6,4},{7,5},{8,10},{9,11},{10,... | collective-permute-start | bytes 24584 | tf_op jit(solution)/shard_map/ppermute | solution.py:414
  19.2 1.4 %shard_map.160 = (bf16[512,256]{1,0:T(8,128)(2,1)S(1)}, bf16[512,256]{1,0:T(8,128)(2,1)S(1)}) custom-call(s32[16,128]{1,0:T(8,128)S(1)} %get-tuple-element.57.refs_0_.refs_1_.refs_3_, bf16[2048,256]{1,0:T(8,128)(2,1)S(1)} %bitcast.7, bf16[2048,256]{1,0:T(8,128)(2,1)S(1)} %bitcast.9), custom_call_target="tpu_custom_call" | custom-call | flops 1073741824 | bytes 2097152 | tf_op jit(solution)/shard_map/pallas_call | solution.py:24
  20.6 2.4 %collective-permute-done.6.refs_6_ = bf16[32,128]{1,0:T(8,128)(2,1)S(1)} collective-permute-done((bf16[32,128]{1,0:T(8,128)(2,1)S(1)}, bf16[32,128]{1,0:T(8,128)(2,1)S(1)}, u32[]{:S(2)}, u32[]{:S(2)}) %collective-permute-start.6) | collective-permute-done | bytes 8224 | tf_op jit(solution)/shard_map/ppermute | solution.py:414
  23.1 0.4 shard_map.161
  23.5 1.5 %collective-permute-start.8 = (bf16[512,256]{1,0:T(8,128)(2,1)S(1)}, bf16[512,256]{1,0:T(8,128)(2,1)S(1)}, u32[]{:S(2)}, u32[]{:S(2)}) collective-permute-start(bf16[512,256]{1,0:T(8,128)(2,1)S(1)} %get-tuple-element.70), channel_id=1, source_target_pairs={{0,6},{1,7},{2,4},{3,5},{6,0},{7,1},{4,2},{5,3},{8,14},{9,15},{10,... | collective-permute-start | bytes 786440 | tf_op jit(solution)/shard_map/ppermute | solution.py:404
  25.0 1.7 %shard_map.162 = (bf16[2048,256]{1,0:T(8,128)(2,1)S(1)}, bf16[512,256]{1,0:T(8,128)(2,1)S(1)}, bf16[512,256]{1,0:T(8,128)(2,1)S(1)}) custom-call(f32[16,128]{1,0:T(8,128)S(1)} %get-tuple-element.67.refs_0_, bf16[2048,256]{1,0:T(8,128)(2,1)S(1)} %bitcast.8, bf16[2048,256]{1,0:T(8,128)(2,1)S(1)} %bitcast.10, ...), custom_call_target="tpu_custom_call" | custom-call | flops 536870912 | bytes 4194304 | tf_op jit(solution)/shard_map/pallas_call | solution.py:24
  26.7 1.2 %collective-permute-start.9 = (bf16[512,256]{1,0:T(8,128)(2,1)S(1)}, bf16[512,256]{1,0:T(8,128)(2,1)S(1)}, u32[]{:S(2)}, u32[]{:S(2)}) collective-permute-start(bf16[512,256]{1,0:T(8,128)(2,1)S(1)} %get-tuple-element.74), channel_id=1, source_target_pairs={{0,2},{1,3},{2,6},{3,7},{6,4},{7,5},{4,0},{5,1},{8,10},{9,11},{10,... | collective-permute-start | bytes 786440 | tf_op jit(solution)/shard_map/ppermute | solution.py:404
  27.9 1.8 %collective-permute-start.10 = (bf16[512,256]{1,0:T(8,128)(2,1)S(1)}, bf16[512,256]{1,0:T(8,128)(2,1)S(1)}, u32[]{:S(2)}, u32[]{:S(2)}) collective-permute-start(bf16[512,256]{1,0:T(8,128)(2,1)S(1)} %get-tuple-element.76), channel_id=1, source_target_pairs={{0,4},{1,5},{2,0},{3,1},{6,2},{7,3},{4,6},{5,7},{8,12},{9,13},{10,... | collective-permute-start | bytes 786440 | tf_op jit(solution)/shard_map/ppermute | solution.py:404
  29.7 4.9 %collective-permute-done.8.refs_3_ = bf16[512,256]{1,0:T(8,128)(2,1)S(1)} collective-permute-done((bf16[512,256]{1,0:T(8,128)(2,1)S(1)}, bf16[512,256]{1,0:T(8,128)(2,1)S(1)}, u32[]{:S(2)}, u32[]{:S(2)}) %collective-permute-start.8) | collective-permute-done | bytes 262176 | tf_op jit(solution)/shard_map/ppermute | solution.py:404
  34.6 2.2 %shard_map.163 = (bf16[2048,256]{1,0:T(8,128)(2,1)}, f32[512,256]{1,0:T(8,128)S(1)}, f32[512,256]{1,0:T(8,128)S(1)}) custom-call(s32[16,128]{1,0:T(8,128)S(1)} %get-tuple-element.57.refs_0_.refs_1_.refs_3_, bf16[2048,256]{1,0:T(8,128)(2,1)S(1)} %get-tuple-element.68.refs_1_, bf16[4,16,128]{2,1,0:T(8,128)(2,1)S(1)} %get-tuple-element.69.refs_2_.refs_1_, ...), custom_call_target="tpu_custom_call" | custom-call | flops 536870912 | bytes 2097152 | tf_op jit(solution)/shard_map/pallas_call | solution.py:24
  36.8 10.7 %collective-permute-done.9.refs_3_ = bf16[512,256]{1,0:T(8,128)(2,1)S(1)} collective-permute-done((bf16[512,256]{1,0:T(8,128)(2,1)S(1)}, bf16[512,256]{1,0:T(8,128)(2,1)S(1)}, u32[]{:S(2)}, u32[]{:S(2)}) %collective-permute-start.9) | collective-permute-done | bytes 262176 | tf_op jit(solution)/shard_map/ppermute | solution.py:404
  47.5 0.4 shard_map.164
  48.6 1.2 %collective-permute-done.11.passed = bf16[512,256]{1,0:T(8,128)(2,1)S(1)} collective-permute-done((bf16[512,256]{1,0:T(8,128)(2,1)S(1)}, bf16[512,256]{1,0:T(8,128)(2,1)S(1)}, u32[]{:S(2)}, u32[]{:S(2)}) %collective-permute-start.11) | collective-permute-done | bytes 262176 | tf_op jit(solution)/shard_map/ppermute | solution.py:467
  49.8 0.8 %shard_map.167 = f32[512,256]{1,0:T(8,128)} custom-call(f32[512,256]{1,0:T(8,128)S(1)} %shard_map.165.mine, bf16[512,256]{1,0:T(8,128)(2,1)S(1)} %collective-permute-done.11.passed), custom_call_target="tpu_custom_call" | custom-call | bytes 1310720 | tf_op jit(solution)/shard_map/pallas_call | solution.py:24
  (16 shorter events, 0.8 us)
Async XLA Ops:
  0.6 18.6 %copy-start = (bf16[1,2048,256]{2,1,0:T(8,128)(2,1)S(1)}, bf16[1,2048,256]{2,1,0:T(8,128)(2,1)}, u32[]{:S(2)}) copy-start(bf16[1,2048,256]{2,1,0:T(8,128)(2,1)} %param.20) | copy-start | bytes 3145732
  0.6 18.5 %copy-start.1 = (bf16[1,2048,256]{2,1,0:T(8,128)(2,1)S(1)}, bf16[1,2048,256]{2,1,0:T(8,128)(2,1)}, u32[]{:S(2)}) copy-start(bf16[1,2048,256]{2,1,0:T(8,128)(2,1)} %param.21) | copy-start | bytes 3145732
  2.2 8.3 %collective-permute-start = (bf16[32,256]{1,0:T(8,128)(2,1)S(1)}, bf16[32,256]{1,0:T(8,128)(2,1)S(1)}, u32[]{:S(2)}, u32[]{:S(2)}) collective-permute-start(bf16[32,256]{1,0:T(8,128)(2,1)S(1)} %get-tuple-element.48), channel_id=1, source_target_pairs={{0,1},{1,0},{2,3},{3,2},{4,5},{5,4},{6,7},{7,6},{8,9},{9,8},{10,11... | collective-permute-start | bytes 49160 | tf_op jit(solution)/shard_map/ppermute | solution.py:368
  2.7 7.7 %collective-permute-start.1 = (bf16[32,256]{1,0:T(8,128)(2,1)S(1)}, bf16[32,256]{1,0:T(8,128)(2,1)S(1)}, u32[]{:S(2)}, u32[]{:S(2)}) collective-permute-start(bf16[32,256]{1,0:T(8,128)(2,1)S(1)} %get-tuple-element.49), channel_id=1, source_target_pairs={{1,2},{3,4},{5,6},{2,1},{4,3},{6,5},{9,10},{11,12},{13,14},{10,9},... | collective-permute-start | bytes 49160 | tf_op jit(solution)/shard_map/ppermute | solution.py:367
  3.4 4.2 %collective-permute-start.2 = (bf16[16,128]{1,0:T(8,128)(2,1)S(1)}, bf16[16,128]{1,0:T(8,128)(2,1)S(1)}, u32[]{:S(2)}, u32[]{:S(2)}) collective-permute-start(bf16[16,128]{1,0:T(8,128)(2,1)S(1)} %get-tuple-element.50), channel_id=1, source_target_pairs={{0,8},{8,0},{16,24},{24,16},{1,9},{9,1},{17,25},{25,17},{2,10},{10... | collective-permute-start | bytes 12296 | tf_op jit(solution)/shard_map/ppermute | solution.py:372
  6.0 4.5 %collective-permute-start.3 = (bf16[16,128]{1,0:T(8,128)(2,1)S(1)}, bf16[16,128]{1,0:T(8,128)(2,1)S(1)}, u32[]{:S(2)}, u32[]{:S(2)}) collective-permute-start(bf16[16,128]{1,0:T(8,128)(2,1)S(1)} %get-tuple-element.51), channel_id=1, source_target_pairs={{0,24},{8,16},{16,8},{24,0},{1,25},{9,17},{17,9},{25,1},{2,26},{10... | collective-permute-start | bytes 12296 | tf_op jit(solution)/shard_map/ppermute | solution.py:369
  11.9 2.4 %collective-permute-start.4 = (bf16[4,16,128]{2,1,0:T(8,128)(2,1)S(1)}, bf16[4,16,128]{2,1,0:T(8,128)(2,1)S(1)}, u32[]{:S(2)}, u32[]{:S(2)}) collective-permute-start(bf16[4,16,128]{2,1,0:T(8,128)(2,1)S(1)} %get-tuple-element.59), channel_id=1, source_target_pairs={{0,1},{1,0},{2,3},{3,2},{4,5},{5,4},{6,7},{7,6},{8,9},{9,8},{10,11... | collective-permute-start | bytes 49160 | tf_op jit(solution)/shard_map/ppermute | solution.py:386
  14.4 6.3 %collective-permute-start.5 = (bf16[32,128]{1,0:T(8,128)(2,1)S(1)}, bf16[32,128]{1,0:T(8,128)(2,1)S(1)}, u32[]{:S(2)}, u32[]{:S(2)}) collective-permute-start(bf16[32,128]{1,0:T(8,128)(2,1)S(1)} %get-tuple-element.64), channel_id=1, source_target_pairs={{0,6},{1,7},{2,4},{3,5},{4,2},{5,3},{6,0},{7,1},{8,14},{9,15},{10,... | collective-permute-start | bytes 24584 | tf_op jit(solution)/shard_map/ppermute | solution.py:414
  18.5 4.5 %collective-permute-start.6 = (bf16[32,128]{1,0:T(8,128)(2,1)S(1)}, bf16[32,128]{1,0:T(8,128)(2,1)S(1)}, u32[]{:S(2)}, u32[]{:S(2)}) collective-permute-start(bf16[32,128]{1,0:T(8,128)(2,1)S(1)} %get-tuple-element.65), channel_id=1, source_target_pairs={{0,4},{1,5},{2,6},{3,7},{4,0},{5,1},{6,2},{7,3},{8,12},{9,13},{10,... | collective-permute-start | bytes 24584 | tf_op jit(solution)/shard_map/ppermute | solution.py:414
  18.5 4.5 %collective-permute-start.7 = (bf16[32,128]{1,0:T(8,128)(2,1)S(1)}, bf16[32,128]{1,0:T(8,128)(2,1)S(1)}, u32[]{:S(2)}, u32[]{:S(2)}) collective-permute-start(bf16[32,128]{1,0:T(8,128)(2,1)S(1)} %get-tuple-element.66), channel_id=1, source_target_pairs={{0,2},{1,3},{2,0},{3,1},{4,6},{5,7},{6,4},{7,5},{8,10},{9,11},{10,... | collective-permute-start | bytes 24584 | tf_op jit(solution)/shard_map/ppermute | solution.py:414
  23.5 11.1 %collective-permute-start.8 = (bf16[512,256]{1,0:T(8,128)(2,1)S(1)}, bf16[512,256]{1,0:T(8,128)(2,1)S(1)}, u32[]{:S(2)}, u32[]{:S(2)}) collective-permute-start(bf16[512,256]{1,0:T(8,128)(2,1)S(1)} %get-tuple-element.70), channel_id=1, source_target_pairs={{0,6},{1,7},{2,4},{3,5},{6,0},{7,1},{4,2},{5,3},{8,14},{9,15},{10,... | collective-permute-start | bytes 786440 | tf_op jit(solution)/shard_map/ppermute | solution.py:404
  26.7 20.7 %collective-permute-start.9 = (bf16[512,256]{1,0:T(8,128)(2,1)S(1)}, bf16[512,256]{1,0:T(8,128)(2,1)S(1)}, u32[]{:S(2)}, u32[]{:S(2)}) collective-permute-start(bf16[512,256]{1,0:T(8,128)(2,1)S(1)} %get-tuple-element.74), channel_id=1, source_target_pairs={{0,2},{1,3},{2,6},{3,7},{6,4},{7,5},{4,0},{5,1},{8,10},{9,11},{10,... | collective-permute-start | bytes 786440 | tf_op jit(solution)/shard_map/ppermute | solution.py:404
  27.9 20.0 %collective-permute-start.10 = (bf16[512,256]{1,0:T(8,128)(2,1)S(1)}, bf16[512,256]{1,0:T(8,128)(2,1)S(1)}, u32[]{:S(2)}, u32[]{:S(2)}) collective-permute-start(bf16[512,256]{1,0:T(8,128)(2,1)S(1)} %get-tuple-element.76), channel_id=1, source_target_pairs={{0,4},{1,5},{2,0},{3,1},{6,2},{7,3},{4,6},{5,7},{8,12},{9,13},{10,... | collective-permute-start | bytes 786440 | tf_op jit(solution)/shard_map/ppermute | solution.py:404
  48.2 1.6 %collective-permute-start.11 = (bf16[512,256]{1,0:T(8,128)(2,1)S(1)}, bf16[512,256]{1,0:T(8,128)(2,1)S(1)}, u32[]{:S(2)}, u32[]{:S(2)}) collective-permute-start(bf16[512,256]{1,0:T(8,128)(2,1)S(1)} %shard_map.166), channel_id=1, source_target_pairs={{0,1},{1,0},{2,3},{3,2},{4,5},{5,4},{6,7},{7,6},{8,9},{9,8},{10,11... | collective-permute-start | bytes 786440 | tf_op jit(solution)/shard_map/ppermute | solution.py:467

commit v8 on v5

--- a/solution.py
+++ b/solution.py
@@ -47,7 +47,7 @@
 
 
 def edges_body(*refs):
-    count = 10
+    count = 2
     targets = refs[count : 2 * count]
     moist, heat = targets[:2]
     sec_near, sec_far, lon_near, lon_far, sems = refs[2 * count :]
@@ -83,15 +83,19 @@
     return out
 
 
-def index_body(listed, home, down, count_in, order, ids, count, sems):
-    copies = fetch((count_in,), (count,), sems)
-    slot = lookup(home[...], down[...] >> 7, down[...] & (LANES - 1))
+def index_body(*refs):
+    count_in, home_in, down_in, listed_in = refs[:4]
+    order, ids = refs[9:11]
+    count, home, down, listed, sems = refs[16:]
+    copies = fetch(refs[:9], (count, home, down, listed, *refs[11:16]), sems)
     pairs, width = listed.shape[0] // 2, listed.shape[1]
     tiles = width // LANES
     chip = lax.axis_index("sec") // 2
     chip_basins = home.shape[0] * LANES // pairs
+    for copy in copies[:4]:
+        copy.wait()
+    slot = lookup(home[...], down[...] >> 7, down[...] & (LANES - 1))
     pos = lax.broadcasted_iota(I32, (1, width), 1)
-    copies[0].wait()
     for m in range(pairs):
         c = count[0, 0, 2 * m]
         second = pltpu.roll(listed[2 * m + 1 : 2 * m + 2, :], lax.rem(c, width), 1)
@@ -108,6 +112,8 @@
         ids[away] = jnp.concatenate(
             [(mine >> 8).astype(F32), (mine & 255).astype(F32), pad], axis=0
         ).astype(BF16)
+    for copy in copies[4:]:
+        copy.wait()
 
 
 def shift_time(x):
@@ -265,16 +271,18 @@
     return total
 
 
-def rest_body(near, order, kept, places, landed, out, theirs, mine, own, sem):
-    copy = pltpu.make_async_copy(kept, out, sem)
-    copy.start()
+def rest_body(
+    near, order, kept, places, landed, moist, heat, out, moist_out, heat_out, theirs, mine, own, sems
+):
+    copies = fetch((kept, moist, heat), (out, moist_out, heat_out), sems)
     hot = picked(order, 0, own.shape[0] // LANES, kept.shape[0])
     own[...] = jnp.dot(hot, kept[...], preferred_element_type=F32).astype(BF16)
     digits = [places[away].astype(F32) for away in (0, near)]
     basins = mine.shape[0]
     theirs[...] = summed(digits, [own, landed], basins, True)
     mine[...] = summed(digits, [own, landed], basins, False)
-    copy.wait()
+    for copy in copies:
+        copy.wait()
 
 
 def early_body(aways, theirs_so_far, mine_so_far, places, *refs):
@@ -324,24 +332,21 @@
     home = basin_home.reshape(-1, LANES)
     down = down_basin.reshape(-1, LANES)
     listed = send_index.reshape(sections, cap)
-    fetched = [
-        moisture, heat, moist_cond, heat_cond, rain, surface_flux, cell_reach, home, down, listed
-    ]
-    *fetched, sec_near, sec_far, lon_near, lon_far = call(
+    moist_v, heat_v, sec_near, sec_far, lon_near, lon_far = call(
         edges_body,
-        [shape(x.shape, x.dtype) for x in fetched]
-        + [
+        [
+            shape(moisture.shape, F32),
+            shape(heat.shape, F32),
             shape((2 * layers, cols), BF16),
             shape((2 * layers, cols), BF16),
             shape((lats, LANES), BF16),
             shape((lats, LANES), BF16),
         ],
-        *fetched,
-        ins=[HBM] * len(fetched),
-        scratch=[dma((len(fetched),))],
+        moisture, heat,
+        ins=[HBM] * 2,
+        scratch=[dma((2,))],
         moved=moisture.size * 8,
     )
-    *land, home_v, down_v, listed_v = fetched
     swap = lambda count: [(i, i ^ 1) for i in range(count)]
     between = lambda count: [(i, i + 1) for i in range(1, count - 1, 2)] + [
         (i + 1, i) for i in range(1, count - 1, 2)
@@ -353,7 +358,20 @@
     )
     got_lon_near = lax.ppermute(lon_near, "lon", swap(lons))
 
-    moist_out, heat_out, keep, give = call(
+    land = [moist_cond, heat_cond, rain, surface_flux, cell_reach]
+    tables = [send_count, home, down, listed]
+    order, ids, *land = call(
+        index_body,
+        [shape((blocks, LANES), I32), shape((pairs, PACK_ROWS, LANES), BF16)]
+        + [shape(x.shape, x.dtype) for x in land],
+        *tables, *land,
+        ins=[HBM] * 9,
+        scratch=[pltpu.SMEM(send_count.shape, I32)]
+        + [pltpu.VMEM(x.shape, I32) for x in tables[1:]]
+        + [dma((9,))],
+        moved=moisture.size * 8,
+    )
+    moist_new, heat_new, keep, give = call(
         land_body,
         [
             shape(moisture.shape, F32),
@@ -361,19 +379,11 @@
             shape((pairs, blocks, LANES), F32),
             shape((pairs, blocks, LANES), BF16),
         ],
-        *land,
+        moist_v, heat_v, *land,
         got_sec_near, got_sec_far, got_lon_near, got_lon_far,
         moved=moisture.size * 24,
     )
     got = lax.ppermute(give, "sec", swap(sections))
-    order, ids = call(
-        index_body,
-        [shape((blocks, LANES), I32), shape((pairs, PACK_ROWS, LANES), BF16)],
-        listed_v, home_v, down_v, send_count,
-        ins=[VMEM] * 3 + [HBM],
-        scratch=[pltpu.SMEM(send_count.shape, I32), dma((1,))],
-        moved=moisture.size * 8,
-    )
     aways = []
     for k in range(1, pairs // 2 + 1):
         aways += [k] if 2 * k == pairs else [pairs - k, k]
@@ -413,12 +423,18 @@
     for away, block in zip(aways[1:], ready):
         arrived[away] = forward(block, away)
     near, late = aways[0], aways[-1:]
-    record_new, theirs, mine = call(
+    record_new, moist_out, heat_out, theirs, mine = call(
         lambda *refs: rest_body(near, *refs),
-        [shape((reaches, steps), BF16), shape((basins, steps), F32), shape((basins, steps), F32)],
-        order, kept, places, arrived[near],
-        out_specs=[HBM, VMEM, VMEM],
-        scratch=[pltpu.VMEM((cap, steps), BF16), dma(())],
+        [
+            shape((reaches, steps), BF16),
+            shape(moisture.shape, F32),
+            shape(heat.shape, F32),
+            shape((basins, steps), F32),
+            shape((basins, steps), F32),
+        ],
+        order, kept, places, arrived[near], moist_new, heat_new,
+        out_specs=[HBM] * 3 + [VMEM] * 2,
+        scratch=[pltpu.VMEM((cap, steps), BF16), dma((3,))],
         mib=16,
         flops=2 * cap * reaches * steps,
         moved=reaches * steps * 4,

time: 50.4 us -> 49.9 us (0.990)
  waiting for transfers between devices: 21.7 us -> 20.8 us
    ppermute x1, waiting for transfers between devices: 2.92 us -> 1.83 us  [per_device(): lax.ppermute(lon_far, 'lon', [(i, (i - 1 + 2 * (i % 2)) % lons) for i in...]
    ppermute x1, waiting for transfers between devices: 0.01 us -> 0.84 us  [per_device(): got = lax.ppermute(give, 'sec', swap(sections))]
    ppermute x6, waiting for transfers between devices: 17.5 us -> 16.9 us  [per_device(): lax.ppermute(block, 'sec', [(i, i ^ 2 * away) for i in range(sections)])]
  transfers between devices with their start and end apart: 12 -> 12, of which waited for: 7 -> 7; matrix products, arithmetic and copies ran while one was open for 0% -> 0% of each run, Pallas kernels for 14% -> 16%
where the time goes in v8:
time: 49.9 us; the launch traced here: 49.7 us
  waiting for transfers between devices  20.8 us (42%)
  starting transfers between devices  16.3 us (33%)
  Pallas kernels  11.8 us (24%)
  between operations  0.76 us (2%)
    ppermute x6, waiting for transfers between devices, per_device(): lax.ppermute(block, 'sec', [(i, i ^ 2 * away) for i in range(sections)])  16.9 us
    pallas_call x12, Pallas kernels, call(): pl.pallas_call(body, out_shape=list(outs), in_specs=ins, out_specs=list(o...  11.8 us
    ppermute x6, starting transfers between devices, per_device(): lax.ppermute(block, 'sec', [(i, i ^ 2 * away) for i in range(sections)])  9.31 us
    ppermute x1, starting transfers between devices, per_device(): got_lon_near = lax.ppermute(lon_near, 'lon', swap(lons))  2.71 us
    ppermute x1, waiting for transfers between devices, per_device(): lax.ppermute(lon_far, 'lon', [(i, (i - 1 + 2 * (i % 2)) % lons) for i in...  1.83 us
    ppermute x1, starting transfers between devices, per_device(): got = lax.ppermute(give, 'sec', swap(sections))  1.58 us
    ppermute x1, starting transfers between devices, per_device(): lax.ppermute(lon_far, 'lon', [(i, (i - 1 + 2 * (i % 2)) % lons) for i in...  1.49 us
    ppermute x1, waiting for transfers between devices, per_device(): passed = lax.ppermute(theirs, 'sec', swap(sections))  1.21 us
  transfers between devices with their start and end apart: 12, of which 7 were waited for; matrix products, arithmetic and copies ran while one was open for 0% of the time, Pallas kernels for 16%

profile of v8, /device:TPU:0, one launch (start us, length us, event | category | flops | bytes accessed | tf_op | source)
XLA Modules:
  0.0 49.7 jit_solution(15131729696680705417)
XLA Ops:
  0.6 1.4 %shard_map.157 = (f32[16,16,256]{2,1,0:T(8,128)S(1)}, f32[16,16,256]{2,1,0:T(8,128)S(1)}, bf16[32,256]{1,0:T(8,128)(2,1)S(1)}, bf16[32,256]{1,0:T(8,128)(2,1)S(1...) custom-call(f32[16,16,256]{2,1,0:T(8,128)} %refs_0_.3, f32[16,16,256]{2,1,0:T(8,128)} %refs_1_.1), custom_call_target="tpu_custom_call" | custom-call | bytes 524288 | tf_op jit(solution)/shard_map/pallas_call | solution.py:24
  2.0 0.5 %collective-permute-start = (bf16[32,256]{1,0:T(8,128)(2,1)S(1)}, bf16[32,256]{1,0:T(8,128)(2,1)S(1)}, u32[]{:S(2)}, u32[]{:S(2)}) collective-permute-start(bf16[32,256]{1,0:T(8,128)(2,1)S(1)} %get-tuple-element.48), channel_id=1, source_target_pairs={{0,1},{1,0},{2,3},{3,2},{4,5},{5,4},{6,7},{7,6},{8,9},{9,8},{10,11... | collective-permute-start | bytes 49160 | tf_op jit(solution)/shard_map/ppermute | solution.py:355
  2.6 0.7 %collective-permute-start.1 = (bf16[32,256]{1,0:T(8,128)(2,1)S(1)}, bf16[32,256]{1,0:T(8,128)(2,1)S(1)}, u32[]{:S(2)}, u32[]{:S(2)}) collective-permute-start(bf16[32,256]{1,0:T(8,128)(2,1)S(1)} %get-tuple-element.49), channel_id=1, source_target_pairs={{1,2},{3,4},{5,6},{2,1},{4,3},{6,5},{9,10},{11,12},{13,14},{10,9},... | collective-permute-start | bytes 49160 | tf_op jit(solution)/shard_map/ppermute | solution.py:354
  3.2 2.7 %collective-permute-start.2 = (bf16[16,128]{1,0:T(8,128)(2,1)S(1)}, bf16[16,128]{1,0:T(8,128)(2,1)S(1)}, u32[]{:S(2)}, u32[]{:S(2)}) collective-permute-start(bf16[16,128]{1,0:T(8,128)(2,1)S(1)} %get-tuple-element.50), channel_id=1, source_target_pairs={{0,8},{8,0},{16,24},{24,16},{1,9},{9,1},{17,25},{25,17},{2,10},{10... | collective-permute-start | bytes 12296 | tf_op jit(solution)/shard_map/ppermute | solution.py:359
  5.9 1.5 %collective-permute-start.3 = (bf16[16,128]{1,0:T(8,128)(2,1)S(1)}, bf16[16,128]{1,0:T(8,128)(2,1)S(1)}, u32[]{:S(2)}, u32[]{:S(2)}) collective-permute-start(bf16[16,128]{1,0:T(8,128)(2,1)S(1)} %get-tuple-element.51), channel_id=1, source_target_pairs={{0,24},{8,16},{16,8},{24,0},{1,25},{9,17},{17,9},{25,1},{2,26},{10... | collective-permute-start | bytes 12296 | tf_op jit(solution)/shard_map/ppermute | solution.py:356
  7.4 1.2 %shard_map.156 = (s32[16,128]{1,0:T(8,128)S(1)}, bf16[4,16,128]{2,1,0:T(8,128)(2,1)S(1)}, f32[16,16,256]{2,1,0:T(8,128)S(1)}, f32[16,16,256]{2,1,0:T(8,128)S(1)}...) custom-call(s32[1,1,8]{2,1,0:T(1,128)} %refs_0_.2, s32[32,128]{1,0:T(8,128)} %bitcast.12, ...), custom_call_target="tpu_custom_call" | custom-call | bytes 524288 | tf_op jit(solution)/shard_map/pallas_call | solution.py:24
  8.6 1.8 %collective-permute-done.3.lon_far = bf16[16,128]{1,0:T(8,128)(2,1)S(1)} collective-permute-done((bf16[16,128]{1,0:T(8,128)(2,1)S(1)}, bf16[16,128]{1,0:T(8,128)(2,1)S(1)}, u32[]{:S(2)}, u32[]{:S(2)}) %collective-permute-start.3) | collective-permute-done | bytes 4128 | tf_op jit(solution)/shard_map/ppermute | solution.py:356
  10.4 1.1 %shard_map.158 = (f32[16,16,256]{2,1,0:T(8,128)S(1)}, f32[16,16,256]{2,1,0:T(8,128)S(1)}, f32[4,16,128]{2,1,0:T(8,128)S(1)}, bf16[4,16,128]{2,1,0:T(8,128)(2,1)S(1)}) custom-call(f32[16,16,256]{2,1,0:T(8,128)S(1)} %get-tuple-element.41.moist, f32[16,16,256]{2,1,0:T(8,128)S(1)} %get-tuple-element.42.heat, f32[16,16,256]{2,1,0:T(8,128)S(1)} %get-tuple-element.43.moist_k, ...), custom_call_target="tpu_custom_call" | custom-call | bytes 1572864 | tf_op jit(solution)/shard_map/pallas_call | solution.py:24
  11.6 1.6 %collective-permute-start.4 = (bf16[4,16,128]{2,1,0:T(8,128)(2,1)S(1)}, bf16[4,16,128]{2,1,0:T(8,128)(2,1)S(1)}, u32[]{:S(2)}, u32[]{:S(2)}) collective-permute-start(bf16[4,16,128]{2,1,0:T(8,128)(2,1)S(1)} %get-tuple-element.53), channel_id=1, source_target_pairs={{0,1},{1,0},{2,3},{3,2},{4,5},{5,4},{6,7},{7,6},{8,9},{9,8},{10,11... | collective-permute-start | bytes 49160 | tf_op jit(solution)/shard_map/ppermute | solution.py:386
  13.2 0.8 %collective-permute-done.4.got = bf16[4,16,128]{2,1,0:T(8,128)(2,1)S(1)} collective-permute-done((bf16[4,16,128]{2,1,0:T(8,128)(2,1)S(1)}, bf16[4,16,128]{2,1,0:T(8,128)(2,1)S(1)}, u32[]{:S(2)}, u32[]{:S(2)}) %collective-permute-start.4) | collective-permute-done | bytes 16416 | tf_op jit(solution)/shard_map/ppermute | solution.py:386
  14.0 4.2 %collective-permute-start.5 = (bf16[32,128]{1,0:T(8,128)(2,1)S(1)}, bf16[32,128]{1,0:T(8,128)(2,1)S(1)}, u32[]{:S(2)}, u32[]{:S(2)}) collective-permute-start(bf16[32,128]{1,0:T(8,128)(2,1)S(1)} %get-tuple-element.58), channel_id=1, source_target_pairs={{0,6},{1,7},{2,4},{3,5},{4,2},{5,3},{6,0},{7,1},{8,14},{9,15},{10,... | collective-permute-start | bytes 24584 | tf_op jit(solution)/shard_map/ppermute | solution.py:396
  18.2 0.6 %collective-permute-start.7 = (bf16[32,128]{1,0:T(8,128)(2,1)S(1)}, bf16[32,128]{1,0:T(8,128)(2,1)S(1)}, u32[]{:S(2)}, u32[]{:S(2)}) collective-permute-start(bf16[32,128]{1,0:T(8,128)(2,1)S(1)} %get-tuple-element.60), channel_id=1, source_target_pairs={{0,2},{1,3},{2,0},{3,1},{4,6},{5,7},{6,4},{7,5},{8,10},{9,11},{10,... | collective-permute-start | bytes 24584 | tf_op jit(solution)/shard_map/ppermute | solution.py:396
  18.8 1.4 %shard_map.160 = (bf16[512,256]{1,0:T(8,128)(2,1)S(1)}, bf16[512,256]{1,0:T(8,128)(2,1)S(1)}) custom-call(s32[16,128]{1,0:T(8,128)S(1)} %get-tuple-element.40.refs_0_.refs_1_.refs_3_, bf16[2048,256]{1,0:T(8,128)(2,1)S(1)} %bitcast.7, bf16[2048,256]{1,0:T(8,128)(2,1)S(1)} %bitcast.9), custom_call_target="tpu_custom_call" | custom-call | flops 1073741824 | bytes 2097152 | tf_op jit(solution)/shard_map/pallas_call | solution.py:24
  20.3 2.4 %collective-permute-done.6.refs_6_ = bf16[32,128]{1,0:T(8,128)(2,1)S(1)} collective-permute-done((bf16[32,128]{1,0:T(8,128)(2,1)S(1)}, bf16[32,128]{1,0:T(8,128)(2,1)S(1)}, u32[]{:S(2)}, u32[]{:S(2)}) %collective-permute-start.6) | collective-permute-done | bytes 8224 | tf_op jit(solution)/shard_map/ppermute | solution.py:396
  23.1 1.5 %collective-permute-start.8 = (bf16[512,256]{1,0:T(8,128)(2,1)S(1)}, bf16[512,256]{1,0:T(8,128)(2,1)S(1)}, u32[]{:S(2)}, u32[]{:S(2)}) collective-permute-start(bf16[512,256]{1,0:T(8,128)(2,1)S(1)} %get-tuple-element.64), channel_id=1, source_target_pairs={{0,6},{1,7},{2,4},{3,5},{4,2},{5,3},{6,0},{7,1},{8,14},{9,15},{10,... | collective-permute-start | bytes 786440 | tf_op jit(solution)/shard_map/ppermute | solution.py:396
  24.6 1.7 %shard_map.162 = (bf16[2048,256]{1,0:T(8,128)(2,1)S(1)}, bf16[512,256]{1,0:T(8,128)(2,1)S(1)}, bf16[512,256]{1,0:T(8,128)(2,1)S(1)}) custom-call(f32[16,128]{1,0:T(8,128)S(1)} %get-tuple-element.61.refs_0_, bf16[2048,256]{1,0:T(8,128)(2,1)S(1)} %bitcast.8, bf16[2048,256]{1,0:T(8,128)(2,1)S(1)} %bitcast.10, ...), custom_call_target="tpu_custom_call" | custom-call | flops 536870912 | bytes 4194304 | tf_op jit(solution)/shard_map/pallas_call | solution.py:24
  26.4 1.2 %collective-permute-start.9 = (bf16[512,256]{1,0:T(8,128)(2,1)S(1)}, bf16[512,256]{1,0:T(8,128)(2,1)S(1)}, u32[]{:S(2)}, u32[]{:S(2)}) collective-permute-start(bf16[512,256]{1,0:T(8,128)(2,1)S(1)} %get-tuple-element.72), channel_id=1, source_target_pairs={{0,2},{1,3},{2,0},{3,1},{4,6},{5,7},{6,4},{7,5},{8,10},{9,11},{10,... | collective-permute-start | bytes 786440 | tf_op jit(solution)/shard_map/ppermute | solution.py:396
  27.6 1.8 %collective-permute-start.10 = (bf16[512,256]{1,0:T(8,128)(2,1)S(1)}, bf16[512,256]{1,0:T(8,128)(2,1)S(1)}, u32[]{:S(2)}, u32[]{:S(2)}) collective-permute-start(bf16[512,256]{1,0:T(8,128)(2,1)S(1)} %get-tuple-element.74), channel_id=1, source_target_pairs={{0,4},{1,5},{2,6},{3,7},{4,0},{5,1},{6,2},{7,3},{8,12},{9,13},{10,... | collective-permute-start | bytes 786440 | tf_op jit(solution)/shard_map/ppermute | solution.py:396
  29.4 4.8 %collective-permute-done.8.refs_3_ = bf16[512,256]{1,0:T(8,128)(2,1)S(1)} collective-permute-done((bf16[512,256]{1,0:T(8,128)(2,1)S(1)}, bf16[512,256]{1,0:T(8,128)(2,1)S(1)}, u32[]{:S(2)}, u32[]{:S(2)}) %collective-permute-start.8) | collective-permute-done | bytes 262176 | tf_op jit(solution)/shard_map/ppermute | solution.py:396
  34.2 2.7 %shard_map.163 = (bf16[2048,256]{1,0:T(8,128)(2,1)}, f32[16,16,256]{2,1,0:T(8,128)}, f32[16,16,256]{2,1,0:T(8,128)}, f32[512,256]{1,0:T(8,128)S(1)}, f32[512,256]{1,0:T(8,128)S(1)}) custom-call(s32[16,128]{1,0:T(8,128)S(1)} %get-tuple-element.40.refs_0_.refs_1_.refs_3_, bf16[2048,256]{1,0:T(8,128)(2,1)S(1)} %get-tuple-element.62.refs_1_, ...), custom_call_target="tpu_custom_call" | custom-call | flops 536870912 | bytes 2097152 | tf_op jit(solution)/shard_map/pallas_call | solution.py:24
  36.9 2.5 %collective-permute-done.9.refs_3_ = bf16[512,256]{1,0:T(8,128)(2,1)S(1)} collective-permute-done((bf16[512,256]{1,0:T(8,128)(2,1)S(1)}, bf16[512,256]{1,0:T(8,128)(2,1)S(1)}, u32[]{:S(2)}, u32[]{:S(2)}) %collective-permute-start.9) | collective-permute-done | bytes 262176 | tf_op jit(solution)/shard_map/ppermute | solution.py:396
  39.9 7.1 %collective-permute-done.10.refs_2_ = bf16[512,256]{1,0:T(8,128)(2,1)S(1)} collective-permute-done((bf16[512,256]{1,0:T(8,128)(2,1)S(1)}, bf16[512,256]{1,0:T(8,128)(2,1)S(1)}, u32[]{:S(2)}, u32[]{:S(2)}) %collective-permute-start.10) | collective-permute-done | bytes 262176 | tf_op jit(solution)/shard_map/ppermute | solution.py:396
  47.6 1.2 %collective-permute-done.11.passed = bf16[512,256]{1,0:T(8,128)(2,1)S(1)} collective-permute-done((bf16[512,256]{1,0:T(8,128)(2,1)S(1)}, bf16[512,256]{1,0:T(8,128)(2,1)S(1)}, u32[]{:S(2)}, u32[]{:S(2)}) %collective-permute-start.11) | collective-permute-done | bytes 262176 | tf_op jit(solution)/shard_map/ppermute | solution.py:456
  48.9 0.8 %shard_map.167 = f32[512,256]{1,0:T(8,128)} custom-call(f32[512,256]{1,0:T(8,128)S(1)} %shard_map.165.mine, bf16[512,256]{1,0:T(8,128)(2,1)S(1)} %collective-permute-done.11.passed), custom_call_target="tpu_custom_call" | custom-call | bytes 1310720 | tf_op jit(solution)/shard_map/pallas_call | solution.py:24
  (16 shorter events, 1.5 us)
Async XLA Ops:
  0.6 18.2 %copy-start.1 = (bf16[1,2048,256]{2,1,0:T(8,128)(2,1)S(1)}, bf16[1,2048,256]{2,1,0:T(8,128)(2,1)}, u32[]{:S(2)}) copy-start(bf16[1,2048,256]{2,1,0:T(8,128)(2,1)} %param.21) | copy-start | bytes 3145732
  2.0 16.8 %copy-start = (bf16[1,2048,256]{2,1,0:T(8,128)(2,1)S(1)}, bf16[1,2048,256]{2,1,0:T(8,128)(2,1)}, u32[]{:S(2)}) copy-start(bf16[1,2048,256]{2,1,0:T(8,128)(2,1)} %param.20) | copy-start | bytes 3145732
  2.0 8.4 %collective-permute-start = (bf16[32,256]{1,0:T(8,128)(2,1)S(1)}, bf16[32,256]{1,0:T(8,128)(2,1)S(1)}, u32[]{:S(2)}, u32[]{:S(2)}) collective-permute-start(bf16[32,256]{1,0:T(8,128)(2,1)S(1)} %get-tuple-element.48), channel_id=1, source_target_pairs={{0,1},{1,0},{2,3},{3,2},{4,5},{5,4},{6,7},{7,6},{8,9},{9,8},{10,11... | collective-permute-start | bytes 49160 | tf_op jit(solution)/shard_map/ppermute | solution.py:355
  2.6 7.9 %collective-permute-start.1 = (bf16[32,256]{1,0:T(8,128)(2,1)S(1)}, bf16[32,256]{1,0:T(8,128)(2,1)S(1)}, u32[]{:S(2)}, u32[]{:S(2)}) collective-permute-start(bf16[32,256]{1,0:T(8,128)(2,1)S(1)} %get-tuple-element.49), channel_id=1, source_target_pairs={{1,2},{3,4},{5,6},{2,1},{4,3},{6,5},{9,10},{11,12},{13,14},{10,9},... | collective-permute-start | bytes 49160 | tf_op jit(solution)/shard_map/ppermute | solution.py:354
  3.2 5.4 %collective-permute-start.2 = (bf16[16,128]{1,0:T(8,128)(2,1)S(1)}, bf16[16,128]{1,0:T(8,128)(2,1)S(1)}, u32[]{:S(2)}, u32[]{:S(2)}) collective-permute-start(bf16[16,128]{1,0:T(8,128)(2,1)S(1)} %get-tuple-element.50), channel_id=1, source_target_pairs={{0,8},{8,0},{16,24},{24,16},{1,9},{9,1},{17,25},{25,17},{2,10},{10... | collective-permute-start | bytes 12296 | tf_op jit(solution)/shard_map/ppermute | solution.py:359
  5.9 4.5 %collective-permute-start.3 = (bf16[16,128]{1,0:T(8,128)(2,1)S(1)}, bf16[16,128]{1,0:T(8,128)(2,1)S(1)}, u32[]{:S(2)}, u32[]{:S(2)}) collective-permute-start(bf16[16,128]{1,0:T(8,128)(2,1)S(1)} %get-tuple-element.51), channel_id=1, source_target_pairs={{0,24},{8,16},{16,8},{24,0},{1,25},{9,17},{17,9},{25,1},{2,26},{10... | collective-permute-start | bytes 12296 | tf_op jit(solution)/shard_map/ppermute | solution.py:356
  11.6 2.4 %collective-permute-start.4 = (bf16[4,16,128]{2,1,0:T(8,128)(2,1)S(1)}, bf16[4,16,128]{2,1,0:T(8,128)(2,1)S(1)}, u32[]{:S(2)}, u32[]{:S(2)}) collective-permute-start(bf16[4,16,128]{2,1,0:T(8,128)(2,1)S(1)} %get-tuple-element.53), channel_id=1, source_target_pairs={{0,1},{1,0},{2,3},{3,2},{4,5},{5,4},{6,7},{7,6},{8,9},{9,8},{10,11... | collective-permute-start | bytes 49160 | tf_op jit(solution)/shard_map/ppermute | solution.py:386
  14.0 6.3 %collective-permute-start.5 = (bf16[32,128]{1,0:T(8,128)(2,1)S(1)}, bf16[32,128]{1,0:T(8,128)(2,1)S(1)}, u32[]{:S(2)}, u32[]{:S(2)}) collective-permute-start(bf16[32,128]{1,0:T(8,128)(2,1)S(1)} %get-tuple-element.58), channel_id=1, source_target_pairs={{0,6},{1,7},{2,4},{3,5},{4,2},{5,3},{6,0},{7,1},{8,14},{9,15},{10,... | collective-permute-start | bytes 24584 | tf_op jit(solution)/shard_map/ppermute | solution.py:396
  18.2 4.5 %collective-permute-start.6 = (bf16[32,128]{1,0:T(8,128)(2,1)S(1)}, bf16[32,128]{1,0:T(8,128)(2,1)S(1)}, u32[]{:S(2)}, u32[]{:S(2)}) collective-permute-start(bf16[32,128]{1,0:T(8,128)(2,1)S(1)} %get-tuple-element.59), channel_id=1, source_target_pairs={{0,4},{1,5},{2,6},{3,7},{4,0},{5,1},{6,2},{7,3},{8,12},{9,13},{10,... | collective-permute-start | bytes 24584 | tf_op jit(solution)/shard_map/ppermute | solution.py:396
  18.2 4.5 %collective-permute-start.7 = (bf16[32,128]{1,0:T(8,128)(2,1)S(1)}, bf16[32,128]{1,0:T(8,128)(2,1)S(1)}, u32[]{:S(2)}, u32[]{:S(2)}) collective-permute-start(bf16[32,128]{1,0:T(8,128)(2,1)S(1)} %get-tuple-element.60), channel_id=1, source_target_pairs={{0,2},{1,3},{2,0},{3,1},{4,6},{5,7},{6,4},{7,5},{8,10},{9,11},{10,... | collective-permute-start | bytes 24584 | tf_op jit(solution)/shard_map/ppermute | solution.py:396
  23.1 11.1 %collective-permute-start.8 = (bf16[512,256]{1,0:T(8,128)(2,1)S(1)}, bf16[512,256]{1,0:T(8,128)(2,1)S(1)}, u32[]{:S(2)}, u32[]{:S(2)}) collective-permute-start(bf16[512,256]{1,0:T(8,128)(2,1)S(1)} %get-tuple-element.64), channel_id=1, source_target_pairs={{0,6},{1,7},{2,4},{3,5},{4,2},{5,3},{6,0},{7,1},{8,14},{9,15},{10,... | collective-permute-start | bytes 786440 | tf_op jit(solution)/shard_map/ppermute | solution.py:396
  26.4 13.1 %collective-permute-start.9 = (bf16[512,256]{1,0:T(8,128)(2,1)S(1)}, bf16[512,256]{1,0:T(8,128)(2,1)S(1)}, u32[]{:S(2)}, u32[]{:S(2)}) collective-permute-start(bf16[512,256]{1,0:T(8,128)(2,1)S(1)} %get-tuple-element.72), channel_id=1, source_target_pairs={{0,2},{1,3},{2,0},{3,1},{4,6},{5,7},{6,4},{7,5},{8,10},{9,11},{10,... | collective-permute-start | bytes 786440 | tf_op jit(solution)/shard_map/ppermute | solution.py:396
  27.6 19.4 %collective-permute-start.10 = (bf16[512,256]{1,0:T(8,128)(2,1)S(1)}, bf16[512,256]{1,0:T(8,128)(2,1)S(1)}, u32[]{:S(2)}, u32[]{:S(2)}) collective-permute-start(bf16[512,256]{1,0:T(8,128)(2,1)S(1)} %get-tuple-element.74), channel_id=1, source_target_pairs={{0,4},{1,5},{2,6},{3,7},{4,0},{5,1},{6,2},{7,3},{8,12},{9,13},{10,... | collective-permute-start | bytes 786440 | tf_op jit(solution)/shard_map/ppermute | solution.py:396
  47.3 1.6 %collective-permute-start.11 = (bf16[512,256]{1,0:T(8,128)(2,1)S(1)}, bf16[512,256]{1,0:T(8,128)(2,1)S(1)}, u32[]{:S(2)}, u32[]{:S(2)}) collective-permute-start(bf16[512,256]{1,0:T(8,128)(2,1)S(1)} %shard_map.166), channel_id=1, source_target_pairs={{0,1},{1,0},{2,3},{3,2},{4,5},{5,4},{6,7},{7,6},{8,9},{9,8},{10,11... | collective-permute-start | bytes 786440 | tf_op jit(solution)/shard_map/ppermute | solution.py:456

commit v9 on v8

--- a/solution.py
+++ b/solution.py
@@ -132,11 +132,10 @@
     return parts[0] if len(parts) == 1 else jnp.concatenate(parts, axis=0)
 
 
-def first_body(away, order, records, hydro, rec_packed, hyd_packed):
-    hot = picked(order, away, rec_packed.shape[0] // LANES, records.shape[0])
-    rec = jnp.dot(hot, records[...], preferred_element_type=F32)
-    rec_packed[...] = shift_time(rec).astype(BF16)
-    hyd_packed[...] = jnp.dot(hot, hydro[...], preferred_element_type=F32).astype(BF16)
+def first_body(away, shifted, order, rows, packed):
+    hot = picked(order, away, packed.shape[0] // LANES, rows.shape[0])
+    out = jnp.dot(hot, rows[...], preferred_element_type=F32)
+    packed[...] = (shift_time(out) if shifted else out).astype(BF16)
 
 
 def land_body(
@@ -208,7 +207,7 @@
     give[...] = jnp.where(sec_even, both[:, 1], both[:, 0]).astype(BF16)
 
 
-def terms_body(keep, got, ids, own, *outs):
+def terms_body(keep, got, ids, packed, own, *outs):
     pairs, blocks = keep.shape[:2]
     chip = lax.axis_index("sec") // 2
     own[...] = keep[chip] + got[chip].astype(F32)
@@ -293,21 +292,22 @@
     mine[...] = mine_so_far[...] + summed(digits, blocks, basins, False)
 
 
-def late_body(aways, other, so_far, places, *refs):
+def late_body(aways, other, part, so_far, places, *refs):
     blocks, out = refs[:-1], refs[-1]
+    cut = pl.ds(part * out.shape[1], out.shape[1])
     digits = [places[away].astype(F32) for away in aways]
-    out[...] = (so_far[...] + summed(digits, blocks, out.shape[0], other)).astype(out.dtype)
-
-
-def final_body(mine, passed, out, held, sems):
-    rows = mine.shape[0]
-    parts = 2
-    size = rows // parts
+    blocks = [block.at[:, cut] for block in blocks]
+    out[...] = (so_far[:, cut] + summed(digits, blocks, out.shape[0], other)).astype(out.dtype)
+
+
+def final_body(mine, *refs):
+    passed, (out, held, sems) = refs[:-3], refs[-3:]
+    size = mine.shape[1] // len(passed)
     copies = []
-    for i in range(parts):
-        at = pl.ds(i * size, size)
-        held[at, :] = mine[at, :] + passed[at, :].astype(F32)
-        copy = pltpu.make_async_copy(held.at[at, :], out.at[at, :], sems.at[i])
+    for i, part in enumerate(passed):
+        cut = pl.ds(i * size, size)
+        held[:, cut] = mine[:, cut] + part[...].astype(F32)
+        copy = pltpu.make_async_copy(held.at[:, cut], out.at[:, cut], sems.at[i])
         copy.start()
         copies.append(copy)
     for copy in copies:
@@ -387,24 +387,26 @@
     aways = []
     for k in range(1, pairs // 2 + 1):
         aways += [k] if 2 * k == pairs else [pairs - k, k]
+    pack_first = lambda rows, shifted: call(
+        lambda *refs: first_body(aways[0], shifted, *refs),
+        [shape((cap, steps), BF16)],
+        order, rows,
+        mib=12,
+        flops=2 * cap * reaches * steps,
+        moved=reaches * steps * 2,
+    )[0]
+    rec_packed = pack_first(records[0], True)
     own_terms, *terms = call(
         terms_body,
         [shape((blocks, LANES), F32)] + [shape((blocks + PACK_ROWS, LANES), BF16)] * (pairs - 1),
-        keep, got, ids,
+        keep, got, ids, rec_packed,
         moved=reaches * 8,
     )
     forward = lambda block, away: lax.ppermute(
         block, "sec", [(i, i ^ (2 * away)) for i in range(sections)]
     )
     terms = [forward(term, flip) for flip, term in zip(range(pairs - 1, 0, -1), terms)]
-    rec_packed, hyd_packed = call(
-        lambda *refs: first_body(aways[0], *refs),
-        [shape((cap, steps), BF16)] * 2,
-        order, records[0], unit_hydro[0],
-        mib=12,
-        flops=4 * cap * reaches * steps,
-        moved=reaches * steps * 4,
-    )
+    hyd_packed = pack_first(unit_hydro[0], False)
     runoff, ready, places = call(
         lambda *refs: send_body(aways[0], *refs),
         [shape((blocks, LANES), F32), shape((cap, steps), BF16), shape(ids.shape, BF16)],
@@ -447,15 +449,18 @@
         mib=12,
         moved=basins * steps * 16,
     )
-    (theirs,) = call(
-        lambda *refs: late_body(late, True, *refs),
-        [shape((basins, steps), BF16)],
-        theirs, places, *[arrived[a] for a in late],
-        moved=basins * steps * 8,
-    )
-    passed = lax.ppermute(theirs, "sec", swap(sections))
+    parts = steps // LANES
+    passed = []
+    for part in range(parts):
+        (sums,) = call(
+            lambda *refs, part=part: late_body(late, True, part, *refs),
+            [shape((basins, LANES), BF16)],
+            theirs, places, *[arrived[a] for a in late],
+            moved=basins * steps * 4,
+        )
+        passed.append(lax.ppermute(sums, "sec", swap(sections)))
     (mine,) = call(
-        lambda *refs: late_body(late, False, *refs),
+        lambda *refs: late_body(late, False, 0, *refs),
         [shape((basins, steps), F32)],
         mine, places, *[arrived[a] for a in late],
         moved=basins * steps * 8,
@@ -463,9 +468,9 @@
     (inflow,) = call(
         final_body,
         [shape((basins, steps), F32)],
-        mine, passed,
+        mine, *passed,
         out_specs=[HBM],
-        scratch=[pltpu.VMEM((basins, steps), F32), dma((2,))],
+        scratch=[pltpu.VMEM((basins, steps), F32), dma((parts,))],
         moved=basins * steps * 10,
     )
     return (moist_out, heat_out, record_new[None], inflow[None])

time: 49.9 us -> 50.3 us (level)
  waiting for transfers between devices: 20.8 us -> 20.1 us
  Pallas kernels: 11.8 us -> 12.4 us
    ppermute x1, waiting for transfers between devices: 0.84 us -> 0.01 us  [per_device(): got = lax.ppermute(give, 'sec', swap(sections))]
    ppermute x6, waiting for transfers between devices: 16.9 us -> 17.6 us  [per_device(): lax.ppermute(block, 'sec', [(i, i ^ 2 * away) for i in range(sections)])]
    pallas_call x12 -> x14, Pallas kernels: 11.8 us -> 12.4 us  [call(): pl.pallas_call(body, out_shape=list(outs), in_specs=ins, out_specs=list(o...]
    ppermute x1 -> x2, starting transfers between devices: 0.07 us -> 0.63 us  [per_device(): passed.append(lax.ppermute(sums, 'sec', swap(sections)))]
    ppermute x1 -> x2, waiting for transfers between devices: 1.21 us -> 0.68 us  [per_device(): passed.append(lax.ppermute(sums, 'sec', swap(sections)))]
  transfers between devices with their start and end apart: 12 -> 13, of which waited for: 7 -> 8; matrix products, arithmetic and copies ran while one was open for 0% -> 0% of each run, Pallas kernels for 16% -> 17%
where the time goes in v9:
time: 50.3 us; the launch traced here: 50.1 us
  waiting for transfers between devices  20.1 us (40%)
  starting transfers between devices  16.8 us (33%)
  Pallas kernels  12.4 us (25%)
  between operations  0.77 us (2%)
    ppermute x6, waiting for transfers between devices, per_device(): lax.ppermute(block, 'sec', [(i, i ^ 2 * away) for i in range(sections)])  17.6 us
    pallas_call x14, Pallas kernels, call(): pl.pallas_call(body, out_shape=list(outs), in_specs=ins, out_specs=list(o...  12.4 us
    ppermute x6, starting transfers between devices, per_device(): lax.ppermute(block, 'sec', [(i, i ^ 2 * away) for i in range(sections)])  9.35 us
    ppermute x1, starting transfers between devices, per_device(): got_lon_near = lax.ppermute(lon_near, 'lon', swap(lons))  2.58 us
    ppermute x1, waiting for transfers between devices, per_device(): lax.ppermute(lon_far, 'lon', [(i, (i - 1 + 2 * (i % 2)) % lons) for i in...  1.83 us
    ppermute x1, starting transfers between devices, per_device(): got = lax.ppermute(give, 'sec', swap(sections))  1.58 us
    ppermute x1, starting transfers between devices, per_device(): lax.ppermute(lon_far, 'lon', [(i, (i - 1 + 2 * (i % 2)) % lons) for i in...  1.49 us
  transfers between devices with their start and end apart: 13, of which 8 were waited for; matrix products, arithmetic and copies ran while one was open for 0% of the time, Pallas kernels for 17%

profile of v9, /device:TPU:0, one launch (start us, length us, event | category | flops | bytes accessed | tf_op | source)
XLA Modules:
  0.0 50.1 jit_solution(7295040060041189779)
XLA Ops:
  0.6 1.4 %shard_map.157 = (f32[16,16,256]{2,1,0:T(8,128)S(1)}, f32[16,16,256]{2,1,0:T(8,128)S(1)}, bf16[32,256]{1,0:T(8,128)(2,1)S(1)}, bf16[32,256]{1,0:T(8,128)(2,1)S(1...) custom-call(f32[16,16,256]{2,1,0:T(8,128)} %refs_0_.3, f32[16,16,256]{2,1,0:T(8,128)} %refs_1_.1), custom_call_target="tpu_custom_call" | custom-call | bytes 524288 | tf_op jit(solution)/shard_map/pallas_call | solution.py:24
  2.0 0.5 %collective-permute-start = (bf16[32,256]{1,0:T(8,128)(2,1)S(1)}, bf16[32,256]{1,0:T(8,128)(2,1)S(1)}, u32[]{:S(2)}, u32[]{:S(2)}) collective-permute-start(bf16[32,256]{1,0:T(8,128)(2,1)S(1)} %get-tuple-element.46), channel_id=1, source_target_pairs={{0,1},{1,0},{2,3},{3,2},{4,5},{5,4},{6,7},{7,6},{8,9},{9,8},{10,11... | collective-permute-start | bytes 49160 | tf_op jit(solution)/shard_map/ppermute | solution.py:355
  2.6 0.7 %collective-permute-start.1 = (bf16[32,256]{1,0:T(8,128)(2,1)S(1)}, bf16[32,256]{1,0:T(8,128)(2,1)S(1)}, u32[]{:S(2)}, u32[]{:S(2)}) collective-permute-start(bf16[32,256]{1,0:T(8,128)(2,1)S(1)} %get-tuple-element.47), channel_id=1, source_target_pairs={{1,2},{3,4},{5,6},{2,1},{4,3},{6,5},{9,10},{11,12},{13,14},{10,9},... | collective-permute-start | bytes 49160 | tf_op jit(solution)/shard_map/ppermute | solution.py:354
  3.2 2.6 %collective-permute-start.2 = (bf16[16,128]{1,0:T(8,128)(2,1)S(1)}, bf16[16,128]{1,0:T(8,128)(2,1)S(1)}, u32[]{:S(2)}, u32[]{:S(2)}) collective-permute-start(bf16[16,128]{1,0:T(8,128)(2,1)S(1)} %get-tuple-element.48), channel_id=1, source_target_pairs={{0,8},{8,0},{16,24},{24,16},{1,9},{9,1},{17,25},{25,17},{2,10},{10... | collective-permute-start | bytes 12296 | tf_op jit(solution)/shard_map/ppermute | solution.py:359
  5.8 1.5 %collective-permute-start.3 = (bf16[16,128]{1,0:T(8,128)(2,1)S(1)}, bf16[16,128]{1,0:T(8,128)(2,1)S(1)}, u32[]{:S(2)}, u32[]{:S(2)}) collective-permute-start(bf16[16,128]{1,0:T(8,128)(2,1)S(1)} %get-tuple-element.49), channel_id=1, source_target_pairs={{0,24},{8,16},{16,8},{24,0},{1,25},{9,17},{17,9},{25,1},{2,26},{10... | collective-permute-start | bytes 12296 | tf_op jit(solution)/shard_map/ppermute | solution.py:356
  7.3 1.2 %shard_map.156 = (s32[16,128]{1,0:T(8,128)S(1)}, bf16[4,16,128]{2,1,0:T(8,128)(2,1)S(1)}, f32[16,16,256]{2,1,0:T(8,128)S(1)}, f32[16,16,256]{2,1,0:T(8,128)S(1)}...) custom-call(s32[1,1,8]{2,1,0:T(1,128)} %refs_0_.2, s32[32,128]{1,0:T(8,128)} %bitcast.12, ...), custom_call_target="tpu_custom_call" | custom-call | bytes 524288 | tf_op jit(solution)/shard_map/pallas_call | solution.py:24
  8.5 1.8 %collective-permute-done.3.lon_far = bf16[16,128]{1,0:T(8,128)(2,1)S(1)} collective-permute-done((bf16[16,128]{1,0:T(8,128)(2,1)S(1)}, bf16[16,128]{1,0:T(8,128)(2,1)S(1)}, u32[]{:S(2)}, u32[]{:S(2)}) %collective-permute-start.3) | collective-permute-done | bytes 4128 | tf_op jit(solution)/shard_map/ppermute | solution.py:356
  10.3 1.1 %shard_map.158 = (f32[16,16,256]{2,1,0:T(8,128)S(1)}, f32[16,16,256]{2,1,0:T(8,128)S(1)}, f32[4,16,128]{2,1,0:T(8,128)S(1)}, bf16[4,16,128]{2,1,0:T(8,128)(2,1)S(1)}) custom-call(f32[16,16,256]{2,1,0:T(8,128)S(1)} %get-tuple-element.39.moist, f32[16,16,256]{2,1,0:T(8,128)S(1)} %get-tuple-element.40.heat, f32[16,16,256]{2,1,0:T(8,128)S(1)} %get-tuple-element.41.moist_k, ...), custom_call_target="tpu_custom_call" | custom-call | bytes 1572864 | tf_op jit(solution)/shard_map/pallas_call | solution.py:24
  11.4 1.6 %collective-permute-start.4 = (bf16[4,16,128]{2,1,0:T(8,128)(2,1)S(1)}, bf16[4,16,128]{2,1,0:T(8,128)(2,1)S(1)}, u32[]{:S(2)}, u32[]{:S(2)}) collective-permute-start(bf16[4,16,128]{2,1,0:T(8,128)(2,1)S(1)} %get-tuple-element.51), channel_id=1, source_target_pairs={{0,1},{1,0},{2,3},{3,2},{4,5},{5,4},{6,7},{7,6},{8,9},{9,8},{10,11... | collective-permute-start | bytes 49160 | tf_op jit(solution)/shard_map/ppermute | solution.py:386
  13.0 0.9 %shard_map.159.packed.refs_3_ = bf16[512,256]{1,0:T(8,128)(2,1)S(1)} custom-call(s32[16,128]{1,0:T(8,128)S(1)} %get-tuple-element.38.refs_0_.refs_1_.refs_3_, bf16[2048,256]{1,0:T(8,128)(2,1)S(1)} %bitcast.7), custom_call_target="tpu_custom_call" | custom-call | flops 536870912 | bytes 1048576 | tf_op jit(solution)/shard_map/pallas_call | solution.py:24
  14.0 4.2 %collective-permute-start.5 = (bf16[32,128]{1,0:T(8,128)(2,1)S(1)}, bf16[32,128]{1,0:T(8,128)(2,1)S(1)}, u32[]{:S(2)}, u32[]{:S(2)}) collective-permute-start(bf16[32,128]{1,0:T(8,128)(2,1)S(1)} %get-tuple-element.54), channel_id=1, source_target_pairs={{0,6},{1,7},{2,4},{3,5},{4,2},{5,3},{6,0},{7,1},{8,14},{9,15},{10,... | collective-permute-start | bytes 24584 | tf_op jit(solution)/shard_map/ppermute | solution.py:405
  18.2 0.6 %collective-permute-start.7 = (bf16[32,128]{1,0:T(8,128)(2,1)S(1)}, bf16[32,128]{1,0:T(8,128)(2,1)S(1)}, u32[]{:S(2)}, u32[]{:S(2)}) collective-permute-start(bf16[32,128]{1,0:T(8,128)(2,1)S(1)} %get-tuple-element.56), channel_id=1, source_target_pairs={{0,2},{1,3},{2,0},{3,1},{4,6},{5,7},{6,4},{7,5},{8,10},{9,11},{10,... | collective-permute-start | bytes 24584 | tf_op jit(solution)/shard_map/ppermute | solution.py:405
  18.8 0.8 %shard_map.161.refs_4_ = bf16[512,256]{1,0:T(8,128)(2,1)S(1)} custom-call(s32[16,128]{1,0:T(8,128)S(1)} %get-tuple-element.38.refs_0_.refs_1_.refs_3_, bf16[2048,256]{1,0:T(8,128)(2,1)S(1)} %bitcast.9), custom_call_target="tpu_custom_call" | custom-call | flops 536870912 | bytes 1048576 | tf_op jit(solution)/shard_map/pallas_call | solution.py:24
  19.8 2.9 %collective-permute-done.6.refs_6_ = bf16[32,128]{1,0:T(8,128)(2,1)S(1)} collective-permute-done((bf16[32,128]{1,0:T(8,128)(2,1)S(1)}, bf16[32,128]{1,0:T(8,128)(2,1)S(1)}, u32[]{:S(2)}, u32[]{:S(2)}) %collective-permute-start.6) | collective-permute-done | bytes 8224 | tf_op jit(solution)/shard_map/ppermute | solution.py:405
  23.1 1.5 %collective-permute-start.8 = (bf16[512,256]{1,0:T(8,128)(2,1)S(1)}, bf16[512,256]{1,0:T(8,128)(2,1)S(1)}, u32[]{:S(2)}, u32[]{:S(2)}) collective-permute-start(bf16[512,256]{1,0:T(8,128)(2,1)S(1)} %get-tuple-element.60), channel_id=1, source_target_pairs={{0,6},{1,7},{2,4},{3,5},{4,2},{5,3},{6,0},{7,1},{8,14},{9,15},{10,... | collective-permute-start | bytes 786440 | tf_op jit(solution)/shard_map/ppermute | solution.py:405
  24.6 1.7 %shard_map.163 = (bf16[2048,256]{1,0:T(8,128)(2,1)S(1)}, bf16[512,256]{1,0:T(8,128)(2,1)S(1)}, bf16[512,256]{1,0:T(8,128)(2,1)S(1)}) custom-call(f32[16,128]{1,0:T(8,128)S(1)} %get-tuple-element.57.refs_0_, bf16[2048,256]{1,0:T(8,128)(2,1)S(1)} %bitcast.8, bf16[2048,256]{1,0:T(8,128)(2,1)S(1)} %bitcast.10, ...), custom_call_target="tpu_custom_call" | custom-call | flops 536870912 | bytes 4194304 | tf_op jit(solution)/shard_map/pallas_call | solution.py:24
  26.4 1.2 %collective-permute-start.9 = (bf16[512,256]{1,0:T(8,128)(2,1)S(1)}, bf16[512,256]{1,0:T(8,128)(2,1)S(1)}, u32[]{:S(2)}, u32[]{:S(2)}) collective-permute-start(bf16[512,256]{1,0:T(8,128)(2,1)S(1)} %get-tuple-element.68), channel_id=1, source_target_pairs={{0,2},{1,3},{2,0},{3,1},{4,6},{5,7},{6,4},{7,5},{8,10},{9,11},{10,... | collective-permute-start | bytes 786440 | tf_op jit(solution)/shard_map/ppermute | solution.py:405
  27.5 1.8 %collective-permute-start.10 = (bf16[512,256]{1,0:T(8,128)(2,1)S(1)}, bf16[512,256]{1,0:T(8,128)(2,1)S(1)}, u32[]{:S(2)}, u32[]{:S(2)}) collective-permute-start(bf16[512,256]{1,0:T(8,128)(2,1)S(1)} %get-tuple-element.70), channel_id=1, source_target_pairs={{0,4},{1,5},{2,6},{3,7},{4,0},{5,1},{6,2},{7,3},{8,12},{9,13},{10,... | collective-permute-start | bytes 786440 | tf_op jit(solution)/shard_map/ppermute | solution.py:405
  29.3 4.8 %collective-permute-done.8.refs_3_ = bf16[512,256]{1,0:T(8,128)(2,1)S(1)} collective-permute-done((bf16[512,256]{1,0:T(8,128)(2,1)S(1)}, bf16[512,256]{1,0:T(8,128)(2,1)S(1)}, u32[]{:S(2)}, u32[]{:S(2)}) %collective-permute-start.8) | collective-permute-done | bytes 262176 | tf_op jit(solution)/shard_map/ppermute | solution.py:405
  34.2 2.7 %shard_map.164 = (bf16[2048,256]{1,0:T(8,128)(2,1)}, f32[16,16,256]{2,1,0:T(8,128)}, f32[16,16,256]{2,1,0:T(8,128)}, f32[512,256]{1,0:T(8,128)S(1)}, f32[512,256]{1,0:T(8,128)S(1)}) custom-call(s32[16,128]{1,0:T(8,128)S(1)} %get-tuple-element.38.refs_0_.refs_1_.refs_3_, bf16[2048,256]{1,0:T(8,128)(2,1)S(1)} %get-tuple-element.58.refs_1_, ...), custom_call_target="tpu_custom_call" | custom-call | flops 536870912 | bytes 2097152 | tf_op jit(solution)/shard_map/pallas_call | solution.py:24
  36.9 2.8 %collective-permute-done.9.refs_3_ = bf16[512,256]{1,0:T(8,128)(2,1)S(1)} collective-permute-done((bf16[512,256]{1,0:T(8,128)(2,1)S(1)}, bf16[512,256]{1,0:T(8,128)(2,1)S(1)}, u32[]{:S(2)}, u32[]{:S(2)}) %collective-permute-start.9) | collective-permute-done | bytes 262176 | tf_op jit(solution)/shard_map/ppermute | solution.py:405
  40.2 6.9 %collective-permute-done.10.refs_2_ = bf16[512,256]{1,0:T(8,128)(2,1)S(1)} collective-permute-done((bf16[512,256]{1,0:T(8,128)(2,1)S(1)}, bf16[512,256]{1,0:T(8,128)(2,1)S(1)}, u32[]{:S(2)}, u32[]{:S(2)}) %collective-permute-start.10) | collective-permute-done | bytes 262176 | tf_op jit(solution)/shard_map/ppermute | solution.py:405
  47.7 0.6 %collective-permute-start.12 = (bf16[512,128]{1,0:T(8,128)(2,1)S(1)}, bf16[512,128]{1,0:T(8,128)(2,1)S(1)}, u32[]{:S(2)}, u32[]{:S(2)}) collective-permute-start(bf16[512,128]{1,0:T(8,128)(2,1)S(1)} %shard_map.168), channel_id=1, source_target_pairs={{0,1},{1,0},{2,3},{3,2},{4,5},{5,4},{6,7},{7,6},{8,9},{9,8},{10,11... | collective-permute-start | bytes 393224 | tf_op jit(solution)/shard_map/ppermute | solution.py:461
  49.3 0.8 %shard_map.169 = f32[512,256]{1,0:T(8,128)} custom-call(f32[512,256]{1,0:T(8,128)S(1)} %shard_map.166.mine, bf16[512,128]{1,0:T(8,128)(2,1)S(1)} %collective-permute-done.11.refs_0_, bf16[512,128]{1,0:T(8,128)(2,1)S(1)} %collective-permute-done.12.refs_1_), custom_call_target="tpu_custom_call" | custom-call | bytes 1310720 | tf_op jit(solution)/shard_map/pallas_call | solution.py:24
  (20 shorter events, 2.7 us)
Async XLA Ops:
  0.6 12.4 %copy-start = (bf16[1,2048,256]{2,1,0:T(8,128)(2,1)S(1)}, bf16[1,2048,256]{2,1,0:T(8,128)(2,1)}, u32[]{:S(2)}) copy-start(bf16[1,2048,256]{2,1,0:T(8,128)(2,1)} %param.20) | copy-start | bytes 3145732
  2.0 8.3 %collective-permute-start = (bf16[32,256]{1,0:T(8,128)(2,1)S(1)}, bf16[32,256]{1,0:T(8,128)(2,1)S(1)}, u32[]{:S(2)}, u32[]{:S(2)}) collective-permute-start(bf16[32,256]{1,0:T(8,128)(2,1)S(1)} %get-tuple-element.46), channel_id=1, source_target_pairs={{0,1},{1,0},{2,3},{3,2},{4,5},{5,4},{6,7},{7,6},{8,9},{9,8},{10,11... | collective-permute-start | bytes 49160 | tf_op jit(solution)/shard_map/ppermute | solution.py:355
  2.6 7.7 %collective-permute-start.1 = (bf16[32,256]{1,0:T(8,128)(2,1)S(1)}, bf16[32,256]{1,0:T(8,128)(2,1)S(1)}, u32[]{:S(2)}, u32[]{:S(2)}) collective-permute-start(bf16[32,256]{1,0:T(8,128)(2,1)S(1)} %get-tuple-element.47), channel_id=1, source_target_pairs={{1,2},{3,4},{5,6},{2,1},{4,3},{6,5},{9,10},{11,12},{13,14},{10,9},... | collective-permute-start | bytes 49160 | tf_op jit(solution)/shard_map/ppermute | solution.py:354
  3.2 5.2 %collective-permute-start.2 = (bf16[16,128]{1,0:T(8,128)(2,1)S(1)}, bf16[16,128]{1,0:T(8,128)(2,1)S(1)}, u32[]{:S(2)}, u32[]{:S(2)}) collective-permute-start(bf16[16,128]{1,0:T(8,128)(2,1)S(1)} %get-tuple-element.48), channel_id=1, source_target_pairs={{0,8},{8,0},{16,24},{24,16},{1,9},{9,1},{17,25},{25,17},{2,10},{10... | collective-permute-start | bytes 12296 | tf_op jit(solution)/shard_map/ppermute | solution.py:359
  5.8 4.5 %collective-permute-start.3 = (bf16[16,128]{1,0:T(8,128)(2,1)S(1)}, bf16[16,128]{1,0:T(8,128)(2,1)S(1)}, u32[]{:S(2)}, u32[]{:S(2)}) collective-permute-start(bf16[16,128]{1,0:T(8,128)(2,1)S(1)} %get-tuple-element.49), channel_id=1, source_target_pairs={{0,24},{8,16},{16,8},{24,0},{1,25},{9,17},{17,9},{25,1},{2,26},{10... | collective-permute-start | bytes 12296 | tf_op jit(solution)/shard_map/ppermute | solution.py:356
  11.4 2.5 %collective-permute-start.4 = (bf16[4,16,128]{2,1,0:T(8,128)(2,1)S(1)}, bf16[4,16,128]{2,1,0:T(8,128)(2,1)S(1)}, u32[]{:S(2)}, u32[]{:S(2)}) collective-permute-start(bf16[4,16,128]{2,1,0:T(8,128)(2,1)S(1)} %get-tuple-element.51), channel_id=1, source_target_pairs={{0,1},{1,0},{2,3},{3,2},{4,5},{5,4},{6,7},{7,6},{8,9},{9,8},{10,11... | collective-permute-start | bytes 49160 | tf_op jit(solution)/shard_map/ppermute | solution.py:386
  13.0 5.8 %copy-start.1 = (bf16[1,2048,256]{2,1,0:T(8,128)(2,1)S(1)}, bf16[1,2048,256]{2,1,0:T(8,128)(2,1)}, u32[]{:S(2)}) copy-start(bf16[1,2048,256]{2,1,0:T(8,128)(2,1)} %param.21) | copy-start | bytes 3145732
  14.0 5.8 %collective-permute-start.5 = (bf16[32,128]{1,0:T(8,128)(2,1)S(1)}, bf16[32,128]{1,0:T(8,128)(2,1)S(1)}, u32[]{:S(2)}, u32[]{:S(2)}) collective-permute-start(bf16[32,128]{1,0:T(8,128)(2,1)S(1)} %get-tuple-element.54), channel_id=1, source_target_pairs={{0,6},{1,7},{2,4},{3,5},{4,2},{5,3},{6,0},{7,1},{8,14},{9,15},{10,... | collective-permute-start | bytes 24584 | tf_op jit(solution)/shard_map/ppermute | solution.py:405
  18.2 4.5 %collective-permute-start.6 = (bf16[32,128]{1,0:T(8,128)(2,1)S(1)}, bf16[32,128]{1,0:T(8,128)(2,1)S(1)}, u32[]{:S(2)}, u32[]{:S(2)}) collective-permute-start(bf16[32,128]{1,0:T(8,128)(2,1)S(1)} %get-tuple-element.55), channel_id=1, source_target_pairs={{0,4},{1,5},{2,6},{3,7},{4,0},{5,1},{6,2},{7,3},{8,12},{9,13},{10,... | collective-permute-start | bytes 24584 | tf_op jit(solution)/shard_map/ppermute | solution.py:405
  18.2 4.5 %collective-permute-start.7 = (bf16[32,128]{1,0:T(8,128)(2,1)S(1)}, bf16[32,128]{1,0:T(8,128)(2,1)S(1)}, u32[]{:S(2)}, u32[]{:S(2)}) collective-permute-start(bf16[32,128]{1,0:T(8,128)(2,1)S(1)} %get-tuple-element.56), channel_id=1, source_target_pairs={{0,2},{1,3},{2,0},{3,1},{4,6},{5,7},{6,4},{7,5},{8,10},{9,11},{10,... | collective-permute-start | bytes 24584 | tf_op jit(solution)/shard_map/ppermute | solution.py:405
  23.1 11.1 %collective-permute-start.8 = (bf16[512,256]{1,0:T(8,128)(2,1)S(1)}, bf16[512,256]{1,0:T(8,128)(2,1)S(1)}, u32[]{:S(2)}, u32[]{:S(2)}) collective-permute-start(bf16[512,256]{1,0:T(8,128)(2,1)S(1)} %get-tuple-element.60), channel_id=1, source_target_pairs={{0,6},{1,7},{2,4},{3,5},{4,2},{5,3},{6,0},{7,1},{8,14},{9,15},{10,... | collective-permute-start | bytes 786440 | tf_op jit(solution)/shard_map/ppermute | solution.py:405
  26.4 13.4 %collective-permute-start.9 = (bf16[512,256]{1,0:T(8,128)(2,1)S(1)}, bf16[512,256]{1,0:T(8,128)(2,1)S(1)}, u32[]{:S(2)}, u32[]{:S(2)}) collective-permute-start(bf16[512,256]{1,0:T(8,128)(2,1)S(1)} %get-tuple-element.68), channel_id=1, source_target_pairs={{0,2},{1,3},{2,0},{3,1},{4,6},{5,7},{6,4},{7,5},{8,10},{9,11},{10,... | collective-permute-start | bytes 786440 | tf_op jit(solution)/shard_map/ppermute | solution.py:405
  27.5 19.5 %collective-permute-start.10 = (bf16[512,256]{1,0:T(8,128)(2,1)S(1)}, bf16[512,256]{1,0:T(8,128)(2,1)S(1)}, u32[]{:S(2)}, u32[]{:S(2)}) collective-permute-start(bf16[512,256]{1,0:T(8,128)(2,1)S(1)} %get-tuple-element.70), channel_id=1, source_target_pairs={{0,4},{1,5},{2,6},{3,7},{4,0},{5,1},{6,2},{7,3},{8,12},{9,13},{10,... | collective-permute-start | bytes 786440 | tf_op jit(solution)/shard_map/ppermute | solution.py:405
  47.4 1.4 %collective-permute-start.11 = (bf16[512,128]{1,0:T(8,128)(2,1)S(1)}, bf16[512,128]{1,0:T(8,128)(2,1)S(1)}, u32[]{:S(2)}, u32[]{:S(2)}) collective-permute-start(bf16[512,128]{1,0:T(8,128)(2,1)S(1)} %shard_map.167), channel_id=1, source_target_pairs={{0,1},{1,0},{2,3},{3,2},{4,5},{5,4},{6,7},{7,6},{8,9},{9,8},{10,11... | collective-permute-start | bytes 393224 | tf_op jit(solution)/shard_map/ppermute | solution.py:461
  47.7 1.5 %collective-permute-start.12 = (bf16[512,128]{1,0:T(8,128)(2,1)S(1)}, bf16[512,128]{1,0:T(8,128)(2,1)S(1)}, u32[]{:S(2)}, u32[]{:S(2)}) collective-permute-start(bf16[512,128]{1,0:T(8,128)(2,1)S(1)} %shard_map.168), channel_id=1, source_target_pairs={{0,1},{1,0},{2,3},{3,2},{4,5},{5,4},{6,7},{7,6},{8,9},{9,8},{10,11... | collective-permute-start | bytes 393224 | tf_op jit(solution)/shard_map/ppermute | solution.py:461

commit v10 on v8

--- a/solution.py
+++ b/solution.py
@@ -148,11 +148,13 @@
     col = lax.broadcasted_iota(I32, (rows, cols), 1)
     sec_even = parity("sec") == 0
     lon_even = parity("lon") == 0
-    south_all = jnp.where(sec_even, sec_near[...].astype(F32), sec_far[...].astype(F32))
-    north_all = jnp.where(sec_even, sec_far[...].astype(F32), sec_near[...].astype(F32))
-    lon = lax.axis_index("lon")
-    outer = (lon == 0) | (lon == lax.axis_size("lon") - 1)
-    lon_beyond = jnp.where(outer, 0.0, lon_far[...].astype(F32))
+    outer = lambda axis: (lax.axis_index(axis) == 0) | (
+        lax.axis_index(axis) == lax.axis_size(axis) - 1
+    )
+    sec_beyond = jnp.where(outer("sec"), 0.0, sec_far[...].astype(F32))
+    lon_beyond = jnp.where(outer("lon"), 0.0, lon_far[...].astype(F32))
+    south_all = jnp.where(sec_even, sec_near[...].astype(F32), sec_beyond)
+    north_all = jnp.where(sec_even, sec_beyond, sec_near[...].astype(F32))
     east_all = jnp.where(lon_even, lon_near[...].astype(F32), lon_beyond)
     west_all = jnp.where(lon_even, lon_beyond, lon_near[...].astype(F32))
     for f, (x_ref, k_ref, top, out) in enumerate(
@@ -348,14 +350,10 @@
         moved=moisture.size * 8,
     )
     swap = lambda count: [(i, i ^ 1) for i in range(count)]
-    between = lambda count: [(i, i + 1) for i in range(1, count - 1, 2)] + [
-        (i + 1, i) for i in range(1, count - 1, 2)
-    ]
+    between = lambda count: [(i, (i - 1 + 2 * (i % 2)) % count) for i in range(count)]
     got_sec_far = lax.ppermute(sec_far, "sec", between(sections))
     got_sec_near = lax.ppermute(sec_near, "sec", swap(sections))
-    got_lon_far = lax.ppermute(
-        lon_far, "lon", [(i, (i - 1 + 2 * (i % 2)) % lons) for i in range(lons)]
-    )
+    got_lon_far = lax.ppermute(lon_far, "lon", between(lons))
     got_lon_near = lax.ppermute(lon_near, "lon", swap(lons))
 
     land = [moist_cond, heat_cond, rain, surface_flux, cell_reach]

time: 49.9 us -> 50.1 us (level)
  starting transfers between devices: 16.3 us -> 17.3 us
  waiting for transfers between devices: 20.8 us -> 20 us
    ppermute x1, starting transfers between devices: 0.65 us -> 4.71 us  [per_device(): got_sec_far = lax.ppermute(sec_far, 'sec', between(sections))]
    ppermute x1, starting transfers between devices: 1.58 us -> 0.07 us  [per_device(): got = lax.ppermute(give, 'sec', swap(sections))]
    ppermute x1, starting transfers between devices: 2.71 us -> 1.49 us  [per_device(): got_lon_near = lax.ppermute(lon_near, 'lon', swap(lons))]
    ppermute x6, waiting for transfers between devices: 16.9 us -> 15.8 us  [per_device(): lax.ppermute(block, 'sec', [(i, i ^ 2 * away) for i in range(sections)])]
where the time goes in v10:
time: 50.1 us; the launch traced here: 49.9 us
  waiting for transfers between devices  20 us (40%)
  starting transfers between devices  17.3 us (35%)
  Pallas kernels  11.8 us (24%)
  between operations  0.78 us (2%)
    ppermute x6, waiting for transfers between devices, per_device(): lax.ppermute(block, 'sec', [(i, i ^ 2 * away) for i in range(sections)])  15.8 us
    pallas_call x12, Pallas kernels, call(): pl.pallas_call(body, out_shape=list(outs), in_specs=ins, out_specs=list(o...  11.8 us
    ppermute x6, starting transfers between devices, per_device(): lax.ppermute(block, 'sec', [(i, i ^ 2 * away) for i in range(sections)])  8.96 us
    ppermute x1, starting transfers between devices, per_device(): got_sec_far = lax.ppermute(sec_far, 'sec', between(sections))  4.71 us
    ppermute x1, waiting for transfers between devices, per_device(): got_lon_far = lax.ppermute(lon_far, 'lon', between(lons))  1.83 us
    ppermute x1, starting transfers between devices, per_device(): got_lon_near = lax.ppermute(lon_near, 'lon', swap(lons))  1.49 us
    ppermute x1, starting transfers between devices, per_device(): got_lon_far = lax.ppermute(lon_far, 'lon', between(lons))  1.49 us
    ppermute x1, waiting for transfers between devices, per_device(): passed = lax.ppermute(theirs, 'sec', swap(sections))  1.22 us
  transfers between devices with their start and end apart: 12, of which 7 were waited for; matrix products, arithmetic and copies ran while one was open for 0% of the time, Pallas kernels for 16%

profile of v10, /device:TPU:0, one launch (start us, length us, event | category | flops | bytes accessed | tf_op | source)
XLA Modules:
  0.0 49.9 jit_solution(16227125053748945367)
XLA Ops:
  0.6 1.4 %shard_map.157 = (f32[16,16,256]{2,1,0:T(8,128)S(1)}, f32[16,16,256]{2,1,0:T(8,128)S(1)}, bf16[32,256]{1,0:T(8,128)(2,1)S(1)}, bf16[32,256]{1,0:T(8,128)(2,1)S(1...) custom-call(f32[16,16,256]{2,1,0:T(8,128)} %refs_0_.3, f32[16,16,256]{2,1,0:T(8,128)} %refs_1_.1), custom_call_target="tpu_custom_call" | custom-call | bytes 524288 | tf_op jit(solution)/shard_map/pallas_call | solution.py:24
  2.0 0.5 %collective-permute-start = (bf16[32,256]{1,0:T(8,128)(2,1)S(1)}, bf16[32,256]{1,0:T(8,128)(2,1)S(1)}, u32[]{:S(2)}, u32[]{:S(2)}) collective-permute-start(bf16[32,256]{1,0:T(8,128)(2,1)S(1)} %get-tuple-element.48), channel_id=1, source_target_pairs={{0,1},{1,0},{2,3},{3,2},{4,5},{5,4},{6,7},{7,6},{8,9},{9,8},{10,11... | collective-permute-start | bytes 49160 | tf_op jit(solution)/shard_map/ppermute | solution.py:355
  2.6 4.7 %collective-permute-start.1 = (bf16[32,256]{1,0:T(8,128)(2,1)S(1)}, bf16[32,256]{1,0:T(8,128)(2,1)S(1)}, u32[]{:S(2)}, u32[]{:S(2)}) collective-permute-start(bf16[32,256]{1,0:T(8,128)(2,1)S(1)} %get-tuple-element.49), channel_id=1, source_target_pairs={{0,7},{1,2},{2,1},{3,4},{4,3},{5,6},{6,5},{7,0},{8,15},{9,10},{10,... | collective-permute-start | bytes 49160 | tf_op jit(solution)/shard_map/ppermute | solution.py:354
  7.3 1.5 %collective-permute-start.2 = (bf16[16,128]{1,0:T(8,128)(2,1)S(1)}, bf16[16,128]{1,0:T(8,128)(2,1)S(1)}, u32[]{:S(2)}, u32[]{:S(2)}) collective-permute-start(bf16[16,128]{1,0:T(8,128)(2,1)S(1)} %get-tuple-element.50), channel_id=1, source_target_pairs={{0,8},{8,0},{16,24},{24,16},{1,9},{9,1},{17,25},{25,17},{2,10},{10... | collective-permute-start | bytes 12296 | tf_op jit(solution)/shard_map/ppermute | solution.py:357
  8.8 1.5 %collective-permute-start.3 = (bf16[16,128]{1,0:T(8,128)(2,1)S(1)}, bf16[16,128]{1,0:T(8,128)(2,1)S(1)}, u32[]{:S(2)}, u32[]{:S(2)}) collective-permute-start(bf16[16,128]{1,0:T(8,128)(2,1)S(1)} %get-tuple-element.51), channel_id=1, source_target_pairs={{0,24},{8,16},{16,8},{24,0},{1,25},{9,17},{17,9},{25,1},{2,26},{10... | collective-permute-start | bytes 12296 | tf_op jit(solution)/shard_map/ppermute | solution.py:356
  10.3 1.2 %shard_map.156 = (s32[16,128]{1,0:T(8,128)S(1)}, bf16[4,16,128]{2,1,0:T(8,128)(2,1)S(1)}, f32[16,16,256]{2,1,0:T(8,128)S(1)}, f32[16,16,256]{2,1,0:T(8,128)S(1)}...) custom-call(s32[1,1,8]{2,1,0:T(1,128)} %refs_0_.2, s32[32,128]{1,0:T(8,128)} %bitcast.12, ...), custom_call_target="tpu_custom_call" | custom-call | bytes 524288 | tf_op jit(solution)/shard_map/pallas_call | solution.py:24
  11.4 1.8 %collective-permute-done.3.lon_far = bf16[16,128]{1,0:T(8,128)(2,1)S(1)} collective-permute-done((bf16[16,128]{1,0:T(8,128)(2,1)S(1)}, bf16[16,128]{1,0:T(8,128)(2,1)S(1)}, u32[]{:S(2)}, u32[]{:S(2)}) %collective-permute-start.3) | collective-permute-done | bytes 4128 | tf_op jit(solution)/shard_map/ppermute | solution.py:356
  13.3 1.1 %shard_map.158 = (f32[16,16,256]{2,1,0:T(8,128)S(1)}, f32[16,16,256]{2,1,0:T(8,128)S(1)}, f32[4,16,128]{2,1,0:T(8,128)S(1)}, bf16[4,16,128]{2,1,0:T(8,128)(2,1)S(1)}) custom-call(f32[16,16,256]{2,1,0:T(8,128)S(1)} %get-tuple-element.41.moist, f32[16,16,256]{2,1,0:T(8,128)S(1)} %get-tuple-element.42.heat, f32[16,16,256]{2,1,0:T(8,128)S(1)} %get-tuple-element.43.moist_k, ...), custom_call_target="tpu_custom_call" | custom-call | bytes 1572864 | tf_op jit(solution)/shard_map/pallas_call | solution.py:24
  14.5 1.2 %collective-permute-done.4.got = bf16[4,16,128]{2,1,0:T(8,128)(2,1)S(1)} collective-permute-done((bf16[4,16,128]{2,1,0:T(8,128)(2,1)S(1)}, bf16[4,16,128]{2,1,0:T(8,128)(2,1)S(1)}, u32[]{:S(2)}, u32[]{:S(2)}) %collective-permute-start.4) | collective-permute-done | bytes 16416 | tf_op jit(solution)/shard_map/ppermute | solution.py:384
  15.7 0.5 %collective-permute-start.5 = (bf16[32,128]{1,0:T(8,128)(2,1)S(1)}, bf16[32,128]{1,0:T(8,128)(2,1)S(1)}, u32[]{:S(2)}, u32[]{:S(2)}) collective-permute-start(bf16[32,128]{1,0:T(8,128)(2,1)S(1)} %get-tuple-element.58), channel_id=1, source_target_pairs={{0,6},{1,7},{2,4},{3,5},{4,2},{5,3},{6,0},{7,1},{8,14},{9,15},{10,... | collective-permute-start | bytes 24584 | tf_op jit(solution)/shard_map/ppermute | solution.py:394
  16.2 3.9 %collective-permute-start.7 = (bf16[32,128]{1,0:T(8,128)(2,1)S(1)}, bf16[32,128]{1,0:T(8,128)(2,1)S(1)}, u32[]{:S(2)}, u32[]{:S(2)}) collective-permute-start(bf16[32,128]{1,0:T(8,128)(2,1)S(1)} %get-tuple-element.60), channel_id=1, source_target_pairs={{0,2},{1,3},{2,0},{3,1},{4,6},{5,7},{6,4},{7,5},{8,10},{9,11},{10,... | collective-permute-start | bytes 24584 | tf_op jit(solution)/shard_map/ppermute | solution.py:394
  20.1 1.4 %shard_map.160 = (bf16[512,256]{1,0:T(8,128)(2,1)S(1)}, bf16[512,256]{1,0:T(8,128)(2,1)S(1)}) custom-call(s32[16,128]{1,0:T(8,128)S(1)} %get-tuple-element.40.refs_0_.refs_1_.refs_3_, bf16[2048,256]{1,0:T(8,128)(2,1)S(1)} %bitcast.7, bf16[2048,256]{1,0:T(8,128)(2,1)S(1)} %bitcast.9), custom_call_target="tpu_custom_call" | custom-call | flops 1073741824 | bytes 2097152 | tf_op jit(solution)/shard_map/pallas_call | solution.py:24
  21.8 0.4 shard_map.161
  22.1 2.4 %collective-permute-start.8 = (bf16[512,256]{1,0:T(8,128)(2,1)S(1)}, bf16[512,256]{1,0:T(8,128)(2,1)S(1)}, u32[]{:S(2)}, u32[]{:S(2)}) collective-permute-start(bf16[512,256]{1,0:T(8,128)(2,1)S(1)} %get-tuple-element.64), channel_id=1, source_target_pairs={{0,6},{1,7},{2,4},{3,5},{4,2},{5,3},{6,0},{7,1},{8,14},{9,15},{10,... | collective-permute-start | bytes 786440 | tf_op jit(solution)/shard_map/ppermute | solution.py:394
  24.6 1.7 %shard_map.162 = (bf16[2048,256]{1,0:T(8,128)(2,1)S(1)}, bf16[512,256]{1,0:T(8,128)(2,1)S(1)}, bf16[512,256]{1,0:T(8,128)(2,1)S(1)}) custom-call(f32[16,128]{1,0:T(8,128)S(1)} %get-tuple-element.61.refs_0_, bf16[2048,256]{1,0:T(8,128)(2,1)S(1)} %bitcast.8, bf16[2048,256]{1,0:T(8,128)(2,1)S(1)} %bitcast.10, ...), custom_call_target="tpu_custom_call" | custom-call | flops 536870912 | bytes 4194304 | tf_op jit(solution)/shard_map/pallas_call | solution.py:24
  26.4 2.0 %collective-permute-start.10 = (bf16[512,256]{1,0:T(8,128)(2,1)S(1)}, bf16[512,256]{1,0:T(8,128)(2,1)S(1)}, u32[]{:S(2)}, u32[]{:S(2)}) collective-permute-start(bf16[512,256]{1,0:T(8,128)(2,1)S(1)} %get-tuple-element.74), channel_id=1, source_target_pairs={{0,4},{1,5},{2,6},{3,7},{4,0},{5,1},{6,2},{7,3},{8,12},{9,13},{10,... | collective-permute-start | bytes 786440 | tf_op jit(solution)/shard_map/ppermute | solution.py:394
  28.4 4.8 %collective-permute-done.8.refs_3_ = bf16[512,256]{1,0:T(8,128)(2,1)S(1)} collective-permute-done((bf16[512,256]{1,0:T(8,128)(2,1)S(1)}, bf16[512,256]{1,0:T(8,128)(2,1)S(1)}, u32[]{:S(2)}, u32[]{:S(2)}) %collective-permute-start.8) | collective-permute-done | bytes 262176 | tf_op jit(solution)/shard_map/ppermute | solution.py:394
  33.2 2.7 %shard_map.163 = (bf16[2048,256]{1,0:T(8,128)(2,1)}, f32[16,16,256]{2,1,0:T(8,128)}, f32[16,16,256]{2,1,0:T(8,128)}, f32[512,256]{1,0:T(8,128)S(1)}, f32[512,256]{1,0:T(8,128)S(1)}) custom-call(s32[16,128]{1,0:T(8,128)S(1)} %get-tuple-element.40.refs_0_.refs_1_.refs_3_, bf16[2048,256]{1,0:T(8,128)(2,1)S(1)} %get-tuple-element.62.refs_1_, ...), custom_call_target="tpu_custom_call" | custom-call | flops 536870912 | bytes 2097152 | tf_op jit(solution)/shard_map/pallas_call | solution.py:24
  36.0 2.1 %collective-permute-done.9.refs_3_ = bf16[512,256]{1,0:T(8,128)(2,1)S(1)} collective-permute-done((bf16[512,256]{1,0:T(8,128)(2,1)S(1)}, bf16[512,256]{1,0:T(8,128)(2,1)S(1)}, u32[]{:S(2)}, u32[]{:S(2)}) %collective-permute-start.9) | collective-permute-done | bytes 262176 | tf_op jit(solution)/shard_map/ppermute | solution.py:394
  38.1 0.4 shard_map.164
  38.5 8.7 %collective-permute-done.10.refs_2_ = bf16[512,256]{1,0:T(8,128)(2,1)S(1)} collective-permute-done((bf16[512,256]{1,0:T(8,128)(2,1)S(1)}, bf16[512,256]{1,0:T(8,128)(2,1)S(1)}, u32[]{:S(2)}, u32[]{:S(2)}) %collective-permute-start.10) | collective-permute-done | bytes 262176 | tf_op jit(solution)/shard_map/ppermute | solution.py:394
  47.2 0.3 shard_map.166
  47.9 1.2 %collective-permute-done.11.passed = bf16[512,256]{1,0:T(8,128)(2,1)S(1)} collective-permute-done((bf16[512,256]{1,0:T(8,128)(2,1)S(1)}, bf16[512,256]{1,0:T(8,128)(2,1)S(1)}, u32[]{:S(2)}, u32[]{:S(2)}) %collective-permute-start.11) | collective-permute-done | bytes 262176 | tf_op jit(solution)/shard_map/ppermute | solution.py:454
  49.1 0.8 %shard_map.167 = f32[512,256]{1,0:T(8,128)} custom-call(f32[512,256]{1,0:T(8,128)S(1)} %shard_map.165.mine, bf16[512,256]{1,0:T(8,128)(2,1)S(1)} %collective-permute-done.11.passed), custom_call_target="tpu_custom_call" | custom-call | bytes 1310720 | tf_op jit(solution)/shard_map/pallas_call | solution.py:24
  (16 shorter events, 0.7 us)
Async XLA Ops:
  0.6 19.5 %copy-start.1 = (bf16[1,2048,256]{2,1,0:T(8,128)(2,1)S(1)}, bf16[1,2048,256]{2,1,0:T(8,128)(2,1)}, u32[]{:S(2)}) copy-start(bf16[1,2048,256]{2,1,0:T(8,128)(2,1)} %param.21) | copy-start | bytes 3145732
  2.0 18.1 %copy-start = (bf16[1,2048,256]{2,1,0:T(8,128)(2,1)S(1)}, bf16[1,2048,256]{2,1,0:T(8,128)(2,1)}, u32[]{:S(2)}) copy-start(bf16[1,2048,256]{2,1,0:T(8,128)(2,1)} %param.20) | copy-start | bytes 3145732
  2.0 11.2 %collective-permute-start = (bf16[32,256]{1,0:T(8,128)(2,1)S(1)}, bf16[32,256]{1,0:T(8,128)(2,1)S(1)}, u32[]{:S(2)}, u32[]{:S(2)}) collective-permute-start(bf16[32,256]{1,0:T(8,128)(2,1)S(1)} %get-tuple-element.48), channel_id=1, source_target_pairs={{0,1},{1,0},{2,3},{3,2},{4,5},{5,4},{6,7},{7,6},{8,9},{9,8},{10,11... | collective-permute-start | bytes 49160 | tf_op jit(solution)/shard_map/ppermute | solution.py:355
  2.6 10.7 %collective-permute-start.1 = (bf16[32,256]{1,0:T(8,128)(2,1)S(1)}, bf16[32,256]{1,0:T(8,128)(2,1)S(1)}, u32[]{:S(2)}, u32[]{:S(2)}) collective-permute-start(bf16[32,256]{1,0:T(8,128)(2,1)S(1)} %get-tuple-element.49), channel_id=1, source_target_pairs={{0,7},{1,2},{2,1},{3,4},{4,3},{5,6},{6,5},{7,0},{8,15},{9,10},{10,... | collective-permute-start | bytes 49160 | tf_op jit(solution)/shard_map/ppermute | solution.py:354
  7.3 4.2 %collective-permute-start.2 = (bf16[16,128]{1,0:T(8,128)(2,1)S(1)}, bf16[16,128]{1,0:T(8,128)(2,1)S(1)}, u32[]{:S(2)}, u32[]{:S(2)}) collective-permute-start(bf16[16,128]{1,0:T(8,128)(2,1)S(1)} %get-tuple-element.50), channel_id=1, source_target_pairs={{0,8},{8,0},{16,24},{24,16},{1,9},{9,1},{17,25},{25,17},{2,10},{10... | collective-permute-start | bytes 12296 | tf_op jit(solution)/shard_map/ppermute | solution.py:357
  8.8 4.5 %collective-permute-start.3 = (bf16[16,128]{1,0:T(8,128)(2,1)S(1)}, bf16[16,128]{1,0:T(8,128)(2,1)S(1)}, u32[]{:S(2)}, u32[]{:S(2)}) collective-permute-start(bf16[16,128]{1,0:T(8,128)(2,1)S(1)} %get-tuple-element.51), channel_id=1, source_target_pairs={{0,24},{8,16},{16,8},{24,0},{1,25},{9,17},{17,9},{25,1},{2,26},{10... | collective-permute-start | bytes 12296 | tf_op jit(solution)/shard_map/ppermute | solution.py:356
  14.4 1.2 %collective-permute-start.4 = (bf16[4,16,128]{2,1,0:T(8,128)(2,1)S(1)}, bf16[4,16,128]{2,1,0:T(8,128)(2,1)S(1)}, u32[]{:S(2)}, u32[]{:S(2)}) collective-permute-start(bf16[4,16,128]{2,1,0:T(8,128)(2,1)S(1)} %get-tuple-element.53), channel_id=1, source_target_pairs={{0,1},{1,0},{2,3},{3,2},{4,5},{5,4},{6,7},{7,6},{8,9},{9,8},{10,11... | collective-permute-start | bytes 49160 | tf_op jit(solution)/shard_map/ppermute | solution.py:384
  15.7 5.9 %collective-permute-start.5 = (bf16[32,128]{1,0:T(8,128)(2,1)S(1)}, bf16[32,128]{1,0:T(8,128)(2,1)S(1)}, u32[]{:S(2)}, u32[]{:S(2)}) collective-permute-start(bf16[32,128]{1,0:T(8,128)(2,1)S(1)} %get-tuple-element.58), channel_id=1, source_target_pairs={{0,6},{1,7},{2,4},{3,5},{4,2},{5,3},{6,0},{7,1},{8,14},{9,15},{10,... | collective-permute-start | bytes 24584 | tf_op jit(solution)/shard_map/ppermute | solution.py:394
  16.2 5.4 %collective-permute-start.6 = (bf16[32,128]{1,0:T(8,128)(2,1)S(1)}, bf16[32,128]{1,0:T(8,128)(2,1)S(1)}, u32[]{:S(2)}, u32[]{:S(2)}) collective-permute-start(bf16[32,128]{1,0:T(8,128)(2,1)S(1)} %get-tuple-element.59), channel_id=1, source_target_pairs={{0,4},{1,5},{2,6},{3,7},{4,0},{5,1},{6,2},{7,3},{8,12},{9,13},{10,... | collective-permute-start | bytes 24584 | tf_op jit(solution)/shard_map/ppermute | solution.py:394
  16.2 5.6 %collective-permute-start.7 = (bf16[32,128]{1,0:T(8,128)(2,1)S(1)}, bf16[32,128]{1,0:T(8,128)(2,1)S(1)}, u32[]{:S(2)}, u32[]{:S(2)}) collective-permute-start(bf16[32,128]{1,0:T(8,128)(2,1)S(1)} %get-tuple-element.60), channel_id=1, source_target_pairs={{0,2},{1,3},{2,0},{3,1},{4,6},{5,7},{6,4},{7,5},{8,10},{9,11},{10,... | collective-permute-start | bytes 24584 | tf_op jit(solution)/shard_map/ppermute | solution.py:394
  22.1 11.1 %collective-permute-start.8 = (bf16[512,256]{1,0:T(8,128)(2,1)S(1)}, bf16[512,256]{1,0:T(8,128)(2,1)S(1)}, u32[]{:S(2)}, u32[]{:S(2)}) collective-permute-start(bf16[512,256]{1,0:T(8,128)(2,1)S(1)} %get-tuple-element.64), channel_id=1, source_target_pairs={{0,6},{1,7},{2,4},{3,5},{4,2},{5,3},{6,0},{7,1},{8,14},{9,15},{10,... | collective-permute-start | bytes 786440 | tf_op jit(solution)/shard_map/ppermute | solution.py:394
  26.3 11.8 %collective-permute-start.9 = (bf16[512,256]{1,0:T(8,128)(2,1)S(1)}, bf16[512,256]{1,0:T(8,128)(2,1)S(1)}, u32[]{:S(2)}, u32[]{:S(2)}) collective-permute-start(bf16[512,256]{1,0:T(8,128)(2,1)S(1)} %get-tuple-element.72), channel_id=1, source_target_pairs={{0,2},{1,3},{2,0},{3,1},{4,6},{5,7},{6,4},{7,5},{8,10},{9,11},{10,... | collective-permute-start | bytes 786440 | tf_op jit(solution)/shard_map/ppermute | solution.py:394
  26.4 20.8 %collective-permute-start.10 = (bf16[512,256]{1,0:T(8,128)(2,1)S(1)}, bf16[512,256]{1,0:T(8,128)(2,1)S(1)}, u32[]{:S(2)}, u32[]{:S(2)}) collective-permute-start(bf16[512,256]{1,0:T(8,128)(2,1)S(1)} %get-tuple-element.74), channel_id=1, source_target_pairs={{0,4},{1,5},{2,6},{3,7},{4,0},{5,1},{6,2},{7,3},{8,12},{9,13},{10,... | collective-permute-start | bytes 786440 | tf_op jit(solution)/shard_map/ppermute | solution.py:394
  47.5 1.6 %collective-permute-start.11 = (bf16[512,256]{1,0:T(8,128)(2,1)S(1)}, bf16[512,256]{1,0:T(8,128)(2,1)S(1)}, u32[]{:S(2)}, u32[]{:S(2)}) collective-permute-start(bf16[512,256]{1,0:T(8,128)(2,1)S(1)} %shard_map.166), channel_id=1, source_target_pairs={{0,1},{1,0},{2,3},{3,2},{4,5},{5,4},{6,7},{7,6},{8,9},{9,8},{10,11... | collective-permute-start | bytes 786440 | tf_op jit(solution)/shard_map/ppermute | solution.py:454

commit v11 on v10

--- a/solution.py
+++ b/solution.py
@@ -132,11 +132,10 @@
     return parts[0] if len(parts) == 1 else jnp.concatenate(parts, axis=0)
 
 
-def first_body(away, order, records, hydro, rec_packed, hyd_packed):
-    hot = picked(order, away, rec_packed.shape[0] // LANES, records.shape[0])
-    rec = jnp.dot(hot, records[...], preferred_element_type=F32)
-    rec_packed[...] = shift_time(rec).astype(BF16)
-    hyd_packed[...] = jnp.dot(hot, hydro[...], preferred_element_type=F32).astype(BF16)
+def first_body(away, shifted, order, rows, packed):
+    hot = picked(order, away, packed.shape[0] // LANES, rows.shape[0])
+    out = jnp.dot(hot, rows[...], preferred_element_type=F32)
+    packed[...] = (shift_time(out) if shifted else out).astype(BF16)
 
 
 def land_body(
@@ -210,7 +209,7 @@
     give[...] = jnp.where(sec_even, both[:, 1], both[:, 0]).astype(BF16)
 
 
-def terms_body(keep, got, ids, own, *outs):
+def terms_body(keep, got, ids, packed, own, *outs):
     pairs, blocks = keep.shape[:2]
     chip = lax.axis_index("sec") // 2
     own[...] = keep[chip] + got[chip].astype(F32)
@@ -385,24 +384,26 @@
     aways = []
     for k in range(1, pairs // 2 + 1):
         aways += [k] if 2 * k == pairs else [pairs - k, k]
+    pack_first = lambda rows, shifted: call(
+        lambda *refs: first_body(aways[0], shifted, *refs),
+        [shape((cap, steps), BF16)],
+        order, rows,
+        mib=12,
+        flops=2 * cap * reaches * steps,
+        moved=reaches * steps * 2,
+    )[0]
+    rec_packed = pack_first(records[0], True)
     own_terms, *terms = call(
         terms_body,
         [shape((blocks, LANES), F32)] + [shape((blocks + PACK_ROWS, LANES), BF16)] * (pairs - 1),
-        keep, got, ids,
+        keep, got, ids, rec_packed,
         moved=reaches * 8,
     )
     forward = lambda block, away: lax.ppermute(
         block, "sec", [(i, i ^ (2 * away)) for i in range(sections)]
     )
     terms = [forward(term, flip) for flip, term in zip(range(pairs - 1, 0, -1), terms)]
-    rec_packed, hyd_packed = call(
-        lambda *refs: first_body(aways[0], *refs),
-        [shape((cap, steps), BF16)] * 2,
-        order, records[0], unit_hydro[0],
-        mib=12,
-        flops=4 * cap * reaches * steps,
-        moved=reaches * steps * 4,
-    )
+    hyd_packed = pack_first(unit_hydro[0], False)
     runoff, ready, places = call(
         lambda *refs: send_body(aways[0], *refs),
         [shape((blocks, LANES), F32), shape((cap, steps), BF16), shape(ids.shape, BF16)],

time: 50.1 us -> 50.2 us (level)
    ppermute x1, waiting for transfers between devices: 1.17 us -> 0.24 us  [per_device(): got = lax.ppermute(give, 'sec', swap(sections))]
    ppermute x6, waiting for transfers between devices: 15.8 us -> 16.5 us  [per_device(): lax.ppermute(block, 'sec', [(i, i ^ 2 * away) for i in range(sections)])]
    pallas_call x12 -> x13, Pallas kernels: 11.8 us -> 12.1 us  [call(): pl.pallas_call(body, out_shape=list(outs), in_specs=ins, out_specs=list(o...]
  transfers between devices with their start and end apart: 12 -> 12, of which waited for: 7 -> 8; matrix products, arithmetic and copies ran while one was open for 0% -> 0% of each run, Pallas kernels for 16% -> 16%
where the time goes in v11:
time: 50.2 us; the launch traced here: 50 us
  waiting for transfers between devices  19.8 us (39%)
  starting transfers between devices  17.3 us (34%)
  Pallas kernels  12.1 us (24%)
  between operations  0.77 us (2%)
    ppermute x6, waiting for transfers between devices, per_device(): lax.ppermute(block, 'sec', [(i, i ^ 2 * away) for i in range(sections)])  16.5 us
    pallas_call x13, Pallas kernels, call(): pl.pallas_call(body, out_shape=list(outs), in_specs=ins, out_specs=list(o...  12.1 us
    ppermute x6, starting transfers between devices, per_device(): lax.ppermute(block, 'sec', [(i, i ^ 2 * away) for i in range(sections)])  8.96 us
    ppermute x1, starting transfers between devices, per_device(): got_sec_far = lax.ppermute(sec_far, 'sec', between(sections))  4.71 us
    ppermute x1, waiting for transfers between devices, per_device(): got_lon_far = lax.ppermute(lon_far, 'lon', between(lons))  1.83 us
    ppermute x1, starting transfers between devices, per_device(): got_lon_near = lax.ppermute(lon_near, 'lon', swap(lons))  1.49 us
    ppermute x1, starting transfers between devices, per_device(): got_lon_far = lax.ppermute(lon_far, 'lon', between(lons))  1.49 us
    ppermute x1, waiting for transfers between devices, per_device(): passed = lax.ppermute(theirs, 'sec', swap(sections))  1.21 us
  transfers between devices with their start and end apart: 12, of which 8 were waited for; matrix products, arithmetic and copies ran while one was open for 0% of the time, Pallas kernels for 16%

profile of v11, /device:TPU:0, one launch (start us, length us, event | category | flops | bytes accessed | tf_op | source)
XLA Modules:
  0.0 50.0 jit_solution(7087118822377021825)
XLA Ops:
  0.6 1.4 %shard_map.157 = (f32[16,16,256]{2,1,0:T(8,128)S(1)}, f32[16,16,256]{2,1,0:T(8,128)S(1)}, bf16[32,256]{1,0:T(8,128)(2,1)S(1)}, bf16[32,256]{1,0:T(8,128)(2,1)S(1...) custom-call(f32[16,16,256]{2,1,0:T(8,128)} %refs_0_.3, f32[16,16,256]{2,1,0:T(8,128)} %refs_1_.1), custom_call_target="tpu_custom_call" | custom-call | bytes 524288 | tf_op jit(solution)/shard_map/pallas_call | solution.py:24
  2.0 0.5 %collective-permute-start = (bf16[32,256]{1,0:T(8,128)(2,1)S(1)}, bf16[32,256]{1,0:T(8,128)(2,1)S(1)}, u32[]{:S(2)}, u32[]{:S(2)}) collective-permute-start(bf16[32,256]{1,0:T(8,128)(2,1)S(1)} %get-tuple-element.46), channel_id=1, source_target_pairs={{0,1},{1,0},{2,3},{3,2},{4,5},{5,4},{6,7},{7,6},{8,9},{9,8},{10,11... | collective-permute-start | bytes 49160 | tf_op jit(solution)/shard_map/ppermute | solution.py:354
  2.6 4.7 %collective-permute-start.1 = (bf16[32,256]{1,0:T(8,128)(2,1)S(1)}, bf16[32,256]{1,0:T(8,128)(2,1)S(1)}, u32[]{:S(2)}, u32[]{:S(2)}) collective-permute-start(bf16[32,256]{1,0:T(8,128)(2,1)S(1)} %get-tuple-element.47), channel_id=1, source_target_pairs={{0,7},{1,2},{2,1},{3,4},{4,3},{5,6},{6,5},{7,0},{8,15},{9,10},{10,... | collective-permute-start | bytes 49160 | tf_op jit(solution)/shard_map/ppermute | solution.py:353
  7.3 1.5 %collective-permute-start.2 = (bf16[16,128]{1,0:T(8,128)(2,1)S(1)}, bf16[16,128]{1,0:T(8,128)(2,1)S(1)}, u32[]{:S(2)}, u32[]{:S(2)}) collective-permute-start(bf16[16,128]{1,0:T(8,128)(2,1)S(1)} %get-tuple-element.48), channel_id=1, source_target_pairs={{0,8},{8,0},{16,24},{24,16},{1,9},{9,1},{17,25},{25,17},{2,10},{10... | collective-permute-start | bytes 12296 | tf_op jit(solution)/shard_map/ppermute | solution.py:356
  8.8 1.5 %collective-permute-start.3 = (bf16[16,128]{1,0:T(8,128)(2,1)S(1)}, bf16[16,128]{1,0:T(8,128)(2,1)S(1)}, u32[]{:S(2)}, u32[]{:S(2)}) collective-permute-start(bf16[16,128]{1,0:T(8,128)(2,1)S(1)} %get-tuple-element.49), channel_id=1, source_target_pairs={{0,24},{8,16},{16,8},{24,0},{1,25},{9,17},{17,9},{25,1},{2,26},{10... | collective-permute-start | bytes 12296 | tf_op jit(solution)/shard_map/ppermute | solution.py:355
  10.2 1.2 %shard_map.156 = (s32[16,128]{1,0:T(8,128)S(1)}, bf16[4,16,128]{2,1,0:T(8,128)(2,1)S(1)}, f32[16,16,256]{2,1,0:T(8,128)S(1)}, f32[16,16,256]{2,1,0:T(8,128)S(1)}...) custom-call(s32[1,1,8]{2,1,0:T(1,128)} %refs_0_.2, s32[32,128]{1,0:T(8,128)} %bitcast.12, ...), custom_call_target="tpu_custom_call" | custom-call | bytes 524288 | tf_op jit(solution)/shard_map/pallas_call | solution.py:24
  11.4 1.8 %collective-permute-done.3.lon_far = bf16[16,128]{1,0:T(8,128)(2,1)S(1)} collective-permute-done((bf16[16,128]{1,0:T(8,128)(2,1)S(1)}, bf16[16,128]{1,0:T(8,128)(2,1)S(1)}, u32[]{:S(2)}, u32[]{:S(2)}) %collective-permute-start.3) | collective-permute-done | bytes 4128 | tf_op jit(solution)/shard_map/ppermute | solution.py:355
  13.3 1.1 %shard_map.158 = (f32[16,16,256]{2,1,0:T(8,128)S(1)}, f32[16,16,256]{2,1,0:T(8,128)S(1)}, f32[4,16,128]{2,1,0:T(8,128)S(1)}, bf16[4,16,128]{2,1,0:T(8,128)(2,1)S(1)}) custom-call(f32[16,16,256]{2,1,0:T(8,128)S(1)} %get-tuple-element.39.moist, f32[16,16,256]{2,1,0:T(8,128)S(1)} %get-tuple-element.40.heat, f32[16,16,256]{2,1,0:T(8,128)S(1)} %get-tuple-element.41.moist_k, ...), custom_call_target="tpu_custom_call" | custom-call | bytes 1572864 | tf_op jit(solution)/shard_map/pallas_call | solution.py:24
  14.5 0.9 %shard_map.159.packed.refs_3_ = bf16[512,256]{1,0:T(8,128)(2,1)S(1)} custom-call(s32[16,128]{1,0:T(8,128)S(1)} %get-tuple-element.38.refs_0_.refs_1_.refs_3_, bf16[2048,256]{1,0:T(8,128)(2,1)S(1)} %bitcast.7), custom_call_target="tpu_custom_call" | custom-call | flops 536870912 | bytes 1048576 | tf_op jit(solution)/shard_map/pallas_call | solution.py:24
  15.7 0.5 %collective-permute-start.5 = (bf16[32,128]{1,0:T(8,128)(2,1)S(1)}, bf16[32,128]{1,0:T(8,128)(2,1)S(1)}, u32[]{:S(2)}, u32[]{:S(2)}) collective-permute-start(bf16[32,128]{1,0:T(8,128)(2,1)S(1)} %get-tuple-element.54), channel_id=1, source_target_pairs={{0,6},{1,7},{2,4},{3,5},{4,2},{5,3},{6,0},{7,1},{8,14},{9,15},{10,... | collective-permute-start | bytes 24584 | tf_op jit(solution)/shard_map/ppermute | solution.py:402
  16.2 3.9 %collective-permute-start.7 = (bf16[32,128]{1,0:T(8,128)(2,1)S(1)}, bf16[32,128]{1,0:T(8,128)(2,1)S(1)}, u32[]{:S(2)}, u32[]{:S(2)}) collective-permute-start(bf16[32,128]{1,0:T(8,128)(2,1)S(1)} %get-tuple-element.56), channel_id=1, source_target_pairs={{0,2},{1,3},{2,0},{3,1},{4,6},{5,7},{6,4},{7,5},{8,10},{9,11},{10,... | collective-permute-start | bytes 24584 | tf_op jit(solution)/shard_map/ppermute | solution.py:402
  20.1 0.8 %shard_map.161.refs_4_ = bf16[512,256]{1,0:T(8,128)(2,1)S(1)} custom-call(s32[16,128]{1,0:T(8,128)S(1)} %get-tuple-element.38.refs_0_.refs_1_.refs_3_, bf16[2048,256]{1,0:T(8,128)(2,1)S(1)} %bitcast.9), custom_call_target="tpu_custom_call" | custom-call | flops 536870912 | bytes 1048576 | tf_op jit(solution)/shard_map/pallas_call | solution.py:24
  21.2 0.6 %collective-permute-done.7.refs_7_ = bf16[32,128]{1,0:T(8,128)(2,1)S(1)} collective-permute-done((bf16[32,128]{1,0:T(8,128)(2,1)S(1)}, bf16[32,128]{1,0:T(8,128)(2,1)S(1)}, u32[]{:S(2)}, u32[]{:S(2)}) %collective-permute-start.7) | collective-permute-done | bytes 8224 | tf_op jit(solution)/shard_map/ppermute | solution.py:402
  21.8 0.4 shard_map.162
  22.1 2.4 %collective-permute-start.8 = (bf16[512,256]{1,0:T(8,128)(2,1)S(1)}, bf16[512,256]{1,0:T(8,128)(2,1)S(1)}, u32[]{:S(2)}, u32[]{:S(2)}) collective-permute-start(bf16[512,256]{1,0:T(8,128)(2,1)S(1)} %get-tuple-element.60), channel_id=1, source_target_pairs={{0,6},{1,7},{2,4},{3,5},{4,2},{5,3},{6,0},{7,1},{8,14},{9,15},{10,... | collective-permute-start | bytes 786440 | tf_op jit(solution)/shard_map/ppermute | solution.py:402
  24.6 1.7 %shard_map.163 = (bf16[2048,256]{1,0:T(8,128)(2,1)S(1)}, bf16[512,256]{1,0:T(8,128)(2,1)S(1)}, bf16[512,256]{1,0:T(8,128)(2,1)S(1)}) custom-call(f32[16,128]{1,0:T(8,128)S(1)} %get-tuple-element.57.refs_0_, bf16[2048,256]{1,0:T(8,128)(2,1)S(1)} %bitcast.8, bf16[2048,256]{1,0:T(8,128)(2,1)S(1)} %bitcast.10, ...), custom_call_target="tpu_custom_call" | custom-call | flops 536870912 | bytes 4194304 | tf_op jit(solution)/shard_map/pallas_call | solution.py:24
  26.4 2.0 %collective-permute-start.10 = (bf16[512,256]{1,0:T(8,128)(2,1)S(1)}, bf16[512,256]{1,0:T(8,128)(2,1)S(1)}, u32[]{:S(2)}, u32[]{:S(2)}) collective-permute-start(bf16[512,256]{1,0:T(8,128)(2,1)S(1)} %get-tuple-element.70), channel_id=1, source_target_pairs={{0,4},{1,5},{2,6},{3,7},{4,0},{5,1},{6,2},{7,3},{8,12},{9,13},{10,... | collective-permute-start | bytes 786440 | tf_op jit(solution)/shard_map/ppermute | solution.py:402
  28.4 4.8 %collective-permute-done.8.refs_3_ = bf16[512,256]{1,0:T(8,128)(2,1)S(1)} collective-permute-done((bf16[512,256]{1,0:T(8,128)(2,1)S(1)}, bf16[512,256]{1,0:T(8,128)(2,1)S(1)}, u32[]{:S(2)}, u32[]{:S(2)}) %collective-permute-start.8) | collective-permute-done | bytes 262176 | tf_op jit(solution)/shard_map/ppermute | solution.py:402
  33.2 2.7 %shard_map.164 = (bf16[2048,256]{1,0:T(8,128)(2,1)}, f32[16,16,256]{2,1,0:T(8,128)}, f32[16,16,256]{2,1,0:T(8,128)}, f32[512,256]{1,0:T(8,128)S(1)}, f32[512,256]{1,0:T(8,128)S(1)}) custom-call(s32[16,128]{1,0:T(8,128)S(1)} %get-tuple-element.38.refs_0_.refs_1_.refs_3_, bf16[2048,256]{1,0:T(8,128)(2,1)S(1)} %get-tuple-element.58.refs_1_, ...), custom_call_target="tpu_custom_call" | custom-call | flops 536870912 | bytes 2097152 | tf_op jit(solution)/shard_map/pallas_call | solution.py:24
  36.0 2.0 %collective-permute-done.9.refs_3_ = bf16[512,256]{1,0:T(8,128)(2,1)S(1)} collective-permute-done((bf16[512,256]{1,0:T(8,128)(2,1)S(1)}, bf16[512,256]{1,0:T(8,128)(2,1)S(1)}, u32[]{:S(2)}, u32[]{:S(2)}) %collective-permute-start.9) | collective-permute-done | bytes 262176 | tf_op jit(solution)/shard_map/ppermute | solution.py:402
  37.9 0.4 shard_map.165
  38.4 8.9 %collective-permute-done.10.refs_2_ = bf16[512,256]{1,0:T(8,128)(2,1)S(1)} collective-permute-done((bf16[512,256]{1,0:T(8,128)(2,1)S(1)}, bf16[512,256]{1,0:T(8,128)(2,1)S(1)}, u32[]{:S(2)}, u32[]{:S(2)}) %collective-permute-start.10) | collective-permute-done | bytes 262176 | tf_op jit(solution)/shard_map/ppermute | solution.py:402
  48.0 1.2 %collective-permute-done.11.passed = bf16[512,256]{1,0:T(8,128)(2,1)S(1)} collective-permute-done((bf16[512,256]{1,0:T(8,128)(2,1)S(1)}, bf16[512,256]{1,0:T(8,128)(2,1)S(1)}, u32[]{:S(2)}, u32[]{:S(2)}) %collective-permute-start.11) | collective-permute-done | bytes 262176 | tf_op jit(solution)/shard_map/ppermute | solution.py:455
  49.2 0.8 %shard_map.168 = f32[512,256]{1,0:T(8,128)} custom-call(f32[512,256]{1,0:T(8,128)S(1)} %shard_map.166.mine, bf16[512,256]{1,0:T(8,128)(2,1)S(1)} %collective-permute-done.11.passed), custom_call_target="tpu_custom_call" | custom-call | bytes 1310720 | tf_op jit(solution)/shard_map/pallas_call | solution.py:24
  (17 shorter events, 1.3 us)
Async XLA Ops:
  0.6 13.9 %copy-start = (bf16[1,2048,256]{2,1,0:T(8,128)(2,1)S(1)}, bf16[1,2048,256]{2,1,0:T(8,128)(2,1)}, u32[]{:S(2)}) copy-start(bf16[1,2048,256]{2,1,0:T(8,128)(2,1)} %param.20) | copy-start | bytes 3145732
  2.0 11.2 %collective-permute-start = (bf16[32,256]{1,0:T(8,128)(2,1)S(1)}, bf16[32,256]{1,0:T(8,128)(2,1)S(1)}, u32[]{:S(2)}, u32[]{:S(2)}) collective-permute-start(bf16[32,256]{1,0:T(8,128)(2,1)S(1)} %get-tuple-element.46), channel_id=1, source_target_pairs={{0,1},{1,0},{2,3},{3,2},{4,5},{5,4},{6,7},{7,6},{8,9},{9,8},{10,11... | collective-permute-start | bytes 49160 | tf_op jit(solution)/shard_map/ppermute | solution.py:354
  2.6 10.7 %collective-permute-start.1 = (bf16[32,256]{1,0:T(8,128)(2,1)S(1)}, bf16[32,256]{1,0:T(8,128)(2,1)S(1)}, u32[]{:S(2)}, u32[]{:S(2)}) collective-permute-start(bf16[32,256]{1,0:T(8,128)(2,1)S(1)} %get-tuple-element.47), channel_id=1, source_target_pairs={{0,7},{1,2},{2,1},{3,4},{4,3},{5,6},{6,5},{7,0},{8,15},{9,10},{10,... | collective-permute-start | bytes 49160 | tf_op jit(solution)/shard_map/ppermute | solution.py:353
  7.3 4.2 %collective-permute-start.2 = (bf16[16,128]{1,0:T(8,128)(2,1)S(1)}, bf16[16,128]{1,0:T(8,128)(2,1)S(1)}, u32[]{:S(2)}, u32[]{:S(2)}) collective-permute-start(bf16[16,128]{1,0:T(8,128)(2,1)S(1)} %get-tuple-element.48), channel_id=1, source_target_pairs={{0,8},{8,0},{16,24},{24,16},{1,9},{9,1},{17,25},{25,17},{2,10},{10... | collective-permute-start | bytes 12296 | tf_op jit(solution)/shard_map/ppermute | solution.py:356
  8.8 4.5 %collective-permute-start.3 = (bf16[16,128]{1,0:T(8,128)(2,1)S(1)}, bf16[16,128]{1,0:T(8,128)(2,1)S(1)}, u32[]{:S(2)}, u32[]{:S(2)}) collective-permute-start(bf16[16,128]{1,0:T(8,128)(2,1)S(1)} %get-tuple-element.49), channel_id=1, source_target_pairs={{0,24},{8,16},{16,8},{24,0},{1,25},{9,17},{17,9},{25,1},{2,26},{10... | collective-permute-start | bytes 12296 | tf_op jit(solution)/shard_map/ppermute | solution.py:355
  14.4 1.2 %collective-permute-start.4 = (bf16[4,16,128]{2,1,0:T(8,128)(2,1)S(1)}, bf16[4,16,128]{2,1,0:T(8,128)(2,1)S(1)}, u32[]{:S(2)}, u32[]{:S(2)}) collective-permute-start(bf16[4,16,128]{2,1,0:T(8,128)(2,1)S(1)} %get-tuple-element.51), channel_id=1, source_target_pairs={{0,1},{1,0},{2,3},{3,2},{4,5},{5,4},{6,7},{7,6},{8,9},{9,8},{10,11... | collective-permute-start | bytes 49160 | tf_op jit(solution)/shard_map/ppermute | solution.py:383
  14.5 5.6 %copy-start.1 = (bf16[1,2048,256]{2,1,0:T(8,128)(2,1)S(1)}, bf16[1,2048,256]{2,1,0:T(8,128)(2,1)}, u32[]{:S(2)}) copy-start(bf16[1,2048,256]{2,1,0:T(8,128)(2,1)} %param.21) | copy-start | bytes 3145732
  15.7 5.5 %collective-permute-start.5 = (bf16[32,128]{1,0:T(8,128)(2,1)S(1)}, bf16[32,128]{1,0:T(8,128)(2,1)S(1)}, u32[]{:S(2)}, u32[]{:S(2)}) collective-permute-start(bf16[32,128]{1,0:T(8,128)(2,1)S(1)} %get-tuple-element.54), channel_id=1, source_target_pairs={{0,6},{1,7},{2,4},{3,5},{4,2},{5,3},{6,0},{7,1},{8,14},{9,15},{10,... | collective-permute-start | bytes 24584 | tf_op jit(solution)/shard_map/ppermute | solution.py:402
  16.2 5.0 %collective-permute-start.6 = (bf16[32,128]{1,0:T(8,128)(2,1)S(1)}, bf16[32,128]{1,0:T(8,128)(2,1)S(1)}, u32[]{:S(2)}, u32[]{:S(2)}) collective-permute-start(bf16[32,128]{1,0:T(8,128)(2,1)S(1)} %get-tuple-element.55), channel_id=1, source_target_pairs={{0,4},{1,5},{2,6},{3,7},{4,0},{5,1},{6,2},{7,3},{8,12},{9,13},{10,... | collective-permute-start | bytes 24584 | tf_op jit(solution)/shard_map/ppermute | solution.py:402
  16.2 5.6 %collective-permute-start.7 = (bf16[32,128]{1,0:T(8,128)(2,1)S(1)}, bf16[32,128]{1,0:T(8,128)(2,1)S(1)}, u32[]{:S(2)}, u32[]{:S(2)}) collective-permute-start(bf16[32,128]{1,0:T(8,128)(2,1)S(1)} %get-tuple-element.56), channel_id=1, source_target_pairs={{0,2},{1,3},{2,0},{3,1},{4,6},{5,7},{6,4},{7,5},{8,10},{9,11},{10,... | collective-permute-start | bytes 24584 | tf_op jit(solution)/shard_map/ppermute | solution.py:402
  22.1 11.1 %collective-permute-start.8 = (bf16[512,256]{1,0:T(8,128)(2,1)S(1)}, bf16[512,256]{1,0:T(8,128)(2,1)S(1)}, u32[]{:S(2)}, u32[]{:S(2)}) collective-permute-start(bf16[512,256]{1,0:T(8,128)(2,1)S(1)} %get-tuple-element.60), channel_id=1, source_target_pairs={{0,6},{1,7},{2,4},{3,5},{4,2},{5,3},{6,0},{7,1},{8,14},{9,15},{10,... | collective-permute-start | bytes 786440 | tf_op jit(solution)/shard_map/ppermute | solution.py:402
  26.3 11.6 %collective-permute-start.9 = (bf16[512,256]{1,0:T(8,128)(2,1)S(1)}, bf16[512,256]{1,0:T(8,128)(2,1)S(1)}, u32[]{:S(2)}, u32[]{:S(2)}) collective-permute-start(bf16[512,256]{1,0:T(8,128)(2,1)S(1)} %get-tuple-element.68), channel_id=1, source_target_pairs={{0,2},{1,3},{2,0},{3,1},{4,6},{5,7},{6,4},{7,5},{8,10},{9,11},{10,... | collective-permute-start | bytes 786440 | tf_op jit(solution)/shard_map/ppermute | solution.py:402
  26.4 20.9 %collective-permute-start.10 = (bf16[512,256]{1,0:T(8,128)(2,1)S(1)}, bf16[512,256]{1,0:T(8,128)(2,1)S(1)}, u32[]{:S(2)}, u32[]{:S(2)}) collective-permute-start(bf16[512,256]{1,0:T(8,128)(2,1)S(1)} %get-tuple-element.70), channel_id=1, source_target_pairs={{0,4},{1,5},{2,6},{3,7},{4,0},{5,1},{6,2},{7,3},{8,12},{9,13},{10,... | collective-permute-start | bytes 786440 | tf_op jit(solution)/shard_map/ppermute | solution.py:402
  47.6 1.6 %collective-permute-start.11 = (bf16[512,256]{1,0:T(8,128)(2,1)S(1)}, bf16[512,256]{1,0:T(8,128)(2,1)S(1)}, u32[]{:S(2)}, u32[]{:S(2)}) collective-permute-start(bf16[512,256]{1,0:T(8,128)(2,1)S(1)} %shard_map.167), channel_id=1, source_target_pairs={{0,1},{1,0},{2,3},{3,2},{4,5},{5,4},{6,7},{7,6},{8,9},{9,8},{10,11... | collective-permute-start | bytes 786440 | tf_op jit(solution)/shard_map/ppermute | solution.py:455

commit v12 on v10

--- a/solution.py
+++ b/solution.py
@@ -214,7 +214,7 @@
     pairs, blocks = keep.shape[:2]
     chip = lax.axis_index("sec") // 2
     own[...] = keep[chip] + got[chip].astype(F32)
-    for flip, out in zip(range(len(outs), 0, -1), outs):
+    for flip, out in enumerate(outs, 1):
         m = chip ^ flip
         out[:blocks, :] = (keep[m] + got[m].astype(F32)).astype(BF16)
         out[blocks:, :] = ids[flip]
@@ -223,7 +223,7 @@
 def send_body(away, own, order, ids, rec_packed, hyd_packed, *refs):
     terms, (runoff, ready, places) = refs[:-3], refs[-3:]
     places[0] = ids[0]
-    for flip, term in zip(range(len(terms), 0, -1), terms):
+    for flip, term in enumerate(terms, 1):
         places[flip] = term[term.shape[0] - PACK_ROWS :, :]
     blocks = runoff.shape[0]
     tiles = ready.shape[0] // LANES
@@ -394,7 +394,7 @@
     forward = lambda block, away: lax.ppermute(
         block, "sec", [(i, i ^ (2 * away)) for i in range(sections)]
     )
-    terms = [forward(term, flip) for flip, term in zip(range(pairs - 1, 0, -1), terms)]
+    terms = [forward(term, flip) for flip, term in enumerate(terms, 1)]
     rec_packed, hyd_packed = call(
         lambda *refs: first_body(aways[0], *refs),
         [shape((cap, steps), BF16)] * 2,

time: 50.1 us -> 48.9 us (0.976)
  waiting for transfers between devices: 20 us -> 18.8 us
    ppermute x6, waiting for transfers between devices: 15.8 us -> 14.6 us  [per_device(): lax.ppermute(block, 'sec', [(i, i ^ 2 * away) for i in range(sections)])]
where the time goes in v12:
time: 48.9 us; the launch traced here: 48.7 us
  waiting for transfers between devices  18.8 us (38%)
  starting transfers between devices  17.3 us (35%)
  Pallas kernels  11.8 us (24%)
  between operations  0.78 us (2%)
    ppermute x6, waiting for transfers between devices, per_device(): lax.ppermute(block, 'sec', [(i, i ^ 2 * away) for i in range(sections)])  14.6 us
    pallas_call x12, Pallas kernels, call(): pl.pallas_call(body, out_shape=list(outs), in_specs=ins, out_specs=list(o...  11.8 us
    ppermute x6, starting transfers between devices, per_device(): lax.ppermute(block, 'sec', [(i, i ^ 2 * away) for i in range(sections)])  8.96 us
    ppermute x1, starting transfers between devices, per_device(): got_sec_far = lax.ppermute(sec_far, 'sec', between(sections))  4.71 us
    ppermute x1, waiting for transfers between devices, per_device(): got_lon_far = lax.ppermute(lon_far, 'lon', between(lons))  1.83 us
    ppermute x1, starting transfers between devices, per_device(): got_lon_near = lax.ppermute(lon_near, 'lon', swap(lons))  1.49 us
    ppermute x1, starting transfers between devices, per_device(): got_lon_far = lax.ppermute(lon_far, 'lon', between(lons))  1.49 us
    ppermute x1, waiting for transfers between devices, per_device(): passed = lax.ppermute(theirs, 'sec', swap(sections))  1.22 us
  transfers between devices with their start and end apart: 12, of which 7 were waited for; matrix products, arithmetic and copies ran while one was open for 0% of the time, Pallas kernels for 16%

profile of v12, /device:TPU:0, one launch (start us, length us, event | category | flops | bytes accessed | tf_op | source)
XLA Modules:
  0.0 48.7 jit_solution(1907497789082739349)
XLA Ops:
  0.6 1.4 %shard_map.157 = (f32[16,16,256]{2,1,0:T(8,128)S(1)}, f32[16,16,256]{2,1,0:T(8,128)S(1)}, bf16[32,256]{1,0:T(8,128)(2,1)S(1)}, bf16[32,256]{1,0:T(8,128)(2,1)S(1...) custom-call(f32[16,16,256]{2,1,0:T(8,128)} %refs_0_.3, f32[16,16,256]{2,1,0:T(8,128)} %refs_1_.1), custom_call_target="tpu_custom_call" | custom-call | bytes 524288 | tf_op jit(solution)/shard_map/pallas_call | solution.py:24
  2.0 0.5 %collective-permute-start = (bf16[32,256]{1,0:T(8,128)(2,1)S(1)}, bf16[32,256]{1,0:T(8,128)(2,1)S(1)}, u32[]{:S(2)}, u32[]{:S(2)}) collective-permute-start(bf16[32,256]{1,0:T(8,128)(2,1)S(1)} %get-tuple-element.48), channel_id=1, source_target_pairs={{0,1},{1,0},{2,3},{3,2},{4,5},{5,4},{6,7},{7,6},{8,9},{9,8},{10,11... | collective-permute-start | bytes 49160 | tf_op jit(solution)/shard_map/ppermute | solution.py:355
  2.6 4.7 %collective-permute-start.1 = (bf16[32,256]{1,0:T(8,128)(2,1)S(1)}, bf16[32,256]{1,0:T(8,128)(2,1)S(1)}, u32[]{:S(2)}, u32[]{:S(2)}) collective-permute-start(bf16[32,256]{1,0:T(8,128)(2,1)S(1)} %get-tuple-element.49), channel_id=1, source_target_pairs={{0,7},{1,2},{2,1},{3,4},{4,3},{5,6},{6,5},{7,0},{8,15},{9,10},{10,... | collective-permute-start | bytes 49160 | tf_op jit(solution)/shard_map/ppermute | solution.py:354
  7.3 1.5 %collective-permute-start.2 = (bf16[16,128]{1,0:T(8,128)(2,1)S(1)}, bf16[16,128]{1,0:T(8,128)(2,1)S(1)}, u32[]{:S(2)}, u32[]{:S(2)}) collective-permute-start(bf16[16,128]{1,0:T(8,128)(2,1)S(1)} %get-tuple-element.50), channel_id=1, source_target_pairs={{0,8},{8,0},{16,24},{24,16},{1,9},{9,1},{17,25},{25,17},{2,10},{10... | collective-permute-start | bytes 12296 | tf_op jit(solution)/shard_map/ppermute | solution.py:357
  8.8 1.5 %collective-permute-start.3 = (bf16[16,128]{1,0:T(8,128)(2,1)S(1)}, bf16[16,128]{1,0:T(8,128)(2,1)S(1)}, u32[]{:S(2)}, u32[]{:S(2)}) collective-permute-start(bf16[16,128]{1,0:T(8,128)(2,1)S(1)} %get-tuple-element.51), channel_id=1, source_target_pairs={{0,24},{8,16},{16,8},{24,0},{1,25},{9,17},{17,9},{25,1},{2,26},{10... | collective-permute-start | bytes 12296 | tf_op jit(solution)/shard_map/ppermute | solution.py:356
  10.3 1.2 %shard_map.156 = (s32[16,128]{1,0:T(8,128)S(1)}, bf16[4,16,128]{2,1,0:T(8,128)(2,1)S(1)}, f32[16,16,256]{2,1,0:T(8,128)S(1)}, f32[16,16,256]{2,1,0:T(8,128)S(1)}...) custom-call(s32[1,1,8]{2,1,0:T(1,128)} %refs_0_.2, s32[32,128]{1,0:T(8,128)} %bitcast.12, ...), custom_call_target="tpu_custom_call" | custom-call | bytes 524288 | tf_op jit(solution)/shard_map/pallas_call | solution.py:24
  11.4 1.8 %collective-permute-done.3.lon_far = bf16[16,128]{1,0:T(8,128)(2,1)S(1)} collective-permute-done((bf16[16,128]{1,0:T(8,128)(2,1)S(1)}, bf16[16,128]{1,0:T(8,128)(2,1)S(1)}, u32[]{:S(2)}, u32[]{:S(2)}) %collective-permute-start.3) | collective-permute-done | bytes 4128 | tf_op jit(solution)/shard_map/ppermute | solution.py:356
  13.3 1.1 %shard_map.158 = (f32[16,16,256]{2,1,0:T(8,128)S(1)}, f32[16,16,256]{2,1,0:T(8,128)S(1)}, f32[4,16,128]{2,1,0:T(8,128)S(1)}, bf16[4,16,128]{2,1,0:T(8,128)(2,1)S(1)}) custom-call(f32[16,16,256]{2,1,0:T(8,128)S(1)} %get-tuple-element.41.moist, f32[16,16,256]{2,1,0:T(8,128)S(1)} %get-tuple-element.42.heat, f32[16,16,256]{2,1,0:T(8,128)S(1)} %get-tuple-element.43.moist_k, ...), custom_call_target="tpu_custom_call" | custom-call | bytes 1572864 | tf_op jit(solution)/shard_map/pallas_call | solution.py:24
  14.5 1.2 %collective-permute-done.4.got = bf16[4,16,128]{2,1,0:T(8,128)(2,1)S(1)} collective-permute-done((bf16[4,16,128]{2,1,0:T(8,128)(2,1)S(1)}, bf16[4,16,128]{2,1,0:T(8,128)(2,1)S(1)}, u32[]{:S(2)}, u32[]{:S(2)}) %collective-permute-start.4) | collective-permute-done | bytes 16416 | tf_op jit(solution)/shard_map/ppermute | solution.py:384
  15.8 1.0 %collective-permute-start.6 = (bf16[32,128]{1,0:T(8,128)(2,1)S(1)}, bf16[32,128]{1,0:T(8,128)(2,1)S(1)}, u32[]{:S(2)}, u32[]{:S(2)}) collective-permute-start(bf16[32,128]{1,0:T(8,128)(2,1)S(1)} %get-tuple-element.59), channel_id=1, source_target_pairs={{0,4},{1,5},{2,6},{3,7},{4,0},{5,1},{6,2},{7,3},{8,12},{9,13},{10,... | collective-permute-start | bytes 24584 | tf_op jit(solution)/shard_map/ppermute | solution.py:394
  16.8 3.4 %collective-permute-start.7 = (bf16[32,128]{1,0:T(8,128)(2,1)S(1)}, bf16[32,128]{1,0:T(8,128)(2,1)S(1)}, u32[]{:S(2)}, u32[]{:S(2)}) collective-permute-start(bf16[32,128]{1,0:T(8,128)(2,1)S(1)} %get-tuple-element.60), channel_id=1, source_target_pairs={{0,6},{1,7},{2,4},{3,5},{4,2},{5,3},{6,0},{7,1},{8,14},{9,15},{10,... | collective-permute-start | bytes 24584 | tf_op jit(solution)/shard_map/ppermute | solution.py:394
  20.1 1.4 %shard_map.160 = (bf16[512,256]{1,0:T(8,128)(2,1)S(1)}, bf16[512,256]{1,0:T(8,128)(2,1)S(1)}) custom-call(s32[16,128]{1,0:T(8,128)S(1)} %get-tuple-element.40.refs_0_.refs_1_.refs_3_, bf16[2048,256]{1,0:T(8,128)(2,1)S(1)} %bitcast.7, bf16[2048,256]{1,0:T(8,128)(2,1)S(1)} %bitcast.9), custom_call_target="tpu_custom_call" | custom-call | flops 1073741824 | bytes 2097152 | tf_op jit(solution)/shard_map/pallas_call | solution.py:24
  21.6 0.6 %collective-permute-done.7.refs_7_ = bf16[32,128]{1,0:T(8,128)(2,1)S(1)} collective-permute-done((bf16[32,128]{1,0:T(8,128)(2,1)S(1)}, bf16[32,128]{1,0:T(8,128)(2,1)S(1)}, u32[]{:S(2)}, u32[]{:S(2)}) %collective-permute-start.7) | collective-permute-done | bytes 8224 | tf_op jit(solution)/shard_map/ppermute | solution.py:394
  22.2 0.4 shard_map.161
  22.6 3.5 %collective-permute-start.8 = (bf16[512,256]{1,0:T(8,128)(2,1)S(1)}, bf16[512,256]{1,0:T(8,128)(2,1)S(1)}, u32[]{:S(2)}, u32[]{:S(2)}) collective-permute-start(bf16[512,256]{1,0:T(8,128)(2,1)S(1)} %get-tuple-element.64), channel_id=1, source_target_pairs={{0,6},{1,7},{2,4},{3,5},{4,2},{5,3},{6,0},{7,1},{8,14},{9,15},{10,... | collective-permute-start | bytes 786440 | tf_op jit(solution)/shard_map/ppermute | solution.py:394
  26.1 1.7 %shard_map.162 = (bf16[2048,256]{1,0:T(8,128)(2,1)S(1)}, bf16[512,256]{1,0:T(8,128)(2,1)S(1)}, bf16[512,256]{1,0:T(8,128)(2,1)S(1)}) custom-call(f32[16,128]{1,0:T(8,128)S(1)} %get-tuple-element.61.refs_0_, bf16[2048,256]{1,0:T(8,128)(2,1)S(1)} %bitcast.8, bf16[2048,256]{1,0:T(8,128)(2,1)S(1)} %bitcast.10, ...), custom_call_target="tpu_custom_call" | custom-call | flops 536870912 | bytes 4194304 | tf_op jit(solution)/shard_map/pallas_call | solution.py:24
  27.9 0.9 %collective-permute-start.10 = (bf16[512,256]{1,0:T(8,128)(2,1)S(1)}, bf16[512,256]{1,0:T(8,128)(2,1)S(1)}, u32[]{:S(2)}, u32[]{:S(2)}) collective-permute-start(bf16[512,256]{1,0:T(8,128)(2,1)S(1)} %get-tuple-element.74), channel_id=1, source_target_pairs={{0,4},{1,5},{2,6},{3,7},{4,0},{5,1},{6,2},{7,3},{8,12},{9,13},{10,... | collective-permute-start | bytes 786440 | tf_op jit(solution)/shard_map/ppermute | solution.py:394
  28.8 4.8 %collective-permute-done.8.refs_3_ = bf16[512,256]{1,0:T(8,128)(2,1)S(1)} collective-permute-done((bf16[512,256]{1,0:T(8,128)(2,1)S(1)}, bf16[512,256]{1,0:T(8,128)(2,1)S(1)}, u32[]{:S(2)}, u32[]{:S(2)}) %collective-permute-start.8) | collective-permute-done | bytes 262176 | tf_op jit(solution)/shard_map/ppermute | solution.py:394
  33.7 2.7 %shard_map.163 = (bf16[2048,256]{1,0:T(8,128)(2,1)}, f32[16,16,256]{2,1,0:T(8,128)}, f32[16,16,256]{2,1,0:T(8,128)}, f32[512,256]{1,0:T(8,128)S(1)}, f32[512,256]{1,0:T(8,128)S(1)}) custom-call(s32[16,128]{1,0:T(8,128)S(1)} %get-tuple-element.40.refs_0_.refs_1_.refs_3_, bf16[2048,256]{1,0:T(8,128)(2,1)S(1)} %get-tuple-element.62.refs_1_, ...), custom_call_target="tpu_custom_call" | custom-call | flops 536870912 | bytes 2097152 | tf_op jit(solution)/shard_map/pallas_call | solution.py:24
  36.4 3.1 %collective-permute-done.9.refs_3_ = bf16[512,256]{1,0:T(8,128)(2,1)S(1)} collective-permute-done((bf16[512,256]{1,0:T(8,128)(2,1)S(1)}, bf16[512,256]{1,0:T(8,128)(2,1)S(1)}, u32[]{:S(2)}, u32[]{:S(2)}) %collective-permute-start.9) | collective-permute-done | bytes 262176 | tf_op jit(solution)/shard_map/ppermute | solution.py:394
  39.5 0.4 shard_map.164
  39.9 6.1 %collective-permute-done.10.refs_2_ = bf16[512,256]{1,0:T(8,128)(2,1)S(1)} collective-permute-done((bf16[512,256]{1,0:T(8,128)(2,1)S(1)}, bf16[512,256]{1,0:T(8,128)(2,1)S(1)}, u32[]{:S(2)}, u32[]{:S(2)}) %collective-permute-start.10) | collective-permute-done | bytes 262176 | tf_op jit(solution)/shard_map/ppermute | solution.py:394
  46.7 1.2 %collective-permute-done.11.passed = bf16[512,256]{1,0:T(8,128)(2,1)S(1)} collective-permute-done((bf16[512,256]{1,0:T(8,128)(2,1)S(1)}, bf16[512,256]{1,0:T(8,128)(2,1)S(1)}, u32[]{:S(2)}, u32[]{:S(2)}) %collective-permute-start.11) | collective-permute-done | bytes 262176 | tf_op jit(solution)/shard_map/ppermute | solution.py:454
  47.9 0.8 %shard_map.167 = f32[512,256]{1,0:T(8,128)} custom-call(f32[512,256]{1,0:T(8,128)S(1)} %shard_map.165.mine, bf16[512,256]{1,0:T(8,128)(2,1)S(1)} %collective-permute-done.11.passed), custom_call_target="tpu_custom_call" | custom-call | bytes 1310720 | tf_op jit(solution)/shard_map/pallas_call | solution.py:24
  (16 shorter events, 0.9 us)
Async XLA Ops:
  0.6 19.5 %copy-start.1 = (bf16[1,2048,256]{2,1,0:T(8,128)(2,1)S(1)}, bf16[1,2048,256]{2,1,0:T(8,128)(2,1)}, u32[]{:S(2)}) copy-start(bf16[1,2048,256]{2,1,0:T(8,128)(2,1)} %param.21) | copy-start | bytes 3145732
  2.0 18.1 %copy-start = (bf16[1,2048,256]{2,1,0:T(8,128)(2,1)S(1)}, bf16[1,2048,256]{2,1,0:T(8,128)(2,1)}, u32[]{:S(2)}) copy-start(bf16[1,2048,256]{2,1,0:T(8,128)(2,1)} %param.20) | copy-start | bytes 3145732
  2.0 11.2 %collective-permute-start = (bf16[32,256]{1,0:T(8,128)(2,1)S(1)}, bf16[32,256]{1,0:T(8,128)(2,1)S(1)}, u32[]{:S(2)}, u32[]{:S(2)}) collective-permute-start(bf16[32,256]{1,0:T(8,128)(2,1)S(1)} %get-tuple-element.48), channel_id=1, source_target_pairs={{0,1},{1,0},{2,3},{3,2},{4,5},{5,4},{6,7},{7,6},{8,9},{9,8},{10,11... | collective-permute-start | bytes 49160 | tf_op jit(solution)/shard_map/ppermute | solution.py:355
  2.6 10.7 %collective-permute-start.1 = (bf16[32,256]{1,0:T(8,128)(2,1)S(1)}, bf16[32,256]{1,0:T(8,128)(2,1)S(1)}, u32[]{:S(2)}, u32[]{:S(2)}) collective-permute-start(bf16[32,256]{1,0:T(8,128)(2,1)S(1)} %get-tuple-element.49), channel_id=1, source_target_pairs={{0,7},{1,2},{2,1},{3,4},{4,3},{5,6},{6,5},{7,0},{8,15},{9,10},{10,... | collective-permute-start | bytes 49160 | tf_op jit(solution)/shard_map/ppermute | solution.py:354
  7.3 4.2 %collective-permute-start.2 = (bf16[16,128]{1,0:T(8,128)(2,1)S(1)}, bf16[16,128]{1,0:T(8,128)(2,1)S(1)}, u32[]{:S(2)}, u32[]{:S(2)}) collective-permute-start(bf16[16,128]{1,0:T(8,128)(2,1)S(1)} %get-tuple-element.50), channel_id=1, source_target_pairs={{0,8},{8,0},{16,24},{24,16},{1,9},{9,1},{17,25},{25,17},{2,10},{10... | collective-permute-start | bytes 12296 | tf_op jit(solution)/shard_map/ppermute | solution.py:357
  8.8 4.5 %collective-permute-start.3 = (bf16[16,128]{1,0:T(8,128)(2,1)S(1)}, bf16[16,128]{1,0:T(8,128)(2,1)S(1)}, u32[]{:S(2)}, u32[]{:S(2)}) collective-permute-start(bf16[16,128]{1,0:T(8,128)(2,1)S(1)} %get-tuple-element.51), channel_id=1, source_target_pairs={{0,24},{8,16},{16,8},{24,0},{1,25},{9,17},{17,9},{25,1},{2,26},{10... | collective-permute-start | bytes 12296 | tf_op jit(solution)/shard_map/ppermute | solution.py:356
  14.4 1.2 %collective-permute-start.4 = (bf16[4,16,128]{2,1,0:T(8,128)(2,1)S(1)}, bf16[4,16,128]{2,1,0:T(8,128)(2,1)S(1)}, u32[]{:S(2)}, u32[]{:S(2)}) collective-permute-start(bf16[4,16,128]{2,1,0:T(8,128)(2,1)S(1)} %get-tuple-element.53), channel_id=1, source_target_pairs={{0,1},{1,0},{2,3},{3,2},{4,5},{5,4},{6,7},{7,6},{8,9},{9,8},{10,11... | collective-permute-start | bytes 49160 | tf_op jit(solution)/shard_map/ppermute | solution.py:384
  15.7 5.9 %collective-permute-start.5 = (bf16[32,128]{1,0:T(8,128)(2,1)S(1)}, bf16[32,128]{1,0:T(8,128)(2,1)S(1)}, u32[]{:S(2)}, u32[]{:S(2)}) collective-permute-start(bf16[32,128]{1,0:T(8,128)(2,1)S(1)} %get-tuple-element.58), channel_id=1, source_target_pairs={{0,2},{1,3},{2,0},{3,1},{4,6},{5,7},{6,4},{7,5},{8,10},{9,11},{10,... | collective-permute-start | bytes 24584 | tf_op jit(solution)/shard_map/ppermute | solution.py:394
  15.8 5.8 %collective-permute-start.6 = (bf16[32,128]{1,0:T(8,128)(2,1)S(1)}, bf16[32,128]{1,0:T(8,128)(2,1)S(1)}, u32[]{:S(2)}, u32[]{:S(2)}) collective-permute-start(bf16[32,128]{1,0:T(8,128)(2,1)S(1)} %get-tuple-element.59), channel_id=1, source_target_pairs={{0,4},{1,5},{2,6},{3,7},{4,0},{5,1},{6,2},{7,3},{8,12},{9,13},{10,... | collective-permute-start | bytes 24584 | tf_op jit(solution)/shard_map/ppermute | solution.py:394
  16.8 5.4 %collective-permute-start.7 = (bf16[32,128]{1,0:T(8,128)(2,1)S(1)}, bf16[32,128]{1,0:T(8,128)(2,1)S(1)}, u32[]{:S(2)}, u32[]{:S(2)}) collective-permute-start(bf16[32,128]{1,0:T(8,128)(2,1)S(1)} %get-tuple-element.60), channel_id=1, source_target_pairs={{0,6},{1,7},{2,4},{3,5},{4,2},{5,3},{6,0},{7,1},{8,14},{9,15},{10,... | collective-permute-start | bytes 24584 | tf_op jit(solution)/shard_map/ppermute | solution.py:394
  22.6 11.1 %collective-permute-start.8 = (bf16[512,256]{1,0:T(8,128)(2,1)S(1)}, bf16[512,256]{1,0:T(8,128)(2,1)S(1)}, u32[]{:S(2)}, u32[]{:S(2)}) collective-permute-start(bf16[512,256]{1,0:T(8,128)(2,1)S(1)} %get-tuple-element.64), channel_id=1, source_target_pairs={{0,6},{1,7},{2,4},{3,5},{4,2},{5,3},{6,0},{7,1},{8,14},{9,15},{10,... | collective-permute-start | bytes 786440 | tf_op jit(solution)/shard_map/ppermute | solution.py:394
  27.9 11.6 %collective-permute-start.9 = (bf16[512,256]{1,0:T(8,128)(2,1)S(1)}, bf16[512,256]{1,0:T(8,128)(2,1)S(1)}, u32[]{:S(2)}, u32[]{:S(2)}) collective-permute-start(bf16[512,256]{1,0:T(8,128)(2,1)S(1)} %get-tuple-element.72), channel_id=1, source_target_pairs={{0,2},{1,3},{2,0},{3,1},{4,6},{5,7},{6,4},{7,5},{8,10},{9,11},{10,... | collective-permute-start | bytes 786440 | tf_op jit(solution)/shard_map/ppermute | solution.py:394
  27.9 18.1 %collective-permute-start.10 = (bf16[512,256]{1,0:T(8,128)(2,1)S(1)}, bf16[512,256]{1,0:T(8,128)(2,1)S(1)}, u32[]{:S(2)}, u32[]{:S(2)}) collective-permute-start(bf16[512,256]{1,0:T(8,128)(2,1)S(1)} %get-tuple-element.74), channel_id=1, source_target_pairs={{0,4},{1,5},{2,6},{3,7},{4,0},{5,1},{6,2},{7,3},{8,12},{9,13},{10,... | collective-permute-start | bytes 786440 | tf_op jit(solution)/shard_map/ppermute | solution.py:394
  46.3 1.6 %collective-permute-start.11 = (bf16[512,256]{1,0:T(8,128)(2,1)S(1)}, bf16[512,256]{1,0:T(8,128)(2,1)S(1)}, u32[]{:S(2)}, u32[]{:S(2)}) collective-permute-start(bf16[512,256]{1,0:T(8,128)(2,1)S(1)} %shard_map.166), channel_id=1, source_target_pairs={{0,1},{1,0},{2,3},{3,2},{4,5},{5,4},{6,7},{7,6},{8,9},{9,8},{10,11... | collective-permute-start | bytes 786440 | tf_op jit(solution)/shard_map/ppermute | solution.py:454

commit v13 on v12

--- a/solution.py
+++ b/solution.py
@@ -210,11 +210,15 @@
     give[...] = jnp.where(sec_even, both[:, 1], both[:, 0]).astype(BF16)
 
 
+def turn(count):
+    return [1, *range(count, 1, -1)]
+
+
 def terms_body(keep, got, ids, own, *outs):
     pairs, blocks = keep.shape[:2]
     chip = lax.axis_index("sec") // 2
     own[...] = keep[chip] + got[chip].astype(F32)
-    for flip, out in enumerate(outs, 1):
+    for flip, out in zip(turn(len(outs)), outs):
         m = chip ^ flip
         out[:blocks, :] = (keep[m] + got[m].astype(F32)).astype(BF16)
         out[blocks:, :] = ids[flip]
@@ -223,7 +227,7 @@
 def send_body(away, own, order, ids, rec_packed, hyd_packed, *refs):
     terms, (runoff, ready, places) = refs[:-3], refs[-3:]
     places[0] = ids[0]
-    for flip, term in enumerate(terms, 1):
+    for flip, term in zip(turn(len(terms)), terms):
         places[flip] = term[term.shape[0] - PACK_ROWS :, :]
     blocks = runoff.shape[0]
     tiles = ready.shape[0] // LANES
@@ -394,7 +398,7 @@
     forward = lambda block, away: lax.ppermute(
         block, "sec", [(i, i ^ (2 * away)) for i in range(sections)]
     )
-    terms = [forward(term, flip) for flip, term in enumerate(terms, 1)]
+    terms = [forward(term, flip) for flip, term in zip(turn(len(terms)), terms)]
     rec_packed, hyd_packed = call(
         lambda *refs: first_body(aways[0], *refs),
         [shape((cap, steps), BF16)] * 2,

time: 48.9 us -> 49.1 us (level)
  waiting for transfers between devices: 18.8 us -> 19.9 us
  starting transfers between devices: 17.3 us -> 16.4 us
    ppermute x6, waiting for transfers between devices: 14.6 us -> 15.7 us  [per_device(): lax.ppermute(block, 'sec', [(i, i ^ 2 * away) for i in range(sections)])]
    ppermute x6, starting transfers between devices: 8.96 us -> 8.06 us  [per_device(): lax.ppermute(block, 'sec', [(i, i ^ 2 * away) for i in range(sections)])]
where the time goes in v13:
time: 49.1 us; the launch traced here: 49 us
  waiting for transfers between devices  19.9 us (41%)
  starting transfers between devices  16.4 us (33%)
  Pallas kernels  11.8 us (24%)
  between operations  0.77 us (2%)
    ppermute x6, waiting for transfers between devices, per_device(): lax.ppermute(block, 'sec', [(i, i ^ 2 * away) for i in range(sections)])  15.7 us
    pallas_call x12, Pallas kernels, call(): pl.pallas_call(body, out_shape=list(outs), in_specs=ins, out_specs=list(o...  11.8 us
    ppermute x6, starting transfers between devices, per_device(): lax.ppermute(block, 'sec', [(i, i ^ 2 * away) for i in range(sections)])  8.06 us
    ppermute x1, starting transfers between devices, per_device(): got_sec_far = lax.ppermute(sec_far, 'sec', between(sections))  4.71 us
    ppermute x1, waiting for transfers between devices, per_device(): got_lon_far = lax.ppermute(lon_far, 'lon', between(lons))  1.83 us
    ppermute x1, starting transfers between devices, per_device(): got_lon_near = lax.ppermute(lon_near, 'lon', swap(lons))  1.49 us
    ppermute x1, starting transfers between devices, per_device(): got_lon_far = lax.ppermute(lon_far, 'lon', between(lons))  1.49 us
    ppermute x1, waiting for transfers between devices, per_device(): passed = lax.ppermute(theirs, 'sec', swap(sections))  1.21 us
  transfers between devices with their start and end apart: 12, of which 7 were waited for; matrix products, arithmetic and copies ran while one was open for 0% of the time, Pallas kernels for 16%

profile of v13, /device:TPU:0, one launch (start us, length us, event | category | flops | bytes accessed | tf_op | source)
XLA Modules:
  0.0 49.0 jit_solution(15161479634015962885)
XLA Ops:
  0.6 1.4 %shard_map.157 = (f32[16,16,256]{2,1,0:T(8,128)S(1)}, f32[16,16,256]{2,1,0:T(8,128)S(1)}, bf16[32,256]{1,0:T(8,128)(2,1)S(1)}, bf16[32,256]{1,0:T(8,128)(2,1)S(1...) custom-call(f32[16,16,256]{2,1,0:T(8,128)} %refs_0_.3, f32[16,16,256]{2,1,0:T(8,128)} %refs_1_.1), custom_call_target="tpu_custom_call" | custom-call | bytes 524288 | tf_op jit(solution)/shard_map/pallas_call | solution.py:24
  2.0 0.5 %collective-permute-start = (bf16[32,256]{1,0:T(8,128)(2,1)S(1)}, bf16[32,256]{1,0:T(8,128)(2,1)S(1)}, u32[]{:S(2)}, u32[]{:S(2)}) collective-permute-start(bf16[32,256]{1,0:T(8,128)(2,1)S(1)} %get-tuple-element.48), channel_id=1, source_target_pairs={{0,1},{1,0},{2,3},{3,2},{4,5},{5,4},{6,7},{7,6},{8,9},{9,8},{10,11... | collective-permute-start | bytes 49160 | tf_op jit(solution)/shard_map/ppermute | solution.py:359
  2.6 4.7 %collective-permute-start.1 = (bf16[32,256]{1,0:T(8,128)(2,1)S(1)}, bf16[32,256]{1,0:T(8,128)(2,1)S(1)}, u32[]{:S(2)}, u32[]{:S(2)}) collective-permute-start(bf16[32,256]{1,0:T(8,128)(2,1)S(1)} %get-tuple-element.49), channel_id=1, source_target_pairs={{0,7},{1,2},{2,1},{3,4},{4,3},{5,6},{6,5},{7,0},{8,15},{9,10},{10,... | collective-permute-start | bytes 49160 | tf_op jit(solution)/shard_map/ppermute | solution.py:358
  7.3 1.5 %collective-permute-start.2 = (bf16[16,128]{1,0:T(8,128)(2,1)S(1)}, bf16[16,128]{1,0:T(8,128)(2,1)S(1)}, u32[]{:S(2)}, u32[]{:S(2)}) collective-permute-start(bf16[16,128]{1,0:T(8,128)(2,1)S(1)} %get-tuple-element.50), channel_id=1, source_target_pairs={{0,8},{8,0},{16,24},{24,16},{1,9},{9,1},{17,25},{25,17},{2,10},{10... | collective-permute-start | bytes 12296 | tf_op jit(solution)/shard_map/ppermute | solution.py:361
  8.8 1.5 %collective-permute-start.3 = (bf16[16,128]{1,0:T(8,128)(2,1)S(1)}, bf16[16,128]{1,0:T(8,128)(2,1)S(1)}, u32[]{:S(2)}, u32[]{:S(2)}) collective-permute-start(bf16[16,128]{1,0:T(8,128)(2,1)S(1)} %get-tuple-element.51), channel_id=1, source_target_pairs={{0,24},{8,16},{16,8},{24,0},{1,25},{9,17},{17,9},{25,1},{2,26},{10... | collective-permute-start | bytes 12296 | tf_op jit(solution)/shard_map/ppermute | solution.py:360
  10.3 1.2 %shard_map.156 = (s32[16,128]{1,0:T(8,128)S(1)}, bf16[4,16,128]{2,1,0:T(8,128)(2,1)S(1)}, f32[16,16,256]{2,1,0:T(8,128)S(1)}, f32[16,16,256]{2,1,0:T(8,128)S(1)}...) custom-call(s32[1,1,8]{2,1,0:T(1,128)} %refs_0_.2, s32[32,128]{1,0:T(8,128)} %bitcast.12, ...), custom_call_target="tpu_custom_call" | custom-call | bytes 524288 | tf_op jit(solution)/shard_map/pallas_call | solution.py:24
  11.4 1.8 %collective-permute-done.3.lon_far = bf16[16,128]{1,0:T(8,128)(2,1)S(1)} collective-permute-done((bf16[16,128]{1,0:T(8,128)(2,1)S(1)}, bf16[16,128]{1,0:T(8,128)(2,1)S(1)}, u32[]{:S(2)}, u32[]{:S(2)}) %collective-permute-start.3) | collective-permute-done | bytes 4128 | tf_op jit(solution)/shard_map/ppermute | solution.py:360
  13.3 1.1 %shard_map.158 = (f32[16,16,256]{2,1,0:T(8,128)S(1)}, f32[16,16,256]{2,1,0:T(8,128)S(1)}, f32[4,16,128]{2,1,0:T(8,128)S(1)}, bf16[4,16,128]{2,1,0:T(8,128)(2,1)S(1)}) custom-call(f32[16,16,256]{2,1,0:T(8,128)S(1)} %get-tuple-element.41.moist, f32[16,16,256]{2,1,0:T(8,128)S(1)} %get-tuple-element.42.heat, f32[16,16,256]{2,1,0:T(8,128)S(1)} %get-tuple-element.43.moist_k, ...), custom_call_target="tpu_custom_call" | custom-call | bytes 1572864 | tf_op jit(solution)/shard_map/pallas_call | solution.py:24
  14.5 1.2 %collective-permute-done.4.got = bf16[4,16,128]{2,1,0:T(8,128)(2,1)S(1)} collective-permute-done((bf16[4,16,128]{2,1,0:T(8,128)(2,1)S(1)}, bf16[4,16,128]{2,1,0:T(8,128)(2,1)S(1)}, u32[]{:S(2)}, u32[]{:S(2)}) %collective-permute-start.4) | collective-permute-done | bytes 16416 | tf_op jit(solution)/shard_map/ppermute | solution.py:388
  15.8 0.9 %collective-permute-start.6 = (bf16[32,128]{1,0:T(8,128)(2,1)S(1)}, bf16[32,128]{1,0:T(8,128)(2,1)S(1)}, u32[]{:S(2)}, u32[]{:S(2)}) collective-permute-start(bf16[32,128]{1,0:T(8,128)(2,1)S(1)} %get-tuple-element.59), channel_id=1, source_target_pairs={{0,6},{1,7},{2,4},{3,5},{4,2},{5,3},{6,0},{7,1},{8,14},{9,15},{10,... | collective-permute-start | bytes 24584 | tf_op jit(solution)/shard_map/ppermute | solution.py:398
  16.7 2.6 %collective-permute-start.7 = (bf16[32,128]{1,0:T(8,128)(2,1)S(1)}, bf16[32,128]{1,0:T(8,128)(2,1)S(1)}, u32[]{:S(2)}, u32[]{:S(2)}) collective-permute-start(bf16[32,128]{1,0:T(8,128)(2,1)S(1)} %get-tuple-element.60), channel_id=1, source_target_pairs={{0,4},{1,5},{2,6},{3,7},{4,0},{5,1},{6,2},{7,3},{8,12},{9,13},{10,... | collective-permute-start | bytes 24584 | tf_op jit(solution)/shard_map/ppermute | solution.py:398
  19.2 1.4 %shard_map.160 = (bf16[512,256]{1,0:T(8,128)(2,1)S(1)}, bf16[512,256]{1,0:T(8,128)(2,1)S(1)}) custom-call(s32[16,128]{1,0:T(8,128)S(1)} %get-tuple-element.40.refs_0_.refs_1_.refs_3_, bf16[2048,256]{1,0:T(8,128)(2,1)S(1)} %bitcast.7, bf16[2048,256]{1,0:T(8,128)(2,1)S(1)} %bitcast.9), custom_call_target="tpu_custom_call" | custom-call | flops 1073741824 | bytes 2097152 | tf_op jit(solution)/shard_map/pallas_call | solution.py:24
  20.7 0.6 %collective-permute-done.6.refs_6_ = bf16[32,128]{1,0:T(8,128)(2,1)S(1)} collective-permute-done((bf16[32,128]{1,0:T(8,128)(2,1)S(1)}, bf16[32,128]{1,0:T(8,128)(2,1)S(1)}, u32[]{:S(2)}, u32[]{:S(2)}) %collective-permute-start.6) | collective-permute-done | bytes 8224 | tf_op jit(solution)/shard_map/ppermute | solution.py:398
  21.3 0.4 shard_map.161
  21.7 3.0 %collective-permute-start.8 = (bf16[512,256]{1,0:T(8,128)(2,1)S(1)}, bf16[512,256]{1,0:T(8,128)(2,1)S(1)}, u32[]{:S(2)}, u32[]{:S(2)}) collective-permute-start(bf16[512,256]{1,0:T(8,128)(2,1)S(1)} %get-tuple-element.64), channel_id=1, source_target_pairs={{0,6},{1,7},{2,4},{3,5},{4,2},{5,3},{6,0},{7,1},{8,14},{9,15},{10,... | collective-permute-start | bytes 786440 | tf_op jit(solution)/shard_map/ppermute | solution.py:398
  24.6 1.7 %shard_map.162 = (bf16[2048,256]{1,0:T(8,128)(2,1)S(1)}, bf16[512,256]{1,0:T(8,128)(2,1)S(1)}, bf16[512,256]{1,0:T(8,128)(2,1)S(1)}) custom-call(f32[16,128]{1,0:T(8,128)S(1)} %get-tuple-element.61.refs_0_, bf16[2048,256]{1,0:T(8,128)(2,1)S(1)} %bitcast.8, bf16[2048,256]{1,0:T(8,128)(2,1)S(1)} %bitcast.10, ...), custom_call_target="tpu_custom_call" | custom-call | flops 536870912 | bytes 4194304 | tf_op jit(solution)/shard_map/pallas_call | solution.py:24
  26.6 1.3 %collective-permute-start.10 = (bf16[512,256]{1,0:T(8,128)(2,1)S(1)}, bf16[512,256]{1,0:T(8,128)(2,1)S(1)}, u32[]{:S(2)}, u32[]{:S(2)}) collective-permute-start(bf16[512,256]{1,0:T(8,128)(2,1)S(1)} %get-tuple-element.74), channel_id=1, source_target_pairs={{0,4},{1,5},{2,6},{3,7},{4,0},{5,1},{6,2},{7,3},{8,12},{9,13},{10,... | collective-permute-start | bytes 786440 | tf_op jit(solution)/shard_map/ppermute | solution.py:398
  27.9 4.8 %collective-permute-done.8.refs_3_ = bf16[512,256]{1,0:T(8,128)(2,1)S(1)} collective-permute-done((bf16[512,256]{1,0:T(8,128)(2,1)S(1)}, bf16[512,256]{1,0:T(8,128)(2,1)S(1)}, u32[]{:S(2)}, u32[]{:S(2)}) %collective-permute-start.8) | collective-permute-done | bytes 262176 | tf_op jit(solution)/shard_map/ppermute | solution.py:398
  32.8 2.7 %shard_map.163 = (bf16[2048,256]{1,0:T(8,128)(2,1)}, f32[16,16,256]{2,1,0:T(8,128)}, f32[16,16,256]{2,1,0:T(8,128)}, f32[512,256]{1,0:T(8,128)S(1)}, f32[512,256]{1,0:T(8,128)S(1)}) custom-call(s32[16,128]{1,0:T(8,128)S(1)} %get-tuple-element.40.refs_0_.refs_1_.refs_3_, bf16[2048,256]{1,0:T(8,128)(2,1)S(1)} %get-tuple-element.62.refs_1_, ...), custom_call_target="tpu_custom_call" | custom-call | flops 536870912 | bytes 2097152 | tf_op jit(solution)/shard_map/pallas_call | solution.py:24
  35.5 2.2 %collective-permute-done.9.refs_3_ = bf16[512,256]{1,0:T(8,128)(2,1)S(1)} collective-permute-done((bf16[512,256]{1,0:T(8,128)(2,1)S(1)}, bf16[512,256]{1,0:T(8,128)(2,1)S(1)}, u32[]{:S(2)}, u32[]{:S(2)}) %collective-permute-start.9) | collective-permute-done | bytes 262176 | tf_op jit(solution)/shard_map/ppermute | solution.py:398
  37.7 0.5 shard_map.164
  38.2 8.0 %collective-permute-done.10.refs_2_ = bf16[512,256]{1,0:T(8,128)(2,1)S(1)} collective-permute-done((bf16[512,256]{1,0:T(8,128)(2,1)S(1)}, bf16[512,256]{1,0:T(8,128)(2,1)S(1)}, u32[]{:S(2)}, u32[]{:S(2)}) %collective-permute-start.10) | collective-permute-done | bytes 262176 | tf_op jit(solution)/shard_map/ppermute | solution.py:398
  46.9 1.2 %collective-permute-done.11.passed = bf16[512,256]{1,0:T(8,128)(2,1)S(1)} collective-permute-done((bf16[512,256]{1,0:T(8,128)(2,1)S(1)}, bf16[512,256]{1,0:T(8,128)(2,1)S(1)}, u32[]{:S(2)}, u32[]{:S(2)}) %collective-permute-start.11) | collective-permute-done | bytes 262176 | tf_op jit(solution)/shard_map/ppermute | solution.py:458
  48.1 0.8 %shard_map.167 = f32[512,256]{1,0:T(8,128)} custom-call(f32[512,256]{1,0:T(8,128)S(1)} %shard_map.165.mine, bf16[512,256]{1,0:T(8,128)(2,1)S(1)} %collective-permute-done.11.passed), custom_call_target="tpu_custom_call" | custom-call | bytes 1310720 | tf_op jit(solution)/shard_map/pallas_call | solution.py:24
  (16 shorter events, 1.1 us)
Async XLA Ops:
  0.6 18.6 %copy-start.1 = (bf16[1,2048,256]{2,1,0:T(8,128)(2,1)S(1)}, bf16[1,2048,256]{2,1,0:T(8,128)(2,1)}, u32[]{:S(2)}) copy-start(bf16[1,2048,256]{2,1,0:T(8,128)(2,1)} %param.21) | copy-start | bytes 3145732
  2.0 17.2 %copy-start = (bf16[1,2048,256]{2,1,0:T(8,128)(2,1)S(1)}, bf16[1,2048,256]{2,1,0:T(8,128)(2,1)}, u32[]{:S(2)}) copy-start(bf16[1,2048,256]{2,1,0:T(8,128)(2,1)} %param.20) | copy-start | bytes 3145732
  2.0 11.2 %collective-permute-start = (bf16[32,256]{1,0:T(8,128)(2,1)S(1)}, bf16[32,256]{1,0:T(8,128)(2,1)S(1)}, u32[]{:S(2)}, u32[]{:S(2)}) collective-permute-start(bf16[32,256]{1,0:T(8,128)(2,1)S(1)} %get-tuple-element.48), channel_id=1, source_target_pairs={{0,1},{1,0},{2,3},{3,2},{4,5},{5,4},{6,7},{7,6},{8,9},{9,8},{10,11... | collective-permute-start | bytes 49160 | tf_op jit(solution)/shard_map/ppermute | solution.py:359
  2.6 10.7 %collective-permute-start.1 = (bf16[32,256]{1,0:T(8,128)(2,1)S(1)}, bf16[32,256]{1,0:T(8,128)(2,1)S(1)}, u32[]{:S(2)}, u32[]{:S(2)}) collective-permute-start(bf16[32,256]{1,0:T(8,128)(2,1)S(1)} %get-tuple-element.49), channel_id=1, source_target_pairs={{0,7},{1,2},{2,1},{3,4},{4,3},{5,6},{6,5},{7,0},{8,15},{9,10},{10,... | collective-permute-start | bytes 49160 | tf_op jit(solution)/shard_map/ppermute | solution.py:358
  7.3 4.2 %collective-permute-start.2 = (bf16[16,128]{1,0:T(8,128)(2,1)S(1)}, bf16[16,128]{1,0:T(8,128)(2,1)S(1)}, u32[]{:S(2)}, u32[]{:S(2)}) collective-permute-start(bf16[16,128]{1,0:T(8,128)(2,1)S(1)} %get-tuple-element.50), channel_id=1, source_target_pairs={{0,8},{8,0},{16,24},{24,16},{1,9},{9,1},{17,25},{25,17},{2,10},{10... | collective-permute-start | bytes 12296 | tf_op jit(solution)/shard_map/ppermute | solution.py:361
  8.8 4.5 %collective-permute-start.3 = (bf16[16,128]{1,0:T(8,128)(2,1)S(1)}, bf16[16,128]{1,0:T(8,128)(2,1)S(1)}, u32[]{:S(2)}, u32[]{:S(2)}) collective-permute-start(bf16[16,128]{1,0:T(8,128)(2,1)S(1)} %get-tuple-element.51), channel_id=1, source_target_pairs={{0,24},{8,16},{16,8},{24,0},{1,25},{9,17},{17,9},{25,1},{2,26},{10... | collective-permute-start | bytes 12296 | tf_op jit(solution)/shard_map/ppermute | solution.py:360
  14.4 1.2 %collective-permute-start.4 = (bf16[4,16,128]{2,1,0:T(8,128)(2,1)S(1)}, bf16[4,16,128]{2,1,0:T(8,128)(2,1)S(1)}, u32[]{:S(2)}, u32[]{:S(2)}) collective-permute-start(bf16[4,16,128]{2,1,0:T(8,128)(2,1)S(1)} %get-tuple-element.53), channel_id=1, source_target_pairs={{0,1},{1,0},{2,3},{3,2},{4,5},{5,4},{6,7},{7,6},{8,9},{9,8},{10,11... | collective-permute-start | bytes 49160 | tf_op jit(solution)/shard_map/ppermute | solution.py:388
  15.7 5.0 %collective-permute-start.5 = (bf16[32,128]{1,0:T(8,128)(2,1)S(1)}, bf16[32,128]{1,0:T(8,128)(2,1)S(1)}, u32[]{:S(2)}, u32[]{:S(2)}) collective-permute-start(bf16[32,128]{1,0:T(8,128)(2,1)S(1)} %get-tuple-element.58), channel_id=1, source_target_pairs={{0,2},{1,3},{2,0},{3,1},{4,6},{5,7},{6,4},{7,5},{8,10},{9,11},{10,... | collective-permute-start | bytes 24584 | tf_op jit(solution)/shard_map/ppermute | solution.py:398
  15.8 5.5 %collective-permute-start.6 = (bf16[32,128]{1,0:T(8,128)(2,1)S(1)}, bf16[32,128]{1,0:T(8,128)(2,1)S(1)}, u32[]{:S(2)}, u32[]{:S(2)}) collective-permute-start(bf16[32,128]{1,0:T(8,128)(2,1)S(1)} %get-tuple-element.59), channel_id=1, source_target_pairs={{0,6},{1,7},{2,4},{3,5},{4,2},{5,3},{6,0},{7,1},{8,14},{9,15},{10,... | collective-permute-start | bytes 24584 | tf_op jit(solution)/shard_map/ppermute | solution.py:398
  16.7 4.6 %collective-permute-start.7 = (bf16[32,128]{1,0:T(8,128)(2,1)S(1)}, bf16[32,128]{1,0:T(8,128)(2,1)S(1)}, u32[]{:S(2)}, u32[]{:S(2)}) collective-permute-start(bf16[32,128]{1,0:T(8,128)(2,1)S(1)} %get-tuple-element.60), channel_id=1, source_target_pairs={{0,4},{1,5},{2,6},{3,7},{4,0},{5,1},{6,2},{7,3},{8,12},{9,13},{10,... | collective-permute-start | bytes 24584 | tf_op jit(solution)/shard_map/ppermute | solution.py:398
  21.7 11.1 %collective-permute-start.8 = (bf16[512,256]{1,0:T(8,128)(2,1)S(1)}, bf16[512,256]{1,0:T(8,128)(2,1)S(1)}, u32[]{:S(2)}, u32[]{:S(2)}) collective-permute-start(bf16[512,256]{1,0:T(8,128)(2,1)S(1)} %get-tuple-element.64), channel_id=1, source_target_pairs={{0,6},{1,7},{2,4},{3,5},{4,2},{5,3},{6,0},{7,1},{8,14},{9,15},{10,... | collective-permute-start | bytes 786440 | tf_op jit(solution)/shard_map/ppermute | solution.py:398
  26.4 11.4 %collective-permute-start.9 = (bf16[512,256]{1,0:T(8,128)(2,1)S(1)}, bf16[512,256]{1,0:T(8,128)(2,1)S(1)}, u32[]{:S(2)}, u32[]{:S(2)}) collective-permute-start(bf16[512,256]{1,0:T(8,128)(2,1)S(1)} %get-tuple-element.72), channel_id=1, source_target_pairs={{0,2},{1,3},{2,0},{3,1},{4,6},{5,7},{6,4},{7,5},{8,10},{9,11},{10,... | collective-permute-start | bytes 786440 | tf_op jit(solution)/shard_map/ppermute | solution.py:398
  26.6 19.6 %collective-permute-start.10 = (bf16[512,256]{1,0:T(8,128)(2,1)S(1)}, bf16[512,256]{1,0:T(8,128)(2,1)S(1)}, u32[]{:S(2)}, u32[]{:S(2)}) collective-permute-start(bf16[512,256]{1,0:T(8,128)(2,1)S(1)} %get-tuple-element.74), channel_id=1, source_target_pairs={{0,4},{1,5},{2,6},{3,7},{4,0},{5,1},{6,2},{7,3},{8,12},{9,13},{10,... | collective-permute-start | bytes 786440 | tf_op jit(solution)/shard_map/ppermute | solution.py:398
  46.5 1.6 %collective-permute-start.11 = (bf16[512,256]{1,0:T(8,128)(2,1)S(1)}, bf16[512,256]{1,0:T(8,128)(2,1)S(1)}, u32[]{:S(2)}, u32[]{:S(2)}) collective-permute-start(bf16[512,256]{1,0:T(8,128)(2,1)S(1)} %shard_map.166), channel_id=1, source_target_pairs={{0,1},{1,0},{2,3},{3,2},{4,5},{5,4},{6,7},{7,6},{8,9},{9,8},{10,11... | collective-permute-start | bytes 786440 | tf_op jit(solution)/shard_map/ppermute | solution.py:458
